TPU v7x, 32 devices: a whole 2x2x4 slice. The times are simulated.
32 devices in a mesh: utt: 8 (over z, core), wide: 4 (over y, x).
Axes of the slice: x: 2, y: 2, z: 4, core: 2. Of those that a mesh axis runs over, the one named last changes fastest.
Arguments:
- frames: bfloat16 [16, 1024, 1024], P('utt', 'wide'), may hold values from -6 to 6
- lengths: int32 [16], P('utt'), may hold values from 512 to 1024, as said below
- masked: int32 [16, 1024], P('utt', 'wide'), may hold values from 0 to 1, as said below
- cotangent: bfloat16 [16, 1024, 1024], P('utt', 'wide'), may hold values from -6 to 6
- first_gain: bfloat16 [1024], replicated, may hold values from 0.25 to 1.75
- first_up: bfloat16 [4096, 1024], P(('utt', 'wide')), may hold values from -0.1875 to 0.1875
- first_down: bfloat16 [4096, 1024], P(('utt', 'wide')), may hold values from -0.09375 to 0.09375
- attn_gain: bfloat16 [1024], replicated, may hold values from 0.25 to 1.75
- query_weight: bfloat16 [1024, 1024], P('wide'), may hold values from -0.1875 to 0.1875
- key_weight: bfloat16 [1024, 1024], P('wide'), may hold values from -0.1875 to 0.1875
- value_weight: bfloat16 [1024, 1024], P('wide'), may hold values from -0.1875 to 0.1875
- out_weight: bfloat16 [1024, 1024], P('wide'), may hold values from -2 to 2
- place_weight: bfloat16 [1024, 1024], P('wide'), may hold values from -0.1875 to 0.1875
- content_bias: bfloat16 [1024], P('wide'), may hold values from -3 to 3
- place_bias: bfloat16 [1024], P('wide'), may hold values from -3 to 3
- conv_gain: bfloat16 [1024], replicated, may hold values from 0.25 to 1.75
- glu_weight: bfloat16 [2048, 1024], P('wide'), may hold values from -0.1875 to 0.1875
- depth_kernel: bfloat16 [31, 1024], replicated, may hold values from -1 to 1
- middle_gain: bfloat16 [1024], replicated, may hold values from 0.25 to 1.75
- point_weight: bfloat16 [1024, 1024], P('wide'), may hold values from -0.1875 to 0.1875
- second_gain: bfloat16 [1024], replicated, may hold values from 0.25 to 1.75
- second_up: bfloat16 [4096, 1024], P(('utt', 'wide')), may hold values from -0.1875 to 0.1875
- second_down: bfloat16 [4096, 1024], P(('utt', 'wide')), may hold values from -0.09375 to 0.09375
- final_gain: bfloat16 [1024], replicated, may hold values from 0.25 to 1.75
Outputs:
- output: bfloat16 [16, 1024, 1024], P('utt', 'wide')
- grad_frames: bfloat16 [16, 1024, 1024], P('utt', 'wide')
- grad_first_gain: float32 [1024], replicated
- grad_first_up: float32 [4096, 1024], P(('utt', 'wide'))
- grad_first_down: float32 [4096, 1024], P(('utt', 'wide'))
- grad_attn_gain: float32 [1024], replicated
- grad_query_weight: float32 [1024, 1024], P('wide')
- grad_key_weight: float32 [1024, 1024], P('wide')
- grad_value_weight: float32 [1024, 1024], P('wide')
- grad_out_weight: float32 [1024, 1024], P('wide')
- grad_place_weight: float32 [1024, 1024], P('wide')
- grad_content_bias: float32 [1024], P('wide')
- grad_place_bias: float32 [1024], P('wide')
- grad_conv_gain: float32 [1024], replicated
- grad_glu_weight: float32 [2048, 1024], P('wide')
- grad_depth_kernel: float32 [31, 1024], replicated
- grad_middle_gain: float32 [1024], replicated
- grad_point_weight: float32 [1024, 1024], P('wide')
- grad_second_gain: float32 [1024], replicated
- grad_second_up: float32 [4096, 1024], P(('utt', 'wide'))
- grad_second_down: float32 [4096, 1024], P(('utt', 'wide'))
- grad_final_gain: float32 [1024], replicated
Inputs may be any that keep to these rules, and one draw needn't show every extreme that they name: `lengths`: in each aligned block of 2 utterances (one index of utt) one utterance has exactly 1024 frames. Each utterance has its own share of masked frames; most shares are small, a few are large; frames past an utterance's length may be marked and count as unmasked.
All inputs are finite; a program needn't handle non-finite values.
Results may differ from a plain program's by a relative error of at most 0.023.
Values may be sent and summed in bfloat16 or wider, within the bound.
A program may use at most 320 MiB of HBM per device.

v0:
```python
from functools import partial
import math

import jax
import jax.numpy as jnp
from jax import lax
from jax.sharding import PartitionSpec as P

HEAD_DIM = 64
KERNEL = 31
QBLK = 512
RIM = 15


EPSILON = 1e-05
MASKED_SCORE = -1e30


def with_halo(block, sides, width):
    for axis, dim in sides:
        count = lax.axis_size(axis)
        forward = [(i, i + 1) for i in range(count - 1)]
        backward = [(target, source) for source, target in forward]
        low = lax.ppermute(
            lax.slice_in_dim(block, block.shape[dim] - width, None, axis=dim), axis, forward
        )
        high = lax.ppermute(lax.slice_in_dim(block, 0, width, axis=dim), axis, backward)
        block = jnp.concatenate([low, block, high], axis=dim)
    return block


def norm_rows(values, gain_vec):
    average = jnp.mean(values, axis=-1, keepdims=True)
    centred = values - average
    spread = jnp.mean(centred * centred, axis=-1, keepdims=True)
    return centred * lax.rsqrt(spread + EPSILON) * gain_vec


def silu_slope(before):
    squash = jax.nn.sigmoid(before)
    return squash * (1.0 + before * (1.0 - squash))


def mult_trans(first_mat, second_mat):
    return lax.dot_general(
        first_mat, second_mat, (((1,), (1,)), ((), ())), preferred_element_type=jnp.float32
    )


def mult_plain(first_mat, second_mat):
    return jnp.dot(first_mat, second_mat, preferred_element_type=jnp.float32)


def mult_rows(first_mat, second_mat):
    return lax.dot_general(
        first_mat, second_mat, (((0,), (0,)), ((), ())), preferred_element_type=jnp.float32
    )


def relative_table(length, channels):
    offsets = length - 1 - jnp.arange(2 * length - 1).astype(jnp.float32)
    rates = jnp.exp(
        jnp.arange(channels // 2).astype(jnp.float32) * (-2.0 * math.log(10000.0) / channels)
    )
    angles = offsets[:, None] * rates[None, :]
    return jnp.concatenate([jnp.sin(angles), jnp.cos(angles)], axis=1)


def skew_rows(reversed_scores):
    block_rows, span = reversed_scores.shape
    flat = reversed_scores.reshape(-1)[block_rows - 1 : block_rows - 1 + block_rows * (span - 1)]
    return flat.reshape(block_rows, span - 1)[:, : span - block_rows + 1]


def unskew_rows(grad_scores, span):
    block_rows, length = grad_scores.shape
    padded = jnp.pad(grad_scores, ((0, 0), (0, span - 1 - length)))
    flat = jnp.pad(padded.reshape(-1), (block_rows - 1, 1))
    return flat.reshape(block_rows, span)


def gather_ffn(up_rows, down_rows):
    return (
        lax.all_gather(up_rows, ("utt", "wide"), axis=0, tiled=True),
        lax.all_gather(down_rows, ("utt", "wide"), axis=0, tiled=True),
    )


def sum_ffn(grad_up, grad_down):
    return (
        lax.psum_scatter(grad_up, ("utt", "wide"), scatter_dimension=0, tiled=True),
        lax.psum_scatter(grad_down, ("utt", "wide"), scatter_dimension=0, tiled=True),
    )


def ffn_forward(stream, gain_vec, up_full, down_full):
    normed, norm_pull = jax.vjp(norm_rows, stream, gain_vec)
    normed_low = normed.astype(jnp.bfloat16)
    before = mult_trans(normed_low, up_full)
    active_low = jax.nn.silu(before).astype(jnp.bfloat16)
    return (
        stream + 0.5 * mult_plain(active_low, down_full),
        (norm_pull, normed_low, before, active_low),
    )


def ffn_backward(grad_stream, saved_ffn, up_full, down_full):
    norm_pull, normed_low, before, active_low = saved_ffn
    grad_out = (0.5 * grad_stream).astype(jnp.bfloat16)
    grad_down = mult_rows(active_low, grad_out)
    grad_before = (mult_trans(grad_out, down_full) * silu_slope(before)).astype(jnp.bfloat16)
    grad_up = mult_rows(grad_before, normed_low)
    grad_input, grad_gain = norm_pull(mult_plain(grad_before, up_full))
    return (grad_stream + grad_input, grad_gain, grad_up, grad_down)


def head_forward(
    query_rows,
    key_rows,
    value_rows,
    place_rows,
    bias_first,
    bias_second,
    key_ok,
    block_rows,
    score_scale,
):
    length, head_width = query_rows.shape
    with_u = (query_rows.astype(jnp.float32) + bias_first).astype(jnp.bfloat16)
    with_v = (query_rows.astype(jnp.float32) + bias_second).astype(jnp.bfloat16)

    def one_block(block_index):
        first_row = block_index * block_rows
        block_u = lax.dynamic_slice_in_dim(with_u, first_row, block_rows, 0)
        block_v = lax.dynamic_slice_in_dim(with_v, first_row, block_rows, 0)
        near_rows = lax.dynamic_slice_in_dim(
            place_rows, length - block_rows - first_row, block_rows + length - 1, 0
        )
        scores = (
            mult_trans(block_u, key_rows) + skew_rows(mult_trans(block_v, near_rows))
        ) * score_scale
        scores = jnp.where(key_ok[None, :], scores, MASKED_SCORE)
        highest = jnp.max(scores, axis=1, keepdims=True)
        weights = jnp.exp(scores - highest)
        running = jnp.sum(weights, axis=1, keepdims=True)
        attend_prob = (weights / running).astype(jnp.bfloat16)
        return (
            mult_plain(attend_prob, value_rows).astype(jnp.bfloat16),
            (highest + jnp.log(running))[:, 0],
        )

    attended, log_total = lax.map(one_block, jnp.arange(length // block_rows, dtype=jnp.int32))
    return (attended.reshape(length, head_width), log_total.reshape(length))


def head_backward(
    query_rows,
    key_rows,
    value_rows,
    place_rows,
    bias_first,
    bias_second,
    key_ok,
    log_total,
    grad_mixed,
    block_rows,
    score_scale,
):
    length, head_width = query_rows.shape
    span = block_rows + length - 1
    with_u = (query_rows.astype(jnp.float32) + bias_first).astype(jnp.bfloat16)
    with_v = (query_rows.astype(jnp.float32) + bias_second).astype(jnp.bfloat16)

    def one_block(carried, block_index):
        grad_key, grad_value, grad_place = carried
        first_row = block_index * block_rows
        place_first = length - block_rows - first_row
        block_u = lax.dynamic_slice_in_dim(with_u, first_row, block_rows, 0)
        block_v = lax.dynamic_slice_in_dim(with_v, first_row, block_rows, 0)
        near_rows = lax.dynamic_slice_in_dim(place_rows, place_first, span, 0)
        block_total = lax.dynamic_slice_in_dim(log_total, first_row, block_rows, 0)
        block_grad = lax.dynamic_slice_in_dim(grad_mixed, first_row, block_rows, 0)
        scores = (
            mult_trans(block_u, key_rows) + skew_rows(mult_trans(block_v, near_rows))
        ) * score_scale
        scores = jnp.where(key_ok[None, :], scores, MASKED_SCORE)
        attend_prob = jnp.exp(scores - block_total[:, None])
        grad_prob = mult_trans(block_grad, value_rows)
        inner = jnp.sum(attend_prob * grad_prob, axis=1, keepdims=True)
        grad_score = jnp.where(key_ok[None, :], attend_prob * (grad_prob - inner), 0.0).astype(
            jnp.bfloat16
        )
        grad_value = grad_value + mult_rows(attend_prob.astype(jnp.bfloat16), block_grad)
        grad_with_u = mult_plain(grad_score, key_rows) * score_scale
        grad_key = grad_key + mult_rows(grad_score, block_u) * score_scale
        spread_grad = unskew_rows(grad_score, span)
        grad_with_v = mult_plain(spread_grad, near_rows) * score_scale
        place_part = (
            lax.dynamic_slice_in_dim(grad_place, place_first, span, 0)
            + mult_rows(spread_grad, block_v) * score_scale
        )
        grad_place = lax.dynamic_update_slice_in_dim(grad_place, place_part, place_first, 0)
        return ((grad_key, grad_value, grad_place), (grad_with_u, grad_with_v))

    zero_rows = jnp.zeros((length, head_width), jnp.float32)
    zero_place = jnp.zeros((2 * length - 1, head_width), jnp.float32)
    (grad_key, grad_value, grad_place), (grad_with_u, grad_with_v) = lax.scan(
        one_block,
        (zero_rows, zero_rows, zero_place),
        jnp.arange(length // block_rows, dtype=jnp.int32),
    )
    grad_with_u = grad_with_u.reshape(length, head_width)
    grad_with_v = grad_with_v.reshape(length, head_width)
    grad_query = (grad_with_u + grad_with_v).astype(jnp.bfloat16)
    return (
        grad_query,
        grad_key.astype(jnp.bfloat16),
        grad_value.astype(jnp.bfloat16),
        grad_place.astype(jnp.bfloat16),
        jnp.sum(grad_with_u, axis=0),
        jnp.sum(grad_with_v, axis=0),
    )


def per_device(
    frames,
    lengths,
    masked,
    cotangent,
    first_gain,
    first_up,
    first_down,
    attn_gain,
    query_weight,
    key_weight,
    value_weight,
    out_weight,
    place_weight,
    content_bias,
    place_bias,
    conv_gain,
    glu_weight,
    depth_kernel,
    middle_gain,
    point_weight,
    second_gain,
    second_up,
    second_down,
    final_gain,
):
    groups, frames_dev, channels = frames.shape
    row_count = groups * frames_dev
    length = frames_dev * lax.axis_size("wide")
    score_scale = 1.0 / math.sqrt(HEAD_DIM)
    positions = lax.axis_index("wide") * frames_dev + jnp.arange(frames_dev, dtype=jnp.int32)
    frame_grid = (positions[None, :] < lengths[:, None]).astype(jnp.float32)
    frame_ok = frame_grid.reshape(row_count, 1)
    key_ok = jnp.arange(length, dtype=jnp.int32)[None, :] < lengths[:, None]
    stream0 = frames.reshape(row_count, channels).astype(jnp.float32)
    up_first, down_first = gather_ffn(first_up, first_down)
    stream1, saved_first = ffn_forward(
        stream0, first_gain.astype(jnp.float32), up_first, down_first
    )
    full_query, full_key, full_value, full_out, full_glu, full_point = (
        lax.all_gather(query_weight, "wide", axis=0, tiled=True),
        lax.all_gather(key_weight, "wide", axis=0, tiled=True),
        lax.all_gather(value_weight, "wide", axis=0, tiled=True),
        lax.all_gather(out_weight, "wide", axis=0, tiled=True),
        lax.all_gather(glu_weight, "wide", axis=0, tiled=True),
        lax.all_gather(point_weight, "wide", axis=0, tiled=True),
    )
    normed_attn, attn_pull = jax.vjp(norm_rows, stream1, attn_gain.astype(jnp.float32))
    attn_low = normed_attn.astype(jnp.bfloat16)
    query_frames = (
        mult_trans(attn_low, full_query).astype(jnp.bfloat16).reshape(groups, frames_dev, -1)
    )
    key_frames = mult_trans(attn_low, full_key).astype(jnp.bfloat16).reshape(groups, frames_dev, -1)
    value_frames = (
        mult_trans(attn_low, full_value).astype(jnp.bfloat16).reshape(groups, frames_dev, -1)
    )
    heads_query, heads_key, heads_value = (
        lax.all_to_all(query_frames, "wide", split_axis=2, concat_axis=1, tiled=True),
        lax.all_to_all(key_frames, "wide", split_axis=2, concat_axis=1, tiled=True),
        lax.all_to_all(value_frames, "wide", split_axis=2, concat_axis=1, tiled=True),
    )
    local_width = heads_query.shape[2]
    head_count = local_width // HEAD_DIM
    rel_table = relative_table(length, channels).astype(jnp.bfloat16)
    place_rows = (
        mult_trans(rel_table, place_weight)
        .astype(jnp.bfloat16)
        .reshape(2 * length - 1, head_count, HEAD_DIM)
    )
    bias_first = content_bias.astype(jnp.float32).reshape(head_count, HEAD_DIM)
    bias_second = place_bias.astype(jnp.float32).reshape(head_count, HEAD_DIM)
    split_query = heads_query.reshape(groups, length, head_count, HEAD_DIM)
    split_key = heads_key.reshape(groups, length, head_count, HEAD_DIM)
    split_value = heads_value.reshape(groups, length, head_count, HEAD_DIM)
    forward_heads = jax.vmap(
        partial(head_forward, block_rows=QBLK, score_scale=score_scale),
        in_axes=(1, 1, 1, 1, 0, 0, None),
        out_axes=(1, 0),
    )

    def attend_utt(unit_items):
        return forward_heads(
            unit_items[0],
            unit_items[1],
            unit_items[2],
            place_rows,
            bias_first,
            bias_second,
            unit_items[3],
        )

    attended, log_total = lax.map(attend_utt, (split_query, split_key, split_value, key_ok))
    framed = lax.all_to_all(
        attended.reshape(groups, length, local_width),
        "wide",
        split_axis=1,
        concat_axis=2,
        tiled=True,
    ).reshape(row_count, -1)
    stream2 = stream1 + mult_plain(framed, full_out)
    normed_conv, conv_pull = jax.vjp(norm_rows, stream2, conv_gain.astype(jnp.float32))
    conv_low = normed_conv.astype(jnp.bfloat16)
    glu_in = mult_trans(conv_low, full_glu)
    linear = glu_in[:, :channels]
    gating = jax.nn.sigmoid(glu_in[:, channels:])
    gated = (linear * gating * frame_ok).astype(jnp.bfloat16).reshape(groups, frames_dev, channels)
    padded = with_halo(gated, (("wide", 1),), RIM)
    kernel_f = depth_kernel.astype(jnp.float32)
    conv_out = jnp.zeros((groups, frames_dev, channels), jnp.float32)
    for offset in range(KERNEL):
        conv_out = conv_out + padded[:, offset : offset + frames_dev, :] * kernel_f[offset]
    conv_out = conv_out.reshape(row_count, channels)
    middle, middle_pull = jax.vjp(norm_rows, conv_out, middle_gain.astype(jnp.float32))
    swished = jax.nn.silu(middle).astype(jnp.bfloat16)
    stream3 = stream2 + mult_trans(swished, full_point)
    up_second, down_second = gather_ffn(second_up, second_down)
    stream4, saved_second = ffn_forward(
        stream3, second_gain.astype(jnp.float32), up_second, down_second
    )
    final_rows, final_pull = jax.vjp(norm_rows, stream4, final_gain.astype(jnp.float32))
    output = final_rows.astype(jnp.bfloat16).reshape(groups, frames_dev, channels)
    seed_weight = (masked.astype(jnp.float32) * frame_grid).reshape(row_count, 1)
    seed_grad = cotangent.reshape(row_count, channels).astype(jnp.float32) * seed_weight
    grad4, grad_final_gain = final_pull(seed_grad)
    back_up_second, back_down_second = gather_ffn(second_up, second_down)
    grad3, grad_second_gain, grad_up_second, grad_down_second = ffn_backward(
        grad4, saved_second, back_up_second, back_down_second
    )
    summed_second = sum_ffn(grad_up_second, grad_down_second)
    grad_branch = grad3.astype(jnp.bfloat16)
    grad_point = mult_rows(grad_branch, swished)
    grad_middle = mult_plain(grad_branch, full_point) * silu_slope(middle)
    grad_conv, grad_middle_gain = middle_pull(grad_middle)
    conv_grad_low = grad_conv.astype(jnp.bfloat16).reshape(groups, frames_dev, channels)
    grad_padded = with_halo(conv_grad_low, (("wide", 1),), RIM)
    grad_gated = jnp.zeros((groups, frames_dev, channels), jnp.float32)
    kernel_rows = []
    for offset in range(KERNEL):
        grad_gated = (
            grad_gated
            + grad_padded[:, 2 * RIM - offset : 2 * RIM - offset + frames_dev, :] * kernel_f[offset]
        )
        kernel_rows.append(
            jnp.einsum(
                "rzn,rzn->n",
                padded[:, offset : offset + frames_dev, :],
                conv_grad_low,
                preferred_element_type=jnp.float32,
            )
        )
    grad_kernel = jnp.stack(kernel_rows)
    grad_gated = grad_gated.reshape(row_count, channels) * frame_ok
    grad_glu_in = jnp.concatenate(
        [grad_gated * gating, grad_gated * linear * gating * (1.0 - gating)], axis=1
    ).astype(jnp.bfloat16)
    grad_glu = mult_rows(grad_glu_in, conv_low)
    grad_conv_in, grad_conv_gain = conv_pull(mult_plain(grad_glu_in, full_glu))
    grad2 = grad3 + grad_conv_in
    grad_attn = grad2.astype(jnp.bfloat16)
    grad_out = mult_rows(framed, grad_attn)
    grad_framed = (
        mult_trans(grad_attn, full_out).astype(jnp.bfloat16).reshape(groups, frames_dev, -1)
    )
    grad_heads = lax.all_to_all(grad_framed, "wide", split_axis=2, concat_axis=1, tiled=True)
    backward_heads = jax.vmap(
        partial(head_backward, block_rows=QBLK, score_scale=score_scale),
        in_axes=(1, 1, 1, 1, 0, 0, None, 0, 1),
        out_axes=(1, 1, 1, 1, 0, 0),
    )

    def attend_back(unit_items):
        return backward_heads(
            unit_items[0],
            unit_items[1],
            unit_items[2],
            place_rows,
            bias_first,
            bias_second,
            unit_items[3],
            unit_items[4],
            unit_items[5],
        )

    grad_query_h, grad_key_h, grad_value_h, grad_place_h, grad_bias_first, grad_bias_second = (
        lax.map(
            attend_back,
            (
                split_query,
                split_key,
                split_value,
                key_ok,
                log_total,
                grad_heads.reshape(groups, length, head_count, HEAD_DIM),
            ),
        )
    )
    back_query, back_key, back_value = (
        lax.all_to_all(
            grad_query_h.reshape(groups, length, local_width),
            "wide",
            split_axis=1,
            concat_axis=2,
            tiled=True,
        ),
        lax.all_to_all(
            grad_key_h.reshape(groups, length, local_width),
            "wide",
            split_axis=1,
            concat_axis=2,
            tiled=True,
        ),
        lax.all_to_all(
            grad_value_h.reshape(groups, length, local_width),
            "wide",
            split_axis=1,
            concat_axis=2,
            tiled=True,
        ),
    )
    back_query = back_query.reshape(row_count, -1)
    back_key = back_key.reshape(row_count, -1)
    back_value = back_value.reshape(row_count, -1)
    grad_query_w = mult_rows(back_query, attn_low)
    grad_key_w = mult_rows(back_key, attn_low)
    grad_value_w = mult_rows(back_value, attn_low)
    grad_normed = (
        mult_plain(back_query, full_query)
        + mult_plain(back_key, full_key)
        + mult_plain(back_value, full_value)
    )
    grad_attn_in, grad_attn_gain = attn_pull(grad_normed)
    grad1 = grad2 + grad_attn_in
    grad_place_w = jnp.einsum(
        "urc,rd->cd",
        grad_place_h.reshape(groups, 2 * length - 1, local_width),
        rel_table,
        preferred_element_type=jnp.float32,
    )
    grad_content = jnp.sum(grad_bias_first, axis=0).reshape(local_width)
    grad_place_b = jnp.sum(grad_bias_second, axis=0).reshape(local_width)
    back_up_first, back_down_first = gather_ffn(first_up, first_down)
    grad0, grad_first_gain, grad_up_first, grad_down_first = ffn_backward(
        grad1, saved_first, back_up_first, back_down_first
    )
    summed_first = sum_ffn(grad_up_first, grad_down_first)
    mixer_grads = (
        lax.psum_scatter(
            grad_query_w.astype(jnp.bfloat16), "wide", scatter_dimension=0, tiled=True
        ).astype(jnp.float32),
        lax.psum_scatter(
            grad_key_w.astype(jnp.bfloat16), "wide", scatter_dimension=0, tiled=True
        ).astype(jnp.float32),
        lax.psum_scatter(
            grad_value_w.astype(jnp.bfloat16), "wide", scatter_dimension=0, tiled=True
        ).astype(jnp.float32),
        lax.psum_scatter(
            grad_out.astype(jnp.bfloat16), "wide", scatter_dimension=0, tiled=True
        ).astype(jnp.float32),
        lax.psum_scatter(
            grad_glu.astype(jnp.bfloat16), "wide", scatter_dimension=0, tiled=True
        ).astype(jnp.float32),
        lax.psum_scatter(
            grad_point.astype(jnp.bfloat16), "wide", scatter_dimension=0, tiled=True
        ).astype(jnp.float32),
    )
    totals = (
        lax.psum(mixer_grads[0].astype(jnp.bfloat16), "utt").astype(jnp.float32),
        lax.psum(mixer_grads[1].astype(jnp.bfloat16), "utt").astype(jnp.float32),
        lax.psum(mixer_grads[2].astype(jnp.bfloat16), "utt").astype(jnp.float32),
        lax.psum(mixer_grads[3].astype(jnp.bfloat16), "utt").astype(jnp.float32),
        lax.psum(mixer_grads[4].astype(jnp.bfloat16), "utt").astype(jnp.float32),
        lax.psum(mixer_grads[5].astype(jnp.bfloat16), "utt").astype(jnp.float32),
        lax.psum(grad_place_w.astype(jnp.bfloat16), "utt").astype(jnp.float32),
        lax.psum(grad_content.astype(jnp.bfloat16), "utt").astype(jnp.float32),
        lax.psum(grad_place_b.astype(jnp.bfloat16), "utt").astype(jnp.float32),
    )
    small_grads = lax.psum(
        (
            grad_first_gain,
            grad_attn_gain,
            grad_conv_gain,
            grad_middle_gain,
            grad_second_gain,
            grad_final_gain,
            grad_kernel,
        ),
        ("utt", "wide"),
    )
    grad_input = grad0.astype(jnp.bfloat16).reshape(groups, frames_dev, channels)
    return (
        output,
        grad_input,
        small_grads[0],
        summed_first[0],
        summed_first[1],
        small_grads[1],
        totals[0],
        totals[1],
        totals[2],
        totals[3],
        totals[6],
        totals[7],
        totals[8],
        small_grads[2],
        totals[4],
        small_grads[6],
        small_grads[3],
        totals[5],
        small_grads[4],
        summed_second[0],
        summed_second[1],
        small_grads[5],
    )


def solution(mesh):
    in_specs = (
        P("utt", "wide", None),
        P("utt"),
        P("utt", "wide"),
        P("utt", "wide", None),
        P(),
        P(("utt", "wide"), None),
        P(("utt", "wide"), None),
        P(),
        P("wide", None),
        P("wide", None),
        P("wide", None),
        P("wide", None),
        P("wide", None),
        P("wide"),
        P("wide"),
        P(),
        P("wide", None),
        P(),
        P(),
        P("wide", None),
        P(),
        P(("utt", "wide"), None),
        P(("utt", "wide"), None),
        P(),
    )
    out_specs = (
        P("utt", "wide", None),
        P("utt", "wide", None),
        P(),
        P(("utt", "wide"), None),
        P(("utt", "wide"), None),
        P(),
        P("wide", None),
        P("wide", None),
        P("wide", None),
        P("wide", None),
        P("wide", None),
        P("wide"),
        P("wide"),
        P(),
        P("wide", None),
        P(),
        P(),
        P("wide", None),
        P(),
        P(("utt", "wide"), None),
        P(("utt", "wide"), None),
        P(),
    )
    return jax.shard_map(
        per_device, mesh=mesh, in_specs=in_specs, out_specs=out_specs, check_vma=False
    )
```

profile of v0, /device:TPU:8, one launch (start us, length us, event | category | flops | bytes accessed | tf_op | source)
XLA Modules:
  0.0 3608.2 jit_solution(241491500542948981)
XLA Ops:
  15.1 74.6 %all-gather.11.cloned.1.call-done = bf16[4096,1024]{1,0:T(8,128)(2,1)} async-done(((bf16[128,1024]{1,0:T(8,128)(2,1)}), bf16[4096,1024]{1,0:T(8,128)(2,1)}) %all-gather.11.cloned.1.call-update) | async-done | bytes 8388624 | tf_op jit(solution)/shard_map/all_gather | solution.py:84
  99.8 68.9 %all-gather.13.cloned.1.call-done = bf16[4096,1024]{1,0:T(8,128)(2,1)} async-done(((bf16[128,1024]{1,0:T(8,128)(2,1)}), bf16[4096,1024]{1,0:T(8,128)(2,1)}) %all-gather.13.cloned.1.call-update) | async-done | bytes 8388624 | tf_op jit(solution)/shard_map/all_gather | solution.py:85
  180.3 24.2 all-gather.19.cloned.1.call-done
  213.0 38.7 %all-gather.17.cloned.1.call-done = bf16[1024,1024]{1,0:T(8,128)(2,1)} async-done(((bf16[256,1024]{1,0:T(8,128)(2,1)}), bf16[1024,1024]{1,0:T(8,128)(2,1)}) %all-gather.17.cloned.1.call-update) | async-done | bytes 2097168 | tf_op jit(solution)/shard_map/all_gather | solution.py:266
  263.3 34.6 all-gather.15.cloned.1.call-done
  310.3 17.2 fusion.73
  344.9 397.0 %while.111 = (s32[]{:T(128)}, bf16[2,1024,4,64]{1,3,2,0:T(8,128)(2,1)}, f32[2,4,1024]{2,1,0:T(4,128)}, bf16[2,1024,4,64]{1,3,2,0:T(8,128)(2,1)}, f32[256]{0:T(25...) while((s32[]{:T(128)}, ...), condition=%wide.region_9.10_spmd, body=%wide.region_4.9_spmd.sunk | while | flops 959576064 | bytes 185863600 | solution.py:316
  362.8 185.6 %while.114 = (s32[]{:T(128)}, bf16[2,4,512,64]{2,3,1,0:T(8,128)(2,1)}, f32[2,4,512]{2,1,0:T(4,128)S(1)}, pred[1024]{0:T(1024)(128)(4,1)S(1)}, s32[2]{0:T(128)S(1...) while((s32[]{:T(128)}, ...), condition=%wide.region_8.8_spmd, body=%wide.region_5.7_spmd.sunk | while | flops 958265344 | bytes 178711376 | solution.py:152
  370.6 19.2 reshape.925
  389.9 14.9 reshape.926
  404.8 13.5 slice.1510
  418.3 14.5 reshape.927
  432.9 13.4 reshape.928
  463.1 19.1 reshape.925
  482.2 16.1 reshape.926
  498.3 13.4 slice.1510
  511.7 14.3 reshape.927
  526.0 13.4 reshape.928
  554.4 183.9 %while.114 = (s32[]{:T(128)}, bf16[2,4,512,64]{2,3,1,0:T(8,128)(2,1)}, f32[2,4,512]{2,1,0:T(4,128)S(1)}, pred[1024]{0:T(1024)(128)(4,1)S(1)}, s32[2]{0:T(128)S(1...) while((s32[]{:T(128)}, ...), condition=%wide.region_8.8_spmd, body=%wide.region_5.7_spmd.sunk | while | flops 958265344 | bytes 178711376 | solution.py:152
  562.3 19.6 reshape.925
  581.8 15.1 reshape.926
  596.9 13.4 slice.1510
  610.3 14.2 reshape.927
  624.4 13.4 reshape.928
  654.6 18.8 reshape.925
  673.4 14.9 reshape.926
  688.4 13.4 slice.1510
  701.7 14.2 reshape.927
  931.3 793.2 %while.113 = (s32[]{:T(128)}, bf16[2,1024,4,64]{1,3,2,0:T(8,128)(2,1)}, bf16[2,1024,4,64]{1,3,2,0:T(8,128)(2,1)}, bf16[2,1024,4,64]{1,3,2,0:T(8,128)(2,1)}, bf16...) while((s32[]{:T(128)}, ...), condition=%wide.region_33.34_spmd, body=%wide.region_26.33_spmd.sunk | while | flops 2844919296 | bytes 433761952 | solution.py:409
  938.7 375.2 %while.115 = (s32[]{:T(128)}, f32[4,1024,64]{1,2,0:T(8,128)}, f32[4,1024,64]{1,2,0:T(8,128)}, f32[4,2047,64]{1,2,0:T(8,128)S(1)}, f32[2,4,512,64]{2,3,1,0:T(8,12...) while((s32[]{:T(128)}, f32[4,1024,64]{1,2,0:T(8,128)}, ...), condition=%wide.region_30.30_spmd.clone, body=%wide.region_27.29_spmd.clone.sunk | while | flops 2841512192 | bytes 377027136 | solution.py:207
  949.8 18.9 reshape.917
  968.7 14.9 reshape.918
  983.6 13.6 slice.1509
  997.2 14.2 reshape.919
  1093.2 13.7 reshape.924
  1135.3 18.8 reshape.917
  1154.1 14.9 reshape.918
  1169.0 13.8 slice.1509
  1182.8 14.2 reshape.919
  1280.0 13.7 reshape.924
  1331.1 374.4 %while.115 = (s32[]{:T(128)}, f32[4,1024,64]{1,2,0:T(8,128)}, f32[4,1024,64]{1,2,0:T(8,128)}, f32[4,2047,64]{1,2,0:T(8,128)S(1)}, f32[2,4,512,64]{2,3,1,0:T(8,12...) while((s32[]{:T(128)}, f32[4,1024,64]{1,2,0:T(8,128)}, ...), condition=%wide.region_30.30_spmd.clone, body=%wide.region_27.29_spmd.clone.sunk | while | flops 2841512192 | bytes 377027136 | solution.py:207
  1341.5 18.8 reshape.917
  1360.3 14.9 reshape.918
  1375.3 13.5 slice.1509
  1388.8 14.2 reshape.919
  1484.8 13.7 reshape.924
  1526.9 18.8 reshape.917
  1545.7 14.9 reshape.918
  1560.7 13.6 slice.1509
  1574.2 14.2 reshape.919
  1671.6 13.7 reshape.924
  1727.0 14.3 all_to_all.120
  1748.1 24.4 all_to_all.121
  1779.5 14.5 all_to_all.122
  1812.7 16.3 reduce-scatter.17.cloned.1.call-done
  1829.0 38.0 %reduce-scatter.19.cloned.1.call-done = bf16[256,1024]{1,0:T(8,128)(2,1)} async-done(((bf16[1024,1024]{1,0:T(8,128)(2,1)}), bf16[256,1024]{1,0:T(8,128)(2,1)}) %reduce-scatter.19.cloned.1.call-update) | async-done | bytes 524304 | tf_op jit(solution)/shard_map/reduce_scatter | solution.py:477
  1867.0 55.8 %reduce-scatter.23.cloned.1.call-done = bf16[512,1024]{1,0:T(8,128)(2,1)} async-done(((bf16[2048,1024]{1,0:T(8,128)(2,1)}), bf16[512,1024]{1,0:T(8,128)(2,1)}) %reduce-scatter.23.cloned.1.call-update) | async-done | bytes 1048592 | tf_op jit(solution)/shard_map/reduce_scatter | solution.py:483
  1938.7 14.8 fusion.208
  2032.8 42.7 %all-reduce.2 = (f32[1024]{0:T(1024)}, f32[1024]{0:T(1024)}, f32[1024]{0:T(1024)}, f32[1024]{0:T(1024)}, f32[1024]{0:T(1024)}, /*index=5*/f32[1024]{0:T(1024)}) all-reduce(f32[1024]{0:T(1024)S(1)} %get-tuple-element.974, f32[1024]{0:T(1024)S(1)} %get-tuple-element.970, ...), channel_id=1, replica_groups=mesh['utt'=8,'wide'=4] {'utt','wide'}, use_global_device_ids=true, to_apply=%region_39.40 | all-reduce | flops 6144 | bytes 49152 | tf_op jit(solution)/shard_map/psum | solution.py:501
  2089.7 64.1 %all-reduce.8.cloned.1.call-done = f32[31,1024]{1,0:T(8,128)} async-done(((f32[31,1024]{1,0:T(8,128)}), f32[31,1024]{1,0:T(8,128)}) %all-reduce.8.cloned.1.call-update) | async-done | bytes 126992 | tf_op jit(solution)/shard_map/psum | solution.py:501
  2153.8 359.8 %reduce-scatter.29.cloned.1.call-done = f32[128,1024]{1,0:T(8,128)} async-done(((f32[4096,1024]{1,0:T(8,128)}), f32[128,1024]{1,0:T(8,128)}) %reduce-scatter.29.cloned.1.call-update) | async-done | bytes 524304 | tf_op jit(solution)/shard_map/reduce_scatter | solution.py:92
  2513.6 361.8 %reduce-scatter.27.cloned.1.call-done = f32[128,1024]{1,0:T(8,128)} async-done(((f32[4096,1024]{1,0:T(8,128)}), f32[128,1024]{1,0:T(8,128)}) %reduce-scatter.27.cloned.1.call-update) | async-done | bytes 524304 | tf_op jit(solution)/shard_map/reduce_scatter | solution.py:91
  2875.4 362.0 %reduce-scatter.13.cloned.1.call-done = f32[128,1024]{1,0:T(8,128)} async-done(((f32[4096,1024]{1,0:T(8,128)}), f32[128,1024]{1,0:T(8,128)}) %reduce-scatter.13.cloned.1.call-update) | async-done | bytes 524304 | tf_op jit(solution)/shard_map/reduce_scatter | solution.py:92
  3237.4 362.0 %reduce-scatter.11.cloned.1.call-done = f32[128,1024]{1,0:T(8,128)} async-done(((f32[4096,1024]{1,0:T(8,128)}), f32[128,1024]{1,0:T(8,128)}) %reduce-scatter.11.cloned.1.call-update) | async-done | bytes 524304 | tf_op jit(solution)/shard_map/reduce_scatter | solution.py:91
  (835 shorter events, 976.1 us)
Async XLA Ops:
  7.2 320.5 %copy-start = (bf16[256,1024]{1,0:T(8,128)(2,1)S(1)}, bf16[256,1024]{1,0:T(8,128)(2,1)}, u32[]{:S(2)}) copy-start(bf16[256,1024]{1,0:T(8,128)(2,1)} %param.46) | copy-start | bytes 1572868
  7.2 82.5 %all-gather.11.cloned.1.call-start = ((), (), s32[]{:S(2)}) async-start(), calls=%async_computation.18 | async-start | bytes 8650752 | tf_op jit(solution)/shard_map/all_gather | solution.py:84
  8.0 160.8 %all-gather.13.cloned.1.call-start = ((), (), s32[]{:S(2)}) async-start(), calls=%async_computation.19 | async-start | bytes 8650752 | tf_op jit(solution)/shard_map/all_gather | solution.py:85
  8.7 195.8 %all-gather.19.cloned.1.call-start = ((), (), s32[]{:S(2)}) async-start(), calls=%async_computation.22 | async-start | bytes 2621440 | tf_op jit(solution)/shard_map/all_gather | solution.py:267
  9.4 242.2 %all-gather.17.cloned.1.call-start = ((), (), s32[]{:S(2)}) async-start(), calls=%async_computation.21 | async-start | bytes 2621440 | tf_op jit(solution)/shard_map/all_gather | solution.py:266
  10.0 287.9 %all-gather.15.cloned.1.call-start = ((), (), s32[]{:S(2)}) async-start(), calls=%async_computation.20 | async-start | bytes 2621440 | tf_op jit(solution)/shard_map/all_gather | solution.py:265
  10.6 752.5 %all-gather.21.cloned.1.call-start = ((), (), s32[]{:S(2)}) async-start(), calls=%async_computation.23 | async-start | bytes 2621440 | tf_op jit(solution)/shard_map/all_gather | solution.py:268
  11.2 757.6 %all-gather.23.cloned.1.call-start = ((), (), s32[]{:S(2)}) async-start(), calls=%async_computation.24 | async-start | bytes 5242880 | tf_op jit(solution)/shard_map/all_gather | solution.py:269
  11.9 787.7 %all-gather.25.cloned.1.call-start = ((), (), s32[]{:S(2)}) async-start(), calls=%async_computation.25 | async-start | bytes 2621440 | tf_op jit(solution)/shard_map/all_gather | solution.py:270
  12.7 792.6 %all-gather.27.cloned.1.call-start = ((), (), s32[]{:S(2)}) async-start(), calls=%async_computation.26 | async-start | bytes 8650752 | tf_op jit(solution)/shard_map/all_gather | solution.py:84
  14.6 164.1 %copy-start.94 = (f32[1024]{0:T(1024)}, f32[1024]{0:T(1024)S(1)}, u32[]{:S(2)}) copy-start(f32[1024]{0:T(1024)S(1)} %convert_element_type.525) | copy-start | bytes 12292
  15.1 84.7 %copy-start.62 = (bf16[512,1024]{1,0:T(8,128)(2,1)}, bf16[512,1024]{1,0:T(8,128)(2,1)S(1)}, u32[]{:S(2)}) copy-start(bf16[512,1024]{1,0:T(8,128)(2,1)S(1)} %fusion.123) | copy-start | bytes 3145732
  180.3 71.3 %copy-start.54 = (bf16[512,1024]{1,0:T(8,128)(2,1)}, bf16[512,1024]{1,0:T(8,128)(2,1)S(1)}, u32[]{:S(2)}) copy-start(bf16[512,1024]{1,0:T(8,128)(2,1)S(1)} %multiply_convert_fusion.13) | copy-start | bytes 3145732
  209.4 49.7 %all-to-all-start.2 = ((bf16[2,256,1024]{1,0,2:T(2,128)(2,1)}), bf16[2,256,1024]{1,0,2:T(2,128)(2,1)S(1)}, u32[]{:S(2)}, u32[]{:S(2)}) async-start(bf16[2,256,1024]{1,0,2:T(2,128)(2,1)} %copy.104), calls=%async_computation.2 | async-start | bytes 2097152 | tf_op jit(solution)/shard_map/all_to_all | solution.py:284
  259.1 46.6 %all-to-all-start.1 = ((bf16[2,256,1024]{1,0,2:T(2,128)(2,1)}), bf16[2,256,1024]{1,0,2:T(2,128)(2,1)S(1)}, u32[]{:S(2)}, u32[]{:S(2)}) async-start(bf16[2,256,1024]{1,0,2:T(2,128)(2,1)} %copy.102), calls=%async_computation.1 | async-start | bytes 2097152 | tf_op jit(solution)/shard_map/all_to_all | solution.py:283
  262.7 554.4 %all-gather.29.cloned.1.call-start = ((), (), s32[]{:S(2)}) async-start(), calls=%async_computation.27 | async-start | bytes 8650752 | tf_op jit(solution)/shard_map/all_gather | solution.py:85
  305.7 21.8 copy-start.42
  305.7 34.5 all-to-all-start
  310.3 17.3 copy-start.158
  310.3 17.3 copy-start.159
  310.3 17.3 copy-start.136
  362.8 185.6 %copy-start.84 = (f32[2,4,1024]{2,1,0:T(4,128)S(1)}, f32[2,4,1024]{2,1,0:T(4,128)}, u32[]{:S(2)}) copy-start(f32[2,4,1024]{2,1,0:T(4,128)} %get-tuple-element.1777) | copy-start | bytes 98308 | tf_op jit(solution)/shard_map/while
  554.4 183.9 %copy-start.84 = (f32[2,4,1024]{2,1,0:T(4,128)S(1)}, f32[2,4,1024]{2,1,0:T(4,128)}, u32[]{:S(2)}) copy-start(f32[2,4,1024]{2,1,0:T(4,128)} %get-tuple-element.1777) | copy-start | bytes 98308 | tf_op jit(solution)/shard_map/while
  745.6 16.5 all-to-all-start.3
  750.7 1062.0 %reduce-scatter.25.cloned.1.call-start = ((), (), s32[]{:S(2)}) async-start(), calls=%async_computation.36 | async-start | bytes 2621440 | tf_op jit(solution)/shard_map/reduce_scatter | solution.py:486
  750.8 139.2 %copy-start.100 = (f32[1,2,2,128]{3,1,2,0:T(2,128)}, f32[1,2,2,128]{3,1,2,0:T(2,128)S(1)}, u32[]{:S(2)}) copy-start(f32[1,2,2,128]{3,1,2,0:T(2,128)S(1)} %copy.346) | copy-start | bytes 6148
  750.8 146.7 %copy-start.128 = (f32[1024]{0:T(1024)}, f32[1024]{0:T(1024)S(1)}, u32[]{:S(2)}) copy-start(f32[1024]{0:T(1024)S(1)} %convert_element_type.535) | copy-start | bytes 12292
  767.1 130.4 %copy-start.112 = (f32[512]{0:T(512)}, f32[512]{0:T(512)S(1)}, u32[]{:S(2)}) copy-start(f32[512]{0:T(512)S(1)} %broadcast_multiply_fusion.2) | copy-start | bytes 6148
  768.8 128.8 %copy-start.134 = (f32[512]{0:T(512)}, f32[512]{0:T(512)S(1)}, u32[]{:S(2)}) copy-start(f32[512]{0:T(512)S(1)} %fusion.197) | copy-start | bytes 6148
  776.1 84.7 %copy-start.10 = (bf16[512,1024]{1,0:T(8,128)(2,1)}, bf16[512,1024]{1,0:T(8,128)(2,1)S(1)}, u32[]{:S(2)}) copy-start(bf16[512,1024]{1,0:T(8,128)(2,1)S(1)} %multiply_convert_fusion.11) | copy-start | bytes 3145732
  776.1 5.2 collective-permute-start
  779.5 6.2 collective-permute-start.1
  780.9 72.1 %copy-start.126 = (f32[1024]{0:T(1024)}, f32[1024]{0:T(1024)S(1)}, u32[]{:S(2)}) copy-start(f32[1024]{0:T(1024)S(1)} %convert_element_type.574) | copy-start | bytes 12292
  781.3 15.1 copy-start.71
  785.6 75.1 %copy-start.69 = (bf16[2,15,1024]{2,1,0:T(8,128)(2,1)}, bf16[2,15,1024]{2,1,0:T(8,128)(2,1)S(1)}, u32[]{:S(2)}) copy-start(bf16[2,15,1024]{2,1,0:T(8,128)(2,1)S(1)} %collective-permute-done.1) | copy-start | bytes 184324
  803.6 49.3 %copy-start.110 = (f32[512]{0:T(512)}, f32[512]{0:T(512)S(1)}, u32[]{:S(2)}) copy-start(f32[512]{0:T(512)S(1)} %broadcast_multiply_fusion.1) | copy-start | bytes 6148
  805.3 47.7 %copy-start.130 = (f32[512]{0:T(512)}, f32[512]{0:T(512)S(1)}, u32[]{:S(2)}) copy-start(f32[512]{0:T(512)S(1)} %fusion.198) | copy-start | bytes 6148
  830.8 14.6 slice-start
  833.0 20.7 copy-start.36
  833.0 20.7 copy-start.132
  833.0 12.4 copy-start.27
  833.0 12.4 slice-start.1
  854.0 22.5 copy-start.37
  860.8 15.7 copy-start.61
  870.0 9.2 collective-permute-start.2
  871.3 8.0 collective-permute-start.3
  904.2 20.2 all-to-all-start.4
  908.6 904.1 %reduce-scatter.21.cloned.1.call-start = ((), (), s32[]{:S(2)}) async-start(), calls=%async_computation.33 | async-start | bytes 2621440 | tf_op jit(solution)/shard_map/reduce_scatter | solution.py:480
  913.2 899.5 %reduce-scatter.15.cloned.1.call-start = ((), (), s32[]{:S(2)}) async-start(), calls=%async_computation.30 | async-start | bytes 2621440 | tf_op jit(solution)/shard_map/reduce_scatter | solution.py:471
  1746.0 83.0 %reduce-scatter.17.cloned.1.call-start = ((), (), s32[]{:S(2)}) async-start(), calls=%async_computation.31 | async-start | bytes 2621440 | tf_op jit(solution)/shard_map/reduce_scatter | solution.py:474
  1777.4 89.6 %reduce-scatter.19.cloned.1.call-start = ((), (), s32[]{:S(2)}) async-start(), calls=%async_computation.32 | async-start | bytes 2621440 | tf_op jit(solution)/shard_map/reduce_scatter | solution.py:477
  1798.9 124.0 %reduce-scatter.23.cloned.1.call-start = ((), (), s32[]{:S(2)}) async-start(), calls=%async_computation.34 | async-start | bytes 5242880 | tf_op jit(solution)/shard_map/reduce_scatter | solution.py:483
  1806.6 272.8 %all-reduce.10.cloned.1.call-start = ((), (), s32[]{:S(2)}) async-start(), calls=%async_computation.39 | async-start | bytes 8388608 | tf_op jit(solution)/shard_map/psum | solution.py:491
  1922.9 230.9 %all-reduce.8.cloned.1.call-start = ((), (), s32[]{:S(2)}) async-start(), calls=%async_computation.35 | async-start | bytes 262144 | tf_op jit(solution)/shard_map/psum | solution.py:501
  1938.6 574.9 %reduce-scatter.29.cloned.1.call-start = ((), (), s32[]{:S(2)}) async-start(), calls=%async_computation.38 | async-start | bytes 17301504 | tf_op jit(solution)/shard_map/reduce_scatter | solution.py:92
  1953.6 921.9 %reduce-scatter.27.cloned.1.call-start = ((), (), s32[]{:S(2)}) async-start(), calls=%async_computation.37 | async-start | bytes 17301504 | tf_op jit(solution)/shard_map/reduce_scatter | solution.py:91
  1965.8 1271.6 %reduce-scatter.13.cloned.1.call-start = ((), (), s32[]{:S(2)}) async-start(), calls=%async_computation.29 | async-start | bytes 17301504 | tf_op jit(solution)/shard_map/reduce_scatter | solution.py:92
  1985.9 1613.4 %reduce-scatter.11.cloned.1.call-start = ((), (), s32[]{:S(2)}) async-start(), calls=%async_computation.28 | async-start | bytes 17301504 | tf_op jit(solution)/shard_map/reduce_scatter | solution.py:91
  1986.3 12.3 copy-start.63
  2006.8 15.1 copy-start.21
  2006.8 15.1 copy-start.97
  2006.8 15.1 copy-start.105
  2022.0 9.7 copy-start.107
  2087.0 1513.9 %copy-start.1 = (bf16[256,1024]{1,0:T(8,128)(2,1)S(1)}, bf16[256,1024]{1,0:T(8,128)(2,1)}, u32[]{:S(2)}) copy-start(bf16[256,1024]{1,0:T(8,128)(2,1)} %param.46) | copy-start | bytes 1572868
  (180 other events, 562.8 us)
Sparse Core Ops, SparseCore 0:
  10.9 78.7 all-gather.10
  92.6 76.1 all-gather.12
  170.6 33.8 all-gather.18
  206.2 45.3 all-gather.16
  253.3 44.5 all-gather.14
  299.6 43.0 all-gather.20
  344.6 52.6 all-gather.22
  399.1 35.3 all-gather.24
  437.4 77.3 all-gather.26
  517.5 76.1 all-gather.28
  879.4 44.8 reduce-scatter.24
  927.3 35.8 reduce-scatter.20
  1746.1 44.6 reduce-scatter.14
  1793.9 35.0 reduce-scatter.16
  1831.8 35.1 reduce-scatter.18
  1870.1 52.6 reduce-scatter.22
  1926.2 99.0 all-reduce.9
  2031.2 122.5 all-reduce.7
  2156.7 356.8 reduce-scatter.28
  2516.3 359.0 reduce-scatter.26
  2878.3 359.0 reduce-scatter.12
  3240.3 359.0 reduce-scatter.10
where the time goes:
time: 3620 us; the launch traced here: 3610 us
  waiting for transfers between devices  1890 us (52%)
  local copies, waits for them, and re-layouts  986 us (27%)
  matrix products  414 us (11%)
  other arithmetic  117 us (3%)
  blocking collectives  109 us (3%)
  loops' own time  37 us (1%)
    reduce_scatter x2, waiting for transfers between devices, sum_ffn(): lax.psum_scatter(grad_up, ('utt', 'wide'), scatter_dimension=0, tiled=True)  724 us
    reduce_scatter x2, waiting for transfers between devices, sum_ffn(): lax.psum_scatter(grad_down, ('utt', 'wide'), scatter_dimension=0, tiled=T...  722 us
    while x188, local copies, waits for them, and re-layouts  366 us
    dot_general x27, matrix products, mult_trans(): lax.dot_general(first_mat, second_mat, (((1,), (1,)), ((), ())), preferre...  168 us
    reshape x8, local copies, waits for them, and re-layouts, skew_rows(): reversed_scores.reshape(-1)  121 us
    slice x8, local copies, waits for them, and re-layouts, skew_rows(): reversed_scores.reshape(-1)  108 us
    reshape x8, local copies, waits for them, and re-layouts, skew_rows(): return flat.reshape(block_rows, span - 1)[:, :span - block_rows + 1]  107 us
    dot_general x22, matrix products, mult_rows(): lax.dot_general(first_mat, second_mat, (((0,), (0,)), ((), ())), preferre...  105 us
  transfers between devices with their start and end apart: 31, of which 17 were waited for; matrix products, arithmetic and copies ran while one was open for 39% of the time, Pallas kernels for 0%

commit v1 on v0

--- a/solution.py
+++ b/solution.py
@@ -4,12 +4,18 @@
 import jax
 import jax.numpy as jnp
 from jax import lax
+from jax.experimental import pallas as pl
+from jax.experimental.pallas import tpu as pltpu
 from jax.sharding import PartitionSpec as P
 
 HEAD_DIM = 64
 KERNEL = 31
 QBLK = 512
 RIM = 15
+PAIR = 128
+ROWS_FWD = 512
+ROWS_BWD = 256
+VMEM = 56 * 2**20
 
 
 EPSILON = 1e-05
@@ -219,6 +225,576 @@
         grad_place.astype(jnp.bfloat16),
         jnp.sum(grad_with_u, axis=0),
         jnp.sum(grad_with_v, axis=0),
+    )
+
+
+def biased(q_ref, bias_ref, scale):
+    return ((q_ref[...].astype(jnp.float32) + bias_ref[...].astype(jnp.float32)).astype(jnp.bfloat16).astype(jnp.float32) * scale).astype(jnp.bfloat16)
+
+def attend_fwd_kernel(len_ref, q_ref, k_ref, v_ref, place_ref, cb_ref, pb_ref, out_ref, prob_ref, *, scale):
+    rows = q_ref.shape[0]
+    length = k_ref.shape[0]
+    span = rows + length
+    first = pl.multiple_of(length - rows - pl.program_id(1) * rows, rows)
+    lanes = lax.broadcasted_iota(jnp.int32, (rows, PAIR), 1)
+    with_u = biased(q_ref, cb_ref, scale)
+    with_v = biased(q_ref, pb_ref, scale)
+    window = place_ref[pl.ds(first, span), :]
+    key_ok = lax.broadcasted_iota(jnp.int32, (rows, length), 1) < len_ref[0]
+    zero = jnp.zeros_like(with_u)
+    mixed = []
+    for head in range(2):
+        mine = (lanes // HEAD_DIM) == head
+        place_part = mult_trans(jnp.where(mine, with_v, zero), window)
+        place_part = pltpu.roll(place_part, span - rows + 1, 1, stride=1, stride_axis=0)
+        scores = mult_trans(jnp.where(mine, with_u, zero), k_ref[...]) + place_part[:, :length]
+        scores = jnp.where(key_ok, scores, MASKED_SCORE)
+        weights = jnp.exp(scores - jnp.max(scores, axis=1, keepdims=True))
+        total = jnp.sum(weights, axis=1, keepdims=True)
+        prob = (weights * (1.0 / total)).astype(jnp.bfloat16)
+        prob_ref[head] = prob
+        mixed.append(mult_plain(prob, v_ref[...]))
+    out_ref[...] = jnp.where(lanes < HEAD_DIM, mixed[0], mixed[1]).astype(jnp.bfloat16)
+
+def attend_fwd(length_arr, q, k, v, place, cb, pb, rows):
+    length, width = q.shape
+    pairs = width // PAIR
+    return pl.pallas_call(
+        partial(attend_fwd_kernel, scale=1.0 / math.sqrt(HEAD_DIM)),
+        grid=(pairs, length // rows),
+        in_specs=[
+            pl.BlockSpec(memory_space=pltpu.SMEM),
+            pl.BlockSpec((rows, PAIR), lambda p, i: (i, p)),
+            pl.BlockSpec((length, PAIR), lambda p, i: (0, p)),
+            pl.BlockSpec((length, PAIR), lambda p, i: (0, p)),
+            pl.BlockSpec((2 * length, PAIR), lambda p, i: (0, p)),
+            pl.BlockSpec((1, PAIR), lambda p, i: (0, p)),
+            pl.BlockSpec((1, PAIR), lambda p, i: (0, p)),
+        ],
+        out_specs=[
+            pl.BlockSpec((rows, PAIR), lambda p, i: (i, p)),
+            pl.BlockSpec((2, rows, length), lambda p, i: (p, i, 0)),
+        ],
+        out_shape=[
+            jax.ShapeDtypeStruct((length, width), jnp.bfloat16),
+            jax.ShapeDtypeStruct((2 * pairs, length, length), jnp.bfloat16),
+        ],
+        compiler_params=pltpu.CompilerParams(vmem_limit_bytes=VMEM),
+        cost_estimate=pl.CostEstimate(flops=40 * 10**9, bytes_accessed=20 * 2**20, transcendentals=pairs * 2 * length * length),
+        name="attend_fwd",
+    )(length_arr, q, k, v, place, cb, pb)
+
+def attend_bwd_kernel(q_ref, k_ref, v_ref, place_ref, cb_ref, pb_ref, prob_ref, g_ref, gq_ref, gk_ref, gv_ref, gp_ref, gb_ref, gk_s, gv_s, gp_s, *, scale, trans):
+    rows = q_ref.shape[0]
+    length = k_ref.shape[0]
+    span = rows + length
+    step = pl.program_id(1)
+    first = pl.multiple_of(length - rows - step * rows, rows)
+    lanes = lax.broadcasted_iota(jnp.int32, (rows, PAIR), 1)
+    flip = (lax.broadcasted_iota(jnp.int32, (rows, rows), 0) + lax.broadcasted_iota(jnp.int32, (rows, rows), 1) == rows - 1).astype(jnp.bfloat16)
+    with_u = biased(q_ref, cb_ref, scale)
+    with_v = mult_plain(flip, biased(q_ref, pb_ref, scale)).astype(jnp.bfloat16)
+    grad = g_ref[...]
+    window = place_ref[pl.ds(first, span), :]
+    zero = jnp.zeros_like(with_u)
+
+    @pl.when(step == 0)
+    def _():
+        gk_s[...] = jnp.zeros_like(gk_s)
+        gv_s[...] = jnp.zeros_like(gv_s)
+        gp_s[...] = jnp.zeros_like(gp_s)
+        gb_ref[...] = jnp.zeros_like(gb_ref)
+
+    if trans:
+        grad_t, with_u_t, with_v_t = grad.T, with_u.T, with_v.T
+    gu = []
+    gw = []
+    for head in range(2):
+        mine = (lanes // HEAD_DIM) == head
+        prob = prob_ref[head]
+        grad_h = jnp.where(mine, grad, zero)
+        grad_prob = mult_trans(grad_h, v_ref[...])
+        weighted = prob.astype(jnp.float32) * grad_prob
+        inner = jnp.sum(weighted, axis=1, keepdims=True)
+        grad_score = (weighted - prob.astype(jnp.float32) * inner).astype(jnp.bfloat16)
+        turned = mult_plain(flip, grad_score).astype(jnp.bfloat16)
+        turned = jnp.concatenate([turned, jnp.zeros((rows, rows), jnp.bfloat16)], axis=1)
+        turned = pltpu.roll(turned, 0, 1, stride=1, stride_axis=0)
+        gu.append(mult_plain(grad_score, k_ref[...]))
+        gw.append(mult_plain(turned, window))
+        if trans:
+            band = slice(head * HEAD_DIM, (head + 1) * HEAD_DIM)
+            gv_s[band, :] += mult_plain(grad_t[band, :], prob)
+            gk_s[band, :] += mult_plain(with_u_t[band, :], grad_score)
+            gp_s[band, pl.ds(first, span)] += mult_plain(with_v_t[band, :], turned)
+        else:
+            gv_s[...] += mult_rows(prob, grad_h)
+            gk_s[...] += mult_rows(grad_score, jnp.where(mine, with_u, zero))
+            gp_s[pl.ds(first, span), :] += mult_rows(turned, jnp.where(mine, with_v, zero))
+    grad_u = jnp.where(lanes < HEAD_DIM, gu[0], gu[1]) * scale
+    grad_w = jnp.where(lanes < HEAD_DIM, gw[0], gw[1]) * scale
+    gb_ref[0:1, :] += jnp.sum(grad_u, axis=0, keepdims=True)
+    gb_ref[1:2, :] += jnp.sum(grad_w, axis=0, keepdims=True)
+    high = grad_w.astype(jnp.bfloat16)
+    rest = (grad_w - high.astype(jnp.float32)).astype(jnp.bfloat16)
+    gq_ref[...] = (grad_u + mult_plain(flip, high) + mult_plain(flip, rest)).astype(jnp.bfloat16)
+
+    @pl.when(step == pl.num_programs(1) - 1)
+    def _():
+        if trans:
+            gk_ref[...] = gk_s[...].T.astype(jnp.bfloat16)
+            gv_ref[...] = gv_s[...].T.astype(jnp.bfloat16)
+            gp_ref[...] = gp_s[...].T.astype(jnp.bfloat16)
+        else:
+            gk_ref[...] = gk_s[...].astype(jnp.bfloat16)
+            gv_ref[...] = gv_s[...].astype(jnp.bfloat16)
+            gp_ref[...] = gp_s[...].astype(jnp.bfloat16)
+
+def attend_bwd(q, k, v, place, cb, pb, prob, grad, rows, trans=True):
+    length, width = q.shape
+    pairs = width // PAIR
+    full = pl.BlockSpec((length, PAIR), lambda p, i: (0, p))
+    part = pl.BlockSpec((rows, PAIR), lambda p, i: (i, p))
+    vec = pl.BlockSpec((1, PAIR), lambda p, i: (0, p))
+    tall = pl.BlockSpec((2 * length, PAIR), lambda p, i: (0, p))
+    shape = (lambda n: (PAIR, n)) if trans else (lambda n: (n, PAIR))
+    return pl.pallas_call(
+        partial(attend_bwd_kernel, scale=1.0 / math.sqrt(HEAD_DIM), trans=trans),
+        grid=(pairs, length // rows),
+        in_specs=[part, full, full, tall, vec, vec, pl.BlockSpec((2, rows, length), lambda p, i: (p, i, 0)), part],
+        out_specs=[part, full, full, tall, pl.BlockSpec((8, PAIR), lambda p, i: (0, p))],
+        out_shape=[
+            jax.ShapeDtypeStruct((length, width), jnp.bfloat16),
+            jax.ShapeDtypeStruct((length, width), jnp.bfloat16),
+            jax.ShapeDtypeStruct((length, width), jnp.bfloat16),
+            jax.ShapeDtypeStruct((2 * length, width), jnp.bfloat16),
+            jax.ShapeDtypeStruct((8, width), jnp.float32),
+        ],
+        scratch_shapes=[
+            pltpu.VMEM(shape(length), jnp.float32),
+            pltpu.VMEM(shape(length), jnp.float32),
+            pltpu.VMEM(shape(2 * length), jnp.float32),
+        ],
+        compiler_params=pltpu.CompilerParams(vmem_limit_bytes=VMEM),
+        cost_estimate=pl.CostEstimate(flops=80 * 10**9, bytes_accessed=20 * 2**20, transcendentals=0),
+        name="attend_bwd",
+    )(q, k, v, place, cb, pb, prob, grad)
+
+
+class Hops:
+    def __init__(self, layers):
+        self.layers = layers
+
+    def send(self, block, dz=0, dc=0, dy=0, dx=0):
+        pairs = []
+        for z in range(self.layers):
+            for c in range(2):
+                for w in range(4):
+                    to = ((z + dz) % self.layers * 2 + (c ^ dc)) * 4 + (w ^ (2 * dy + dx))
+                    pairs.append(((z * 2 + c) * 4 + w, to))
+        return lax.ppermute(block, ("utt", "wide"), pairs)
+
+    def turn(self, block, step):
+        pairs = []
+        for z in range(self.layers):
+            for c in range(2):
+                for w in range(4):
+                    to = (z * 2 + w // 2) * 4 + 2 * c + ((w % 2) ^ step)
+                    pairs.append(((z * 2 + c) * 4 + w, to))
+        return lax.ppermute(block, ("utt", "wide"), pairs)
+
+    def gather_rows(self, chunk):
+        half = self.layers // 2
+        along = [chunk] + [self.send(chunk, dz=k) for k in range(1, self.layers)]
+        low = jnp.concatenate(along[:half])
+        high = jnp.concatenate(along[half:])
+        low_y = self.send(low, dy=1)
+        high_x = self.send(high, dx=1)
+        near = [low, low_y, high, high_x]
+        far = [
+            self.send(low, dx=1),
+            self.send(low_y, dx=1),
+            self.send(high, dy=1),
+            self.send(high_x, dy=1),
+        ]
+        mine = near + far
+        return mine + [self.send(block, dc=1) for block in mine]
+
+    def reduce_rows(self, own, other):
+        swapped = self.send(other(), dc=1)
+        total = own(swapped)
+        size = total.shape[0] // 8
+        part = lambda block, at, count=1: lax.slice_in_dim(block, at * size, (at + count) * size)
+        plus = lambda a, b: (a.astype(jnp.float32) + b.astype(jnp.float32)).astype(jnp.bfloat16)
+        low_far = self.send(part(total, 4, 2), dx=1)
+        high_far = self.send(part(total, 6, 2), dy=1)
+        low = plus(part(total, 0, 2), low_far)
+        high = plus(part(total, 2, 2), high_far)
+        low_y = self.send(part(low, 1), dy=1)
+        high_x = self.send(part(high, 1), dx=1)
+        both = jnp.concatenate([plus(part(low, 0), low_y), plus(part(high, 0), high_x)])
+        return self.reduce_layers(both)
+
+    def reduce_layers(self, block):
+        size = block.shape[0] // self.layers
+        result = block[:size].astype(jnp.float32)
+        for k in range(1, self.layers):
+            result = result + self.send(block[k * size : (k + 1) * size], dz=-k).astype(jnp.float32)
+        return result
+
+    def gather_plane(self, first, second):
+        first_x = self.send(first, dx=1)
+        second_y = self.send(second, dy=1)
+        return (
+            [first, first_x, self.send(first, dy=1), self.send(first_x, dy=1)],
+            [second, self.send(second, dx=1), second_y, self.send(second_y, dx=1)],
+        )
+
+    def reduce_plane(self, first, second):
+        plus = lambda a, b: (a.astype(jnp.float32) + b.astype(jnp.float32)).astype(jnp.bfloat16)
+        first_got = self.send(jnp.concatenate(first[2:]), dy=1)
+        second_got = self.send(jnp.concatenate([second[1], second[3]]), dx=1)
+        rows = first[0].shape[0]
+        first_own = plus(first[0], first_got[:rows])
+        first_x = plus(first[1], first_got[rows:])
+        rows = second[0].shape[0]
+        second_own = plus(second[0], second_got[:rows])
+        second_y = plus(second[2], second_got[rows:])
+        return (
+            plus(first_own, self.send(first_x, dx=1)),
+            plus(second_own, self.send(second_y, dy=1)),
+        )
+
+    def sum_layers(self, block):
+        z = lax.axis_index("utt") // 2
+        size = block.shape[0] // self.layers
+        piece = lambda k: lax.dynamic_slice_in_dim(block, (z + k) % self.layers * size, size)
+        total = piece(0).astype(jnp.float32)
+        for k in range(1, self.layers):
+            total = total + self.send(piece(k), dz=k).astype(jnp.float32)
+        total = total.astype(jnp.bfloat16)
+        result = jnp.zeros(block.shape, jnp.bfloat16)
+        for k in range(self.layers):
+            got = total if k == 0 else self.send(total, dz=k)
+            result = lax.dynamic_update_slice_in_dim(result, got, (z - k) % self.layers * size, 0)
+        return result
+
+
+def taps_forward(padded, kernel_f, count):
+    total = jnp.zeros((count, padded.shape[1]), jnp.float32)
+    for offset in range(KERNEL):
+        total = total + padded[offset : offset + count] * kernel_f[offset]
+    return total
+
+
+def with_rim(hops, block, core):
+    edge = jnp.where(core == 0, block[-16:], block[:16])
+    got = hops.send(edge, dc=1)
+    zero = jnp.zeros_like(got)
+    low = jnp.where(core == 0, zero, got)[1:]
+    high = jnp.where(core == 0, got, zero)[:RIM]
+    return jnp.concatenate([low, block, high])
+
+
+def per_chip(
+    frames,
+    lengths,
+    masked,
+    cotangent,
+    first_gain,
+    first_up,
+    first_down,
+    attn_gain,
+    query_weight,
+    key_weight,
+    value_weight,
+    out_weight,
+    place_weight,
+    content_bias,
+    place_bias,
+    conv_gain,
+    glu_weight,
+    depth_kernel,
+    middle_gain,
+    point_weight,
+    second_gain,
+    second_up,
+    second_down,
+    final_gain,
+):
+    utt_at, wide_at = lax.axis_index("utt"), lax.axis_index("wide")
+    core, y, x = utt_at % 2, wide_at // 2, wide_at % 2
+    hops = Hops(lax.axis_size("utt") // 2)
+    groups, quarter, channels = frames.shape
+    rows = groups * quarter
+    length = 2 * rows
+    f32 = lambda v: v.astype(jnp.float32)
+    low = lambda v: v.astype(jnp.bfloat16)
+
+    def pick(flag, one, two):
+        return jnp.where(flag, one, two), jnp.where(flag, two, one)
+
+    def turn_in(block):
+        swap = [lax.dynamic_index_in_dim(block, x ^ step, 0, keepdims=False) for step in range(2)]
+        got = [hops.turn(swap[step], step) for step in range(2)]
+        return jnp.concatenate(pick(x == 0, *got))
+
+    def turn_out(block):
+        parts = pick(x == 0, block[:quarter], block[quarter:])
+        got = [hops.turn(parts[step], step) for step in range(2)]
+        return jnp.stack(pick(x == 0, *got))
+
+    frames_own = turn_in(frames)
+    first_pieces = hops.gather_rows(first_up)
+    first_pieces_down = hops.gather_rows(first_down)
+    positions = wide_at * quarter + jnp.arange(quarter, dtype=jnp.int32)
+    seed_weight = f32(masked) * f32(positions[None, :] < lengths[:, None])
+    seed_own_low = low(f32(cotangent) * seed_weight[:, :, None])
+    all_lengths = lax.all_gather(lengths, "utt", axis=0, tiled=True)
+    own_length = lax.dynamic_slice_in_dim(all_lengths, utt_at // 2 * 4 + wide_at, 1)
+    own_rows = core * rows + jnp.arange(rows, dtype=jnp.int32)
+    frame_ok = f32(own_rows < own_length[0])[:, None]
+
+    def own_half(weight):
+        count = weight.shape[0] // 2
+        return lax.dynamic_slice_in_dim(weight, core * count, count)
+
+    band = query_weight.shape[0] // 2
+    qk_pieces, vp_pieces = hops.gather_plane(
+        jnp.concatenate([own_half(query_weight), own_half(key_weight)]),
+        jnp.concatenate([own_half(value_weight), own_half(place_weight)]),
+    )
+    query_own = jnp.concatenate([piece[:band] for piece in qk_pieces])
+    key_own = jnp.concatenate([piece[band:] for piece in qk_pieces])
+    value_own = jnp.concatenate([piece[:band] for piece in vp_pieces])
+    place_own = jnp.concatenate([piece[band:] for piece in vp_pieces])
+    op_pieces, glu_pieces = hops.gather_plane(
+        jnp.concatenate([own_half(out_weight), own_half(point_weight)]),
+        own_half(glu_weight),
+    )
+    op_both = op_pieces + [hops.send(piece, dc=1) for piece in op_pieces]
+    glu_both = glu_pieces + [hops.send(piece, dc=1) for piece in glu_pieces]
+    here = wide_at * 2 + core
+    place_at = [((piece % 4) * 2 + piece // 4) ^ here for piece in range(8)]
+
+    def in_order(pieces):
+        size = pieces[0].shape[0]
+        result = jnp.zeros((8 * size, channels), jnp.bfloat16)
+        for piece, at in zip(pieces, place_at):
+            result = lax.dynamic_update_slice_in_dim(result, piece, at * size, 0)
+        return result
+
+    def by_piece(matrix):
+        size = matrix.shape[0] // 8
+        return [lax.dynamic_slice_in_dim(matrix, at * size, size) for at in place_at]
+
+    full_out = jnp.concatenate([piece[:band] for piece in op_both])
+    full_point = in_order([piece[band:] for piece in op_both])
+    full_glu = in_order(glu_both)
+
+    biases = jnp.stack([content_bias, place_bias])
+    all_biases = lax.all_gather(biases, "wide", axis=1, tiled=True)
+    pair_at = [((piece * 2) ^ (wide_at * 2)) + core for piece in range(4)]
+    own_biases = jnp.concatenate(
+        [lax.dynamic_slice_in_dim(all_biases, at * band, band, 1) for at in pair_at], axis=1
+    )
+
+    stream0 = f32(frames_own)
+    up_first, down_first = jnp.concatenate(first_pieces), jnp.concatenate(first_pieces_down)
+    stream1, saved_first = ffn_forward(stream0, f32(first_gain), up_first, down_first)
+    normed_attn, attn_pull = jax.vjp(norm_rows, stream1, f32(attn_gain))
+    attn_half = low(normed_attn)
+    attn_other = hops.send(attn_half, dc=1)
+    attn_low = jnp.concatenate(pick(core == 0, attn_half, attn_other))
+    rel_table = low(relative_table(length, channels))
+    rel_table = jnp.concatenate([rel_table, jnp.zeros((1, channels), jnp.bfloat16)])
+    query = low(mult_trans(attn_low, query_own))
+    key = low(mult_trans(attn_low, key_own))
+    value = low(mult_trans(attn_low, value_own))
+    place = low(mult_trans(rel_table, place_own))
+    attended, prob = attend_fwd(
+        own_length, query, key, value, place, own_biases[:1], own_biases[1:], ROWS_FWD
+    )
+
+    def halves(matrix):
+        own = lax.dynamic_slice_in_dim(matrix, core * rows, rows)
+        other = lax.dynamic_slice_in_dim(matrix, (1 - core) * rows, rows)
+        return own, other
+
+    att_own, att_other = halves(attended)
+    framed = jnp.concatenate([att_own, hops.send(att_other, dc=1)], axis=1)
+    stream2 = stream1 + mult_plain(framed, full_out)
+    normed_conv, conv_pull = jax.vjp(norm_rows, stream2, f32(conv_gain))
+    conv_low = low(normed_conv)
+    glu_in = mult_trans(conv_low, full_glu)
+    linear = glu_in[:, :channels]
+    gating = jax.nn.sigmoid(glu_in[:, channels:])
+    gated = low(linear * gating * frame_ok)
+    padded = with_rim(hops, gated, core)
+    kernel_f = f32(depth_kernel)
+    conv_out = taps_forward(padded, kernel_f, rows)
+    middle, middle_pull = jax.vjp(norm_rows, conv_out, f32(middle_gain))
+    swished = low(jax.nn.silu(middle))
+    stream3 = stream2 + mult_trans(swished, full_point)
+    up_second = jnp.concatenate(hops.gather_rows(second_up))
+    down_second = jnp.concatenate(hops.gather_rows(second_down))
+    stream4, saved_second = ffn_forward(stream3, f32(second_gain), up_second, down_second)
+    final_rows, final_pull = jax.vjp(norm_rows, stream4, f32(final_gain))
+    output = turn_out(low(final_rows))
+
+    seed_own = turn_in(seed_own_low)
+    grad4, grad_final_gain = final_pull(f32(seed_own))
+
+    def ffn_back(grad_stream, saved_ffn, up_full, down_full):
+        norm_pull, normed_low, before, active_low = saved_ffn
+        grad_out = low(0.5 * grad_stream)
+        side = active_low.shape[1] // 2
+
+        def reduced(left, right):
+            def half(at):
+                return mult_rows(lax.slice_in_dim(left, at * side, (at + 1) * side, axis=1), right)
+
+            return hops.reduce_rows(
+                lambda got: low(half(0) + f32(got)), lambda: low(half(1))
+            )
+
+        sum_down = reduced(active_low, grad_out)
+        grad_before = low(mult_trans(grad_out, down_full) * silu_slope(before))
+        sum_up = reduced(grad_before, normed_low)
+        grad_input, grad_gain = norm_pull(mult_plain(grad_before, up_full))
+        return grad_stream + grad_input, grad_gain, sum_up, sum_down
+
+    grad3, grad_second_gain, sum_up_second, sum_down_second = ffn_back(
+        grad4, saved_second, up_second, down_second
+    )
+    grad_branch = low(grad3)
+    grad_point = mult_rows(grad_branch, swished)
+    grad_middle = mult_plain(grad_branch, full_point) * silu_slope(middle)
+    grad_conv, grad_middle_gain = middle_pull(grad_middle)
+    conv_grad_low = low(grad_conv)
+    grad_padded = with_rim(hops, conv_grad_low, core)
+    grad_gated = taps_forward(grad_padded, kernel_f[::-1], rows)
+    grad_kernel = jnp.stack(
+        [
+            jnp.sum(f32(padded[offset : offset + rows]) * f32(conv_grad_low), axis=0)
+            for offset in range(KERNEL)
+        ]
+    )
+    grad_gated = grad_gated * frame_ok
+    grad_glu_in = low(
+        jnp.concatenate(
+            [grad_gated * gating, grad_gated * linear * gating * (1.0 - gating)], axis=1
+        )
+    )
+    grad_glu = mult_rows(grad_glu_in, conv_low)
+    grad_conv_in, grad_conv_gain = conv_pull(mult_plain(grad_glu_in, full_glu))
+    grad2 = grad3 + grad_conv_in
+    grad_attn = low(grad2)
+    grad_out = mult_rows(framed, grad_attn)
+    grad_framed = low(mult_trans(grad_attn, full_out))
+    side = channels // 2
+    grad_heads = jnp.concatenate(
+        pick(core == 0, grad_framed[:, :side], hops.send(grad_framed[:, side:], dc=1))
+    )
+    grad_query, grad_key, grad_value, grad_place, grad_biases = attend_bwd(
+        query, key, value, place, own_biases[:1], own_biases[1:], prob, grad_heads, ROWS_BWD
+    )
+    grad_query_w = mult_rows(grad_query, attn_low)
+    grad_key_w = mult_rows(grad_key, attn_low)
+    grad_value_w = mult_rows(grad_value, attn_low)
+    grad_place_w = mult_rows(grad_place, rel_table)
+    grad_normed = (
+        mult_plain(grad_query, query_own)
+        + mult_plain(grad_key, key_own)
+        + mult_plain(grad_value, value_own)
+    )
+    normed_own, normed_other = halves(grad_normed)
+    grad_attn_in, grad_attn_gain = attn_pull(normed_own + f32(hops.send(low(normed_other), dc=1)))
+    grad1 = grad2 + grad_attn_in
+    grad0, grad_first_gain, sum_up_first, sum_down_first = ffn_back(
+        grad1, saved_first, up_first, down_first
+    )
+    grad_input = turn_out(low(grad0))
+
+    def split4(matrix):
+        size = matrix.shape[0] // 4
+        return [matrix[at * size : (at + 1) * size] for at in range(4)]
+
+    def joined(*lists):
+        return [jnp.concatenate([low(part) for part in parts]) for parts in zip(*lists)]
+
+    out_size = band
+    out_pieces = [grad_out[at * out_size : (at + 1) * out_size] for at in range(8)]
+    point_pieces, glu_parts = by_piece(grad_point), by_piece(grad_glu)
+    sent = joined(out_pieces[4:], point_pieces[4:], glu_parts[4:])
+    kept = joined(out_pieces[:4], point_pieces[:4], glu_parts[:4])
+    got = hops.send(jnp.concatenate(sent), dc=1)
+    summed = split4(low(f32(jnp.concatenate(kept)) + f32(got)))
+    op_sum, glu_sum = hops.reduce_plane(
+        [part[: 2 * band] for part in summed], [part[2 * band :] for part in summed]
+    )
+    op_glu = hops.sum_layers(jnp.concatenate([op_sum, glu_sum]))
+    qk_sum, vp_sum = hops.reduce_plane(
+        joined(split4(grad_query_w), split4(grad_key_w)),
+        joined(split4(grad_value_w), split4(grad_place_w)),
+    )
+    qkvp = hops.sum_layers(jnp.concatenate([qk_sum, vp_sum]))
+    both_core = [jnp.concatenate([op_glu, qkvp])]
+    both_core.append(hops.send(both_core[0], dc=1))
+
+    def owned(start, count):
+        parts = [part[start : start + count] for part in both_core]
+        return f32(jnp.concatenate(pick(core == 0, *parts)))
+
+    total_out, total_point = owned(0, band), owned(band, band)
+    total_glu = owned(2 * band, 2 * band)
+    total_query, total_key = owned(4 * band, band), owned(5 * band, band)
+    total_value, total_place = owned(6 * band, band), owned(7 * band, band)
+
+    spread = jnp.zeros((2, channels), jnp.float32)
+    for piece, at in enumerate(pair_at):
+        spread = lax.dynamic_update_slice(
+            spread, grad_biases[:2, piece * band : (piece + 1) * band], (0, at * band)
+        )
+    small = lax.psum(
+        jnp.concatenate(
+            [
+                grad_first_gain[None],
+                grad_attn_gain[None],
+                grad_conv_gain[None],
+                grad_middle_gain[None],
+                grad_second_gain[None],
+                grad_final_gain[None],
+                spread,
+                grad_kernel,
+            ]
+        ),
+        ("utt", "wide"),
+    )
+    own_bias = lax.dynamic_slice_in_dim(small[6:8], wide_at * 2 * band, 2 * band, 1)
+    return (
+        output,
+        grad_input,
+        small[0],
+        sum_up_first,
+        sum_down_first,
+        small[1],
+        total_query,
+        total_key,
+        total_value,
+        total_out,
+        total_place,
+        own_bias[0],
+        own_bias[1],
+        small[2],
+        total_glu,
+        small[8:],
+        small[3],
+        total_point,
+        small[4],
+        sum_up_second,
+        sum_down_second,
+        small[5],
     )
 
 
@@ -588,6 +1164,8 @@
         P(("utt", "wide"), None),
         P(),
     )
+    shape = dict(mesh.shape)
+    body = per_chip if shape["wide"] == 4 and shape["utt"] % 4 == 0 else per_device
     return jax.shard_map(
-        per_device, mesh=mesh, in_specs=in_specs, out_specs=out_specs, check_vma=False
-    )
+        body, mesh=mesh, in_specs=in_specs, out_specs=out_specs, check_vma=False
+    )

time: 3620 us -> 1250 us (0.35)
  waiting for transfers between devices: 1890 us -> 549 us
  local copies, waits for them, and re-layouts: 986 us -> 134 us
  matrix products: 414 us -> 160 us
  starting transfers between devices: 33.4 us -> 148 us
  blocking collectives: 109 us -> 20.7 us
  Pallas kernels: 0 us -> 86 us
  loops' own time: 37 us -> 0 us
    reduce_scatter x10 -> x0, waiting for transfers between devices: 1560 us -> none  [the longest x2 724 us: sum_ffn(): lax.psum_scatter(grad_up, ('utt', 'wide'), scatter_dimension=0, tiled=True)]
    ppermute x4 -> x156, waiting for transfers between devices: 4.72 us -> 432 us  [the longest x148 418 us: send(): return lax.ppermute(block, ('utt', 'wide'), pairs)]
    while x192 -> x0, local copies, waits for them, and re-layouts: 366 us -> none
    reshape x36 -> x0, local copies, waits for them, and re-layouts: 341 us -> none  [the longest x8 121 us: skew_rows(): reversed_scores.reshape(-1)]
    all_gather x10 -> x0, waiting for transfers between devices: 241 us -> none  [the longest x2 74.6 us: gather_ffn(): lax.all_gather(up_rows, ('utt', 'wide'), axis=0, tiled=True)]
    ppermute x4 -> x156, starting transfers between devices: 11.1 us -> 148 us  [the longest x148 139 us: send(): return lax.ppermute(block, ('utt', 'wide'), pairs)]
    dot_general x27 -> x11, matrix products: 168 us -> 61.7 us  [mult_trans(): lax.dot_general(first_mat, second_mat, (((1,), (1,)), ((), ())), preferre...]
    slice x12 -> x39, local copies, waits for them, and re-layouts: 108 us -> 15.4 us  [the longest x3 3.5 us: per_chip(): key_own = jnp.concatenate([piece[band:] for piece in qk_pieces])]
  transfers between devices with their start and end apart: 31 -> 157, of which waited for: 17 -> 62; matrix products, arithmetic and copies ran while one was open for 39% -> 25% of each run, Pallas kernels for 0% -> 7%
where the time goes in v1:
time: 1250 us; the launch traced here: 1240 us
  waiting for transfers between devices  549 us (44%)
  matrix products  160 us (13%)
  starting transfers between devices  148 us (12%)
  local copies, waits for them, and re-layouts  134 us (11%)
  other arithmetic  126 us (10%)
  Pallas kernels  86 us (7%)
  blocking collectives  20.7 us (2%)
  between operations  18.2 us (1%)
    ppermute x148, waiting for transfers between devices, send(): return lax.ppermute(block, ('utt', 'wide'), pairs)  418 us
    ppermute x148, starting transfers between devices, send(): return lax.ppermute(block, ('utt', 'wide'), pairs)  139 us
    psum x1, waiting for transfers between devices, per_chip(): lax.psum(jnp.concatenate([grad_first_gain[None], grad_attn_gain[None], gr...  117 us
    unnamed x441, local copies, waits for them, and re-layouts  80.8 us
    dot_general x11, matrix products, mult_trans(): lax.dot_general(first_mat, second_mat, (((1,), (1,)), ((), ())), preferre...  61.7 us
    pallas_call x1, Pallas kernels, attend_bwd(): pl.pallas_call(partial(attend_bwd_kernel, scale=1.0 / math.sqrt(HEAD_DIM)...  51.1 us
    dot_general x15, matrix products, mult_rows(): lax.dot_general(first_mat, second_mat, (((0,), (0,)), ((), ())), preferre...  49.8 us
    dot_general x10, matrix products, mult_plain(): return jnp.dot(first_mat, second_mat, preferred_element_type=jnp.float32)  48.1 us
  transfers between devices with their start and end apart: 157, of which 62 were waited for; matrix products, arithmetic and copies ran while one was open for 25% of the time, Pallas kernels for 7%

profile of v1, /device:TPU:8, one launch (start us, length us, event | category | flops | bytes accessed | tf_op | source)
XLA Modules:
  0.0 1241.5 jit_solution(5691409568986696833)
XLA Ops:
  18.6 11.7 all_gather.7
  37.0 17.1 %fusion.2 = (bf16[2047,512]{1,0:T(8,128)(2,1)}, bf16[2047,512]{1,0:T(8,128)(2,1)}) fusion(f32[512]{0:T(512)S(1)} %multiply_exponential_fusion, f32[2047]{0:T(1024)S(1)} %convert_subtract_fusion.1), kind=kLoop, calls=%fused_computation.104 | loop fusion | flops 3144192 | bytes 4202492 | tf_op jit(solution)/shard_map/convert.26
  60.5 8.9 all-reduce.1
  97.6 5.5 collective-permute-done.1
  103.1 5.2 collective-permute-done.41
  114.5 11.0 collective-permute-done.44
  128.3 8.4 collective-permute-done.96
  140.4 5.4 collective-permute-done.51
  169.5 5.6 collective-permute-done.60
  179.0 8.7 collective-permute-done.61
  188.5 5.1 collective-permute-start.79
  194.5 10.0 collective-permute-done.78
  211.1 7.1 collective-permute-done.42
  223.9 9.5 collective-permute-done.46
  236.0 12.2 collective-permute-done.53
  261.2 9.5 collective-permute-done.7
  272.5 9.5 collective-permute-done.8
  285.1 8.1 collective-permute-done.23
  294.9 9.5 collective-permute-done.24
  306.2 9.4 collective-permute-done.25
  318.8 8.1 collective-permute-done.63
  328.6 9.5 collective-permute-done.64
  339.9 9.5 collective-permute-done.65
  352.3 8.4 collective-permute-done.80
  362.6 9.4 collective-permute-done.81
  373.8 8.9 collective-permute-done.82
  388.3 7.9 collective-permute-done.10
  405.8 7.8 collective-permute-done.27
  423.1 7.9 collective-permute-done.67
  436.5 12.1 multiply_convert_fusion.3
  449.4 8.3 fusion.280
  465.1 8.0 collective-permute-done.84
  485.5 35.0 %attend_fwd.1 = (bf16[1024,512]{1,0:T(8,128)(2,1)}, bf16[8,1024,1024]{2,1,0:T(8,128)(2,1)}) custom-call(s32[1]{0:T(128)} %dynamic_slice.138.len_ref, bf16[1024,512]{1,0:T(8,128)(2,1)} %convolution_convert_fusion.12.q_ref, bf16[1024,512]{1,0:T(8,128)(2,1)} %convolution_convert_fusion.11.k_ref, bf16[1024,512]{1,0:T(8,128)(2,1)} %convolution_convert_fusion.10.v_ref, ...), custom_call_target="tpu_custom_call" | custom-call | flops 40000000000 | bytes 20971520 | tf_op jit(solution)/shard_map/attend_fwd/pallas_call | solution.py:262
  539.6 10.2 fusion.254
  552.4 11.4 multiply_convert_fusion.2
  563.7 8.3 fusion.283
  575.9 11.7 multiply_convert_fusion.1
  587.6 9.5 multiply_reduce_fusion
  603.3 8.1 fusion.95
  634.3 15.9 %multiply_convert_fusion.6 = (bf16[512,1024]{1,0:T(8,128)(2,1)S(1)}, f32[512,1024]{1,0:T(8,128)S(1)}) fusion(f32[512,2048]{1,0:T(8,128)S(1)} %fusion.243, f32[512]{0:T(512)S(1)} %fusion.219, f32[1024]{0:T(1024)S(1)} %bitcast.150, bf16[15,1024]{1,0:T(8,128)(2,1)S(1)} %get-tuple-element.313, bf16[512,1024]{1,0:T(8,128)(2,1)S(1)} %get-tuple-element.83, ...), kind=kLoop, calls=%fused_computation.286 | loop fusion | flops 98566144 | bytes 6481920 | tf_op jit(solution)/shard_map/convert.24
  651.1 5.5 multiply_reduce_fusion.2
  677.6 51.1 %attend_bwd.1 = (bf16[1024,512]{1,0:T(8,128)(2,1)}, bf16[1024,512]{1,0:T(8,128)(2,1)}, bf16[1024,512]{1,0:T(8,128)(2,1)}, bf16[2048,512]{1,0:T(8,128)(2,1)}, f32[8,512]{1,0:T(8,128)}) custom-call(bf16[1024,512]{1,0:T(8,128)(2,1)} %convolution_convert_fusion.12.q_ref, bf16[1024,512]{1,0:T(8,128)(2,1)} %convolution_convert_fusion.11.k_ref, ...), custom_call_target="tpu_custom_call" | custom-call | flops 80000000000 | bytes 20971520 | tf_op jit(solution)/shard_map/attend_bwd/pallas_call | solution.py:361
  750.2 18.5 %collective-permute-done.120 = bf16[512,1024]{1,0:T(8,128)(2,1)S(1)} collective-permute-done((bf16[512,1024]{1,0:T(8,128)(2,1)S(1)}, bf16[512,1024]{1,0:T(8,128)(2,1)S(1)}, u32[]{:S(2)}, u32[]{:S(2)}) %collective-permute-start.120) | collective-permute-done | bytes 1048608 | tf_op jit(solution)/shard_map/ppermute | solution.py:395
  777.9 8.5 multiply_convert_fusion
  786.4 8.7 fusion.48
  830.8 116.7 %all-reduce.4.cloned.1.call-done = f32[39,1024]{1,0:T(8,128)} async-done(((f32[39,1024]{1,0:T(8,128)}), f32[39,1024]{1,0:T(8,128)}) %all-reduce.4.cloned.1.call-update) | async-done | bytes 159760 | tf_op jit(solution)/shard_map/psum | solution.py:759
  957.8 7.5 collective-permute-start.110
  966.4 7.1 collective-permute-done.125
  997.9 10.3 collective-permute-done.149
  1008.3 6.8 collective-permute-done.152
  1019.0 11.6 collective-permute-done.141
  1031.9 5.5 collective-permute-done.144
  1039.7 13.4 %collective-permute-done.131 = bf16[512,1024]{1,0:T(8,128)(2,1)S(1)} collective-permute-done((bf16[512,1024]{1,0:T(8,128)(2,1)S(1)}, bf16[512,1024]{1,0:T(8,128)(2,1)S(1)}, u32[]{:S(2)}, u32[]{:S(2)}) %collective-permute-start.131) | collective-permute-done | bytes 1048608 | tf_op jit(solution)/shard_map/ppermute | solution.py:395
  1054.6 7.7 collective-permute-done.153
  1062.8 6.2 collective-permute-done.150
  1074.7 9.2 collective-permute-done.142
  1107.8 7.6 collective-permute-done.155
  1118.9 7.6 collective-permute-done.146
  1126.6 8.6 collective-permute-done.147
  1141.0 10.6 collective-permute-done.134
  1151.6 6.3 collective-permute-done.135
  1161.8 9.0 collective-permute-done.136
  1176.4 6.4 collective-permute-done.115
  1199.4 13.0 %collective-permute-done.117 = bf16[128,1024]{1,0:T(8,128)(2,1)S(1)} collective-permute-done((bf16[128,1024]{1,0:T(8,128)(2,1)S(1)}, bf16[128,1024]{1,0:T(8,128)(2,1)S(1)}, u32[]{:S(2)}, u32[]{:S(2)}) %collective-permute-start.117) | collective-permute-done | bytes 262176 | tf_op jit(solution)/shard_map/ppermute | solution.py:395
  (957 shorter events, 466.6 us)
Async XLA Ops:
  7.3 940.3 %all-reduce.4.cloned.1.call-start = ((), (), s32[]{:S(2)}) async-start(), calls=%async_computation | async-start | bytes 327680 | tf_op jit(solution)/shard_map/psum | solution.py:759
  7.3 68.1 %collective-permute-start.2 = (bf16[128,1024]{1,0:T(8,128)(2,1)}, bf16[128,1024]{1,0:T(8,128)(2,1)}, u32[]{:S(2)}, u32[]{:S(2)}) collective-permute-start(bf16[128,1024]{1,0:T(8,128)(2,1)} %param.29), channel_id=1, source_target_pairs={{0,8},{1,9},{2,10},{3,11},{4,12},{5,13},{6,14},{7,15},{8,16},{9,17... | collective-permute-start | bytes 786440 | tf_op jit(solution)/shard_map/ppermute | solution.py:395
  8.9 147.7 %collective-permute-start.4 = (bf16[128,1024]{1,0:T(8,128)(2,1)}, bf16[128,1024]{1,0:T(8,128)(2,1)}, u32[]{:S(2)}, u32[]{:S(2)}) collective-permute-start(bf16[128,1024]{1,0:T(8,128)(2,1)} %param.29), channel_id=1, source_target_pairs={{0,16},{1,17},{2,18},{3,19},{4,20},{5,21},{6,22},{7,23},{8,24},{9,... | collective-permute-start | bytes 786440 | tf_op jit(solution)/shard_map/ppermute | solution.py:395
  10.0 67.3 %collective-permute-start.19 = (bf16[128,1024]{1,0:T(8,128)(2,1)}, bf16[128,1024]{1,0:T(8,128)(2,1)}, u32[]{:S(2)}, u32[]{:S(2)}) collective-permute-start(bf16[128,1024]{1,0:T(8,128)(2,1)} %param.30), channel_id=1, source_target_pairs={{0,8},{1,9},{2,10},{3,11},{4,12},{5,13},{6,14},{7,15},{8,16},{9,17... | collective-permute-start | bytes 786440 | tf_op jit(solution)/shard_map/ppermute | solution.py:395
  10.8 68.9 %collective-permute-start.59 = (bf16[128,1024]{1,0:T(8,128)(2,1)}, bf16[128,1024]{1,0:T(8,128)(2,1)}, u32[]{:S(2)}, u32[]{:S(2)}) collective-permute-start(bf16[128,1024]{1,0:T(8,128)(2,1)} %param.45), channel_id=1, source_target_pairs={{0,8},{1,9},{2,10},{3,11},{4,12},{5,13},{6,14},{7,15},{8,16},{9,17... | collective-permute-start | bytes 786440 | tf_op jit(solution)/shard_map/ppermute | solution.py:395
  14.4 71.1 %collective-permute-start.38 = (bf16[256,1024]{1,0:T(8,128)(2,1)}, bf16[256,1024]{1,0:T(8,128)(2,1)}, u32[]{:S(2)}, u32[]{:S(2)}) collective-permute-start(bf16[256,1024]{1,0:T(8,128)(2,1)} %pad_maximum_fusion.24), channel_id=1, source_target_pairs={{0,2},{1,3},{2,0},{3,1},{4,6},{5,7},{6,4},{7,5},{8,10},{9,11},{10,... | collective-permute-start | bytes 1572872 | tf_op jit(solution)/shard_map/ppermute | solution.py:395
  92.6 45.4 %collective-permute-start.45 = (bf16[256,1024]{1,0:T(8,128)(2,1)S(1)}, bf16[256,1024]{1,0:T(8,128)(2,1)S(1)}, u32[]{:S(2)}, u32[]{:S(2)}) collective-permute-start(bf16[256,1024]{1,0:T(8,128)(2,1)S(1)} %copy-done.54), channel_id=1, source_target_pairs={{0,2},{1,3},{2,0},{3,1},{4,6},{5,7},{6,4},{7,5},{8,10},{9,11},{10,... | collective-permute-start | bytes 1572872 | tf_op jit(solution)/shard_map/ppermute | solution.py:395
  145.8 60.5 %collective-permute-start.5 = (bf16[128,1024]{1,0:T(8,128)(2,1)S(1)}, bf16[128,1024]{1,0:T(8,128)(2,1)S(1)}, u32[]{:S(2)}, u32[]{:S(2)}) collective-permute-start(bf16[128,1024]{1,0:T(8,128)(2,1)S(1)} %copy-done.63), channel_id=1, source_target_pairs={{0,24},{1,25},{2,26},{3,27},{4,28},{5,29},{6,30},{7,31},{8,0},{9,1... | collective-permute-start | bytes 786440 | tf_op jit(solution)/shard_map/ppermute | solution.py:395
  148.3 26.8 %collective-permute-start.60 = (bf16[256,1024]{1,0:T(8,128)(2,1)S(1)}, bf16[256,1024]{1,0:T(8,128)(2,1)S(1)}, u32[]{:S(2)}, u32[]{:S(2)}) collective-permute-start(bf16[256,1024]{1,0:T(8,128)(2,1)S(1)} %copy-done.91), channel_id=1, source_target_pairs={{0,2},{1,3},{2,0},{3,1},{4,6},{5,7},{6,4},{7,5},{8,10},{9,11},{10,... | collective-permute-start | bytes 1572872 | tf_op jit(solution)/shard_map/ppermute | solution.py:395
  156.6 32.0 %collective-permute-start.77 = (bf16[256,1024]{1,0:T(8,128)(2,1)S(1)}, bf16[256,1024]{1,0:T(8,128)(2,1)S(1)}, u32[]{:S(2)}, u32[]{:S(2)}) collective-permute-start(bf16[256,1024]{1,0:T(8,128)(2,1)S(1)} %get-tuple-element.247), channel_id=1, source_target_pairs={{0,2},{1,3},{2,0},{3,1},{4,6},{5,7},{6,4},{7,5},{8,10},{9,11},{10,... | collective-permute-start | bytes 1572872 | tf_op jit(solution)/shard_map/ppermute | solution.py:395
  167.8 39.3 %collective-permute-start.22 = (bf16[128,1024]{1,0:T(8,128)(2,1)S(1)}, bf16[128,1024]{1,0:T(8,128)(2,1)S(1)}, u32[]{:S(2)}, u32[]{:S(2)}) collective-permute-start(bf16[128,1024]{1,0:T(8,128)(2,1)S(1)} %copy-done.65), channel_id=1, source_target_pairs={{0,24},{1,25},{2,26},{3,27},{4,28},{5,29},{6,30},{7,31},{8,0},{9,1... | collective-permute-start | bytes 786440 | tf_op jit(solution)/shard_map/ppermute | solution.py:395
  175.1 29.4 %collective-permute-start.78 = (bf16[128,1024]{1,0:T(8,128)(2,1)S(1)}, bf16[128,1024]{1,0:T(8,128)(2,1)S(1)}, u32[]{:S(2)}, u32[]{:S(2)}) collective-permute-start(bf16[128,1024]{1,0:T(8,128)(2,1)S(1)} %copy-done.69), channel_id=1, source_target_pairs={{0,16},{1,17},{2,18},{3,19},{4,20},{5,21},{6,22},{7,23},{8,24},{9,... | collective-permute-start | bytes 786440 | tf_op jit(solution)/shard_map/ppermute | solution.py:395
  206.3 27.1 %collective-permute-start.47 = (bf16[256,1024]{1,0:T(8,128)(2,1)S(1)}, bf16[256,1024]{1,0:T(8,128)(2,1)S(1)}, u32[]{:S(2)}, u32[]{:S(2)}) collective-permute-start(bf16[256,1024]{1,0:T(8,128)(2,1)S(1)} %copy-done.54), channel_id=1, source_target_pairs={{0,4},{1,5},{2,6},{3,7},{4,0},{5,1},{6,2},{7,3},{8,12},{9,13},{10,... | collective-permute-start | bytes 1572872 | tf_op jit(solution)/shard_map/ppermute | solution.py:395
  207.1 42.9 %collective-permute-start.54 = (bf16[256,1024]{1,0:T(8,128)(2,1)S(1)}, bf16[256,1024]{1,0:T(8,128)(2,1)S(1)}, u32[]{:S(2)}, u32[]{:S(2)}) collective-permute-start(bf16[256,1024]{1,0:T(8,128)(2,1)S(1)} %copy-done.58), channel_id=1, source_target_pairs={{0,4},{1,5},{2,6},{3,7},{4,0},{5,1},{6,2},{7,3},{8,12},{9,13},{10,... | collective-permute-start | bytes 1572872 | tf_op jit(solution)/shard_map/ppermute | solution.py:395
  250.0 32.0 %collective-permute-start.8 = (bf16[256,1024]{1,0:T(8,128)(2,1)S(1)}, bf16[256,1024]{1,0:T(8,128)(2,1)S(1)}, u32[]{:S(2)}, u32[]{:S(2)}) collective-permute-start(bf16[256,1024]{1,0:T(8,128)(2,1)S(1)} %collective-permute-done.3), channel_id=1, source_target_pairs={{0,1},{1,0},{2,3},{3,2},{4,5},{5,4},{6,7},{7,6},{8,9},{9,8},{10,11... | collective-permute-start | bytes 1572872 | tf_op jit(solution)/shard_map/ppermute | solution.py:395
  251.9 32.1 %collective-permute-start.9 = (bf16[256,1024]{1,0:T(8,128)(2,1)S(1)}, bf16[256,1024]{1,0:T(8,128)(2,1)S(1)}, u32[]{:S(2)}, u32[]{:S(2)}) collective-permute-start(bf16[256,1024]{1,0:T(8,128)(2,1)S(1)} %get-tuple-element.267), channel_id=1, source_target_pairs={{0,2},{1,3},{2,0},{3,1},{4,6},{5,7},{6,4},{7,5},{8,10},{9,11},{10,... | collective-permute-start | bytes 1572872 | tf_op jit(solution)/shard_map/ppermute | solution.py:395
  254.0 39.2 %collective-permute-start.23 = (bf16[256,1024]{1,0:T(8,128)(2,1)S(1)}, bf16[256,1024]{1,0:T(8,128)(2,1)S(1)}, u32[]{:S(2)}, u32[]{:S(2)}) collective-permute-start(bf16[256,1024]{1,0:T(8,128)(2,1)S(1)} %get-tuple-element.259), channel_id=1, source_target_pairs={{0,1},{1,0},{2,3},{3,2},{4,5},{5,4},{6,7},{7,6},{8,9},{9,8},{10,11... | collective-permute-start | bytes 1572872 | tf_op jit(solution)/shard_map/ppermute | solution.py:395
  259.5 44.9 %collective-permute-start.24 = (bf16[256,1024]{1,0:T(8,128)(2,1)S(1)}, bf16[256,1024]{1,0:T(8,128)(2,1)S(1)}, u32[]{:S(2)}, u32[]{:S(2)}) collective-permute-start(bf16[256,1024]{1,0:T(8,128)(2,1)S(1)} %copy-done.92), channel_id=1, source_target_pairs={{0,1},{1,0},{2,3},{3,2},{4,5},{5,4},{6,7},{7,6},{8,9},{9,8},{10,11... | collective-permute-start | bytes 1572872 | tf_op jit(solution)/shard_map/ppermute | solution.py:395
  270.7 44.9 %collective-permute-start.25 = (bf16[256,1024]{1,0:T(8,128)(2,1)S(1)}, bf16[256,1024]{1,0:T(8,128)(2,1)S(1)}, u32[]{:S(2)}, u32[]{:S(2)}) collective-permute-start(bf16[256,1024]{1,0:T(8,128)(2,1)S(1)} %collective-permute-done.20), channel_id=1, source_target_pairs={{0,1},{1,0},{2,3},{3,2},{4,5},{5,4},{6,7},{7,6},{8,9},{9,8},{10,11... | collective-permute-start | bytes 1572872 | tf_op jit(solution)/shard_map/ppermute | solution.py:395
  281.9 35.8 %collective-permute-start.26 = (bf16[256,1024]{1,0:T(8,128)(2,1)S(1)}, bf16[256,1024]{1,0:T(8,128)(2,1)S(1)}, u32[]{:S(2)}, u32[]{:S(2)}) collective-permute-start(bf16[256,1024]{1,0:T(8,128)(2,1)S(1)} %get-tuple-element.259), channel_id=1, source_target_pairs={{0,2},{1,3},{2,0},{3,1},{4,6},{5,7},{6,4},{7,5},{8,10},{9,11},{10,... | collective-permute-start | bytes 1572872 | tf_op jit(solution)/shard_map/ppermute | solution.py:395
  284.0 42.9 %collective-permute-start.63 = (bf16[256,1024]{1,0:T(8,128)(2,1)}, bf16[256,1024]{1,0:T(8,128)(2,1)S(1)}, u32[]{:S(2)}, u32[]{:S(2)}) collective-permute-start(bf16[256,1024]{1,0:T(8,128)(2,1)} %get-tuple-element.251), channel_id=1, source_target_pairs={{0,1},{1,0},{2,3},{3,2},{4,5},{5,4},{6,7},{7,6},{8,9},{9,8},{10,11... | collective-permute-start | bytes 1572872 | tf_op jit(solution)/shard_map/ppermute | solution.py:395
  293.2 44.9 %collective-permute-start.64 = (bf16[256,1024]{1,0:T(8,128)(2,1)S(1)}, bf16[256,1024]{1,0:T(8,128)(2,1)S(1)}, u32[]{:S(2)}, u32[]{:S(2)}) collective-permute-start(bf16[256,1024]{1,0:T(8,128)(2,1)S(1)} %copy-done.91), channel_id=1, source_target_pairs={{0,1},{1,0},{2,3},{3,2},{4,5},{5,4},{6,7},{7,6},{8,9},{9,8},{10,11... | collective-permute-start | bytes 1572872 | tf_op jit(solution)/shard_map/ppermute | solution.py:395
  304.4 44.9 %collective-permute-start.65 = (bf16[256,1024]{1,0:T(8,128)(2,1)S(1)}, bf16[256,1024]{1,0:T(8,128)(2,1)S(1)}, u32[]{:S(2)}, u32[]{:S(2)}) collective-permute-start(bf16[256,1024]{1,0:T(8,128)(2,1)S(1)} %collective-permute-done.60), channel_id=1, source_target_pairs={{0,1},{1,0},{2,3},{3,2},{4,5},{5,4},{6,7},{7,6},{8,9},{9,8},{10,11... | collective-permute-start | bytes 1572872 | tf_op jit(solution)/shard_map/ppermute | solution.py:395
  315.6 35.8 %collective-permute-start.66 = (bf16[256,1024]{1,0:T(8,128)(2,1)}, bf16[256,1024]{1,0:T(8,128)(2,1)S(1)}, u32[]{:S(2)}, u32[]{:S(2)}) collective-permute-start(bf16[256,1024]{1,0:T(8,128)(2,1)} %get-tuple-element.251), channel_id=1, source_target_pairs={{0,2},{1,3},{2,0},{3,1},{4,6},{5,7},{6,4},{7,5},{8,10},{9,11},{10,... | collective-permute-start | bytes 1572872 | tf_op jit(solution)/shard_map/ppermute | solution.py:395
  317.7 43.0 %collective-permute-start.80 = (bf16[256,1024]{1,0:T(8,128)(2,1)S(1)}, bf16[256,1024]{1,0:T(8,128)(2,1)}, u32[]{:S(2)}, u32[]{:S(2)}) collective-permute-start(bf16[256,1024]{1,0:T(8,128)(2,1)S(1)} %get-tuple-element.243), channel_id=1, source_target_pairs={{0,1},{1,0},{2,3},{3,2},{4,5},{5,4},{6,7},{7,6},{8,9},{9,8},{10,11... | collective-permute-start | bytes 1572872 | tf_op jit(solution)/shard_map/ppermute | solution.py:395
  326.9 45.0 %collective-permute-start.81 = (bf16[256,1024]{1,0:T(8,128)(2,1)S(1)}, bf16[256,1024]{1,0:T(8,128)(2,1)}, u32[]{:S(2)}, u32[]{:S(2)}) collective-permute-start(bf16[256,1024]{1,0:T(8,128)(2,1)S(1)} %get-tuple-element.247), channel_id=1, source_target_pairs={{0,1},{1,0},{2,3},{3,2},{4,5},{5,4},{6,7},{7,6},{8,9},{9,8},{10,11... | collective-permute-start | bytes 1572872 | tf_op jit(solution)/shard_map/ppermute | solution.py:395
  338.1 44.6 %collective-permute-start.82 = (bf16[256,1024]{1,0:T(8,128)(2,1)S(1)}, bf16[256,1024]{1,0:T(8,128)(2,1)S(1)}, u32[]{:S(2)}, u32[]{:S(2)}) collective-permute-start(bf16[256,1024]{1,0:T(8,128)(2,1)S(1)} %collective-permute-done.77), channel_id=1, source_target_pairs={{0,1},{1,0},{2,3},{3,2},{4,5},{5,4},{6,7},{7,6},{8,9},{9,8},{10,11... | collective-permute-start | bytes 1572872 | tf_op jit(solution)/shard_map/ppermute | solution.py:395
  349.3 35.4 %collective-permute-start.83 = (bf16[256,1024]{1,0:T(8,128)(2,1)S(1)}, bf16[256,1024]{1,0:T(8,128)(2,1)}, u32[]{:S(2)}, u32[]{:S(2)}) collective-permute-start(bf16[256,1024]{1,0:T(8,128)(2,1)S(1)} %get-tuple-element.243), channel_id=1, source_target_pairs={{0,2},{1,3},{2,0},{3,1},{4,6},{5,7},{6,4},{7,5},{8,10},{9,11},{10,... | collective-permute-start | bytes 1572872 | tf_op jit(solution)/shard_map/ppermute | solution.py:395
  351.4 35.2 %collective-permute-start.50 = (bf16[256,1024]{1,0:T(8,128)(2,1)S(1)}, bf16[256,1024]{1,0:T(8,128)(2,1)S(1)}, u32[]{:S(2)}, u32[]{:S(2)}) collective-permute-start(bf16[256,1024]{1,0:T(8,128)(2,1)S(1)} %collective-permute-done.46), channel_id=1, source_target_pairs={{0,4},{1,5},{2,6},{3,7},{4,0},{5,1},{6,2},{7,3},{8,12},{9,13},{10,... | collective-permute-start | bytes 1572872 | tf_op jit(solution)/shard_map/ppermute | solution.py:395
  360.7 36.4 %collective-permute-start.11 = (bf16[256,1024]{1,0:T(8,128)(2,1)S(1)}, bf16[256,1024]{1,0:T(8,128)(2,1)S(1)}, u32[]{:S(2)}, u32[]{:S(2)}) collective-permute-start(bf16[256,1024]{1,0:T(8,128)(2,1)S(1)} %copy-done.93), channel_id=1, source_target_pairs={{0,4},{1,5},{2,6},{3,7},{4,0},{5,1},{6,2},{7,3},{8,12},{9,13},{10,... | collective-permute-start | bytes 1572872 | tf_op jit(solution)/shard_map/ppermute | solution.py:395
  422.0 37.8 %collective-permute-start.70 = (bf16[256,1024]{1,0:T(8,128)(2,1)}, bf16[256,1024]{1,0:T(8,128)(2,1)S(1)}, u32[]{:S(2)}, u32[]{:S(2)}) collective-permute-start(bf16[256,1024]{1,0:T(8,128)(2,1)} %get-tuple-element.251), channel_id=1, source_target_pairs={{0,4},{1,5},{2,6},{3,7},{4,0},{5,1},{6,2},{7,3},{8,12},{9,13},{10,... | collective-permute-start | bytes 1572872 | tf_op jit(solution)/shard_map/ppermute | solution.py:395
  431.1 27.4 %collective-permute-start.72 = (bf16[256,1024]{1,0:T(8,128)(2,1)S(1)}, bf16[256,1024]{1,0:T(8,128)(2,1)S(1)}, u32[]{:S(2)}, u32[]{:S(2)}) collective-permute-start(bf16[256,1024]{1,0:T(8,128)(2,1)S(1)} %collective-permute-done.64), channel_id=1, source_target_pairs={{0,4},{1,5},{2,6},{3,7},{4,0},{5,1},{6,2},{7,3},{8,12},{9,13},{10,... | collective-permute-start | bytes 1572872 | tf_op jit(solution)/shard_map/ppermute | solution.py:395
  433.0 29.1 %collective-permute-start.74 = (bf16[256,1024]{1,0:T(8,128)(2,1)S(1)}, bf16[256,1024]{1,0:T(8,128)(2,1)S(1)}, u32[]{:S(2)}, u32[]{:S(2)}) collective-permute-start(bf16[256,1024]{1,0:T(8,128)(2,1)S(1)} %collective-permute-done.66), channel_id=1, source_target_pairs={{0,4},{1,5},{2,6},{3,7},{4,0},{5,1},{6,2},{7,3},{8,12},{9,13},{10,... | collective-permute-start | bytes 1572872 | tf_op jit(solution)/shard_map/ppermute | solution.py:395
  434.3 26.6 %collective-permute-start.71 = (bf16[256,1024]{1,0:T(8,128)(2,1)S(1)}, bf16[256,1024]{1,0:T(8,128)(2,1)S(1)}, u32[]{:S(2)}, u32[]{:S(2)}) collective-permute-start(bf16[256,1024]{1,0:T(8,128)(2,1)S(1)} %collective-permute-done.63), channel_id=1, source_target_pairs={{0,4},{1,5},{2,6},{3,7},{4,0},{5,1},{6,2},{7,3},{8,12},{9,13},{10,... | collective-permute-start | bytes 1572872 | tf_op jit(solution)/shard_map/ppermute | solution.py:395
  473.1 50.7 %collective-permute-start.89 = (bf16[256,1024]{1,0:T(8,128)(2,1)}, bf16[256,1024]{1,0:T(8,128)(2,1)}, u32[]{:S(2)}, u32[]{:S(2)}) collective-permute-start(bf16[256,1024]{1,0:T(8,128)(2,1)} %collective-permute-done.81), channel_id=1, source_target_pairs={{0,4},{1,5},{2,6},{3,7},{4,0},{5,1},{6,2},{7,3},{8,12},{9,13},{10,... | collective-permute-start | bytes 1572872 | tf_op jit(solution)/shard_map/ppermute | solution.py:395
  474.0 54.2 %collective-permute-start.91 = (bf16[256,1024]{1,0:T(8,128)(2,1)}, bf16[256,1024]{1,0:T(8,128)(2,1)}, u32[]{:S(2)}, u32[]{:S(2)}) collective-permute-start(bf16[256,1024]{1,0:T(8,128)(2,1)} %collective-permute-done.83), channel_id=1, source_target_pairs={{0,4},{1,5},{2,6},{3,7},{4,0},{5,1},{6,2},{7,3},{8,12},{9,13},{10,... | collective-permute-start | bytes 1572872 | tf_op jit(solution)/shard_map/ppermute | solution.py:395
  475.3 46.5 %collective-permute-start.88 = (bf16[256,1024]{1,0:T(8,128)(2,1)}, bf16[256,1024]{1,0:T(8,128)(2,1)}, u32[]{:S(2)}, u32[]{:S(2)}) collective-permute-start(bf16[256,1024]{1,0:T(8,128)(2,1)} %collective-permute-done.80), channel_id=1, source_target_pairs={{0,4},{1,5},{2,6},{3,7},{4,0},{5,1},{6,2},{7,3},{8,12},{9,13},{10,... | collective-permute-start | bytes 1572872 | tf_op jit(solution)/shard_map/ppermute | solution.py:395
  476.2 50.2 %collective-permute-start.90 = (bf16[256,1024]{1,0:T(8,128)(2,1)S(1)}, bf16[256,1024]{1,0:T(8,128)(2,1)}, u32[]{:S(2)}, u32[]{:S(2)}) collective-permute-start(bf16[256,1024]{1,0:T(8,128)(2,1)S(1)} %collective-permute-done.82), channel_id=1, source_target_pairs={{0,4},{1,5},{2,6},{3,7},{4,0},{5,1},{6,2},{7,3},{8,12},{9,13},{10,... | collective-permute-start | bytes 1572872 | tf_op jit(solution)/shard_map/ppermute | solution.py:395
  477.5 52.6 %collective-permute-start.75 = (bf16[256,1024]{1,0:T(8,128)(2,1)}, bf16[256,1024]{1,0:T(8,128)(2,1)S(1)}, u32[]{:S(2)}, u32[]{:S(2)}) collective-permute-start(bf16[256,1024]{1,0:T(8,128)(2,1)} %collective-permute-done.67), channel_id=1, source_target_pairs={{0,4},{1,5},{2,6},{3,7},{4,0},{5,1},{6,2},{7,3},{8,12},{9,13},{10,... | collective-permute-start | bytes 1572872 | tf_op jit(solution)/shard_map/ppermute | solution.py:395
  629.9 44.2 %collective-permute-start.93 = (bf16[256,1024]{1,0:T(8,128)(2,1)S(1)}, bf16[256,1024]{1,0:T(8,128)(2,1)S(1)}, u32[]{:S(2)}, u32[]{:S(2)}) collective-permute-start(bf16[256,1024]{1,0:T(8,128)(2,1)S(1)} %get-tuple-element.201), channel_id=1, source_target_pairs={{0,0},{1,1},{2,4},{3,5},{4,2},{5,3},{6,6},{7,7},{8,8},{9,9},{10,12... | collective-permute-start | bytes 1572872 | tf_op jit(solution)/shard_map/ppermute | solution.py:404
  630.6 43.5 %collective-permute-start.94 = (bf16[256,1024]{1,0:T(8,128)(2,1)S(1)}, bf16[256,1024]{1,0:T(8,128)(2,1)S(1)}, u32[]{:S(2)}, u32[]{:S(2)}) collective-permute-start(bf16[256,1024]{1,0:T(8,128)(2,1)S(1)} %get-tuple-element.202), channel_id=1, source_target_pairs={{0,1},{1,0},{2,5},{3,4},{4,3},{5,2},{6,7},{7,6},{8,9},{9,8},{10,13... | collective-permute-start | bytes 1572872 | tf_op jit(solution)/shard_map/ppermute | solution.py:404
  631.5 343.4 %collective-permute-start.148 = (bf16[2048,1024]{1,0:T(8,128)(2,1)}, bf16[2048,1024]{1,0:T(8,128)(2,1)}, u32[]{:S(2)}, u32[]{:S(2)}) collective-permute-start(bf16[2048,1024]{1,0:T(8,128)(2,1)} %convolution_convert_fusion), channel_id=1, source_target_pairs={{0,4},{1,5},{2,6},{3,7},{4,0},{5,1},{6,2},{7,3},{8,12},{9,13},{10,... | collective-permute-start | bytes 12582920 | tf_op jit(solution)/shard_map/ppermute | solution.py:395
  634.3 347.6 %collective-permute-start.140 = (bf16[2048,1024]{1,0:T(8,128)(2,1)}, bf16[2048,1024]{1,0:T(8,128)(2,1)}, u32[]{:S(2)}, u32[]{:S(2)}) collective-permute-start(bf16[2048,1024]{1,0:T(8,128)(2,1)} %convolution_convert_fusion.1), channel_id=1, source_target_pairs={{0,4},{1,5},{2,6},{3,7},{4,0},{5,1},{6,2},{7,3},{8,12},{9,13},{10,... | collective-permute-start | bytes 12582920 | tf_op jit(solution)/shard_map/ppermute | solution.py:395
  768.6 220.0 %collective-permute-start.128 = (bf16[2048,1024]{1,0:T(8,128)(2,1)}, bf16[2048,1024]{1,0:T(8,128)(2,1)}, u32[]{:S(2)}, u32[]{:S(2)}) collective-permute-start(bf16[2048,1024]{1,0:T(8,128)(2,1)} %get-tuple-element.119), channel_id=1, source_target_pairs={{0,4},{1,5},{2,6},{3,7},{4,0},{5,1},{6,2},{7,3},{8,12},{9,13},{10,... | collective-permute-start | bytes 12582920 | tf_op jit(solution)/shard_map/ppermute | solution.py:395
  769.8 42.0 %collective-permute-start.121 = (bf16[256,1024]{1,0:T(8,128)(2,1)}, bf16[256,1024]{1,0:T(8,128)(2,1)}, u32[]{:S(2)}, u32[]{:S(2)}) collective-permute-start(bf16[256,1024]{1,0:T(8,128)(2,1)} %add_convert_fusion.26), channel_id=1, source_target_pairs={{0,2},{1,3},{2,0},{3,1},{4,6},{5,7},{6,4},{7,5},{8,10},{9,11},{10,... | collective-permute-start | bytes 1572872 | tf_op jit(solution)/shard_map/ppermute | solution.py:395
  772.0 41.6 %collective-permute-start.119 = (bf16[256,1024]{1,0:T(8,128)(2,1)}, bf16[256,1024]{1,0:T(8,128)(2,1)}, u32[]{:S(2)}, u32[]{:S(2)}) collective-permute-start(bf16[256,1024]{1,0:T(8,128)(2,1)} %add_convert_fusion.29), channel_id=1, source_target_pairs={{0,1},{1,0},{2,3},{3,2},{4,5},{5,4},{6,7},{7,6},{8,9},{9,8},{10,11... | collective-permute-start | bytes 1572872 | tf_op jit(solution)/shard_map/ppermute | solution.py:395
  818.4 130.0 %collective-permute-start.123 = (bf16[128,1024]{1,0:T(8,128)(2,1)}, bf16[128,1024]{1,0:T(8,128)(2,1)S(1)}, u32[]{:S(2)}, u32[]{:S(2)}) collective-permute-start(bf16[128,1024]{1,0:T(8,128)(2,1)} %get-tuple-element.173), channel_id=1, source_target_pairs={{0,16},{1,17},{2,18},{3,19},{4,20},{5,21},{6,22},{7,23},{8,24},{9,... | collective-permute-start | bytes 786440 | tf_op jit(solution)/shard_map/ppermute | solution.py:395
  826.8 123.9 %collective-permute-start.124 = (bf16[128,1024]{1,0:T(8,128)(2,1)}, bf16[128,1024]{1,0:T(8,128)(2,1)S(1)}, u32[]{:S(2)}, u32[]{:S(2)}) collective-permute-start(bf16[128,1024]{1,0:T(8,128)(2,1)} %get-tuple-element.174), channel_id=1, source_target_pairs={{0,24},{1,25},{2,26},{3,27},{4,28},{5,29},{6,30},{7,31},{8,0},{9,1... | collective-permute-start | bytes 786440 | tf_op jit(solution)/shard_map/ppermute | solution.py:395
  957.8 129.2 %collective-permute-start.110 = (bf16[2048,1024]{1,0:T(8,128)(2,1)}, bf16[2048,1024]{1,0:T(8,128)(2,1)}, u32[]{:S(2)}, u32[]{:S(2)}) collective-permute-start(bf16[2048,1024]{1,0:T(8,128)(2,1)} %convolution_convert_fusion.2), channel_id=1, source_target_pairs={{0,4},{1,5},{2,6},{3,7},{4,0},{5,1},{6,2},{7,3},{8,12},{9,13},{10,... | collective-permute-start | bytes 12582920 | tf_op jit(solution)/shard_map/ppermute | solution.py:395
  994.4 36.2 %collective-permute-start.141 = (bf16[512,1024]{1,0:T(8,128)(2,1)}, bf16[512,1024]{1,0:T(8,128)(2,1)S(1)}, u32[]{:S(2)}, u32[]{:S(2)}) collective-permute-start(bf16[512,1024]{1,0:T(8,128)(2,1)} %get-tuple-element.110), channel_id=1, source_target_pairs={{0,1},{1,0},{2,3},{3,2},{4,5},{5,4},{6,7},{7,6},{8,9},{9,8},{10,11... | collective-permute-start | bytes 3145736 | tf_op jit(solution)/shard_map/ppermute | solution.py:395
  996.3 41.1 %collective-permute-start.144 = (bf16[512,1024]{1,0:T(8,128)(2,1)S(1)}, bf16[512,1024]{1,0:T(8,128)(2,1)S(1)}, u32[]{:S(2)}, u32[]{:S(2)}) collective-permute-start(bf16[512,1024]{1,0:T(8,128)(2,1)S(1)} %get-tuple-element.111), channel_id=1, source_target_pairs={{0,2},{1,3},{2,0},{3,1},{4,6},{5,7},{6,4},{7,5},{8,10},{9,11},{10,... | collective-permute-start | bytes 3145736 | tf_op jit(solution)/shard_map/ppermute | solution.py:395
  1008.3 87.1 %collective-permute-start.102 = (bf16[2048,1024]{1,0:T(8,128)(2,1)S(1)}, bf16[2048,1024]{1,0:T(8,128)(2,1)}, u32[]{:S(2)}, u32[]{:S(2)}) collective-permute-start(bf16[2048,1024]{1,0:T(8,128)(2,1)S(1)} %copy-done.164), channel_id=1, source_target_pairs={{0,4},{1,5},{2,6},{3,7},{4,0},{5,1},{6,2},{7,3},{8,12},{9,13},{10,... | collective-permute-start | bytes 12582920 | tf_op jit(solution)/shard_map/ppermute | solution.py:395
  1015.1 38.0 %collective-permute-start.131 = (bf16[512,1024]{1,0:T(8,128)(2,1)S(1)}, bf16[512,1024]{1,0:T(8,128)(2,1)S(1)}, u32[]{:S(2)}, u32[]{:S(2)}) collective-permute-start(bf16[512,1024]{1,0:T(8,128)(2,1)S(1)} %pad_maximum_fusion.21), channel_id=1, source_target_pairs={{0,1},{1,0},{2,3},{3,2},{4,5},{5,4},{6,7},{7,6},{8,9},{9,8},{10,11... | collective-permute-start | bytes 3145736 | tf_op jit(solution)/shard_map/ppermute | solution.py:395
  1030.6 62.6 %collective-permute-start.129 = (bf16[512,1024]{1,0:T(8,128)(2,1)S(1)}, bf16[512,1024]{1,0:T(8,128)(2,1)S(1)}, u32[]{:S(2)}, u32[]{:S(2)}) collective-permute-start(bf16[512,1024]{1,0:T(8,128)(2,1)S(1)} %pad_maximum_fusion.20), channel_id=1, source_target_pairs={{0,2},{1,3},{2,0},{3,1},{4,6},{5,7},{6,4},{7,5},{8,10},{9,11},{10,... | collective-permute-start | bytes 3145736 | tf_op jit(solution)/shard_map/ppermute | solution.py:395
  1087.0 28.5 %collective-permute-start.155 = (bf16[128,1024]{1,0:T(8,128)(2,1)S(1)}, bf16[128,1024]{1,0:T(8,128)(2,1)S(1)}, u32[]{:S(2)}, u32[]{:S(2)}) collective-permute-start(bf16[128,1024]{1,0:T(8,128)(2,1)S(1)} %get-tuple-element.210), channel_id=1, source_target_pairs={{0,8},{1,9},{2,10},{3,11},{4,12},{5,13},{6,14},{7,15},{8,16},{9,17... | collective-permute-start | bytes 786440 | tf_op jit(solution)/shard_map/ppermute | solution.py:395
  1093.9 32.6 %collective-permute-start.146 = (bf16[128,1024]{1,0:T(8,128)(2,1)S(1)}, bf16[128,1024]{1,0:T(8,128)(2,1)S(1)}, u32[]{:S(2)}, u32[]{:S(2)}) collective-permute-start(bf16[128,1024]{1,0:T(8,128)(2,1)S(1)} %get-tuple-element.211), channel_id=1, source_target_pairs={{0,16},{1,17},{2,18},{3,19},{4,20},{5,21},{6,22},{7,23},{8,24},{9,... | collective-permute-start | bytes 786440 | tf_op jit(solution)/shard_map/ppermute | solution.py:395
  1105.1 30.0 %collective-permute-start.147 = (bf16[128,1024]{1,0:T(8,128)(2,1)S(1)}, bf16[128,1024]{1,0:T(8,128)(2,1)S(1)}, u32[]{:S(2)}, u32[]{:S(2)}) collective-permute-start(bf16[128,1024]{1,0:T(8,128)(2,1)S(1)} %get-tuple-element.212), channel_id=1, source_target_pairs={{0,8},{1,9},{2,10},{3,11},{4,12},{5,13},{6,14},{7,15},{8,16},{9,17... | collective-permute-start | bytes 786440 | tf_op jit(solution)/shard_map/ppermute | solution.py:395
  1115.5 42.9 %collective-permute-start.111 = (bf16[512,1024]{1,0:T(8,128)(2,1)S(1)}, bf16[512,1024]{1,0:T(8,128)(2,1)S(1)}, u32[]{:S(2)}, u32[]{:S(2)}) collective-permute-start(bf16[512,1024]{1,0:T(8,128)(2,1)S(1)} %get-tuple-element.128), channel_id=1, source_target_pairs={{0,1},{1,0},{2,3},{3,2},{4,5},{5,4},{6,7},{7,6},{8,9},{9,8},{10,11... | collective-permute-start | bytes 3145736 | tf_op jit(solution)/shard_map/ppermute | solution.py:395
  1116.4 42.1 %collective-permute-start.114 = (bf16[512,1024]{1,0:T(8,128)(2,1)S(1)}, bf16[512,1024]{1,0:T(8,128)(2,1)S(1)}, u32[]{:S(2)}, u32[]{:S(2)}) collective-permute-start(bf16[512,1024]{1,0:T(8,128)(2,1)S(1)} %get-tuple-element.129), channel_id=1, source_target_pairs={{0,2},{1,3},{2,0},{3,1},{4,6},{5,7},{6,4},{7,5},{8,10},{9,11},{10,... | collective-permute-start | bytes 3145736 | tf_op jit(solution)/shard_map/ppermute | solution.py:395
  1140.0 32.6 %collective-permute-start.103 = (bf16[512,1024]{1,0:T(8,128)(2,1)S(1)}, bf16[512,1024]{1,0:T(8,128)(2,1)S(1)}, u32[]{:S(2)}, u32[]{:S(2)}) collective-permute-start(bf16[512,1024]{1,0:T(8,128)(2,1)S(1)} %get-tuple-element.132), channel_id=1, source_target_pairs={{0,1},{1,0},{2,3},{3,2},{4,5},{5,4},{6,7},{7,6},{8,9},{9,8},{10,11... | collective-permute-start | bytes 3145736 | tf_op jit(solution)/shard_map/ppermute | solution.py:395
  1172.5 53.5 %collective-permute-start.139 = (bf16[1024,1024]{1,0:T(8,128)(2,1)S(1)}, bf16[1024,1024]{1,0:T(8,128)(2,1)S(1)}, u32[]{:S(2)}, u32[]{:S(2)}) collective-permute-start(bf16[1024,1024]{1,0:T(8,128)(2,1)S(1)} %pad_maximum_fusion.2), channel_id=1, source_target_pairs={{0,4},{1,5},{2,6},{3,7},{4,0},{5,1},{6,2},{7,3},{8,12},{9,13},{10,... | collective-permute-start | bytes 6291464 | tf_op jit(solution)/shard_map/ppermute | solution.py:395
  1185.2 27.3 %collective-permute-start.117 = (bf16[128,1024]{1,0:T(8,128)(2,1)S(1)}, bf16[128,1024]{1,0:T(8,128)(2,1)S(1)}, u32[]{:S(2)}, u32[]{:S(2)}) collective-permute-start(bf16[128,1024]{1,0:T(8,128)(2,1)S(1)} %get-tuple-element.214), channel_id=1, source_target_pairs={{0,8},{1,9},{2,10},{3,11},{4,12},{5,13},{6,14},{7,15},{8,16},{9,17... | collective-permute-start | bytes 786440 | tf_op jit(solution)/shard_map/ppermute | solution.py:395
  1192.3 28.7 %collective-permute-start.108 = (bf16[128,1024]{1,0:T(8,128)(2,1)S(1)}, bf16[128,1024]{1,0:T(8,128)(2,1)S(1)}, u32[]{:S(2)}, u32[]{:S(2)}) collective-permute-start(bf16[128,1024]{1,0:T(8,128)(2,1)S(1)} %get-tuple-element.215), channel_id=1, source_target_pairs={{0,16},{1,17},{2,18},{3,19},{4,20},{5,21},{6,22},{7,23},{8,24},{9,... | collective-permute-start | bytes 786440 | tf_op jit(solution)/shard_map/ppermute | solution.py:395
  1195.7 28.1 %collective-permute-start.109 = (bf16[128,1024]{1,0:T(8,128)(2,1)S(1)}, bf16[128,1024]{1,0:T(8,128)(2,1)S(1)}, u32[]{:S(2)}, u32[]{:S(2)}) collective-permute-start(bf16[128,1024]{1,0:T(8,128)(2,1)S(1)} %get-tuple-element.216), channel_id=1, source_target_pairs={{0,8},{1,9},{2,10},{3,11},{4,12},{5,13},{6,14},{7,15},{8,16},{9,17... | collective-permute-start | bytes 786440 | tf_op jit(solution)/shard_map/ppermute | solution.py:395
  (276 other events, 8110.1 us)
Sparse Core Ops, SparseCore 0:
  811.1 136.4 all-reduce.3

commit v2 on v1

--- a/solution.py
+++ b/solution.py
@@ -381,6 +381,282 @@
     )(q, k, v, place, cb, pb, prob, grad)
 
 
+MESH = pl.DeviceIdType.MESH
+
+
+def chip_place(layers):
+    z, c, y, x = (lax.axis_index(axis) for axis in ("z", "core", "y", "x"))
+
+    def at(dz=0, dc=0, dy=0, dx=0):
+        return (
+            lax.rem(z + dz, layers),
+            lax.rem(c + dc, 2),
+            lax.rem(y + dy, 2),
+            lax.rem(x + dx, 2),
+        )
+
+    return at
+
+
+def greet(at, layers):
+    barrier = pltpu.get_barrier_semaphore()
+    peers = [at(dz=k) for k in range(1, layers)] + [at(dc=1), at(dy=1), at(dx=1)]
+    for peer in peers:
+        pl.semaphore_signal(barrier, inc=1, device_id=peer, device_id_type=MESH)
+    pl.semaphore_wait(barrier, len(peers))
+
+
+def remote(source, target, sems, index, device):
+    return pltpu.make_async_remote_copy(
+        src_ref=source,
+        dst_ref=target,
+        send_sem=sems.at[(0, *index)],
+        recv_sem=sems.at[(1, *index)],
+        device_id=device,
+        device_id_type=MESH,
+    )
+
+
+def far_first(layers):
+    return sorted(range(1, layers), key=lambda k: -min(k, layers - k)) + [0]
+
+
+def gather_plan(layers, shards, fulls, z_sem, p_sem, d_sem, c_sem, own_sem):
+    at = chip_place(layers)
+    arrays = range(len(shards))
+    half = shards[0].shape[0] // 2
+    items = [(dz, a) for dz in reversed(far_first(layers)) for a in arrays]
+    own = [pltpu.make_async_copy(shards[a], fulls[a].at[0, 0, 0, 0], own_sem.at[a]) for a in arrays]
+    along, flat, cross, core = {}, {}, {}, {}
+    for dz, a in items:
+        full = fulls[a].at[0, dz]
+        source = full.at[0, 0] if dz else shards[a]
+        if dz:
+            along[dz, a] = remote(shards[a], full.at[0, 0], z_sem, (a, dz), at(dz=dz))
+        flat[dz, a] = (
+            remote(source, full.at[0, 1], p_sem, (a, dz, 0), at(dx=1)),
+            remote(source, full.at[1, 0], p_sem, (a, dz, 1), at(dy=1)),
+        )
+        first, second = pl.ds(0, half), pl.ds(half, half)
+        cross[dz, a] = (
+            remote(full.at[0, 1, second], full.at[1, 1, second], d_sem, (a, dz, 0), at(dy=1)),
+            remote(full.at[1, 0, first], full.at[1, 1, first], d_sem, (a, dz, 1), at(dx=1)),
+        )
+        core[dz, a] = remote(full, fulls[a].at[1, dz], c_sem, (a, dz), at(dc=1))
+
+    def enter():
+        greet(at, layers)
+        for dz in far_first(layers)[:-1]:
+            for a in arrays:
+                along[dz, a].start()
+        for copy in own:
+            copy.start()
+
+    def spread(item):
+        if item[0]:
+            along[item].wait_recv()
+        for copy in flat[item]:
+            copy.start()
+
+    def turn(item):
+        for got, out in zip(flat[item], cross[item]):
+            got.wait_recv()
+            out.start()
+
+    def share(item):
+        for got in cross[item]:
+            got.wait_recv()
+        if not item[0]:
+            own[item[1]].wait()
+        core[item].start()
+
+    steps = []
+    for turn_at in range(len(items) + 4):
+        for action, lag in ((spread, 0), (turn, 2), (share, 4)):
+            if 0 <= turn_at - lag < len(items):
+                steps.append(partial(action, items[turn_at - lag]))
+
+    def leave():
+        for item in items:
+            core[item].wait_recv()
+        for item in items:
+            if item[0]:
+                along[item].wait_send()
+            for copy in (*flat[item], *cross[item], core[item]):
+                copy.wait_send()
+
+    return enter, steps, leave
+
+
+def gather_sems(count, layers):
+    dma = pltpu.SemaphoreType.DMA
+    return [
+        dma((2, count, layers)),
+        dma((2, count, layers, 2)),
+        dma((2, count, layers, 2)),
+        dma((2, count, layers)),
+        dma((count,)),
+    ]
+
+
+def gather_kernel(layers, count, *refs):
+    enter, steps, leave = gather_plan(layers, refs[:count], refs[count : 2 * count], *refs[2 * count :])
+    enter()
+    for step in steps:
+        step()
+    leave()
+
+
+def gather_all(layers, shards, collective_id):
+    count = len(shards)
+    rows, width = shards[0].shape
+    fulls = pl.pallas_call(
+        partial(gather_kernel, layers, count),
+        in_specs=[pl.BlockSpec(memory_space=pl.ANY)] * count,
+        out_specs=[pl.BlockSpec(memory_space=pl.ANY)] * count,
+        out_shape=[jax.ShapeDtypeStruct((2, layers, 2, 2, rows, width), jnp.bfloat16)] * count,
+        scratch_shapes=gather_sems(count, layers),
+        compiler_params=pltpu.CompilerParams(collective_id=collective_id, has_side_effects=True),
+        cost_estimate=pl.CostEstimate(flops=0, bytes_accessed=200 * 2**20, transcendentals=0),
+        name="gather_all",
+    )(*shards)
+    return [full.reshape(8 * layers * rows, width) for full in fulls]
+
+
+def add_rows(target, one, two):
+    target[...] = (one[...].astype(jnp.float32) + two[...].astype(jnp.float32)).astype(target.dtype)
+
+
+def reduce_plan(layers, parts, outs, sums, got_c, got_d, got_p, got_z, load_sem, c_sem, d_sem, p_sem, z_sem):
+    at = chip_place(layers)
+    arrays = range(len(parts))
+    half = parts[0].shape[4] // 2
+    items = [(dz, a) for dz in far_first(layers) for a in arrays]
+    first, second = pl.ds(0, half), pl.ds(half, half)
+    load, core, cross, flat, along = {}, {}, {}, {}, {}
+    for dz, a in items:
+        total = sums.at[a, dz]
+        load[dz, a] = pltpu.make_async_copy(parts[a].at[0, dz], total, load_sem.at[a, dz])
+        core[dz, a] = remote(parts[a].at[1, dz], got_c.at[a, dz], c_sem, (a, dz), at(dc=1))
+        cross[dz, a] = (
+            remote(total.at[1, 1, first], got_d.at[a, dz, 0], d_sem, (a, dz, 0), at(dx=1)),
+            remote(total.at[1, 1, second], got_d.at[a, dz, 1], d_sem, (a, dz, 1), at(dy=1)),
+        )
+        flat[dz, a] = (
+            remote(total.at[1, 0], got_p.at[a, dz, 0], p_sem, (a, dz, 0), at(dy=1)),
+            remote(total.at[0, 1], got_p.at[a, dz, 1], p_sem, (a, dz, 1), at(dx=1)),
+        )
+        if dz:
+            along[dz, a] = remote(
+                total.at[0, 0], got_z.at[a, dz], z_sem, (a, dz), at(dz=layers - dz)
+            )
+
+    def enter():
+        greet(at, layers)
+        for item in items:
+            core[item].start()
+            load[item].start()
+
+    def join_core(item):
+        dz, a = item
+        load[item].wait()
+        core[item].wait_recv()
+        for dy, dx in ((1, 1), (1, 0), (0, 1), (0, 0)):
+            here = sums.at[a, dz, dy, dx]
+            add_rows(here, here, got_c.at[a, dz, dy, dx])
+            if dy and dx:
+                for copy in cross[item]:
+                    copy.start()
+
+    def join_cross(item):
+        dz, a = item
+        one, two = sums.at[a, dz, 1, 0, first], sums.at[a, dz, 0, 1, second]
+        cross[item][0].wait_recv()
+        add_rows(one, one, got_d.at[a, dz, 0])
+        flat[item][0].start()
+        cross[item][1].wait_recv()
+        add_rows(two, two, got_d.at[a, dz, 1])
+        flat[item][1].start()
+
+    def join_flat(item):
+        dz, a = item
+        here = sums.at[a, dz, 0, 0]
+        for copy in flat[item]:
+            copy.wait_recv()
+        here[...] = (
+            here[...].astype(jnp.float32)
+            + got_p[a, dz, 0].astype(jnp.float32)
+            + got_p[a, dz, 1].astype(jnp.float32)
+        ).astype(jnp.bfloat16)
+        if dz:
+            along[item].start()
+
+    steps = []
+    lags = ((join_core, 0), (join_cross, 3), (join_flat, 5))
+    for turn_at in range(len(items) + 5):
+        for action, lag in lags:
+            if 0 <= turn_at - lag < len(items):
+                steps.append(partial(action, items[turn_at - lag]))
+
+    def leave():
+        for a in arrays:
+            total = sums[a, 0, 0, 0].astype(jnp.float32)
+            for dz in range(1, layers):
+                along[dz, a].wait_recv()
+                total = total + got_z[a, dz].astype(jnp.float32)
+            outs[a][...] = total
+        for item in items:
+            if item[0]:
+                along[item].wait_send()
+            for copy in (core[item], *cross[item], *flat[item]):
+                copy.wait_send()
+
+    return enter, steps, leave
+
+
+def reduce_scratch(count, layers, rows, width):
+    dma = pltpu.SemaphoreType.DMA
+    low = lambda *shape: pltpu.VMEM((count, layers, *shape, width), jnp.bfloat16)
+    return [
+        low(2, 2, rows),
+        low(2, 2, rows),
+        low(2, rows // 2),
+        low(2, rows),
+        low(rows),
+        dma((count, layers)),
+        dma((2, count, layers)),
+        dma((2, count, layers, 2)),
+        dma((2, count, layers, 2)),
+        dma((2, count, layers)),
+    ]
+
+
+def reduce_kernel(layers, count, *refs):
+    enter, steps, leave = reduce_plan(layers, refs[:count], refs[count : 2 * count], *refs[2 * count :])
+    enter()
+    for step in steps:
+        step()
+    leave()
+
+
+def reduce_all(layers, parts, collective_id):
+    count = len(parts)
+    total, width = parts[0].shape
+    rows = total // (8 * layers)
+    return pl.pallas_call(
+        partial(reduce_kernel, layers, count),
+        in_specs=[pl.BlockSpec(memory_space=pl.ANY)] * count,
+        out_specs=[pl.BlockSpec(memory_space=pltpu.VMEM)] * count,
+        out_shape=[jax.ShapeDtypeStruct((rows, width), jnp.float32)] * count,
+        scratch_shapes=reduce_scratch(count, layers, rows, width),
+        compiler_params=pltpu.CompilerParams(
+            collective_id=collective_id, has_side_effects=True, vmem_limit_bytes=VMEM
+        ),
+        cost_estimate=pl.CostEstimate(flops=0, bytes_accessed=200 * 2**20, transcendentals=0),
+        name="reduce_all",
+    )(*(part.reshape(2, layers, 2, 2, rows, width) for part in parts))
+
+
 class Hops:
     def __init__(self, layers):
         self.layers = layers
@@ -392,7 +668,7 @@
                 for w in range(4):
                     to = ((z + dz) % self.layers * 2 + (c ^ dc)) * 4 + (w ^ (2 * dy + dx))
                     pairs.append(((z * 2 + c) * 4 + w, to))
-        return lax.ppermute(block, ("utt", "wide"), pairs)
+        return lax.ppermute(block, ("z", "core", "y", "x"), pairs)
 
     def turn(self, block, step):
         pairs = []
@@ -401,83 +677,7 @@
                 for w in range(4):
                     to = (z * 2 + w // 2) * 4 + 2 * c + ((w % 2) ^ step)
                     pairs.append(((z * 2 + c) * 4 + w, to))
-        return lax.ppermute(block, ("utt", "wide"), pairs)
-
-    def gather_rows(self, chunk):
-        half = self.layers // 2
-        along = [chunk] + [self.send(chunk, dz=k) for k in range(1, self.layers)]
-        low = jnp.concatenate(along[:half])
-        high = jnp.concatenate(along[half:])
-        low_y = self.send(low, dy=1)
-        high_x = self.send(high, dx=1)
-        near = [low, low_y, high, high_x]
-        far = [
-            self.send(low, dx=1),
-            self.send(low_y, dx=1),
-            self.send(high, dy=1),
-            self.send(high_x, dy=1),
-        ]
-        mine = near + far
-        return mine + [self.send(block, dc=1) for block in mine]
-
-    def reduce_rows(self, own, other):
-        swapped = self.send(other(), dc=1)
-        total = own(swapped)
-        size = total.shape[0] // 8
-        part = lambda block, at, count=1: lax.slice_in_dim(block, at * size, (at + count) * size)
-        plus = lambda a, b: (a.astype(jnp.float32) + b.astype(jnp.float32)).astype(jnp.bfloat16)
-        low_far = self.send(part(total, 4, 2), dx=1)
-        high_far = self.send(part(total, 6, 2), dy=1)
-        low = plus(part(total, 0, 2), low_far)
-        high = plus(part(total, 2, 2), high_far)
-        low_y = self.send(part(low, 1), dy=1)
-        high_x = self.send(part(high, 1), dx=1)
-        both = jnp.concatenate([plus(part(low, 0), low_y), plus(part(high, 0), high_x)])
-        return self.reduce_layers(both)
-
-    def reduce_layers(self, block):
-        size = block.shape[0] // self.layers
-        result = block[:size].astype(jnp.float32)
-        for k in range(1, self.layers):
-            result = result + self.send(block[k * size : (k + 1) * size], dz=-k).astype(jnp.float32)
-        return result
-
-    def gather_plane(self, first, second):
-        first_x = self.send(first, dx=1)
-        second_y = self.send(second, dy=1)
-        return (
-            [first, first_x, self.send(first, dy=1), self.send(first_x, dy=1)],
-            [second, self.send(second, dx=1), second_y, self.send(second_y, dx=1)],
-        )
-
-    def reduce_plane(self, first, second):
-        plus = lambda a, b: (a.astype(jnp.float32) + b.astype(jnp.float32)).astype(jnp.bfloat16)
-        first_got = self.send(jnp.concatenate(first[2:]), dy=1)
-        second_got = self.send(jnp.concatenate([second[1], second[3]]), dx=1)
-        rows = first[0].shape[0]
-        first_own = plus(first[0], first_got[:rows])
-        first_x = plus(first[1], first_got[rows:])
-        rows = second[0].shape[0]
-        second_own = plus(second[0], second_got[:rows])
-        second_y = plus(second[2], second_got[rows:])
-        return (
-            plus(first_own, self.send(first_x, dx=1)),
-            plus(second_own, self.send(second_y, dy=1)),
-        )
-
-    def sum_layers(self, block):
-        z = lax.axis_index("utt") // 2
-        size = block.shape[0] // self.layers
-        piece = lambda k: lax.dynamic_slice_in_dim(block, (z + k) % self.layers * size, size)
-        total = piece(0).astype(jnp.float32)
-        for k in range(1, self.layers):
-            total = total + self.send(piece(k), dz=k).astype(jnp.float32)
-        total = total.astype(jnp.bfloat16)
-        result = jnp.zeros(block.shape, jnp.bfloat16)
-        for k in range(self.layers):
-            got = total if k == 0 else self.send(total, dz=k)
-            result = lax.dynamic_update_slice_in_dim(result, got, (z - k) % self.layers * size, 0)
-        return result
+        return lax.ppermute(block, ("z", "core", "y", "x"), pairs)
 
 
 def taps_forward(padded, kernel_f, count):
@@ -522,9 +722,10 @@
     second_down,
     final_gain,
 ):
-    utt_at, wide_at = lax.axis_index("utt"), lax.axis_index("wide")
-    core, y, x = utt_at % 2, wide_at // 2, wide_at % 2
-    hops = Hops(lax.axis_size("utt") // 2)
+    core, y, x = lax.axis_index("core"), lax.axis_index("y"), lax.axis_index("x")
+    wide_at = 2 * y + x
+    layers = lax.axis_size("z")
+    hops = Hops(layers)
     groups, quarter, channels = frames.shape
     rows = groups * quarter
     length = 2 * rows
@@ -545,13 +746,12 @@
         return jnp.stack(pick(x == 0, *got))
 
     frames_own = turn_in(frames)
-    first_pieces = hops.gather_rows(first_up)
-    first_pieces_down = hops.gather_rows(first_down)
+    up_first, down_first = gather_all(layers, [first_up, first_down], 1)
     positions = wide_at * quarter + jnp.arange(quarter, dtype=jnp.int32)
     seed_weight = f32(masked) * f32(positions[None, :] < lengths[:, None])
     seed_own_low = low(f32(cotangent) * seed_weight[:, :, None])
-    all_lengths = lax.all_gather(lengths, "utt", axis=0, tiled=True)
-    own_length = lax.dynamic_slice_in_dim(all_lengths, utt_at // 2 * 4 + wide_at, 1)
+    near_lengths = jnp.where(core == y, lengths, hops.send(lengths, dc=1))
+    own_length = lax.dynamic_slice_in_dim(near_lengths, x, 1)
     own_rows = core * rows + jnp.arange(rows, dtype=jnp.int32)
     frame_ok = f32(own_rows < own_length[0])[:, None]
 
@@ -560,47 +760,32 @@
         return lax.dynamic_slice_in_dim(weight, core * count, count)
 
     band = query_weight.shape[0] // 2
-    qk_pieces, vp_pieces = hops.gather_plane(
-        jnp.concatenate([own_half(query_weight), own_half(key_weight)]),
-        jnp.concatenate([own_half(value_weight), own_half(place_weight)]),
-    )
-    query_own = jnp.concatenate([piece[:band] for piece in qk_pieces])
-    key_own = jnp.concatenate([piece[band:] for piece in qk_pieces])
-    value_own = jnp.concatenate([piece[:band] for piece in vp_pieces])
-    place_own = jnp.concatenate([piece[band:] for piece in vp_pieces])
-    op_pieces, glu_pieces = hops.gather_plane(
-        jnp.concatenate([own_half(out_weight), own_half(point_weight)]),
-        own_half(glu_weight),
-    )
-    op_both = op_pieces + [hops.send(piece, dc=1) for piece in op_pieces]
-    glu_both = glu_pieces + [hops.send(piece, dc=1) for piece in glu_pieces]
-    here = wide_at * 2 + core
-    place_at = [((piece % 4) * 2 + piece // 4) ^ here for piece in range(8)]
-
-    def in_order(pieces):
-        size = pieces[0].shape[0]
-        result = jnp.zeros((8 * size, channels), jnp.bfloat16)
-        for piece, at in zip(pieces, place_at):
-            result = lax.dynamic_update_slice_in_dim(result, piece, at * size, 0)
-        return result
-
-    def by_piece(matrix):
-        size = matrix.shape[0] // 8
-        return [lax.dynamic_slice_in_dim(matrix, at * size, size) for at in place_at]
-
-    full_out = jnp.concatenate([piece[:band] for piece in op_both])
-    full_point = in_order([piece[band:] for piece in op_both])
-    full_glu = in_order(glu_both)
-
-    biases = jnp.stack([content_bias, place_bias])
-    all_biases = lax.all_gather(biases, "wide", axis=1, tiled=True)
-    pair_at = [((piece * 2) ^ (wide_at * 2)) + core for piece in range(4)]
-    own_biases = jnp.concatenate(
-        [lax.dynamic_slice_in_dim(all_biases, at * band, band, 1) for at in pair_at], axis=1
-    )
+    own_bias = own_half(jnp.stack([content_bias, place_bias], axis=1)).T
+    attn_chunk = jnp.concatenate(
+        [
+            own_half(query_weight),
+            own_half(key_weight),
+            own_half(value_weight),
+            own_half(place_weight),
+            jnp.pad(own_bias, ((0, 14), (0, channels - band))),
+        ]
+    )
+    conv_chunk = jnp.concatenate([own_half(out_weight), own_half(point_weight), own_half(glu_weight)])
+    attn_all = lax.all_gather(attn_chunk, ("y", "x"), axis=0)
+    conv_all = lax.all_gather(conv_chunk, ("y", "x"), axis=0)
+
+    def heads_of(at):
+        return attn_all[:, at * band : (at + 1) * band].reshape(4 * band, channels)
+
+    query_own, key_own, value_own, place_own = (heads_of(at) for at in range(4))
+    own_biases = attn_all[:, 4 * band : 4 * band + 2, :band].transpose(1, 0, 2).reshape(2, 4 * band)
+    conv_other = hops.send(conv_all, dc=1)
+    conv_both = jnp.stack(pick(core == 0, conv_all, conv_other), axis=1)
+    full_out = jnp.concatenate([conv_all[:, :band], conv_other[:, :band]]).reshape(8 * band, channels)
+    full_point = conv_both[:, :, band : 2 * band].reshape(8 * band, channels)
+    full_glu = conv_both[:, :, 2 * band :].reshape(16 * band, channels)
 
     stream0 = f32(frames_own)
-    up_first, down_first = jnp.concatenate(first_pieces), jnp.concatenate(first_pieces_down)
     stream1, saved_first = ffn_forward(stream0, f32(first_gain), up_first, down_first)
     normed_attn, attn_pull = jax.vjp(norm_rows, stream1, f32(attn_gain))
     attn_half = low(normed_attn)
@@ -636,8 +821,7 @@
     middle, middle_pull = jax.vjp(norm_rows, conv_out, f32(middle_gain))
     swished = low(jax.nn.silu(middle))
     stream3 = stream2 + mult_trans(swished, full_point)
-    up_second = jnp.concatenate(hops.gather_rows(second_up))
-    down_second = jnp.concatenate(hops.gather_rows(second_down))
+    up_second, down_second = gather_all(layers, [second_up, second_down], 1)
     stream4, saved_second = ffn_forward(stream3, f32(second_gain), up_second, down_second)
     final_rows, final_pull = jax.vjp(norm_rows, stream4, f32(final_gain))
     output = turn_out(low(final_rows))
@@ -648,20 +832,11 @@
     def ffn_back(grad_stream, saved_ffn, up_full, down_full):
         norm_pull, normed_low, before, active_low = saved_ffn
         grad_out = low(0.5 * grad_stream)
-        side = active_low.shape[1] // 2
-
-        def reduced(left, right):
-            def half(at):
-                return mult_rows(lax.slice_in_dim(left, at * side, (at + 1) * side, axis=1), right)
-
-            return hops.reduce_rows(
-                lambda got: low(half(0) + f32(got)), lambda: low(half(1))
-            )
-
-        sum_down = reduced(active_low, grad_out)
+        grad_down = low(mult_rows(active_low, grad_out))
         grad_before = low(mult_trans(grad_out, down_full) * silu_slope(before))
-        sum_up = reduced(grad_before, normed_low)
+        grad_up = low(mult_rows(grad_before, normed_low))
         grad_input, grad_gain = norm_pull(mult_plain(grad_before, up_full))
+        sum_up, sum_down = reduce_all(layers, [grad_up, grad_down], 2)
         return grad_stream + grad_input, grad_gain, sum_up, sum_down
 
     grad3, grad_second_gain, sum_up_second, sum_down_second = ffn_back(
@@ -716,46 +891,44 @@
     )
     grad_input = turn_out(low(grad0))
 
-    def split4(matrix):
-        size = matrix.shape[0] // 4
-        return [matrix[at * size : (at + 1) * size] for at in range(4)]
-
-    def joined(*lists):
-        return [jnp.concatenate([low(part) for part in parts]) for parts in zip(*lists)]
-
-    out_size = band
-    out_pieces = [grad_out[at * out_size : (at + 1) * out_size] for at in range(8)]
-    point_pieces, glu_parts = by_piece(grad_point), by_piece(grad_glu)
-    sent = joined(out_pieces[4:], point_pieces[4:], glu_parts[4:])
-    kept = joined(out_pieces[:4], point_pieces[:4], glu_parts[:4])
-    got = hops.send(jnp.concatenate(sent), dc=1)
-    summed = split4(low(f32(jnp.concatenate(kept)) + f32(got)))
-    op_sum, glu_sum = hops.reduce_plane(
-        [part[: 2 * band] for part in summed], [part[2 * band :] for part in summed]
-    )
-    op_glu = hops.sum_layers(jnp.concatenate([op_sum, glu_sum]))
-    qk_sum, vp_sum = hops.reduce_plane(
-        joined(split4(grad_query_w), split4(grad_key_w)),
-        joined(split4(grad_value_w), split4(grad_place_w)),
-    )
-    qkvp = hops.sum_layers(jnp.concatenate([qk_sum, vp_sum]))
-    both_core = [jnp.concatenate([op_glu, qkvp])]
-    both_core.append(hops.send(both_core[0], dc=1))
-
-    def owned(start, count):
-        parts = [part[start : start + count] for part in both_core]
-        return f32(jnp.concatenate(pick(core == 0, *parts)))
-
-    total_out, total_point = owned(0, band), owned(band, band)
-    total_glu = owned(2 * band, 2 * band)
-    total_query, total_key = owned(4 * band, band), owned(5 * band, band)
-    total_value, total_place = owned(6 * band, band), owned(7 * band, band)
-
-    spread = jnp.zeros((2, channels), jnp.float32)
-    for piece, at in enumerate(pair_at):
-        spread = lax.dynamic_update_slice(
-            spread, grad_biases[:2, piece * band : (piece + 1) * band], (0, at * band)
-        )
+    def by_wide(matrix):
+        return low(matrix).reshape(4, -1, channels)
+
+    def by_core(matrix):
+        parts = low(matrix).reshape(4, 2, -1, channels)
+        own = lax.dynamic_index_in_dim(parts, core, 1, keepdims=False)
+        return own, lax.dynamic_index_in_dim(parts, 1 - core, 1, keepdims=False)
+
+    out_parts = (by_wide(grad_out[: 4 * band]), by_wide(grad_out[4 * band :]))
+    kept, sent = (
+        jnp.concatenate(parts, axis=1)
+        for parts in zip(out_parts, by_core(grad_point), by_core(grad_glu))
+    )
+    conv_part = low(f32(kept) + f32(hops.send(sent, dc=1)))
+    attn_part = jnp.concatenate(
+        [by_wide(part) for part in (grad_query_w, grad_key_w, grad_value_w, grad_place_w)], axis=1
+    )
+
+    def totals_of(part):
+        mine = lax.psum_scatter(part, ("y", "x"), scatter_dimension=0, tiled=False)
+        mine = lax.psum(mine, "z")
+        return pick(core == 0, mine, hops.send(mine, dc=1))
+
+    conv_totals, attn_totals = totals_of(conv_part), totals_of(attn_part)
+
+    def owned(totals, start, count):
+        return f32(jnp.concatenate([part[start : start + count] for part in totals]))
+
+    total_out, total_point = owned(conv_totals, 0, band), owned(conv_totals, band, band)
+    total_glu = owned(conv_totals, 2 * band, 2 * band)
+    total_query, total_key, total_value, total_place = (
+        owned(attn_totals, at * band, band) for at in range(4)
+    )
+
+    spread = jnp.zeros((2, 4, 2, band), jnp.float32)
+    spread = lax.dynamic_update_slice(
+        spread, grad_biases[:2].reshape(2, 4, 1, band), (0, 0, core, 0)
+    ).reshape(2, channels)
     small = lax.psum(
         jnp.concatenate(
             [
@@ -769,9 +942,9 @@
                 grad_kernel,
             ]
         ),
-        ("utt", "wide"),
-    )
-    own_bias = lax.dynamic_slice_in_dim(small[6:8], wide_at * 2 * band, 2 * band, 1)
+        ("z", "core", "y", "x"),
+    )
+    own_bias_grad = lax.dynamic_slice_in_dim(small[6:8], wide_at * 2 * band, 2 * band, 1)
     return (
         output,
         grad_input,
@@ -784,8 +957,8 @@
         total_value,
         total_out,
         total_place,
-        own_bias[0],
-        own_bias[1],
+        own_bias_grad[0],
+        own_bias_grad[1],
         small[2],
         total_glu,
         small[8:],
@@ -1114,58 +1287,65 @@
 
 
 def solution(mesh):
+    shape = dict(mesh.shape)
+    if shape["wide"] == 4 and shape["utt"] % 4 == 0:
+        mesh = jax.sharding.Mesh(
+            mesh.devices.reshape(shape["utt"] // 2, 2, 2, 2), ("z", "core", "y", "x")
+        )
+        utt, wide, body = ("z", "core"), ("y", "x"), per_chip
+    else:
+        utt, wide, body = "utt", "wide", per_device
+    every = (utt, wide) if utt == "utt" else (*utt, *wide)
     in_specs = (
-        P("utt", "wide", None),
-        P("utt"),
-        P("utt", "wide"),
-        P("utt", "wide", None),
+        P(utt, wide, None),
+        P(utt),
+        P(utt, wide),
+        P(utt, wide, None),
         P(),
-        P(("utt", "wide"), None),
-        P(("utt", "wide"), None),
+        P(every, None),
+        P(every, None),
         P(),
-        P("wide", None),
-        P("wide", None),
-        P("wide", None),
-        P("wide", None),
-        P("wide", None),
-        P("wide"),
-        P("wide"),
+        P(wide, None),
+        P(wide, None),
+        P(wide, None),
+        P(wide, None),
+        P(wide, None),
+        P(wide),
+        P(wide),
         P(),
-        P("wide", None),
+        P(wide, None),
         P(),
         P(),
-        P("wide", None),
+        P(wide, None),
         P(),
-        P(("utt", "wide"), None),
-        P(("utt", "wide"), None),
+        P(every, None),
+        P(every, None),
         P(),
     )
     out_specs = (
-        P("utt", "wide", None),
-        P("utt", "wide", None),
+        P(utt, wide, None),
+        P(utt, wide, None),
         P(),
-        P(("utt", "wide"), None),
-        P(("utt", "wide"), None),
+        P(every, None),
+        P(every, None),
         P(),
-        P("wide", None),
-        P("wide", None),
-        P("wide", None),
-        P("wide", None),
-        P("wide", None),
-        P("wide"),
-        P("wide"),
+        P(wide, None),
+        P(wide, None),
+        P(wide, None),
+        P(wide, None),
+        P(wide, None),
+        P(wide),
+        P(wide),
         P(),
-        P("wide", None),
+        P(wide, None),
         P(),
         P(),
-        P("wide", None),
+        P(wide, None),
         P(),
-        P(("utt", "wide"), None),
-        P(("utt", "wide"), None),
+        P(every, None),
+        P(every, None),
         P(),
     )
-    shape = dict(mesh.shape)
-    body = per_chip if shape["wide"] == 4 and shape["utt"] % 4 == 0 else per_device
     return jax.shard_map(
         body, mesh=mesh, in_specs=in_specs, out_specs=out_specs, check_vma=False
     )

time: 1250 us -> 1000 us (0.80)
  Pallas kernels: 86 us -> 491 us
  waiting for transfers between devices: 549 us -> 151 us
  starting transfers between devices: 148 us -> 26.7 us
  local copies, waits for them, and re-layouts: 134 us -> 37.7 us
  blocking collectives: 20.7 us -> 0 us
    ppermute x156 -> x19, waiting for transfers between devices: 432 us -> 0.75 us  [the longest x11 0.73 us: send(): return lax.ppermute(block, ('z', 'core', 'y', 'x'), pairs)]
    pallas_call x0 -> x4, Pallas kernels: none -> 406 us  [the longest x2 240 us: gather_all(): pl.pallas_call(partial(gather_kernel, layers, count), in_specs=[pl.BlockS...]
    ppermute x156 -> x19, starting transfers between devices: 148 us -> 26 us  [the longest x8 22.1 us: turn(): return lax.ppermute(block, ('z', 'core', 'y', 'x'), pairs)]
    psum x0 -> x1, waiting for transfers between devices: none -> 76.8 us  [totals_of(): mine = lax.psum(mine, 'z')]
    unnamed x441 -> x262, local copies, waits for them, and re-layouts: 80.8 us -> 14.7 us
    psum x1, waiting for transfers between devices: 117 us -> 53.5 us  [per_chip(): lax.psum(jnp.concatenate([grad_first_gain[None], grad_attn_gain[None], gr...]
    unnamed x1 -> x8, waiting for transfers between devices: 0.02 us -> 20 us
    concatenate x14 -> x1, local copies, waits for them, and re-layouts: 16.1 us -> 0.01 us  [per_chip(): jnp.concatenate([own_half(query_weight), own_half(key_weight), own_half(v...]
  transfers between devices with their start and end apart: 157 -> 25, of which waited for: 62 -> 4; matrix products, arithmetic and copies ran while one was open for 25% -> 21% of each run, Pallas kernels for 7% -> 49%
where the time goes in v2:
time: 1000 us; the launch traced here: 994 us
  Pallas kernels  491 us (49%)
  matrix products  157 us (16%)
  waiting for transfers between devices  151 us (15%)
  other arithmetic  114 us (11%)
  local copies, waits for them, and re-layouts  37.7 us (4%)
  starting transfers between devices  26.7 us (3%)
  between operations  16.4 us (2%)
    pallas_call x2, Pallas kernels, gather_all(): pl.pallas_call(partial(gather_kernel, layers, count), in_specs=[pl.BlockS...  240 us
    pallas_call x2, Pallas kernels, reduce_all(): pl.pallas_call(partial(reduce_kernel, layers, count), in_specs=[pl.BlockS...  165 us
    psum x1, waiting for transfers between devices, totals_of(): mine = lax.psum(mine, 'z')  76.8 us
    dot_general x11, matrix products, mult_trans(): lax.dot_general(first_mat, second_mat, (((1,), (1,)), ((), ())), preferre...  60.7 us
    psum x1, waiting for transfers between devices, per_chip(): lax.psum(jnp.concatenate([grad_first_gain[None], grad_attn_gain[None], gr...  53.5 us
    dot_general x11, matrix products, mult_rows(): lax.dot_general(first_mat, second_mat, (((0,), (0,)), ((), ())), preferre...  53.4 us
    pallas_call x1, Pallas kernels, attend_bwd(): pl.pallas_call(partial(attend_bwd_kernel, scale=1.0 / math.sqrt(HEAD_DIM)...  50.9 us
    dot_general x10, matrix products, mult_plain(): return jnp.dot(first_mat, second_mat, preferred_element_type=jnp.float32)  42.8 us
  transfers between devices with their start and end apart: 25, of which 4 were waited for; matrix products, arithmetic and copies ran while one was open for 21% of the time, Pallas kernels for 49%

profile of v2, /device:TPU:8, one launch (start us, length us, event | category | flops | bytes accessed | tf_op | source)
XLA Modules:
  0.0 993.7 jit_solution(15328056287009972098)
XLA Ops:
  11.8 1.7 collective-permute-start
  13.5 1.5 collective-permute-start.1
  15.0 1.4 collective-permute-start.2
  17.8 5.5 collective-permute-start.9
  25.4 132.8 %gather_all.2 = (bf16[2,4,2,2,128,1024]{5,4,3,2,1,0:T(8,128)(2,1)}, bf16[2,4,2,2,128,1024]{5,4,3,2,1,0:T(8,128)(2,1)}) custom-call(bf16[128,1024]{1,0:T(8,128)(2,1)} %refs_0_.2, bf16[128,1024]{1,0:T(8,128)(2,1)} %refs_1_.2), custom_call_target="tpu_custom_call" | custom-call | bytes 209715200 | tf_op jit(solution)/shard_map/gather_all/pallas_call | solution.py:513
  159.2 11.2 %fusion.186 = f32[512,4096]{1,0:T(8,128)} fusion(bf16[4096,1024]{1,0:T(8,128)(2,1)} %bitcast.322, f32[1024]{0:T(1024)S(1)} %convert_element_type.449, f32[512]{0:T(512)S(1)} %fusion.165, f32[512]{0:T(512)S(1)} %broadcast_multiply_fusion.5, bf16[256,1024]{1,0:T(8,128)(2,1)S(1)} %get-tuple-element.160, bf16[256,1024]{1,0:T(8,128)(2,1)S(1)} %get-tuple-element.159), kind=kOutput, calls=%fused_computation.503 | convolution fusion | flops 4299161600 | bytes 17833984 | tf_op jit(solution)/shard_map/dot_general | solution.py:51
  170.4 7.7 fusion.209
  179.5 107.5 %gather_all.3 = (bf16[2,4,2,2,128,1024]{5,4,3,2,1,0:T(8,128)(2,1)}, bf16[2,4,2,2,128,1024]{5,4,3,2,1,0:T(8,128)(2,1)}) custom-call(bf16[128,1024]{1,0:T(8,128)(2,1)} %refs_0_.3, bf16[128,1024]{1,0:T(8,128)(2,1)} %refs_1_.3), custom_call_target="tpu_custom_call" | custom-call | bytes 209715200 | tf_op jit(solution)/shard_map/gather_all/pallas_call | solution.py:513
  287.1 17.4 %fusion.2 = (bf16[2047,512]{1,0:T(8,128)(2,1)}, bf16[2047,512]{1,0:T(8,128)(2,1)}) fusion(f32[512]{0:T(512)S(1)} %multiply_exponential_fusion, f32[2047]{0:T(1024)S(1)} %convert_subtract_fusion.1), kind=kLoop, calls=%fused_computation.106 | loop fusion | flops 3144192 | bytes 4202492 | tf_op jit(solution)/shard_map/convert.4
  305.1 3.1 broadcast_select_fusion.5
  308.7 2.8 fusion.199
  312.2 2.3 convolution_convert_fusion.14.q_ref
  314.5 2.3 convolution_convert_fusion.13.k_ref
  316.8 2.3 convolution_convert_fusion.12.v_ref
  319.6 3.7 convolution_convert_fusion.5.place_ref
  323.3 34.8 %attend_fwd.1 = (bf16[1024,512]{1,0:T(8,128)(2,1)}, bf16[8,1024,1024]{2,1,0:T(8,128)(2,1)}) custom-call(s32[1]{0:T(128)} %dynamic_slice.71.len_ref, bf16[1024,512]{1,0:T(8,128)(2,1)} %convolution_convert_fusion.14.q_ref, bf16[1024,512]{1,0:T(8,128)(2,1)} %convolution_convert_fusion.13.k_ref, bf16[1024,512]{1,0:T(8,128)(2,1)} %convolution_convert_fusion.12.v_ref, ...), custom_call_target="tpu_custom_call" | custom-call | flops 40000000000 | bytes 20971520 | tf_op jit(solution)/shard_map/attend_fwd/pallas_call | solution.py:262
  358.1 1.4 constant_dynamic-slice_fusion.6
  363.5 1.4 fusion.210
  365.3 2.9 select_bitcast_fusion.1
  368.8 2.4 fusion.189
  373.2 10.2 %fusion.197 = (f32[512]{0:T(512)S(1)}, f32[512,1024]{1,0:T(8,128)S(1)}) fusion(f32[1024]{0:T(1024)S(1)} %bitcast.235, bf16[15,1024]{1,0:T(8,128)(2,1)S(1)} %get-tuple-element.203, bf16[512,1024]{1,0:T(8,128)(2,1)S(1)} %multiply_convert_fusion.12, f32[1024]{0:T(1024)S(1)} %bitcast.233, f32[1024]{0:T(1024)S(1)} %bitcast.231, f32[1024]{0:T(1024)S(1)} %bitcast.229, ...), kind=kLoop, calls=%fused_computation.512 | loop fusion | flops 95944192 | bytes 3336192 | tf_op jit(solution)/shard_map/jvp()/reduce_sum | solution.py:39
  383.8 1.6 fusion.211
  385.8 10.7 %fusion.190 = f32[512,4096]{1,0:T(8,128)} fusion(bf16[4096,1024]{1,0:T(8,128)(2,1)} %bitcast.330, f32[512,1024]{1,0:T(8,128)S(1)} %get-tuple-element.215, f32[1024]{0:T(1024)S(1)} %convert_element_type.498, f32[512]{0:T(512)S(1)} %fusion.169, f32[512]{0:T(512)S(1)} %broadcast_multiply_fusion.1), kind=kOutput, calls=%fused_computation.506 | convolution fusion | flops 4297064448 | bytes 18882560 | tf_op jit(solution)/shard_map/dot_general | solution.py:51
  396.5 10.1 %fusion.212 = (f32[512]{0:T(512)S(1)}, f32[512,1024]{1,0:T(8,128)S(1)}) fusion(f32[512,1024]{1,0:T(8,128)S(1)} %get-tuple-element.215, bf16[4096,1024]{1,0:T(8,128)(2,1)} %bitcast.332, f32[512,4096]{1,0:T(8,128)} %fusion.190), kind=kOutput, calls=%fused_computation.526 | convolution fusion | flops 4307025408 | bytes 20973568 | tf_op jit(solution)/shard_map/dot_general | solution.py:57
  406.9 1.4 fusion.47
  408.3 1.8 fusion.196
  410.1 12.3 %multiply_convert_fusion.1 = bf16[512,4096]{1,0:T(8,128)(2,1)} fusion(f32[512,4096]{1,0:T(8,128)} %fusion.190, bf16[4096,1024]{1,0:T(8,128)(2,1)} %bitcast.333, f32[512,1024]{1,0:T(8,128)S(1)} %get-tuple-element.109, f32[512]{0:T(512)S(1)} %negate_multiply_fusion.5), kind=kOutput, calls=%fused_computation.39 | convolution fusion | flops 4315414528 | bytes 23070720 | tf_op jit(solution)/shard_map/dot_general | solution.py:51
  422.4 9.2 multiply_reduce_fusion
  433.9 2.7 multiply_reduce_fusion.1
  437.4 8.3 fusion.96
  447.1 5.3 collective-permute-start.7
  452.8 15.7 %multiply_convert_fusion.6 = (bf16[512,1024]{1,0:T(8,128)(2,1)S(1)}, f32[512,1024]{1,0:T(8,128)S(1)}) fusion(f32[512,2048]{1,0:T(8,128)S(1)} %fusion.189, f32[512]{0:T(512)S(1)} %fusion.164, f32[1024]{0:T(1024)S(1)} %bitcast.238, bf16[15,1024]{1,0:T(8,128)(2,1)S(1)} %get-tuple-element.201, bf16[512,1024]{1,0:T(8,128)(2,1)S(1)} %get-tuple-element.97, ...), kind=kLoop, calls=%fused_computation.273 | loop fusion | flops 98566144 | bytes 6481920 | tf_op jit(solution)/shard_map/convert.2
  469.6 3.2 multiply_reduce_fusion.2
  476.6 1.6 convolution_convert_fusion.6
  480.6 50.9 %attend_bwd.1 = (bf16[1024,512]{1,0:T(8,128)(2,1)}, bf16[1024,512]{1,0:T(8,128)(2,1)}, bf16[1024,512]{1,0:T(8,128)(2,1)}, bf16[2048,512]{1,0:T(8,128)(2,1)}, f32[8,512]{1,0:T(8,128)}) custom-call(bf16[1024,512]{1,0:T(8,128)(2,1)} %convolution_convert_fusion.14.q_ref, bf16[1024,512]{1,0:T(8,128)(2,1)} %convolution_convert_fusion.13.k_ref, ...), custom_call_target="tpu_custom_call" | custom-call | flops 80000000000 | bytes 20971520 | tf_op jit(solution)/shard_map/attend_bwd/pallas_call | solution.py:361
  531.5 4.1 convolution_convert_fusion.15
  539.5 2.2 pad_maximum_fusion
  542.3 12.5 %convolution_convert_fusion = bf16[4096,1024]{1,0:T(8,128)(2,1)} fusion(f32[512,1024]{1,0:T(8,128)} %copy-done.21, f32[512]{0:T(512)S(1)} %negate_multiply_fusion.5, f32[512,4096]{1,0:T(8,128)} %fusion.190), kind=kOutput, calls=%fused_computation.44 | convolution fusion | flops 4311220224 | bytes 18876416 | tf_op jit(solution)/shard_map/dot_general | solution.py:61
  554.7 2.5 convolution_convert_fusion.4
  560.6 2.6 pad_maximum_fusion.1
  565.0 7.1 convolution_convert_fusion.1
  572.2 87.3 %reduce_all.3 = (f32[128,1024]{1,0:T(8,128)}, f32[128,1024]{1,0:T(8,128)}) custom-call(bf16[2,4,2,2,128,1024]{5,4,3,2,1,0:T(8,128)(2,1)} %bitcast.184, bf16[2,4,2,2,128,1024]{5,4,3,2,1,0:T(8,128)(2,1)} %bitcast.181), custom_call_target="tpu_custom_call" | custom-call | bytes 209715200 | tf_op jit(solution)/shard_map/reduce_all/pallas_call | solution.py:646
  659.6 2.5 fusion.95
  662.1 2.7 fusion.80
  669.2 1.9 copy-done.8
  672.7 5.2 add_convert_fusion
  678.0 1.9 fusion.79
  680.0 1.4 select_bitcast_fusion.5
  683.4 3.2 multiply_reduce_fusion.3
  687.2 2.2 fusion.191
  689.7 10.8 %multiply_convert_fusion = bf16[512,4096]{1,0:T(8,128)(2,1)S(1)} fusion(f32[512,4096]{1,0:T(8,128)} %fusion.186, bf16[4096,1024]{1,0:T(8,128)(2,1)} %bitcast.326, f32[512,1024]{1,0:T(8,128)S(1)} %add_add_fusion.7), kind=kOutput, calls=%fused_computation.38 | convolution fusion | flops 4314890240 | bytes 23068672 | tf_op jit(solution)/shard_map/dot_general | solution.py:51
  700.6 4.7 fusion.49
  708.3 5.4 collective-permute-start.14
  713.7 1.7 collective-permute-start.15
  715.5 3.3 concatenate.153
  718.8 19.9 %reduce-scatter.9.cloned.1.call-done = bf16[1,512,1024]{2,1,0:T(8,128)(2,1)} async-done(((bf16[4,512,1024]{2,1,0:T(8,128)(2,1)}), bf16[1,512,1024]{2,1,0:T(8,128)(2,1)}) %reduce-scatter.9.cloned.1.call-update) | async-done | bytes 1048592
  738.7 11.4 %convolution_convert_fusion.2 = bf16[4096,1024]{1,0:T(8,128)(2,1)} fusion(f32[512,1024]{1,0:T(8,128)S(1)} %add_add_fusion.7, f32[512,4096]{1,0:T(8,128)} %fusion.186), kind=kOutput, calls=%fused_computation.46 | convolution fusion | flops 4310695936 | bytes 18874368 | tf_op jit(solution)/shard_map/dot_general | solution.py:61
  750.1 76.8 %all-reduce.10.cloned.1.call-done = (bf16[512,1024]{1,0:T(8,128)(2,1)}, bf16[512,1024]{1,0:T(8,128)(2,1)}) async-done(((bf16[512,1024]{1,0:T(8,128)(2,1)}, bf16[512,1024]{1,0:T(8,128)(2,1)}), (bf16[512,1024]{1,0:T(8,128)(2,1)}, bf16[512,1024]{1,0:T(8,128)(2,1)})) %all-reduce.10.cloned.1.call-update) | async-done | bytes 2097168 | tf_op jit(solution)/shard_map/psum | solution.py:914
  827.0 9.2 convolution_convert_fusion.3
  836.1 78.0 %reduce_all.2 = (f32[128,1024]{1,0:T(8,128)}, f32[128,1024]{1,0:T(8,128)}) custom-call(bf16[2,4,2,2,128,1024]{5,4,3,2,1,0:T(8,128)(2,1)} %bitcast.183, bf16[2,4,2,2,128,1024]{5,4,3,2,1,0:T(8,128)(2,1)} %bitcast.182), custom_call_target="tpu_custom_call" | custom-call | bytes 209715200 | tf_op jit(solution)/shard_map/reduce_all/pallas_call | solution.py:646
  914.1 53.5 %all-reduce.8.cloned.1.call-done = f32[39,1024]{1,0:T(8,128)} async-done(((f32[39,1024]{1,0:T(8,128)}), f32[39,1024]{1,0:T(8,128)}) %all-reduce.8.cloned.1.call-update) | async-done | bytes 159760 | tf_op jit(solution)/shard_map/psum | solution.py:932
  968.4 1.6 slice.932
  970.6 1.7 fusion.205
  980.9 1.6 maximum_convert_fusion
  (430 shorter events, 67.4 us)
Async XLA Ops:
  7.2 301.0 %all-gather.7.cloned.1.call-start = ((), (), s32[]{:S(2)}) async-start(), calls=%async_computation.4 | async-start | bytes 5242880 | tf_op jit(solution)/shard_map/all_gather | solution.py:775
  10.7 297.9 %all-gather.5.cloned.1.call-start = ((), (), s32[]{:S(2)}) async-start(), calls=%async_computation.3 | async-start | bytes 5406720 | tf_op jit(solution)/shard_map/all_gather | solution.py:774
  11.8 146.5 %collective-permute-start = (bf16[256,1024]{1,0:T(8,128)(2,1)}, bf16[256,1024]{1,0:T(8,128)(2,1)S(1)}, u32[]{:S(2)}, u32[]{:S(2)}) collective-permute-start(bf16[256,1024]{1,0:T(8,128)(2,1)} %get-tuple-element.161), channel_id=1, source_target_pairs={{0,0},{1,1},{2,4},{3,5},{4,2},{5,3},{6,6},{7,7},{8,8},{9,9},{10,12... | collective-permute-start | bytes 1572872 | tf_op jit(solution)/shard_map/ppermute | solution.py:680
  13.5 144.8 %collective-permute-start.1 = (bf16[256,1024]{1,0:T(8,128)(2,1)}, bf16[256,1024]{1,0:T(8,128)(2,1)S(1)}, u32[]{:S(2)}, u32[]{:S(2)}) collective-permute-start(bf16[256,1024]{1,0:T(8,128)(2,1)} %get-tuple-element.162), channel_id=1, source_target_pairs={{0,1},{1,0},{2,5},{3,4},{4,3},{5,2},{6,7},{7,6},{8,9},{9,8},{10,13... | collective-permute-start | bytes 1572872 | tf_op jit(solution)/shard_map/ppermute | solution.py:680
  15.0 289.4 %collective-permute-start.2 = (s32[2]{0:T(128)S(1)}, s32[2]{0:T(128)S(1)}, u32[]{:S(2)}, u32[]{:S(2)}) collective-permute-start(s32[2]{0:T(128)S(1)} %copy-done.111), channel_id=1, source_target_pairs={{0,4},{1,5},{2,6},{3,7},{4,0},{5,1},{6,2},{7,3},{8,12},{9,13},{10,... | collective-permute-start | bytes 32 | tf_op jit(solution)/shard_map/ppermute | solution.py:671
  17.8 140.5 %copy-start.64 = (bf16[31,1024]{1,0:T(8,128)(2,1)S(1)}, bf16[31,1024]{1,0:T(8,128)(2,1)}, u32[]{:S(2)}) copy-start(bf16[31,1024]{1,0:T(8,128)(2,1)} %param.41) | copy-start | bytes 190468
  17.8 342.7 %collective-permute-start.9 = (bf16[256,1024]{1,0:T(8,128)(2,1)}, bf16[256,1024]{1,0:T(8,128)(2,1)}, u32[]{:S(2)}, u32[]{:S(2)}) collective-permute-start(bf16[256,1024]{1,0:T(8,128)(2,1)} %get-tuple-element.151), channel_id=1, source_target_pairs={{0,0},{1,1},{2,4},{3,5},{4,2},{5,3},{6,6},{7,7},{8,8},{9,9},{10,12... | collective-permute-start | bytes 1572872 | tf_op jit(solution)/shard_map/ppermute | solution.py:680
  23.3 337.2 %collective-permute-start.10 = (bf16[256,1024]{1,0:T(8,128)(2,1)}, bf16[256,1024]{1,0:T(8,128)(2,1)}, u32[]{:S(2)}, u32[]{:S(2)}) collective-permute-start(bf16[256,1024]{1,0:T(8,128)(2,1)} %get-tuple-element.152), channel_id=1, source_target_pairs={{0,1},{1,0},{2,5},{3,4},{4,3},{5,2},{6,7},{7,6},{8,9},{9,8},{10,13... | collective-permute-start | bytes 1572872 | tf_op jit(solution)/shard_map/ppermute | solution.py:680
  25.3 693.5 %reduce-scatter.7.cloned.1.call-start = ((), (), s32[]{:S(2)}) async-start(), calls=%async_computation.5 | async-start | bytes 5242880
  25.4 133.7 %copy-start.75 = (f32[1024]{0:T(1024)}, f32[1024]{0:T(1024)S(1)}, u32[]{:S(2)}) copy-start(f32[1024]{0:T(1024)S(1)} %convert_element_type.449) | copy-start | bytes 12292
  25.4 279.6 %copy-start.69 = (f32[1024]{0:T(1024)}, f32[1024]{0:T(1024)S(1)}, u32[]{:S(2)}) copy-start(f32[1024]{0:T(1024)S(1)} %convert_element_type.452) | copy-start | bytes 12292
  158.4 11.9 %copy-start.10 = (bf16[256,1024]{1,0:T(8,128)(2,1)}, bf16[256,1024]{1,0:T(8,128)(2,1)S(1)}, u32[]{:S(2)}) copy-start(bf16[256,1024]{1,0:T(8,128)(2,1)S(1)} %get-tuple-element.159) | copy-start | bytes 1572868
  158.5 11.9 %copy-start.12 = (bf16[256,1024]{1,0:T(8,128)(2,1)}, bf16[256,1024]{1,0:T(8,128)(2,1)S(1)}, u32[]{:S(2)}) copy-start(bf16[256,1024]{1,0:T(8,128)(2,1)S(1)} %get-tuple-element.160) | copy-start | bytes 1572868
  158.7 11.7 %copy-start.77 = (f32[512]{0:T(512)}, f32[512]{0:T(512)S(1)}, u32[]{:S(2)}) copy-start(f32[512]{0:T(512)S(1)} %broadcast_multiply_fusion.5) | copy-start | bytes 6148
  158.7 11.7 %slice-start.2 = ((s8[8388608]{0:T(1024)(128)(4,1)}), s8[4194304]{0:T(1024)(128)(4,1)S(1)}, s32[]{:S(2)}) async-start(s8[8388608]{0:T(1024)(128)(4,1)} %bitcast.327), calls=%async_computation.10 | async-start | bytes 8388608
  159.1 11.2 %copy-start.81 = (f32[512]{0:T(512)}, f32[512]{0:T(512)S(1)}, u32[]{:S(2)}) copy-start(f32[512]{0:T(512)S(1)} %fusion.48) | copy-start | bytes 6148
  159.1 11.2 %copy-start.79 = (f32[512]{0:T(512)}, f32[512]{0:T(512)S(1)}, u32[]{:S(2)}) copy-start(f32[512]{0:T(512)S(1)} %fusion.165) | copy-start | bytes 6148
  159.2 11.2 %slice-start.3 = ((s8[8388608]{0:T(1024)(128)(4,1)}), s8[4194304]{0:T(1024)(128)(4,1)S(1)}, s32[]{:S(2)}) async-start(s8[8388608]{0:T(1024)(128)(4,1)} %bitcast.327), calls=%async_computation.11 | async-start | bytes 8388608
  178.1 185.3 %copy-start.2 = (f32[512,1024]{1,0:T(8,128)}, f32[512,1024]{1,0:T(8,128)S(1)}, u32[]{:S(2)}) copy-start(f32[512,1024]{1,0:T(8,128)S(1)} %get-tuple-element.211) | copy-start | bytes 6291460
  178.1 126.9 %copy-start.71 = (f32[512]{0:T(512)}, f32[512]{0:T(512)S(1)}, u32[]{:S(2)}) copy-start(f32[512]{0:T(512)S(1)} %broadcast_multiply_fusion.4) | copy-start | bytes 6148
  178.5 108.5 %copy-start.85 = (f32[512]{0:T(512)}, f32[512]{0:T(512)S(1)}, u32[]{:S(2)}) copy-start(f32[512]{0:T(512)S(1)} %multiply_reduce_fusion.12) | copy-start | bytes 6148
  178.6 126.5 %copy-start.73 = (f32[512]{0:T(512)}, f32[512]{0:T(512)S(1)}, u32[]{:S(2)}) copy-start(f32[512]{0:T(512)S(1)} %fusion.166) | copy-start | bytes 6148
  178.9 126.1 %collective-permute-start.3 = (bf16[512,1024]{1,0:T(8,128)(2,1)S(1)}, bf16[512,1024]{1,0:T(8,128)(2,1)}, u32[]{:S(2)}, u32[]{:S(2)}) collective-permute-start(bf16[512,1024]{1,0:T(8,128)(2,1)S(1)} %multiply_convert_fusion.14), channel_id=1, source_target_pairs={{0,4},{1,5},{2,6},{3,7},{4,0},{5,1},{6,2},{7,3},{8,12},{9,13},{10,... | collective-permute-start | bytes 3145736 | tf_op jit(solution)/shard_map/ppermute | solution.py:671
  179.5 252.1 %copy-start.97 = (f32[1024]{0:T(1024)}, f32[1024]{0:T(1024)S(1)}, u32[]{:S(2)}) copy-start(f32[1024]{0:T(1024)S(1)} %convert_element_type.498) | copy-start | bytes 12292
  308.2 53.7 %collective-permute-start.5 = (bf16[4,512,1024]{2,1,0:T(8,128)(2,1)}, bf16[4,512,1024]{2,1,0:T(8,128)(2,1)}, u32[]{:S(2)}, u32[]{:S(2)}) collective-permute-start(bf16[4,512,1024]{2,1,0:T(8,128)(2,1)} %bitcast.185), channel_id=1, source_target_pairs={{0,4},{1,5},{2,6},{3,7},{4,0},{5,1},{6,2},{7,3},{8,12},{9,13},{10,... | collective-permute-start | bytes 12582920 | tf_op jit(solution)/shard_map/ppermute | solution.py:671
  359.5 3.9 collective-permute-start.4
  364.9 107.9 %copy-start.14 = (f32[512,1024]{1,0:T(8,128)}, f32[512,1024]{1,0:T(8,128)S(1)}, u32[]{:S(2)}) copy-start(f32[512,1024]{1,0:T(8,128)S(1)} %get-tuple-element.213) | copy-start | bytes 6291460
  371.8 65.5 %copy-start.4 = (bf16[512,1024]{1,0:T(8,128)(2,1)}, bf16[512,1024]{1,0:T(8,128)(2,1)S(1)}, u32[]{:S(2)}) copy-start(bf16[512,1024]{1,0:T(8,128)(2,1)S(1)} %multiply_convert_fusion.12) | copy-start | bytes 3145732
  371.9 1.3 collective-permute-start.6
  372.4 11.4 %copy-start.27 = (bf16[4,2,128,1024]{3,2,1,0:T(8,128)(2,1)}, bf16[4,2,128,1024]{3,2,1,0:T(8,128)(2,1)S(1)}, u32[]{:S(2)}) copy-start(bf16[4,2,128,1024]{3,2,1,0:T(8,128)(2,1)S(1)} %pad_maximum_fusion.2) | copy-start | bytes 6291460
  373.2 64.2 %copy-start.56 = (bf16[15,1024]{1,0:T(8,128)(2,1)}, bf16[15,1024]{1,0:T(8,128)(2,1)S(1)}, u32[]{:S(2)}) copy-start(bf16[15,1024]{1,0:T(8,128)(2,1)S(1)} %get-tuple-element.203) | copy-start | bytes 92164
  385.4 46.2 %copy-start.16 = (f32[512,1024]{1,0:T(8,128)}, f32[512,1024]{1,0:T(8,128)S(1)}, u32[]{:S(2)}) copy-start(f32[512,1024]{1,0:T(8,128)S(1)} %get-tuple-element.215) | copy-start | bytes 6291460
  385.4 46.2 %copy-start.83 = (f32[512]{0:T(512)}, f32[512]{0:T(512)S(1)}, u32[]{:S(2)}) copy-start(f32[512]{0:T(512)S(1)} %broadcast_multiply_fusion.1) | copy-start | bytes 6148
  385.7 45.9 %copy-start.99 = (f32[512]{0:T(512)}, f32[512]{0:T(512)S(1)}, u32[]{:S(2)}) copy-start(f32[512]{0:T(512)S(1)} %fusion.169) | copy-start | bytes 6148
  410.1 22.2 %copy-start.21 = (f32[512,1024]{1,0:T(8,128)}, f32[512,1024]{1,0:T(8,128)S(1)}, u32[]{:S(2)}) copy-start(f32[512,1024]{1,0:T(8,128)S(1)} %get-tuple-element.109) | copy-start | bytes 6291460
  445.7 22.8 %copy-start.6 = (bf16[512,1024]{1,0:T(8,128)(2,1)}, bf16[512,1024]{1,0:T(8,128)(2,1)S(1)}, u32[]{:S(2)}) copy-start(bf16[512,1024]{1,0:T(8,128)(2,1)S(1)} %get-tuple-element.97) | copy-start | bytes 3145732
  445.7 7.1 collective-permute-start.11
  447.1 232.9 %collective-permute-start.7 = (bf16[256,1024]{1,0:T(8,128)(2,1)}, bf16[256,1024]{1,0:T(8,128)(2,1)}, u32[]{:S(2)}, u32[]{:S(2)}) collective-permute-start(bf16[256,1024]{1,0:T(8,128)(2,1)} %get-tuple-element.155), channel_id=1, source_target_pairs={{0,0},{1,1},{2,4},{3,5},{4,2},{5,3},{6,6},{7,7},{8,8},{9,9},{10,12... | collective-permute-start | bytes 1572872 | tf_op jit(solution)/shard_map/ppermute | solution.py:680
  452.5 227.6 %collective-permute-start.8 = (bf16[256,1024]{1,0:T(8,128)(2,1)}, bf16[256,1024]{1,0:T(8,128)(2,1)}, u32[]{:S(2)}, u32[]{:S(2)}) collective-permute-start(bf16[256,1024]{1,0:T(8,128)(2,1)} %get-tuple-element.156), channel_id=1, source_target_pairs={{0,1},{1,0},{2,5},{3,4},{4,3},{5,2},{6,7},{7,6},{8,9},{9,8},{10,13... | collective-permute-start | bytes 1572872 | tf_op jit(solution)/shard_map/ppermute | solution.py:680
  476.6 2.9 collective-permute-start.12
  480.6 50.9 %copy-start.32 = (bf16[2047,512]{1,0:T(8,128)(2,1)S(1)}, bf16[2047,512]{1,0:T(8,128)(2,1)}, u32[]{:S(2)}) copy-start(bf16[2047,512]{1,0:T(8,128)(2,1)} %get-tuple-element.204) | copy-start | bytes 6288388
  480.6 50.9 %copy-start.34 = (bf16[2047,512]{1,0:T(8,128)(2,1)S(1)}, bf16[2047,512]{1,0:T(8,128)(2,1)}, u32[]{:S(2)}) copy-start(bf16[2047,512]{1,0:T(8,128)(2,1)} %get-tuple-element.205) | copy-start | bytes 6288388
  541.8 12.9 %copy-start.15 = (f32[512,1024]{1,0:T(8,128)S(1)}, f32[512,1024]{1,0:T(8,128)}, u32[]{:S(2)}) copy-start(f32[512,1024]{1,0:T(8,128)} %copy-done.14) | copy-start | bytes 6291460
  541.8 196.9 %reduce-scatter.9.cloned.1.call-start = ((), (), s32[]{:S(2)}) async-start(), calls=%async_computation.6 | async-start | bytes 5242880
  542.2 12.5 %copy-start.40 = (bf16[512,1024]{1,0:T(8,128)(2,1)S(1)}, bf16[512,1024]{1,0:T(8,128)(2,1)}, u32[]{:S(2)}) copy-start(bf16[512,1024]{1,0:T(8,128)(2,1)} %copy-done.39) | copy-start | bytes 3145732
  542.2 12.5 %copy-start.49 = (bf16[512,1024]{1,0:T(8,128)(2,1)S(1)}, bf16[512,1024]{1,0:T(8,128)(2,1)}, u32[]{:S(2)}) copy-start(bf16[512,1024]{1,0:T(8,128)(2,1)} %copy-done.48) | copy-start | bytes 3145732
  563.2 109.1 %collective-permute-start.17 = (bf16[4,512,1024]{2,1,0:T(8,128)(2,1)}, bf16[4,512,1024]{2,1,0:T(8,128)(2,1)}, u32[]{:S(2)}, u32[]{:S(2)}) collective-permute-start(bf16[4,512,1024]{2,1,0:T(8,128)(2,1)} %pad_maximum_fusion.1), channel_id=1, source_target_pairs={{0,4},{1,5},{2,6},{3,7},{4,0},{5,1},{6,2},{7,3},{8,12},{9,13},{10,... | collective-permute-start | bytes 12582920 | tf_op jit(solution)/shard_map/ppermute | solution.py:671
  572.2 87.3 %copy-start.5 = (bf16[512,1024]{1,0:T(8,128)(2,1)S(1)}, bf16[512,1024]{1,0:T(8,128)(2,1)}, u32[]{:S(2)}) copy-start(bf16[512,1024]{1,0:T(8,128)(2,1)} %copy-done.4) | copy-start | bytes 3145732
  572.2 87.4 %copy-start.7 = (bf16[512,1024]{1,0:T(8,128)(2,1)S(1)}, bf16[512,1024]{1,0:T(8,128)(2,1)}, u32[]{:S(2)}) copy-start(bf16[512,1024]{1,0:T(8,128)(2,1)} %copy-done.6) | copy-start | bytes 3145732
  572.2 87.4 %copy-start.57 = (bf16[15,1024]{1,0:T(8,128)(2,1)S(1)}, bf16[15,1024]{1,0:T(8,128)(2,1)}, u32[]{:S(2)}) copy-start(bf16[15,1024]{1,0:T(8,128)(2,1)} %copy-done.56) | copy-start | bytes 92164
  672.3 11.1 %collective-permute-start.13 = (bf16[512,1024]{1,0:T(8,128)(2,1)}, bf16[512,1024]{1,0:T(8,128)(2,1)}, u32[]{:S(2)}, u32[]{:S(2)}) collective-permute-start(bf16[512,1024]{1,0:T(8,128)(2,1)} %dynamic-slice_convert_fusion), channel_id=1, source_target_pairs={{0,4},{1,5},{2,6},{3,7},{4,0},{5,1},{6,2},{7,3},{8,12},{9,13},{10,... | collective-permute-start | bytes 3145736 | tf_op jit(solution)/shard_map/ppermute | solution.py:671
  678.0 149.0 %all-reduce.10.cloned.1.call-start = ((), (), s32[]{:S(2)}) async-start(), calls=%async_computation.7 | async-start | bytes 4194304 | tf_op jit(solution)/shard_map/psum | solution.py:914
  689.4 11.1 %slice-start = ((s8[8388608]{0:T(1024)(128)(4,1)}), s8[4194304]{0:T(1024)(128)(4,1)S(1)}, s32[]{:S(2)}) async-start(s8[8388608]{0:T(1024)(128)(4,1)} %bitcast.323), calls=%async_computation.8 | async-start | bytes 8388608
  689.7 10.8 %copy-start.11 = (bf16[256,1024]{1,0:T(8,128)(2,1)S(1)}, bf16[256,1024]{1,0:T(8,128)(2,1)}, u32[]{:S(2)}) copy-start(bf16[256,1024]{1,0:T(8,128)(2,1)} %copy-done.10) | copy-start | bytes 1572868
  689.7 10.8 %copy-start.13 = (bf16[256,1024]{1,0:T(8,128)(2,1)S(1)}, bf16[256,1024]{1,0:T(8,128)(2,1)}, u32[]{:S(2)}) copy-start(bf16[256,1024]{1,0:T(8,128)(2,1)} %copy-done.12) | copy-start | bytes 1572868
  689.7 10.8 %copy-start.76 = (f32[1024]{0:T(1024)S(1)}, f32[1024]{0:T(1024)}, u32[]{:S(2)}) copy-start(f32[1024]{0:T(1024)} %copy-done.75) | copy-start | bytes 12292
  689.7 10.8 %copy-start.78 = (f32[512]{0:T(512)S(1)}, f32[512]{0:T(512)}, u32[]{:S(2)}) copy-start(f32[512]{0:T(512)} %copy-done.77) | copy-start | bytes 6148
  689.7 10.8 %slice-start.1 = ((s8[8388608]{0:T(1024)(128)(4,1)}), s8[4194304]{0:T(1024)(128)(4,1)S(1)}, s32[]{:S(2)}) async-start(s8[8388608]{0:T(1024)(128)(4,1)} %bitcast.323), calls=%async_computation.9 | async-start | bytes 8388608
  708.3 264.1 %collective-permute-start.14 = (bf16[256,1024]{1,0:T(8,128)(2,1)}, bf16[256,1024]{1,0:T(8,128)(2,1)}, u32[]{:S(2)}, u32[]{:S(2)}) collective-permute-start(bf16[256,1024]{1,0:T(8,128)(2,1)} %get-tuple-element.147), channel_id=1, source_target_pairs={{0,0},{1,1},{2,4},{3,5},{4,2},{5,3},{6,6},{7,7},{8,8},{9,9},{10,12... | collective-permute-start | bytes 1572872 | tf_op jit(solution)/shard_map/ppermute | solution.py:680
  713.7 258.7 %collective-permute-start.15 = (bf16[256,1024]{1,0:T(8,128)(2,1)}, bf16[256,1024]{1,0:T(8,128)(2,1)}, u32[]{:S(2)}, u32[]{:S(2)}) collective-permute-start(bf16[256,1024]{1,0:T(8,128)(2,1)} %get-tuple-element.148), channel_id=1, source_target_pairs={{0,1},{1,0},{2,5},{3,4},{4,3},{5,2},{6,7},{7,6},{8,9},{9,8},{10,13... | collective-permute-start | bytes 1572872 | tf_op jit(solution)/shard_map/ppermute | solution.py:680
  738.7 228.9 %all-reduce.8.cloned.1.call-start = ((), (), s32[]{:S(2)}) async-start(), calls=%async_computation.2 | async-start | bytes 327680 | tf_op jit(solution)/shard_map/psum | solution.py:932
  827.0 147.9 %collective-permute-start.18 = (bf16[512,1024]{1,0:T(8,128)(2,1)}, bf16[512,1024]{1,0:T(8,128)(2,1)S(1)}, u32[]{:S(2)}, u32[]{:S(2)}) collective-permute-start(bf16[512,1024]{1,0:T(8,128)(2,1)} %get-tuple-element.96), channel_id=1, source_target_pairs={{0,4},{1,5},{2,6},{3,7},{4,0},{5,1},{6,2},{7,3},{8,12},{9,13},{10,... | collective-permute-start | bytes 3145736 | tf_op jit(solution)/shard_map/ppermute | solution.py:671
  836.1 136.2 %copy-start.38 = (bf16[512,1024]{1,0:T(8,128)(2,1)S(1)}, bf16[512,1024]{1,0:T(8,128)(2,1)}, u32[]{:S(2)}) copy-start(bf16[512,1024]{1,0:T(8,128)(2,1)} %get-tuple-element.95) | copy-start | bytes 3145732
  972.3 2.8 collective-permute-start.16
  (87 other events, 367.0 us)
Sparse Core Ops, SparseCore 0:
  10.8 87.2 all-gather.6
  99.9 75.9 all-gather.4
  541.9 62.5 reduce-scatter.6
  678.1 60.5 reduce-scatter.8
  740.9 85.9 all-reduce.9
  833.9 133.7 all-reduce.7

commit v3 on v2

--- a/solution.py
+++ b/solution.py
@@ -284,7 +284,7 @@
         name="attend_fwd",
     )(length_arr, q, k, v, place, cb, pb)
 
-def attend_bwd_kernel(q_ref, k_ref, v_ref, place_ref, cb_ref, pb_ref, prob_ref, g_ref, gq_ref, gk_ref, gv_ref, gp_ref, gb_ref, gk_s, gv_s, gp_s, *, scale, trans):
+def attend_bwd_kernel(q_ref, k_ref, v_ref, place_ref, cb_ref, pb_ref, prob_ref, g_ref, gq_ref, gk_ref, gv_ref, gp_ref, gb_ref, gk_s, gv_s, gp_s, *, scale):
     rows = q_ref.shape[0]
     length = k_ref.shape[0]
     span = rows + length
@@ -305,8 +305,7 @@
         gp_s[...] = jnp.zeros_like(gp_s)
         gb_ref[...] = jnp.zeros_like(gb_ref)
 
-    if trans:
-        grad_t, with_u_t, with_v_t = grad.T, with_u.T, with_v.T
+    grad_t, with_u_t, with_v_t = grad.T, with_u.T, with_v.T
     gu = []
     gw = []
     for head in range(2):
@@ -322,15 +321,10 @@
         turned = pltpu.roll(turned, 0, 1, stride=1, stride_axis=0)
         gu.append(mult_plain(grad_score, k_ref[...]))
         gw.append(mult_plain(turned, window))
-        if trans:
-            band = slice(head * HEAD_DIM, (head + 1) * HEAD_DIM)
-            gv_s[band, :] += mult_plain(grad_t[band, :], prob)
-            gk_s[band, :] += mult_plain(with_u_t[band, :], grad_score)
-            gp_s[band, pl.ds(first, span)] += mult_plain(with_v_t[band, :], turned)
-        else:
-            gv_s[...] += mult_rows(prob, grad_h)
-            gk_s[...] += mult_rows(grad_score, jnp.where(mine, with_u, zero))
-            gp_s[pl.ds(first, span), :] += mult_rows(turned, jnp.where(mine, with_v, zero))
+        band = slice(head * HEAD_DIM, (head + 1) * HEAD_DIM)
+        gv_s[band, :] += mult_plain(grad_t[band, :], prob)
+        gk_s[band, :] += mult_plain(with_u_t[band, :], grad_score)
+        gp_s[band, pl.ds(first, span)] += mult_plain(with_v_t[band, :], turned)
     grad_u = jnp.where(lanes < HEAD_DIM, gu[0], gu[1]) * scale
     grad_w = jnp.where(lanes < HEAD_DIM, gw[0], gw[1]) * scale
     gb_ref[0:1, :] += jnp.sum(grad_u, axis=0, keepdims=True)
@@ -341,44 +335,89 @@
 
     @pl.when(step == pl.num_programs(1) - 1)
     def _():
-        if trans:
-            gk_ref[...] = gk_s[...].T.astype(jnp.bfloat16)
-            gv_ref[...] = gv_s[...].T.astype(jnp.bfloat16)
-            gp_ref[...] = gp_s[...].T.astype(jnp.bfloat16)
-        else:
-            gk_ref[...] = gk_s[...].astype(jnp.bfloat16)
-            gv_ref[...] = gv_s[...].astype(jnp.bfloat16)
-            gp_ref[...] = gp_s[...].astype(jnp.bfloat16)
-
-def attend_bwd(q, k, v, place, cb, pb, prob, grad, rows, trans=True):
+        gk_ref[...] = gk_s[...].T.astype(jnp.bfloat16)
+        gv_ref[...] = gv_s[...].T.astype(jnp.bfloat16)
+        gp_ref[...] = gp_s[...].T.astype(jnp.bfloat16)
+
+
+def attend_bwd_sum_kernel(layers, shared, count, *refs, scale):
+    ins, parts = refs[:8], refs[8 : 8 + count]
+    refs = refs[8 + count :]
+    outs, sums, scratch, own = refs[:5], refs[5 : 5 + count], refs[5 + count : 8 + count], refs[8 + count :]
+    at = pl.program_id(0) * pl.num_programs(1) + pl.program_id(1)
+    enter, step, turns, leave = reduce_plan(layers, shared, parts, sums, None, own)
+    blocks = pl.num_programs(0) * pl.num_programs(1)
+    pl.when(at == 0)(enter)
+    for turn_at in range(min(turns, blocks)):
+        pl.when(at == turn_at)(partial(step, turn_at))
+    attend_bwd_kernel(*ins, *outs, *scratch, scale=scale)
+
+    @pl.when(at == blocks - 1)
+    def _():
+        for turn_at in range(blocks, turns):
+            step(turn_at)
+        leave()
+
+
+def attend_bwd(q, k, v, place, cb, pb, prob, grad, rows, layers, shared, parts, collective_id):
     length, width = q.shape
     pairs = width // PAIR
+    count = len(parts)
+    blocks, shapes = reduce_shapes(layers, shared, parts)
+    shard, channels = shapes[shared].shape[2:]
+    still = lambda shape: pl.BlockSpec(shape, lambda p, i: (0,) * len(shape))
     full = pl.BlockSpec((length, PAIR), lambda p, i: (0, p))
     part = pl.BlockSpec((rows, PAIR), lambda p, i: (i, p))
     vec = pl.BlockSpec((1, PAIR), lambda p, i: (0, p))
     tall = pl.BlockSpec((2 * length, PAIR), lambda p, i: (0, p))
-    shape = (lambda n: (PAIR, n)) if trans else (lambda n: (n, PAIR))
     return pl.pallas_call(
-        partial(attend_bwd_kernel, scale=1.0 / math.sqrt(HEAD_DIM), trans=trans),
+        partial(attend_bwd_sum_kernel, layers, shared, count, scale=1.0 / math.sqrt(HEAD_DIM)),
         grid=(pairs, length // rows),
-        in_specs=[part, full, full, tall, vec, vec, pl.BlockSpec((2, rows, length), lambda p, i: (p, i, 0)), part],
-        out_specs=[part, full, full, tall, pl.BlockSpec((8, PAIR), lambda p, i: (0, p))],
+        in_specs=[
+            part,
+            full,
+            full,
+            tall,
+            vec,
+            vec,
+            pl.BlockSpec((2, rows, length), lambda p, i: (p, i, 0)),
+            part,
+        ]
+        + [pl.BlockSpec(memory_space=pl.ANY)] * count,
+        out_specs=[part, full, full, tall, pl.BlockSpec((8, PAIR), lambda p, i: (0, p))]
+        + [still(shape.shape) for shape in shapes],
         out_shape=[
             jax.ShapeDtypeStruct((length, width), jnp.bfloat16),
             jax.ShapeDtypeStruct((length, width), jnp.bfloat16),
             jax.ShapeDtypeStruct((length, width), jnp.bfloat16),
             jax.ShapeDtypeStruct((2 * length, width), jnp.bfloat16),
             jax.ShapeDtypeStruct((8, width), jnp.float32),
-        ],
+        ]
+        + shapes,
         scratch_shapes=[
-            pltpu.VMEM(shape(length), jnp.float32),
-            pltpu.VMEM(shape(length), jnp.float32),
-            pltpu.VMEM(shape(2 * length), jnp.float32),
-        ],
-        compiler_params=pltpu.CompilerParams(vmem_limit_bytes=VMEM),
-        cost_estimate=pl.CostEstimate(flops=80 * 10**9, bytes_accessed=20 * 2**20, transcendentals=0),
+            pltpu.VMEM((PAIR, length), jnp.float32),
+            pltpu.VMEM((PAIR, length), jnp.float32),
+            pltpu.VMEM((PAIR, 2 * length), jnp.float32),
+        ]
+        + reduce_scratch(count, layers, shard, channels),
+        compiler_params=pltpu.CompilerParams(
+            vmem_limit_bytes=VMEM, collective_id=collective_id, has_side_effects=True
+        ),
+        cost_estimate=pl.CostEstimate(
+            flops=100 * 10**9, bytes_accessed=40 * 2**20, transcendentals=0
+        ),
         name="attend_bwd",
-    )(q, k, v, place, cb, pb, prob, grad)
+    )(
+        q,
+        k,
+        v,
+        place,
+        cb,
+        pb,
+        prob,
+        grad,
+        *blocks,
+    )
 
 
 MESH = pl.DeviceIdType.MESH
@@ -395,7 +434,10 @@
             lax.rem(x + dx, 2),
         )
 
-    return at
+    def spot(dz=0, dc=0, dy=0, dx=0):
+        return at(layers - dz, dc, dy, dx)
+
+    return at, spot
 
 
 def greet(at, layers):
@@ -422,27 +464,29 @@
 
 
 def gather_plan(layers, shards, fulls, z_sem, p_sem, d_sem, c_sem, own_sem):
-    at = chip_place(layers)
+    at, spot = chip_place(layers)
     arrays = range(len(shards))
     half = shards[0].shape[0] // 2
     items = [(dz, a) for dz in reversed(far_first(layers)) for a in arrays]
-    own = [pltpu.make_async_copy(shards[a], fulls[a].at[0, 0, 0, 0], own_sem.at[a]) for a in arrays]
+    own = [pltpu.make_async_copy(shards[a], fulls[a].at[spot()], own_sem.at[a]) for a in arrays]
     along, flat, cross, core = {}, {}, {}, {}
     for dz, a in items:
-        full = fulls[a].at[0, dz]
-        source = full.at[0, 0] if dz else shards[a]
+        full = fulls[a]
+        source = full.at[spot(dz)] if dz else shards[a]
         if dz:
-            along[dz, a] = remote(shards[a], full.at[0, 0], z_sem, (a, dz), at(dz=dz))
+            along[dz, a] = remote(shards[a], full.at[spot()], z_sem, (a, dz), at(dz=dz))
         flat[dz, a] = (
-            remote(source, full.at[0, 1], p_sem, (a, dz, 0), at(dx=1)),
-            remote(source, full.at[1, 0], p_sem, (a, dz, 1), at(dy=1)),
-        )
-        first, second = pl.ds(0, half), pl.ds(half, half)
+            remote(source, full.at[spot(dz)], p_sem, (a, dz, 0), at(dx=1)),
+            remote(source, full.at[spot(dz)], p_sem, (a, dz, 1), at(dy=1)),
+        )
+        from_x = full.at[(*spot(dz, dx=1), pl.ds(half, half))]
+        from_y = full.at[(*spot(dz, dy=1), pl.ds(0, half))]
         cross[dz, a] = (
-            remote(full.at[0, 1, second], full.at[1, 1, second], d_sem, (a, dz, 0), at(dy=1)),
-            remote(full.at[1, 0, first], full.at[1, 1, first], d_sem, (a, dz, 1), at(dx=1)),
-        )
-        core[dz, a] = remote(full, fulls[a].at[1, dz], c_sem, (a, dz), at(dc=1))
+            remote(from_x, from_x, d_sem, (a, dz, 0), at(dy=1)),
+            remote(from_y, from_y, d_sem, (a, dz, 1), at(dx=1)),
+        )
+        plane = full.at[spot(dz)[:2]]
+        core[dz, a] = remote(plane, plane, c_sem, (a, dz), at(dc=1))
 
     def enter():
         greet(at, layers)
@@ -514,7 +558,7 @@
         partial(gather_kernel, layers, count),
         in_specs=[pl.BlockSpec(memory_space=pl.ANY)] * count,
         out_specs=[pl.BlockSpec(memory_space=pl.ANY)] * count,
-        out_shape=[jax.ShapeDtypeStruct((2, layers, 2, 2, rows, width), jnp.bfloat16)] * count,
+        out_shape=[jax.ShapeDtypeStruct((layers, 2, 2, 2, rows, width), jnp.bfloat16)] * count,
         scratch_shapes=gather_sems(count, layers),
         compiler_params=pltpu.CompilerParams(collective_id=collective_id, has_side_effects=True),
         cost_estimate=pl.CostEstimate(flops=0, bytes_accessed=200 * 2**20, transcendentals=0),
@@ -527,50 +571,80 @@
     target[...] = (one[...].astype(jnp.float32) + two[...].astype(jnp.float32)).astype(target.dtype)
 
 
-def reduce_plan(layers, parts, outs, sums, got_c, got_d, got_p, got_z, load_sem, c_sem, d_sem, p_sem, z_sem):
-    at = chip_place(layers)
+def reduce_plan(layers, shared, parts, outs, small, scratch):
+    at, spot = chip_place(layers)
+    sums, got_c, got_d, got_p, got_z, got_s, load_sem, c_sem, d_sem, p_sem, z_sem, s_sem, *tiny = scratch
     arrays = range(len(parts))
-    half = parts[0].shape[4] // 2
-    items = [(dz, a) for dz in far_first(layers) for a in arrays]
+    rows = sums.shape[4]
+    half = rows // 2
+    order = far_first(layers)
+    items = [(dz, shared) for dz in order]
+    items += [(dz, a) for dz in order for a in arrays if a != shared]
     first, second = pl.ds(0, half), pl.ds(half, half)
+    here, by_y, by_x, far = (spot(0, 0, dy, dx)[2:] for dy, dx in ((0, 0), (1, 0), (0, 1), (1, 1)))
+    whole = [len(part.shape) == 6 for part in parts]
+    core_at = spot()[1]
     load, core, cross, flat, along = {}, {}, {}, {}, {}
     for dz, a in items:
         total = sums.at[a, dz]
-        load[dz, a] = pltpu.make_async_copy(parts[a].at[0, dz], total, load_sem.at[a, dz])
-        core[dz, a] = remote(parts[a].at[1, dz], got_c.at[a, dz], c_sem, (a, dz), at(dc=1))
+        source = parts[a].at[spot(dz)[:2]] if whole[a] else parts[a].at[spot(dz)[0]]
+        load[dz, a] = pltpu.make_async_copy(source, total, load_sem.at[a, dz])
+        if whole[a]:
+            core[dz, a] = remote(
+                parts[a].at[spot(dz, dc=1)[:2]], got_c.at[a, dz], c_sem, (a, dz), at(dc=1)
+            )
         cross[dz, a] = (
-            remote(total.at[1, 1, first], got_d.at[a, dz, 0], d_sem, (a, dz, 0), at(dx=1)),
-            remote(total.at[1, 1, second], got_d.at[a, dz, 1], d_sem, (a, dz, 1), at(dy=1)),
+            remote(total.at[(*far, first)], got_d.at[a, dz, 0], d_sem, (a, dz, 0), at(dx=1)),
+            remote(total.at[(*far, second)], got_d.at[a, dz, 1], d_sem, (a, dz, 1), at(dy=1)),
         )
         flat[dz, a] = (
-            remote(total.at[1, 0], got_p.at[a, dz, 0], p_sem, (a, dz, 0), at(dy=1)),
-            remote(total.at[0, 1], got_p.at[a, dz, 1], p_sem, (a, dz, 1), at(dx=1)),
+            remote(total.at[by_y], got_p.at[a, dz, 0], p_sem, (a, dz, 0), at(dy=1)),
+            remote(total.at[by_x], got_p.at[a, dz, 1], p_sem, (a, dz, 1), at(dx=1)),
         )
         if dz:
             along[dz, a] = remote(
-                total.at[0, 0], got_z.at[a, dz], z_sem, (a, dz), at(dz=layers - dz)
+                total.at[here], got_z.at[a, dz], z_sem, (a, dz), at(dz=layers - dz)
             )
+    own = got_s.at[(core_at, spot()[0])]
+    handed = {k: remote(own, own, s_sem, (k,), at(dz=k)) for k in range(1, layers)}
+    swapped = remote(got_s.at[core_at], got_s.at[core_at], s_sem, (0,), at(dc=1))
+    hops = []
+    if small:
+        level, got_t, t_sem = tiny
+        hops = [
+            remote(level.at[i], got_t.at[i], t_sem, (i,), device)
+            for i, device in enumerate((at(dc=1), at(dx=1), at(dy=1)))
+        ]
+        hops += [
+            remote(level.at[3], got_t.at[2 + k], t_sem, (2 + k,), at(dz=k)) for k in range(1, layers)
+        ]
 
     def enter():
         greet(at, layers)
+        if small:
+            level[0] = small[0][...]
+            hops[0].start()
         for item in items:
-            core[item].start()
+            if item in core:
+                core[item].start()
             load[item].start()
 
     def join_core(item):
         dz, a = item
         load[item].wait()
-        core[item].wait_recv()
-        for dy, dx in ((1, 1), (1, 0), (0, 1), (0, 0)):
-            here = sums.at[a, dz, dy, dx]
-            add_rows(here, here, got_c.at[a, dz, dy, dx])
-            if dy and dx:
+        if whole[a]:
+            core[item].wait_recv()
+        for place in (far, by_y, by_x, here):
+            target = sums.at[(a, dz, *place)]
+            if whole[a]:
+                add_rows(target, target, got_c.at[(a, dz, *place)])
+            if place is far:
                 for copy in cross[item]:
                     copy.start()
 
     def join_cross(item):
         dz, a = item
-        one, two = sums.at[a, dz, 1, 0, first], sums.at[a, dz, 0, 1, second]
+        one, two = sums.at[(a, dz, *by_y, first)], sums.at[(a, dz, *by_x, second)]
         cross[item][0].wait_recv()
         add_rows(one, one, got_d.at[a, dz, 0])
         flat[item][0].start()
@@ -580,81 +654,147 @@
 
     def join_flat(item):
         dz, a = item
-        here = sums.at[a, dz, 0, 0]
+        target = sums.at[(a, dz, *here)]
         for copy in flat[item]:
             copy.wait_recv()
-        here[...] = (
-            here[...].astype(jnp.float32)
+        target[...] = (
+            target[...].astype(jnp.float32)
             + got_p[a, dz, 0].astype(jnp.float32)
             + got_p[a, dz, 1].astype(jnp.float32)
         ).astype(jnp.bfloat16)
         if dz:
             along[item].start()
 
-    steps = []
-    lags = ((join_core, 0), (join_cross, 3), (join_flat, 5))
-    for turn_at in range(len(items) + 5):
-        for action, lag in lags:
+    def total_of(a):
+        total = sums[(a, 0, *here)].astype(jnp.float32)
+        for dz in range(1, layers):
+            along[dz, a].wait_recv()
+            total = total + got_z[a, dz].astype(jnp.float32)
+        return total
+
+    def join_small(turn_at):
+        if turn_at < 3:
+            hops[turn_at].wait_recv()
+            level[turn_at + 1] = level[turn_at] + got_t[turn_at]
+            for hop in hops[turn_at + 1 : turn_at + 2] if turn_at < 2 else hops[3:]:
+                hop.start()
+        else:
+            total = level[3]
+            for k in range(1, layers):
+                hops[2 + k].wait_recv()
+                total = total + got_t[2 + k]
+            small[1][...] = total
+
+    def hand_on():
+        own[...] = total_of(shared).astype(jnp.bfloat16)
+        for copy in handed.values():
+            copy.start()
+
+    def swap():
+        for copy in handed.values():
+            copy.wait_recv()
+        swapped.start()
+
+    handed_at = layers - 1 + 5 + 2
+    turns = max(len(items) + 5, handed_at + 4)
+
+    def step(turn_at):
+        for action, lag in ((join_core, 0), (join_cross, 3), (join_flat, 5)):
             if 0 <= turn_at - lag < len(items):
-                steps.append(partial(action, items[turn_at - lag]))
+                action(items[turn_at - lag])
+        if small and 1 <= turn_at <= 4:
+            join_small(turn_at - 1)
+        if turn_at == handed_at:
+            hand_on()
+        if turn_at == handed_at + 3:
+            swap()
 
     def leave():
         for a in arrays:
-            total = sums[a, 0, 0, 0].astype(jnp.float32)
-            for dz in range(1, layers):
-                along[dz, a].wait_recv()
-                total = total + got_z[a, dz].astype(jnp.float32)
-            outs[a][...] = total
+            if a != shared:
+                outs[a][...] = total_of(a)
+        swapped.wait_recv()
+        outs[shared][...] = got_s[...]
         for item in items:
             if item[0]:
                 along[item].wait_send()
-            for copy in (core[item], *cross[item], *flat[item]):
+            for copy in (*cross[item], *flat[item]):
                 copy.wait_send()
-
-    return enter, steps, leave
-
-
-def reduce_scratch(count, layers, rows, width):
+            if item in core:
+                core[item].wait_send()
+        for copy in (*handed.values(), swapped, *hops):
+            copy.wait_send()
+
+    return enter, step, turns, leave
+
+
+def reduce_scratch(count, layers, rows, width, small=None):
     dma = pltpu.SemaphoreType.DMA
     low = lambda *shape: pltpu.VMEM((count, layers, *shape, width), jnp.bfloat16)
-    return [
+    scratch = [
         low(2, 2, rows),
         low(2, 2, rows),
         low(2, rows // 2),
         low(2, rows),
         low(rows),
+        pltpu.VMEM((2, layers, rows, width), jnp.bfloat16),
         dma((count, layers)),
         dma((2, count, layers)),
         dma((2, count, layers, 2)),
         dma((2, count, layers, 2)),
         dma((2, count, layers)),
+        dma((2, layers)),
     ]
-
-
-def reduce_kernel(layers, count, *refs):
-    enter, steps, leave = reduce_plan(layers, refs[:count], refs[count : 2 * count], *refs[2 * count :])
+    if small is not None:
+        scratch += [
+            pltpu.VMEM((4, *small.shape), jnp.float32),
+            pltpu.VMEM((2 + layers, *small.shape), jnp.float32),
+            dma((2, 2 + layers)),
+        ]
+    return scratch
+
+
+def reduce_shapes(layers, shared, parts):
+    blocks, shapes = [], []
+    for a, (part, count) in enumerate(parts):
+        width = part.shape[-1]
+        rows = part.size // width // (4 * count * layers)
+        blocks.append(part.reshape(layers, *((2,) if count == 2 else ()), 2, 2, rows, width))
+        if a == shared:
+            shapes.append(jax.ShapeDtypeStruct((2, layers, rows, width), jnp.bfloat16))
+        else:
+            shapes.append(jax.ShapeDtypeStruct((rows, width), jnp.float32))
+    return blocks, shapes
+
+
+def reduce_kernel(layers, shared, count, *refs):
+    parts, small, outs, total = refs[:count], refs[count], refs[count + 1 : 2 * count + 1], refs[2 * count + 1]
+    enter, step, turns, leave = reduce_plan(
+        layers, shared, parts, outs, (small, total), refs[2 * count + 2 :]
+    )
     enter()
-    for step in steps:
-        step()
+    for turn_at in range(turns):
+        step(turn_at)
     leave()
 
 
-def reduce_all(layers, parts, collective_id):
+def reduce_all(layers, shared, parts, small, collective_id):
     count = len(parts)
-    total, width = parts[0].shape
-    rows = total // (8 * layers)
+    blocks, shapes = reduce_shapes(layers, shared, parts)
+    rows, width = shapes[shared].shape[2:]
+    near = pl.BlockSpec(memory_space=pltpu.VMEM)
     return pl.pallas_call(
-        partial(reduce_kernel, layers, count),
-        in_specs=[pl.BlockSpec(memory_space=pl.ANY)] * count,
-        out_specs=[pl.BlockSpec(memory_space=pltpu.VMEM)] * count,
-        out_shape=[jax.ShapeDtypeStruct((rows, width), jnp.float32)] * count,
-        scratch_shapes=reduce_scratch(count, layers, rows, width),
+        partial(reduce_kernel, layers, shared, count),
+        in_specs=[pl.BlockSpec(memory_space=pl.ANY)] * count + [near],
+        out_specs=[near] * (count + 1),
+        out_shape=shapes + [jax.ShapeDtypeStruct(small.shape, jnp.float32)],
+        scratch_shapes=reduce_scratch(count, layers, rows, width, small),
         compiler_params=pltpu.CompilerParams(
             collective_id=collective_id, has_side_effects=True, vmem_limit_bytes=VMEM
         ),
-        cost_estimate=pl.CostEstimate(flops=0, bytes_accessed=200 * 2**20, transcendentals=0),
+        cost_estimate=pl.CostEstimate(flops=0, bytes_accessed=300 * 2**20, transcendentals=0),
         name="reduce_all",
-    )(*(part.reshape(2, layers, 2, 2, rows, width) for part in parts))
+    )(*blocks, small)
 
 
 class Hops:
@@ -678,6 +818,20 @@
                     to = (z * 2 + w // 2) * 4 + 2 * c + ((w % 2) ^ step)
                     pairs.append(((z * 2 + c) * 4 + w, to))
         return lax.ppermute(block, ("z", "core", "y", "x"), pairs)
+
+
+def relative_waves(length, channels):
+    step = 32
+    rates = jnp.exp(
+        jnp.arange(channels // 2).astype(jnp.float32) * (-2.0 * math.log(10000.0) / channels)
+    )
+    coarse = (length - 1 - step * jnp.arange(2 * length // step)).astype(jnp.float32)
+    fine = jnp.arange(step).astype(jnp.float32)
+    coarse, fine = coarse[:, None, None] * rates, fine[None, :, None] * rates
+    sin_c, cos_c, sin_f, cos_f = jnp.sin(coarse), jnp.cos(coarse), jnp.sin(fine), jnp.cos(fine)
+    return jnp.concatenate(
+        [sin_c * cos_f - cos_c * sin_f, cos_c * cos_f + sin_c * sin_f], axis=2
+    ).reshape(2 * length, channels)
 
 
 def taps_forward(padded, kernel_f, count):
@@ -773,6 +927,10 @@
     conv_chunk = jnp.concatenate([own_half(out_weight), own_half(point_weight), own_half(glu_weight)])
     attn_all = lax.all_gather(attn_chunk, ("y", "x"), axis=0)
     conv_all = lax.all_gather(conv_chunk, ("y", "x"), axis=0)
+    up_second, down_second = (
+        lax.all_gather(shard, ("z", "core", "y", "x"), axis=0, tiled=True)
+        for shard in (second_up, second_down)
+    )
 
     def heads_of(at):
         return attn_all[:, at * band : (at + 1) * band].reshape(4 * band, channels)
@@ -781,7 +939,7 @@
     own_biases = attn_all[:, 4 * band : 4 * band + 2, :band].transpose(1, 0, 2).reshape(2, 4 * band)
     conv_other = hops.send(conv_all, dc=1)
     conv_both = jnp.stack(pick(core == 0, conv_all, conv_other), axis=1)
-    full_out = jnp.concatenate([conv_all[:, :band], conv_other[:, :band]]).reshape(8 * band, channels)
+    full_out = conv_both[:, :, :band].reshape(8 * band, channels)
     full_point = conv_both[:, :, band : 2 * band].reshape(8 * band, channels)
     full_glu = conv_both[:, :, 2 * band :].reshape(16 * band, channels)
 
@@ -791,8 +949,7 @@
     attn_half = low(normed_attn)
     attn_other = hops.send(attn_half, dc=1)
     attn_low = jnp.concatenate(pick(core == 0, attn_half, attn_other))
-    rel_table = low(relative_table(length, channels))
-    rel_table = jnp.concatenate([rel_table, jnp.zeros((1, channels), jnp.bfloat16)])
+    rel_table = low(relative_waves(length, channels))
     query = low(mult_trans(attn_low, query_own))
     key = low(mult_trans(attn_low, key_own))
     value = low(mult_trans(attn_low, value_own))
@@ -807,7 +964,9 @@
         return own, other
 
     att_own, att_other = halves(attended)
-    framed = jnp.concatenate([att_own, hops.send(att_other, dc=1)], axis=1)
+    att_parts = pick(core == 0, att_own, hops.send(att_other, dc=1))
+    framed = jnp.stack([part.reshape(rows, 4, band) for part in att_parts], axis=2)
+    framed = framed.reshape(rows, 8 * band)
     stream2 = stream1 + mult_plain(framed, full_out)
     normed_conv, conv_pull = jax.vjp(norm_rows, stream2, f32(conv_gain))
     conv_low = low(normed_conv)
@@ -821,7 +980,6 @@
     middle, middle_pull = jax.vjp(norm_rows, conv_out, f32(middle_gain))
     swished = low(jax.nn.silu(middle))
     stream3 = stream2 + mult_trans(swished, full_point)
-    up_second, down_second = gather_all(layers, [second_up, second_down], 1)
     stream4, saved_second = ffn_forward(stream3, f32(second_gain), up_second, down_second)
     final_rows, final_pull = jax.vjp(norm_rows, stream4, f32(final_gain))
     output = turn_out(low(final_rows))
@@ -836,10 +994,9 @@
         grad_before = low(mult_trans(grad_out, down_full) * silu_slope(before))
         grad_up = low(mult_rows(grad_before, normed_low))
         grad_input, grad_gain = norm_pull(mult_plain(grad_before, up_full))
-        sum_up, sum_down = reduce_all(layers, [grad_up, grad_down], 2)
-        return grad_stream + grad_input, grad_gain, sum_up, sum_down
-
-    grad3, grad_second_gain, sum_up_second, sum_down_second = ffn_back(
+        return grad_stream + grad_input, grad_gain, grad_up, grad_down
+
+    grad3, grad_second_gain, grad_up_second, grad_down_second = ffn_back(
         grad4, saved_second, up_second, down_second
     )
     grad_branch = low(grad3)
@@ -867,13 +1024,34 @@
     grad_attn = low(grad2)
     grad_out = mult_rows(framed, grad_attn)
     grad_framed = low(mult_trans(grad_attn, full_out))
-    side = channels // 2
-    grad_heads = jnp.concatenate(
-        pick(core == 0, grad_framed[:, :side], hops.send(grad_framed[:, side:], dc=1))
-    )
-    grad_query, grad_key, grad_value, grad_place, grad_biases = attend_bwd(
-        query, key, value, place, own_biases[:1], own_biases[1:], prob, grad_heads, ROWS_BWD
-    )
+    grad_parts = grad_framed.reshape(rows, 4, 2, band)
+    grad_parts = [grad_parts[:, :, at].reshape(rows, 4 * band) for at in range(2)]
+    grad_kept, grad_sent = pick(core == 0, *grad_parts)
+    grad_heads = jnp.concatenate(pick(core == 0, grad_kept, hops.send(grad_sent, dc=1)))
+
+    def by_place(matrix, cores):
+        blocks = low(matrix).reshape(4, cores, layers, -1, channels)
+        return blocks.transpose(2, 1, 0, 3, 4)
+
+    conv_part = jnp.concatenate(
+        [by_place(part, 2) for part in (grad_out, grad_point, grad_glu)], axis=3
+    )
+    *attn_grads, sum_up_second, sum_down_second, conv_sums = attend_bwd(
+        query,
+        key,
+        value,
+        place,
+        own_biases[:1],
+        own_biases[1:],
+        prob,
+        grad_heads,
+        ROWS_BWD,
+        layers,
+        2,
+        [(grad_up_second, 2), (grad_down_second, 2), (conv_part, 2)],
+        3,
+    )
+    grad_query, grad_key, grad_value, grad_place, grad_biases = attn_grads
     grad_query_w = mult_rows(grad_query, attn_low)
     grad_key_w = mult_rows(grad_key, attn_low)
     grad_value_w = mult_rows(grad_value, attn_low)
@@ -886,72 +1064,50 @@
     normed_own, normed_other = halves(grad_normed)
     grad_attn_in, grad_attn_gain = attn_pull(normed_own + f32(hops.send(low(normed_other), dc=1)))
     grad1 = grad2 + grad_attn_in
-    grad0, grad_first_gain, sum_up_first, sum_down_first = ffn_back(
+    grad0, grad_first_gain, grad_up_first, grad_down_first = ffn_back(
         grad1, saved_first, up_first, down_first
     )
     grad_input = turn_out(low(grad0))
 
-    def by_wide(matrix):
-        return low(matrix).reshape(4, -1, channels)
-
-    def by_core(matrix):
-        parts = low(matrix).reshape(4, 2, -1, channels)
-        own = lax.dynamic_index_in_dim(parts, core, 1, keepdims=False)
-        return own, lax.dynamic_index_in_dim(parts, 1 - core, 1, keepdims=False)
-
-    out_parts = (by_wide(grad_out[: 4 * band]), by_wide(grad_out[4 * band :]))
-    kept, sent = (
-        jnp.concatenate(parts, axis=1)
-        for parts in zip(out_parts, by_core(grad_point), by_core(grad_glu))
-    )
-    conv_part = low(f32(kept) + f32(hops.send(sent, dc=1)))
     attn_part = jnp.concatenate(
-        [by_wide(part) for part in (grad_query_w, grad_key_w, grad_value_w, grad_place_w)], axis=1
-    )
-
-    def totals_of(part):
-        mine = lax.psum_scatter(part, ("y", "x"), scatter_dimension=0, tiled=False)
-        mine = lax.psum(mine, "z")
-        return pick(core == 0, mine, hops.send(mine, dc=1))
-
-    conv_totals, attn_totals = totals_of(conv_part), totals_of(attn_part)
-
-    def owned(totals, start, count):
-        return f32(jnp.concatenate([part[start : start + count] for part in totals]))
-
-    total_out, total_point = owned(conv_totals, 0, band), owned(conv_totals, band, band)
-    total_glu = owned(conv_totals, 2 * band, 2 * band)
-    total_query, total_key, total_value, total_place = (
-        owned(attn_totals, at * band, band) for at in range(4)
-    )
-
+        [by_place(part, 1) for part in (grad_query_w, grad_key_w, grad_value_w, grad_place_w)],
+        axis=3,
+    )
     spread = jnp.zeros((2, 4, 2, band), jnp.float32)
     spread = lax.dynamic_update_slice(
         spread, grad_biases[:2].reshape(2, 4, 1, band), (0, 0, core, 0)
     ).reshape(2, channels)
-    small = lax.psum(
-        jnp.concatenate(
-            [
-                grad_first_gain[None],
-                grad_attn_gain[None],
-                grad_conv_gain[None],
-                grad_middle_gain[None],
-                grad_second_gain[None],
-                grad_final_gain[None],
-                spread,
-                grad_kernel,
-            ]
-        ),
-        ("z", "core", "y", "x"),
+    gains = (
+        grad_conv_gain,
+        grad_middle_gain,
+        grad_second_gain,
+        grad_final_gain,
+        grad_first_gain,
+        grad_attn_gain,
+    )
+    small = jnp.concatenate([jnp.stack(gains), spread, grad_kernel])
+    small = jnp.pad(small, ((0, -small.shape[0] % 8), (0, 0)))
+    sum_up_first, sum_down_first, attn_sums, small = reduce_all(
+        layers, 2, [(grad_up_first, 2), (grad_down_first, 2), (attn_part, 1)], small, 2
+    )
+
+    def owned(sums, start, count):
+        return f32(sums[:, :, start : start + count]).reshape(-1, channels)
+
+    step = band // layers
+    total_out, total_point = owned(conv_sums, 0, step), owned(conv_sums, step, step)
+    total_glu = owned(conv_sums, 2 * step, 2 * step)
+    total_query, total_key, total_value, total_place = (
+        owned(attn_sums, at * step, step) for at in range(4)
     )
     own_bias_grad = lax.dynamic_slice_in_dim(small[6:8], wide_at * 2 * band, 2 * band, 1)
     return (
         output,
         grad_input,
-        small[0],
+        small[4],
         sum_up_first,
         sum_down_first,
-        small[1],
+        small[5],
         total_query,
         total_key,
         total_value,
@@ -959,15 +1115,15 @@
         total_place,
         own_bias_grad[0],
         own_bias_grad[1],
+        small[0],
+        total_glu,
+        small[8 : 8 + KERNEL],
+        small[1],
+        total_point,
         small[2],
-        total_glu,
-        small[8:],
-        small[3],
-        total_point,
-        small[4],
         sum_up_second,
         sum_down_second,
-        small[5],
+        small[3],
     )
 
 

time: 1000 us -> 862 us (0.86)
  waiting for transfers between devices: 151 us -> 49.2 us
  Pallas kernels: 491 us -> 442 us
  local copies, waits for them, and re-layouts: 37.7 us -> 60.4 us
  other arithmetic: 114 us -> 101 us
    psum x2 -> x0, waiting for transfers between devices: 130 us -> none  [the longest x1 76.8 us: totals_of(): mine = lax.psum(mine, 'z')]
    pallas_call x2 -> x1, Pallas kernels: 240 us -> 140 us  [gather_all(): pl.pallas_call(partial(gather_kernel, layers, count), in_specs=[pl.BlockS...]
    pallas_call x3 -> x2, Pallas kernels: 216 us -> 267 us  [the longest x1 134 us: reduce_all(): pl.pallas_call(partial(reduce_kernel, layers, shared, count), in_specs=[p...]
    all_gather x0 -> x2, waiting for transfers between devices: none -> 40 us  [per_chip(): lax.all_gather(shard, ('z', 'core', 'y', 'x'), axis=0, tiled=True)]
    unnamed x8 -> x4, waiting for transfers between devices: 20 us -> 0.73 us
    another operation x3, other arithmetic: 33.9 us -> 20.3 us
    unnamed x262 -> x284, local copies, waits for them, and re-layouts: 14.7 us -> 28.1 us
  transfers between devices with their start and end apart: 25 -> 20, of which waited for: 4 -> 3; matrix products, arithmetic and copies ran while one was open for 21% -> 19% of each run, Pallas kernels for 49% -> 21%
where the time goes in v3:
time: 862 us; the launch traced here: 853 us
  Pallas kernels  442 us (51%)
  matrix products  163 us (19%)
  other arithmetic  101 us (12%)
  local copies, waits for them, and re-layouts  60.4 us (7%)
  waiting for transfers between devices  49.2 us (6%)
  starting transfers between devices  21 us (2%)
  between operations  16.3 us (2%)
    pallas_call x1, Pallas kernels, gather_all(): pl.pallas_call(partial(gather_kernel, layers, count), in_specs=[pl.BlockS...  140 us
    pallas_call x1, Pallas kernels, reduce_all(): pl.pallas_call(partial(reduce_kernel, layers, shared, count), in_specs=[p...  134 us
    pallas_call x1, Pallas kernels, attend_bwd(): pl.pallas_call(partial(attend_bwd_sum_kernel, layers, shared, count, scal...  132 us
    dot_general x11, matrix products, mult_trans(): lax.dot_general(first_mat, second_mat, (((1,), (1,)), ((), ())), preferre...  64.1 us
    dot_general x11, matrix products, mult_rows(): lax.dot_general(first_mat, second_mat, (((0,), (0,)), ((), ())), preferre...  52.7 us
    dot_general x10, matrix products, mult_plain(): return jnp.dot(first_mat, second_mat, preferred_element_type=jnp.float32)  46.5 us
    all_gather x2, waiting for transfers between devices, per_chip(): lax.all_gather(shard, ('z', 'core', 'y', 'x'), axis=0, tiled=True)  40 us
    pallas_call x1, Pallas kernels, attend_fwd(): pl.pallas_call(partial(attend_fwd_kernel, scale=1.0 / math.sqrt(HEAD_DIM)...  35.2 us
  transfers between devices with their start and end apart: 20, of which 3 were waited for; matrix products, arithmetic and copies ran while one was open for 19% of the time, Pallas kernels for 21%

profile of v3, /device:TPU:8, one launch (start us, length us, event | category | flops | bytes accessed | tf_op | source)
XLA Modules:
  0.0 852.7 jit_solution(22522941065829843)
XLA Ops:
  16.0 1.7 collective-permute-start
  17.7 1.5 collective-permute-start.1
  21.9 5.4 collective-permute-start.9
  28.0 139.7 %gather_all.1 = (bf16[4,2,2,2,128,1024]{5,4,3,2,1,0:T(8,128)(2,1)}, bf16[4,2,2,2,128,1024]{5,4,3,2,1,0:T(8,128)(2,1)}) custom-call(bf16[128,1024]{1,0:T(8,128)(2,1)} %refs_0_.1, bf16[128,1024]{1,0:T(8,128)(2,1)} %refs_1_.1), custom_call_target="tpu_custom_call" | custom-call | bytes 209715200 | tf_op jit(solution)/shard_map/gather_all/pallas_call | solution.py:557
  168.5 11.1 %fusion.175 = f32[512,4096]{1,0:T(8,128)} fusion(bf16[4096,1024]{1,0:T(8,128)(2,1)} %bitcast.383, f32[1024]{0:T(1024)S(1)} %convert_element_type.438, f32[512]{0:T(512)S(1)} %fusion.160, f32[512]{0:T(512)S(1)} %broadcast_multiply_fusion.5, bf16[256,1024]{1,0:T(8,128)(2,1)S(1)} %get-tuple-element.150, bf16[256,1024]{1,0:T(8,128)(2,1)S(1)} %get-tuple-element.149), kind=kOutput, calls=%fused_computation.501 | convolution fusion | flops 4299161600 | bytes 17833984 | tf_op jit(solution)/shard_map/dot_general | solution.py:51
  179.7 7.9 fusion.196
  190.8 3.6 subtract_convert_fusion
  195.0 3.1 broadcast_select_fusion.1
  198.4 2.8 fusion.188
  202.0 2.3 convolution_convert_fusion.14.q_ref.refs_0_
  204.9 2.3 convolution_convert_fusion.13.k_ref.refs_1_
  207.2 2.3 convolution_convert_fusion.12.v_ref.refs_2_
  209.4 3.8 convolution_convert_fusion.5.place_ref.refs_3_
  213.2 35.2 %attend_fwd.1 = (bf16[1024,512]{1,0:T(8,128)(2,1)}, bf16[8,1024,1024]{2,1,0:T(8,128)(2,1)}) custom-call(s32[1]{0:T(128)} %dynamic_slice.57.len_ref, bf16[1024,512]{1,0:T(8,128)(2,1)} %convolution_convert_fusion.14.q_ref.refs_0_, bf16[1024,512]{1,0:T(8,128)(2,1)} %convolution_convert_fusion.13.k_ref.refs_1_, ...), custom_call_target="tpu_custom_call" | custom-call | flops 40000000000 | bytes 20971520 | tf_op jit(solution)/shard_map/attend_fwd/pallas_call | solution.py:262
  256.9 4.4 select_bitcast_fusion.1
  261.2 1.8 pad_maximum_fusion.5
  265.8 2.4 fusion.178
  268.9 1.4 copy-done.4
  270.6 2.3 broadcast_select_fusion.9
  274.2 10.4 %fusion.186 = (f32[512]{0:T(512)S(1)}, f32[512,1024]{1,0:T(8,128)S(1)}) fusion(f32[1024]{0:T(1024)S(1)} %bitcast.296, bf16[15,1024]{1,0:T(8,128)(2,1)S(1)} %get-tuple-element.195, bf16[512,1024]{1,0:T(8,128)(2,1)S(1)} %multiply_convert_fusion.12, f32[1024]{0:T(1024)S(1)} %bitcast.294, f32[1024]{0:T(1024)S(1)} %bitcast.292, f32[1024]{0:T(1024)S(1)} %bitcast.290, ...), kind=kLoop, calls=%fused_computation.510 | loop fusion | flops 95944192 | bytes 3336192 | tf_op jit(solution)/shard_map/jvp()/reduce_sum | solution.py:39
  285.0 1.6 fusion.198
  288.3 12.1 %fusion.179 = f32[512,4096]{1,0:T(8,128)} fusion(bf16[4096,1024]{1,0:T(8,128)(2,1)} %all-gather.7.cloned.1.call-done, f32[512,1024]{1,0:T(8,128)} %copy-done.17, f32[1024]{0:T(1024)S(1)} %convert_element_type.488, f32[512]{0:T(512)S(1)} %fusion.164, f32[512]{0:T(512)S(1)} %broadcast_multiply_fusion.1), kind=kOutput, calls=%fused_computation.504 | convolution fusion | flops 4297064448 | bytes 18882560 | tf_op jit(solution)/shard_map/dot_general | solution.py:51
  300.4 39.9 %all-gather.9.cloned.1.call-done = bf16[4096,1024]{1,0:T(8,128)(2,1)} async-done(((bf16[128,1024]{1,0:T(8,128)(2,1)}), bf16[4096,1024]{1,0:T(8,128)(2,1)}) %all-gather.9.cloned.1.call-update) | async-done | bytes 8388624 | tf_op jit(solution)/shard_map/all_gather | solution.py:931
  340.3 11.0 %fusion.199 = (f32[512]{0:T(512)S(1)}, f32[512,1024]{1,0:T(8,128)S(1)}) fusion(f32[512,1024]{1,0:T(8,128)} %copy-done.17, bf16[4096,1024]{1,0:T(8,128)(2,1)} %all-gather.9.cloned.1.call-done, f32[512,4096]{1,0:T(8,128)} %fusion.179), kind=kOutput, calls=%fused_computation.522 | convolution fusion | flops 4307025408 | bytes 20973568 | tf_op jit(solution)/shard_map/dot_general | solution.py:57
  352.5 1.4 fusion.43
  354.8 11.5 %convolution_convert_fusion.2 = bf16[4096,1024]{1,0:T(8,128)(2,1)} fusion(f32[512,1024]{1,0:T(8,128)S(1)} %get-tuple-element.109, f32[512]{0:T(512)S(1)} %negate_multiply_fusion.5, f32[512,4096]{1,0:T(8,128)} %fusion.179), kind=kOutput, calls=%fused_computation.43 | convolution fusion | flops 4311220224 | bytes 18876416 | tf_op jit(solution)/shard_map/dot_general | solution.py:61
  366.3 11.7 %multiply_convert_fusion.1 = bf16[512,4096]{1,0:T(8,128)(2,1)} fusion(f32[512,4096]{1,0:T(8,128)} %fusion.179, bf16[4096,1024]{1,0:T(8,128)(2,1)} %all-gather.9.cloned.1.call-done, f32[512,1024]{1,0:T(8,128)S(1)} %get-tuple-element.109, f32[512]{0:T(512)S(1)} %negate_multiply_fusion.5), kind=kOutput, calls=%fused_computation.36 | convolution fusion | flops 4315414528 | bytes 23070720 | tf_op jit(solution)/shard_map/dot_general | solution.py:51
  378.0 9.3 %convolution_convert_fusion.3 = bf16[4096,1024]{1,0:T(8,128)(2,1)} fusion(bf16[512,4096]{1,0:T(8,128)(2,1)} %multiply_convert_fusion.1, f32[512,1024]{1,0:T(8,128)S(1)} %copy-done.18, f32[1024]{0:T(1024)S(1)} %convert_element_type.488, f32[512]{0:T(512)S(1)} %fusion.164, f32[512]{0:T(512)S(1)} %broadcast_multiply_fusion.1), kind=kOutput, calls=%fused_computation.44 | convolution fusion | flops 4301258752 | bytes 14688256 | tf_op jit(solution)/shard_map/dot_general | solution.py:61
  387.2 8.0 multiply_reduce_fusion.1
  397.6 2.6 multiply_reduce_fusion.2
  400.2 1.6 convolution_convert_fusion.6
  402.6 8.1 fusion.92
  410.7 2.6 fusion.75
  413.3 3.3 fusion.76
  416.6 3.1 fusion.91
  421.0 5.3 collective-permute-start.7
  426.4 1.4 collective-permute-start.8
  427.8 1.6 copy.112
  430.7 15.8 %multiply_convert_fusion.6 = (bf16[512,1024]{1,0:T(8,128)(2,1)S(1)}, f32[512,1024]{1,0:T(8,128)S(1)}) fusion(f32[512,2048]{1,0:T(8,128)S(1)} %copy-done.5, f32[512]{0:T(512)S(1)} %fusion.159, f32[1024]{0:T(1024)S(1)} %bitcast.299, bf16[15,1024]{1,0:T(8,128)(2,1)S(1)} %get-tuple-element.193, bf16[512,1024]{1,0:T(8,128)(2,1)S(1)} %get-tuple-element.97, ...), kind=kLoop, calls=%fused_computation.270 | loop fusion | flops 98566144 | bytes 6481920 | tf_op jit(solution)/shard_map/convert.7
  449.4 3.2 multiply_reduce_fusion.3
  452.6 4.5 convolution_convert_fusion.4
  459.5 2.3 convolution_convert_fusion.11
  461.8 1.8 reshape.527
  463.6 1.5 fusion.191
  465.8 1.5 copy-done.26
  471.3 3.9 pad_maximum_fusion
  478.7 132.4 %attend_bwd.1 = (bf16[1024,512]{1,0:T(8,128)(2,1)}, bf16[1024,512]{1,0:T(8,128)(2,1)}, bf16[1024,512]{1,0:T(8,128)(2,1)}, bf16[2048,512]{1,0:T(8,128)(2,1)}, f32...) custom-call(bf16[1024,512]{1,0:T(8,128)(2,1)} %convolution_convert_fusion.14.q_ref, ...), custom_call_target="tpu_custom_call" | custom-call | flops 99999997952 | bytes 41943040 | tf_op jit(solution)/shard_map/attend_bwd/pallas_call | solution.py:373
  611.2 2.6 fusion.201
  620.6 2.0 copy-done.6
  624.5 2.4 fusion.97
  634.1 2.3 bitcast_convert_fusion.1
  636.4 1.6 bitcast_convert_fusion
  638.1 2.6 pad_maximum_fusion.2
  640.7 1.7 copy-done.7
  642.4 2.0 multiply_reduce_fusion
  644.5 2.0 fusion.180
  646.9 12.3 %multiply_convert_fusion = bf16[512,4096]{1,0:T(8,128)(2,1)} fusion(f32[512,4096]{1,0:T(8,128)} %fusion.175, bf16[4096,1024]{1,0:T(8,128)(2,1)} %bitcast.387, f32[512,1024]{1,0:T(8,128)S(1)} %add_add_fusion.7), kind=kOutput, calls=%fused_computation.35 | convolution fusion | flops 4314890240 | bytes 23068672 | tf_op jit(solution)/shard_map/dot_general | solution.py:51
  659.2 7.2 fusion.45
  666.4 7.3 convolution_convert_fusion.1
  673.7 11.0 %convolution_convert_fusion = bf16[4096,1024]{1,0:T(8,128)(2,1)} fusion(f32[512,1024]{1,0:T(8,128)S(1)} %add_add_fusion.7, f32[512,4096]{1,0:T(8,128)} %fusion.175), kind=kOutput, calls=%fused_computation.41 | convolution fusion | flops 4310695936 | bytes 18874368 | tf_op jit(solution)/shard_map/dot_general | solution.py:61
  687.5 134.3 %reduce_all.1 = (f32[128,1024]{1,0:T(8,128)}, f32[128,1024]{1,0:T(8,128)}, bf16[2,4,128,1024]{3,2,1,0:T(8,128)(2,1)}, f32[40,1024]{1,0:T(8,128)}) custom-call(bf16[4,2,2,2,128,1024]{5,4,3,2,1,0:T(8,128)(2,1)} %bitcast.234, bf16[4,2,2,2,128,1024]{5,4,3,2,1,0:T(8,128)(2,1)} %bitcast.235, bf16[4,2,2,128,1024]{4,3,2,1,0:T(8,128)(2,1)} %bitcast.232, ...), custom_call_target="tpu_custom_call" | custom-call | bytes 314572800 | tf_op jit(solution)/shard_map/reduce_all/pallas_call | solution.py:786
  821.7 1.7 fusion.192
  824.2 1.6 slice.697
  833.6 7.7 collective-permute-done.15
  (445 shorter events, 85.8 us)
Async XLA Ops:
  7.2 191.0 %all-gather.13.cloned.1.call-start = ((), (), s32[]{:S(2)}) async-start(), calls=%async_computation.3 | async-start | bytes 5242880 | tf_op jit(solution)/shard_map/all_gather | solution.py:929
  10.7 187.7 %all-gather.11.cloned.1.call-start = ((), (), s32[]{:S(2)}) async-start(), calls=%async_computation.2 | async-start | bytes 5406720 | tf_op jit(solution)/shard_map/all_gather | solution.py:928
  12.0 7.2 copy-start.123
  12.0 8.5 %copy-start.122 = (s32[2,256]{1,0:T(2,128)S(1)}, s32[2,256]{1,0:T(2,128)}, u32[]{:S(2)}) copy-start(s32[2,256]{1,0:T(2,128)} %param.26) | copy-start | bytes 6148
  12.0 8.6 %copy-start.45 = (bf16[2,256,1024]{2,1,0:T(8,128)(2,1)S(1)}, bf16[2,256,1024]{2,1,0:T(8,128)(2,1)}, u32[]{:S(2)}) copy-start(bf16[2,256,1024]{2,1,0:T(8,128)(2,1)} %param.27) | copy-start | bytes 3145732
  14.1 274.1 %all-gather.7.cloned.1.call-start = ((), (), s32[]{:S(2)}) async-start(), calls=%async_computation | async-start | bytes 8650752 | tf_op jit(solution)/shard_map/all_gather | solution.py:931
  14.9 325.5 %all-gather.9.cloned.1.call-start = ((), (), s32[]{:S(2)}) async-start(), calls=%async_computation.1 | async-start | bytes 8650752 | tf_op jit(solution)/shard_map/all_gather | solution.py:931
  16.0 151.8 %collective-permute-start = (bf16[256,1024]{1,0:T(8,128)(2,1)}, bf16[256,1024]{1,0:T(8,128)(2,1)S(1)}, u32[]{:S(2)}, u32[]{:S(2)}) collective-permute-start(bf16[256,1024]{1,0:T(8,128)(2,1)} %get-tuple-element.151), channel_id=1, source_target_pairs={{0,0},{1,1},{2,4},{3,5},{4,2},{5,3},{6,6},{7,7},{8,8},{9,9},{10,12... | collective-permute-start | bytes 1572872 | tf_op jit(solution)/shard_map/ppermute | solution.py:820
  17.7 150.1 %collective-permute-start.1 = (bf16[256,1024]{1,0:T(8,128)(2,1)}, bf16[256,1024]{1,0:T(8,128)(2,1)S(1)}, u32[]{:S(2)}, u32[]{:S(2)}) collective-permute-start(bf16[256,1024]{1,0:T(8,128)(2,1)} %get-tuple-element.152), channel_id=1, source_target_pairs={{0,1},{1,0},{2,5},{3,4},{4,3},{5,2},{6,7},{7,6},{8,9},{9,8},{10,13... | collective-permute-start | bytes 1572872 | tf_op jit(solution)/shard_map/ppermute | solution.py:820
  19.2 175.3 %collective-permute-start.2 = (s32[2]{0:T(128)S(1)}, s32[2]{0:T(128)S(1)}, u32[]{:S(2)}, u32[]{:S(2)}) collective-permute-start(s32[2]{0:T(128)S(1)} %copy-done.123), channel_id=1, source_target_pairs={{0,4},{1,5},{2,6},{3,7},{4,0},{5,1},{6,2},{7,3},{8,12},{9,13},{10,... | collective-permute-start | bytes 32 | tf_op jit(solution)/shard_map/ppermute | solution.py:811
  20.6 7.3 copy-start.116
  20.6 7.3 copy-start.117
  21.9 248.7 %collective-permute-start.9 = (bf16[256,1024]{1,0:T(8,128)(2,1)}, bf16[256,1024]{1,0:T(8,128)(2,1)}, u32[]{:S(2)}, u32[]{:S(2)}) collective-permute-start(bf16[256,1024]{1,0:T(8,128)(2,1)} %get-tuple-element.143), channel_id=1, source_target_pairs={{0,0},{1,1},{2,4},{3,5},{4,2},{5,3},{6,6},{7,7},{8,8},{9,9},{10,12... | collective-permute-start | bytes 1572872 | tf_op jit(solution)/shard_map/ppermute | solution.py:820
  27.2 243.3 %collective-permute-start.10 = (bf16[256,1024]{1,0:T(8,128)(2,1)}, bf16[256,1024]{1,0:T(8,128)(2,1)}, u32[]{:S(2)}, u32[]{:S(2)}) collective-permute-start(bf16[256,1024]{1,0:T(8,128)(2,1)} %get-tuple-element.144), channel_id=1, source_target_pairs={{0,1},{1,0},{2,5},{3,4},{4,3},{5,2},{6,7},{7,6},{8,9},{9,8},{10,13... | collective-permute-start | bytes 1572872 | tf_op jit(solution)/shard_map/ppermute | solution.py:820
  27.9 140.6 %copy-start.69 = (f32[1024]{0:T(1024)}, f32[1024]{0:T(1024)S(1)}, u32[]{:S(2)}) copy-start(f32[1024]{0:T(1024)S(1)} %convert_element_type.438) | copy-start | bytes 12292
  28.0 167.1 %copy-start.63 = (f32[1024]{0:T(1024)}, f32[1024]{0:T(1024)S(1)}, u32[]{:S(2)}) copy-start(f32[1024]{0:T(1024)S(1)} %convert_element_type.441) | copy-start | bytes 12292
  167.8 11.9 %copy-start.8 = (bf16[256,1024]{1,0:T(8,128)(2,1)}, bf16[256,1024]{1,0:T(8,128)(2,1)S(1)}, u32[]{:S(2)}) copy-start(bf16[256,1024]{1,0:T(8,128)(2,1)S(1)} %get-tuple-element.149) | copy-start | bytes 1572868
  167.8 11.9 %copy-start.10 = (bf16[256,1024]{1,0:T(8,128)(2,1)}, bf16[256,1024]{1,0:T(8,128)(2,1)S(1)}, u32[]{:S(2)}) copy-start(bf16[256,1024]{1,0:T(8,128)(2,1)S(1)} %get-tuple-element.150) | copy-start | bytes 1572868
  168.1 11.6 %copy-start.71 = (f32[512]{0:T(512)}, f32[512]{0:T(512)S(1)}, u32[]{:S(2)}) copy-start(f32[512]{0:T(512)S(1)} %broadcast_multiply_fusion.5) | copy-start | bytes 6148
  168.1 11.6 %slice-start.2 = ((s8[8388608]{0:T(1024)(128)(4,1)}), s8[4194304]{0:T(1024)(128)(4,1)S(1)}, s32[]{:S(2)}) async-start(s8[8388608]{0:T(1024)(128)(4,1)} %bitcast.388), calls=%async_computation.6 | async-start | bytes 8388608
  168.5 11.2 %copy-start.75 = (f32[512]{0:T(512)}, f32[512]{0:T(512)S(1)}, u32[]{:S(2)}) copy-start(f32[512]{0:T(512)S(1)} %fusion.44) | copy-start | bytes 6148
  168.5 11.2 %copy-start.73 = (f32[512]{0:T(512)}, f32[512]{0:T(512)S(1)}, u32[]{:S(2)}) copy-start(f32[512]{0:T(512)S(1)} %fusion.160) | copy-start | bytes 6148
  168.5 11.2 %slice-start.3 = ((s8[8388608]{0:T(1024)(128)(4,1)}), s8[4194304]{0:T(1024)(128)(4,1)S(1)}, s32[]{:S(2)}) async-start(s8[8388608]{0:T(1024)(128)(4,1)} %bitcast.388), calls=%async_computation.7 | async-start | bytes 8388608
  187.7 75.4 %copy-start.2 = (f32[512,1024]{1,0:T(8,128)}, f32[512,1024]{1,0:T(8,128)S(1)}, u32[]{:S(2)}) copy-start(f32[512,1024]{1,0:T(8,128)S(1)} %get-tuple-element.205) | copy-start | bytes 6291460
  187.7 7.3 copy-start.65
  189.1 6.0 copy-start.67
  189.4 5.6 collective-permute-start.3
  198.2 58.7 %collective-permute-start.5 = (bf16[4,512,1024]{2,1,0:T(8,128)(2,1)}, bf16[4,512,1024]{2,1,0:T(8,128)(2,1)}, u32[]{:S(2)}, u32[]{:S(2)}) collective-permute-start(bf16[4,512,1024]{2,1,0:T(8,128)(2,1)} %bitcast.239), channel_id=1, source_target_pairs={{0,4},{1,5},{2,6},{3,7},{4,0},{5,1},{6,2},{7,3},{8,12},{9,13},{10,... | collective-permute-start | bytes 12582920 | tf_op jit(solution)/shard_map/ppermute | solution.py:811
  201.3 5.9 copy-start.24
  213.2 36.7 %copy-start.60 = (bf16[31,1024]{1,0:T(8,128)(2,1)S(1)}, bf16[31,1024]{1,0:T(8,128)(2,1)}, u32[]{:S(2)}) copy-start(bf16[31,1024]{1,0:T(8,128)(2,1)} %param.41) | copy-start | bytes 190468
  249.5 2.0 collective-permute-start.4
  256.8 6.2 copy-start.31
  270.3 4.0 collective-permute-start.6
  274.2 10.8 %copy-start.13 = (f32[512,1024]{1,0:T(8,128)S(1)}, f32[512,1024]{1,0:T(8,128)}, u32[]{:S(2)}) copy-start(f32[512,1024]{1,0:T(8,128)} %copy-done.12) | copy-start | bytes 6291460
  274.2 10.8 %copy-start.41 = (bf16[4,2,128,1024]{3,2,1,0:T(8,128)(2,1)S(1)}, bf16[4,2,128,1024]{3,2,1,0:T(8,128)(2,1)}, u32[]{:S(2)}) copy-start(bf16[4,2,128,1024]{3,2,1,0:T(8,128)(2,1)} %get-tuple-element.112) | copy-start | bytes 6291460
  354.8 32.4 %slice-start.4 = ((s8[8388608]{0:T(1024)(128)(4,1)}), s8[4194304]{0:T(1024)(128)(4,1)S(1)}, s32[]{:S(2)}) async-start(s8[8388608]{0:T(1024)(128)(4,1)} %bitcast.391), calls=%async_computation.8 | async-start | bytes 8388608
  366.3 11.7 %copy-start.18 = (f32[512,1024]{1,0:T(8,128)S(1)}, f32[512,1024]{1,0:T(8,128)}, u32[]{:S(2)}) copy-start(f32[512,1024]{1,0:T(8,128)} %copy-done.17) | copy-start | bytes 6291460
  366.3 20.9 %slice-start.5 = ((s8[8388608]{0:T(1024)(128)(4,1)}), s8[4194304]{0:T(1024)(128)(4,1)S(1)}, s32[]{:S(2)}) async-start(s8[8388608]{0:T(1024)(128)(4,1)} %bitcast.391), calls=%async_computation.9 | async-start | bytes 8388608
  419.7 9.7 %collective-permute-start.11 = (bf16[16,1024]{1,0:T(8,128)(2,1)S(1)}, bf16[16,1024]{1,0:T(8,128)(2,1)S(1)}, u32[]{:S(2)}, u32[]{:S(2)}) collective-permute-start(bf16[16,1024]{1,0:T(8,128)(2,1)S(1)} %slice_select_fusion.2), channel_id=1, source_target_pairs={{0,4},{1,5},{2,6},{3,7},{4,0},{5,1},{6,2},{7,3},{8,12},{9,13},{10,... | collective-permute-start | bytes 98312 | tf_op jit(solution)/shard_map/ppermute | solution.py:811
  421.0 54.2 %collective-permute-start.7 = (bf16[256,1024]{1,0:T(8,128)(2,1)}, bf16[256,1024]{1,0:T(8,128)(2,1)}, u32[]{:S(2)}, u32[]{:S(2)}) collective-permute-start(bf16[256,1024]{1,0:T(8,128)(2,1)} %get-tuple-element.147), channel_id=1, source_target_pairs={{0,0},{1,1},{2,4},{3,5},{4,2},{5,3},{6,6},{7,7},{8,8},{9,9},{10,12... | collective-permute-start | bytes 1572872 | tf_op jit(solution)/shard_map/ppermute | solution.py:820
  426.4 48.9 %collective-permute-start.8 = (bf16[256,1024]{1,0:T(8,128)(2,1)}, bf16[256,1024]{1,0:T(8,128)(2,1)}, u32[]{:S(2)}, u32[]{:S(2)}) collective-permute-start(bf16[256,1024]{1,0:T(8,128)(2,1)} %get-tuple-element.148), channel_id=1, source_target_pairs={{0,1},{1,0},{2,5},{3,4},{4,3},{5,2},{6,7},{7,6},{8,9},{9,8},{10,13... | collective-permute-start | bytes 1572872 | tf_op jit(solution)/shard_map/ppermute | solution.py:820
  452.6 4.5 copy-start.80
  465.7 11.9 %collective-permute-start.12 = (bf16[512,512]{1,0:T(8,128)(2,1)S(1)}, bf16[512,512]{1,0:T(8,128)(2,1)S(1)}, u32[]{:S(2)}, u32[]{:S(2)}) collective-permute-start(bf16[512,512]{1,0:T(8,128)(2,1)S(1)} %bitcast.273), channel_id=1, source_target_pairs={{0,4},{1,5},{2,6},{3,7},{4,0},{5,1},{6,2},{7,3},{8,12},{9,13},{10,... | collective-permute-start | bytes 1572872 | tf_op jit(solution)/shard_map/ppermute | solution.py:811
  478.7 132.4 %copy-start.55 = (bf16[4,128,1024]{2,1,0:T(8,128)(2,1)S(1)}, bf16[4,128,1024]{2,1,0:T(8,128)(2,1)}, u32[]{:S(2)}) copy-start(bf16[4,128,1024]{2,1,0:T(8,128)(2,1)} %copy-done.54) | copy-start | bytes 3145732
  619.3 4.4 copy-start.36
  619.3 4.4 copy-start.128
  623.7 17.0 %collective-permute-start.13 = (bf16[512,1024]{1,0:T(8,128)(2,1)}, bf16[512,1024]{1,0:T(8,128)(2,1)}, u32[]{:S(2)}, u32[]{:S(2)}) collective-permute-start(bf16[512,1024]{1,0:T(8,128)(2,1)} %dynamic-slice_convert_fusion), channel_id=1, source_target_pairs={{0,4},{1,5},{2,6},{3,7},{4,0},{5,1},{6,2},{7,3},{8,12},{9,13},{10,... | collective-permute-start | bytes 3145736 | tf_op jit(solution)/shard_map/ppermute | solution.py:811
  638.1 4.3 copy-start.7
  638.1 4.3 copy-start.64
  638.1 4.3 copy-start.66
  646.5 12.7 %slice-start = ((s8[8388608]{0:T(1024)(128)(4,1)}), s8[4194304]{0:T(1024)(128)(4,1)S(1)}, s32[]{:S(2)}) async-start(s8[8388608]{0:T(1024)(128)(4,1)} %bitcast.384), calls=%async_computation.4 | async-start | bytes 8388608
  646.8 26.9 %copy-start.15 = (f32[512,1024]{1,0:T(8,128)}, f32[512,1024]{1,0:T(8,128)S(1)}, u32[]{:S(2)}) copy-start(f32[512,1024]{1,0:T(8,128)S(1)} %add_add_fusion.7) | copy-start | bytes 6291460
  646.8 12.3 %copy-start.9 = (bf16[256,1024]{1,0:T(8,128)(2,1)S(1)}, bf16[256,1024]{1,0:T(8,128)(2,1)}, u32[]{:S(2)}) copy-start(bf16[256,1024]{1,0:T(8,128)(2,1)} %copy-done.8) | copy-start | bytes 1572868
  646.8 12.3 %copy-start.11 = (bf16[256,1024]{1,0:T(8,128)(2,1)S(1)}, bf16[256,1024]{1,0:T(8,128)(2,1)}, u32[]{:S(2)}) copy-start(bf16[256,1024]{1,0:T(8,128)(2,1)} %copy-done.10) | copy-start | bytes 1572868
  646.8 12.3 %copy-start.70 = (f32[1024]{0:T(1024)S(1)}, f32[1024]{0:T(1024)}, u32[]{:S(2)}) copy-start(f32[1024]{0:T(1024)} %copy-done.69) | copy-start | bytes 12292
  646.8 12.3 %copy-start.72 = (f32[512]{0:T(512)S(1)}, f32[512]{0:T(512)}, u32[]{:S(2)}) copy-start(f32[512]{0:T(512)} %copy-done.71) | copy-start | bytes 6148
  646.8 12.3 %slice-start.1 = ((s8[8388608]{0:T(1024)(128)(4,1)}), s8[4194304]{0:T(1024)(128)(4,1)S(1)}, s32[]{:S(2)}) async-start(s8[8388608]{0:T(1024)(128)(4,1)} %bitcast.384), calls=%async_computation.5 | async-start | bytes 8388608
  659.2 7.2 copy-start.74
  659.2 7.2 copy-start.129
  673.7 11.4 %copy-start.76 = (f32[512]{0:T(512)S(1)}, f32[512]{0:T(512)}, u32[]{:S(2)}) copy-start(f32[512]{0:T(512)} %copy-done.75) | copy-start | bytes 6148
  687.5 138.3 %copy-start.16 = (f32[512,1024]{1,0:T(8,128)S(1)}, f32[512,1024]{1,0:T(8,128)}, u32[]{:S(2)}) copy-start(f32[512,1024]{1,0:T(8,128)} %copy-done.15) | copy-start | bytes 6291460
  826.5 7.1 collective-permute-start.14
  827.4 13.9 %collective-permute-start.15 = (bf16[256,1024]{1,0:T(8,128)(2,1)S(1)}, bf16[256,1024]{1,0:T(8,128)(2,1)S(1)}, u32[]{:S(2)}, u32[]{:S(2)}) collective-permute-start(bf16[256,1024]{1,0:T(8,128)(2,1)S(1)} %get-tuple-element.136), channel_id=1, source_target_pairs={{0,1},{1,0},{2,5},{3,4},{4,3},{5,2},{6,7},{7,6},{8,9},{9,8},{10,13... | collective-permute-start | bytes 1572872 | tf_op jit(solution)/shard_map/ppermute | solution.py:820
  833.6 8.9 %copy-start.59 = (f32[128,1024]{1,0:T(8,128)S(1)}, f32[128,1024]{1,0:T(8,128)}, u32[]{:S(2)}) copy-start(f32[128,1024]{1,0:T(8,128)} %get-tuple-element.246) | copy-start | bytes 1572868
  (92 other events, 172.7 us)
Sparse Core Ops, SparseCore 0:
  10.8 92.9 all-gather.12
  105.6 74.4 all-gather.10
  183.0 78.3 all-gather.6
  264.1 76.1 all-gather.8

commit v4 on v3

--- a/solution.py
+++ b/solution.py
@@ -13,9 +13,10 @@
 QBLK = 512
 RIM = 15
 PAIR = 128
-ROWS_FWD = 512
+ROWS_FWD = 256
 ROWS_BWD = 256
-VMEM = 56 * 2**20
+FF_BLOCK = 512
+VMEM = 58 * 2**20
 
 
 EPSILON = 1e-05
@@ -256,33 +257,46 @@
         mixed.append(mult_plain(prob, v_ref[...]))
     out_ref[...] = jnp.where(lanes < HEAD_DIM, mixed[0], mixed[1]).astype(jnp.bfloat16)
 
-def attend_fwd(length_arr, q, k, v, place, cb, pb, rows):
+def attend_fwd_gather_kernel(layers, count, blocks, *refs, scale):
+    ins, shards, refs = refs[:7], refs[7 : 7 + count], refs[7 + count :]
+    outs, fulls, sems = refs[:2], refs[2 : 2 + count], refs[2 + count :]
+    at = pl.program_id(0) * pl.num_programs(1) + pl.program_id(1)
+    plan = gather_plan(layers, shards, fulls, (), *sems)
+    run_between(*plan, at, blocks, partial(attend_fwd_kernel, *ins, *outs, scale=scale))
+
+
+def attend_fwd(length_arr, q, k, v, place, cb, pb, rows, layers, shards, collective_id):
     length, width = q.shape
     pairs = width // PAIR
-    return pl.pallas_call(
-        partial(attend_fwd_kernel, scale=1.0 / math.sqrt(HEAD_DIM)),
+    count = len(shards)
+    shard = shards[0].shape
+    part = pl.BlockSpec((rows, PAIR), lambda p, i: (i, p))
+    full = pl.BlockSpec((length, PAIR), lambda p, i: (0, p))
+    tall = pl.BlockSpec((2 * length, PAIR), lambda p, i: (0, p))
+    vec = pl.BlockSpec((1, PAIR), lambda p, i: (0, p))
+    far = [pl.BlockSpec(memory_space=pl.ANY)] * count
+    blocks = pairs * (length // rows)
+    attended, prob, *fulls = pl.pallas_call(
+        partial(attend_fwd_gather_kernel, layers, count, blocks, scale=1.0 / math.sqrt(HEAD_DIM)),
         grid=(pairs, length // rows),
-        in_specs=[
-            pl.BlockSpec(memory_space=pltpu.SMEM),
-            pl.BlockSpec((rows, PAIR), lambda p, i: (i, p)),
-            pl.BlockSpec((length, PAIR), lambda p, i: (0, p)),
-            pl.BlockSpec((length, PAIR), lambda p, i: (0, p)),
-            pl.BlockSpec((2 * length, PAIR), lambda p, i: (0, p)),
-            pl.BlockSpec((1, PAIR), lambda p, i: (0, p)),
-            pl.BlockSpec((1, PAIR), lambda p, i: (0, p)),
-        ],
-        out_specs=[
-            pl.BlockSpec((rows, PAIR), lambda p, i: (i, p)),
-            pl.BlockSpec((2, rows, length), lambda p, i: (p, i, 0)),
-        ],
+        in_specs=[pl.BlockSpec(memory_space=pltpu.SMEM), part, full, full, tall, vec, vec] + far,
+        out_specs=[part, pl.BlockSpec((2, rows, length), lambda p, i: (p, i, 0))] + far,
         out_shape=[
             jax.ShapeDtypeStruct((length, width), jnp.bfloat16),
             jax.ShapeDtypeStruct((2 * pairs, length, length), jnp.bfloat16),
-        ],
-        compiler_params=pltpu.CompilerParams(vmem_limit_bytes=VMEM),
-        cost_estimate=pl.CostEstimate(flops=40 * 10**9, bytes_accessed=20 * 2**20, transcendentals=pairs * 2 * length * length),
+        ]
+        + [jax.ShapeDtypeStruct((layers, 2, 2, 2, *shard), jnp.bfloat16)] * count,
+        scratch_shapes=gather_sems(count, layers),
+        compiler_params=pltpu.CompilerParams(
+            vmem_limit_bytes=VMEM, collective_id=collective_id, has_side_effects=True
+        ),
+        cost_estimate=pl.CostEstimate(
+            flops=40 * 10**9, bytes_accessed=20 * 2**20, transcendentals=2 * pairs * length * length
+        ),
         name="attend_fwd",
-    )(length_arr, q, k, v, place, cb, pb)
+    )(length_arr, q, k, v, place, cb, pb, *shards)
+    return attended, prob, [full.reshape(-1, shard[1]) for full in fulls]
+
 
 def attend_bwd_kernel(q_ref, k_ref, v_ref, place_ref, cb_ref, pb_ref, prob_ref, g_ref, gq_ref, gk_ref, gv_ref, gp_ref, gb_ref, gk_s, gv_s, gp_s, *, scale):
     rows = q_ref.shape[0]
@@ -340,30 +354,21 @@
         gp_ref[...] = gp_s[...].T.astype(jnp.bfloat16)
 
 
-def attend_bwd_sum_kernel(layers, shared, count, *refs, scale):
+def attend_bwd_sum_kernel(layers, shared, count, blocks, *refs, scale):
     ins, parts = refs[:8], refs[8 : 8 + count]
     refs = refs[8 + count :]
     outs, sums, scratch, own = refs[:5], refs[5 : 5 + count], refs[5 + count : 8 + count], refs[8 + count :]
     at = pl.program_id(0) * pl.num_programs(1) + pl.program_id(1)
-    enter, step, turns, leave = reduce_plan(layers, shared, parts, sums, None, own)
-    blocks = pl.num_programs(0) * pl.num_programs(1)
-    pl.when(at == 0)(enter)
-    for turn_at in range(min(turns, blocks)):
-        pl.when(at == turn_at)(partial(step, turn_at))
-    attend_bwd_kernel(*ins, *outs, *scratch, scale=scale)
-
-    @pl.when(at == blocks - 1)
-    def _():
-        for turn_at in range(blocks, turns):
-            step(turn_at)
-        leave()
+    plan = reduce_plan(layers, shared, parts, sums, None, own)
+    body = partial(attend_bwd_kernel, *ins, *outs, *scratch, scale=scale)
+    run_between(*plan, at, blocks, body)
 
 
 def attend_bwd(q, k, v, place, cb, pb, prob, grad, rows, layers, shared, parts, collective_id):
     length, width = q.shape
     pairs = width // PAIR
     count = len(parts)
-    blocks, shapes = reduce_shapes(layers, shared, parts)
+    inputs, shapes = reduce_shapes(layers, shared, parts)
     shard, channels = shapes[shared].shape[2:]
     still = lambda shape: pl.BlockSpec(shape, lambda p, i: (0,) * len(shape))
     full = pl.BlockSpec((length, PAIR), lambda p, i: (0, p))
@@ -371,7 +376,7 @@
     vec = pl.BlockSpec((1, PAIR), lambda p, i: (0, p))
     tall = pl.BlockSpec((2 * length, PAIR), lambda p, i: (0, p))
     return pl.pallas_call(
-        partial(attend_bwd_sum_kernel, layers, shared, count, scale=1.0 / math.sqrt(HEAD_DIM)),
+        partial(attend_bwd_sum_kernel, layers, shared, count, pairs * (length // rows), scale=1.0 / math.sqrt(HEAD_DIM)),
         grid=(pairs, length // rows),
         in_specs=[
             part,
@@ -416,7 +421,7 @@
         pb,
         prob,
         grad,
-        *blocks,
+        *inputs,
     )
 
 
@@ -463,41 +468,48 @@
     return sorted(range(1, layers), key=lambda k: -min(k, layers - k)) + [0]
 
 
-def gather_plan(layers, shards, fulls, z_sem, p_sem, d_sem, c_sem, own_sem):
+def gather_plan(layers, shards, fulls, flat_only, z_sem, p_sem, d_sem, c_sem, own_sem):
     at, spot = chip_place(layers)
     arrays = range(len(shards))
-    half = shards[0].shape[0] // 2
-    items = [(dz, a) for dz in reversed(far_first(layers)) for a in arrays]
-    own = [pltpu.make_async_copy(shards[a], fulls[a].at[spot()], own_sem.at[a]) for a in arrays]
-    along, flat, cross, core = {}, {}, {}, {}
+    z, _, _, _ = spot()
+    odd = lax.rem(z, 2)
+    pair = at(dz=1 + odd * (layers - 2))
+    items = [(0, a) for a in flat_only]
+    items += [(dz, a) for dz in reversed(far_first(layers)) for a in arrays if a not in flat_only]
+    own, along, flat, cross, last = {}, {}, {}, {}, {}
     for dz, a in items:
         full = fulls[a]
-        source = full.at[spot(dz)] if dz else shards[a]
+        flat_at = a in flat_only
+        place = (lambda *_, **by: (odd, *spot(**by)[2:])) if flat_at else (lambda **by: spot(dz, **by))
+        half = shards[a].shape[0] // 32 * 16
+        source = full.at[place()] if dz else shards[a]
         if dz:
             along[dz, a] = remote(shards[a], full.at[spot()], z_sem, (a, dz), at(dz=dz))
+        else:
+            own[dz, a] = pltpu.make_async_copy(shards[a], full.at[place()], own_sem.at[a])
         flat[dz, a] = (
-            remote(source, full.at[spot(dz)], p_sem, (a, dz, 0), at(dx=1)),
-            remote(source, full.at[spot(dz)], p_sem, (a, dz, 1), at(dy=1)),
+            remote(source, full.at[place()], p_sem, (a, dz, 0), at(dx=1)),
+            remote(source, full.at[place()], p_sem, (a, dz, 1), at(dy=1)),
         )
-        from_x = full.at[(*spot(dz, dx=1), pl.ds(half, half))]
-        from_y = full.at[(*spot(dz, dy=1), pl.ds(0, half))]
+        from_x = full.at[(*place(dx=1), pl.ds(half, shards[a].shape[0] - half))]
+        from_y = full.at[(*place(dy=1), pl.ds(0, half))]
         cross[dz, a] = (
             remote(from_x, from_x, d_sem, (a, dz, 0), at(dy=1)),
             remote(from_y, from_y, d_sem, (a, dz, 1), at(dx=1)),
         )
-        plane = full.at[spot(dz)[:2]]
-        core[dz, a] = remote(plane, plane, c_sem, (a, dz), at(dc=1))
+        plane = full.at[place()[:-2]]
+        last[dz, a] = remote(plane, plane, c_sem, (a, dz), pair if flat_at else at(dc=1))
 
     def enter():
         greet(at, layers)
-        for dz in far_first(layers)[:-1]:
-            for a in arrays:
-                along[dz, a].start()
-        for copy in own:
+        for item in items:
+            if item[0]:
+                along[item].start()
+        for copy in own.values():
             copy.start()
 
     def spread(item):
-        if item[0]:
+        if item in along:
             along[item].wait_recv()
         for copy in flat[item]:
             copy.start()
@@ -510,26 +522,25 @@
     def share(item):
         for got in cross[item]:
             got.wait_recv()
-        if not item[0]:
-            own[item[1]].wait()
-        core[item].start()
-
-    steps = []
-    for turn_at in range(len(items) + 4):
+        if item in own:
+            own[item].wait()
+        last[item].start()
+
+    def step(turn_at):
         for action, lag in ((spread, 0), (turn, 2), (share, 4)):
             if 0 <= turn_at - lag < len(items):
-                steps.append(partial(action, items[turn_at - lag]))
+                action(items[turn_at - lag])
 
     def leave():
         for item in items:
-            core[item].wait_recv()
+            last[item].wait_recv()
         for item in items:
-            if item[0]:
+            if item in along:
                 along[item].wait_send()
-            for copy in (*flat[item], *cross[item], core[item]):
+            for copy in (*flat[item], *cross[item], last[item]):
                 copy.wait_send()
 
-    return enter, steps, leave
+    return enter, step, len(items) + 4, leave
 
 
 def gather_sems(count, layers):
@@ -544,55 +555,61 @@
 
 
 def gather_kernel(layers, count, *refs):
-    enter, steps, leave = gather_plan(layers, refs[:count], refs[count : 2 * count], *refs[2 * count :])
+    enter, step, turns, leave = gather_plan(
+        layers, refs[:count], refs[count : 2 * count], (count - 1,), *refs[2 * count :]
+    )
     enter()
-    for step in steps:
-        step()
+    for turn_at in range(turns):
+        step(turn_at)
     leave()
 
 
-def gather_all(layers, shards, collective_id):
-    count = len(shards)
-    rows, width = shards[0].shape
-    fulls = pl.pallas_call(
+def gather_all(layers, shards, flat_shard, collective_id):
+    ins = [*shards, flat_shard]
+    count = len(ins)
+    width = flat_shard.shape[1]
+    shapes = [(layers, 2, 2, 2, *shard.shape) for shard in shards] + [(2, 2, 2, *flat_shard.shape)]
+    *fulls, flat_full = pl.pallas_call(
         partial(gather_kernel, layers, count),
         in_specs=[pl.BlockSpec(memory_space=pl.ANY)] * count,
         out_specs=[pl.BlockSpec(memory_space=pl.ANY)] * count,
-        out_shape=[jax.ShapeDtypeStruct((layers, 2, 2, 2, rows, width), jnp.bfloat16)] * count,
+        out_shape=[jax.ShapeDtypeStruct(shape, jnp.bfloat16) for shape in shapes],
         scratch_shapes=gather_sems(count, layers),
         compiler_params=pltpu.CompilerParams(collective_id=collective_id, has_side_effects=True),
-        cost_estimate=pl.CostEstimate(flops=0, bytes_accessed=200 * 2**20, transcendentals=0),
+        cost_estimate=pl.CostEstimate(flops=0, bytes_accessed=300 * 2**20, transcendentals=0),
         name="gather_all",
-    )(*shards)
-    return [full.reshape(8 * layers * rows, width) for full in fulls]
+    )(*ins)
+    return [full.reshape(-1, width) for full in fulls], flat_full
 
 
 def add_rows(target, one, two):
     target[...] = (one[...].astype(jnp.float32) + two[...].astype(jnp.float32)).astype(target.dtype)
 
 
-def reduce_plan(layers, shared, parts, outs, small, scratch):
+def reduce_plan(layers, shared, parts, outs, small, scratch, made=None, summed=None):
     at, spot = chip_place(layers)
     sums, got_c, got_d, got_p, got_z, got_s, load_sem, c_sem, d_sem, p_sem, z_sem, s_sem, *tiny = scratch
     arrays = range(len(parts))
     rows = sums.shape[4]
     half = rows // 2
     order = far_first(layers)
-    items = [(dz, shared) for dz in order]
+    items = [(dz, shared) for dz in order if summed is None]
     items += [(dz, a) for dz in order for a in arrays if a != shared]
     first, second = pl.ds(0, half), pl.ds(half, half)
     here, by_y, by_x, far = (spot(0, 0, dy, dx)[2:] for dy, dx in ((0, 0), (1, 0), (0, 1), (1, 1)))
-    whole = [len(part.shape) == 6 for part in parts]
+    made = made or {}
+    whole = [a in made or len(parts[a].shape) == 6 for a in arrays]
     core_at = spot()[1]
     load, core, cross, flat, along = {}, {}, {}, {}, {}
     for dz, a in items:
         total = sums.at[a, dz]
-        source = parts[a].at[spot(dz)[:2]] if whole[a] else parts[a].at[spot(dz)[0]]
-        load[dz, a] = pltpu.make_async_copy(source, total, load_sem.at[a, dz])
+        if a not in made:
+            source = parts[a].at[spot(dz)[:2]] if whole[a] else parts[a].at[spot(dz)[0]]
+            load[dz, a] = pltpu.make_async_copy(source, total, load_sem.at[a, dz])
         if whole[a]:
-            core[dz, a] = remote(
-                parts[a].at[spot(dz, dc=1)[:2]], got_c.at[a, dz], c_sem, (a, dz), at(dc=1)
-            )
+            slot = order.index(dz) % 2
+            source = parts[a].at[slot] if a in made else parts[a].at[spot(dz, dc=1)[:2]]
+            core[dz, a] = remote(source, got_c.at[a, dz], c_sem, (a, dz), at(dc=1))
         cross[dz, a] = (
             remote(total.at[(*far, first)], got_d.at[a, dz, 0], d_sem, (a, dz, 0), at(dx=1)),
             remote(total.at[(*far, second)], got_d.at[a, dz, 1], d_sem, (a, dz, 1), at(dy=1)),
@@ -608,9 +625,16 @@
     own = got_s.at[(core_at, spot()[0])]
     handed = {k: remote(own, own, s_sem, (k,), at(dz=k)) for k in range(1, layers)}
     swapped = remote(got_s.at[core_at], got_s.at[core_at], s_sem, (0,), at(dc=1))
+    sent = {}
+    if summed:
+        got_m, m_sem = tiny[3:]
+        sent = {
+            k: remote(summed[0].at[spot(k)[0]], got_m.at[k], m_sem, (k,), at(dz=layers - k))
+            for k in range(1, layers)
+        }
     hops = []
     if small:
-        level, got_t, t_sem = tiny
+        level, got_t, t_sem = tiny[:3]
         hops = [
             remote(level.at[i], got_t.at[i], t_sem, (i,), device)
             for i, device in enumerate((at(dc=1), at(dx=1), at(dy=1)))
@@ -624,14 +648,38 @@
         if small:
             level[0] = small[0][...]
             hops[0].start()
+        for copy in sent.values():
+            copy.start()
         for item in items:
-            if item in core:
+            if item in load:
+                load[item].start()
+                if item in core:
+                    core[item].start()
+
+    def make(item):
+        dz, a = item
+        if a not in made:
+            return
+        left, right = made[a]
+        size = 4 * rows
+        turn_of = order.index(dz)
+        if turn_of >= 2:
+            core[order[turn_of - 2], a].wait_send()
+        for dc, target in ((1, parts[a].at[turn_of % 2]), (0, sums.at[a, dz])):
+            z_at, c_at = spot(dz, dc)[:2]
+            columns = pl.ds(pl.multiple_of((2 * z_at + c_at) * size, size), size)
+            block = mult_rows(left[:, columns], right[...]).astype(jnp.bfloat16)
+            for at_y in range(2):
+                for at_x in range(2):
+                    row = (2 * at_y + at_x) * rows
+                    target[at_y, at_x] = block[row : row + rows]
+            if dc:
                 core[item].start()
-            load[item].start()
 
     def join_core(item):
         dz, a = item
-        load[item].wait()
+        if item in load:
+            load[item].wait()
         if whole[a]:
             core[item].wait_recv()
         for place in (far, by_y, by_x, here):
@@ -686,7 +734,14 @@
             small[1][...] = total
 
     def hand_on():
-        own[...] = total_of(shared).astype(jnp.bfloat16)
+        if summed:
+            total = summed[0][spot()[0]].astype(jnp.float32)
+            for k, copy in sent.items():
+                copy.wait_recv()
+                total = total + got_m[k].astype(jnp.float32)
+        else:
+            total = total_of(shared)
+        own[...] = total.astype(jnp.bfloat16)
         for copy in handed.values():
             copy.start()
 
@@ -695,11 +750,13 @@
             copy.wait_recv()
         swapped.start()
 
-    handed_at = layers - 1 + 5 + 2
-    turns = max(len(items) + 5, handed_at + 4)
+    lead = 2 if made else 0
+    handed_at = 5 if summed else layers - 1 + 5 + 2 + lead
+    turns = max(len(items) + 5 + lead, handed_at + 4)
 
     def step(turn_at):
-        for action, lag in ((join_core, 0), (join_cross, 3), (join_flat, 5)):
+        actions = ((make, 0), (join_core, lead), (join_cross, lead + 3), (join_flat, lead + 5))
+        for action, lag in actions:
             if 0 <= turn_at - lag < len(items):
                 action(items[turn_at - lag])
         if small and 1 <= turn_at <= 4:
@@ -714,15 +771,15 @@
             if a != shared:
                 outs[a][...] = total_of(a)
         swapped.wait_recv()
-        outs[shared][...] = got_s[...]
+        (summed[1] if summed else outs[shared])[...] = got_s[...]
         for item in items:
             if item[0]:
                 along[item].wait_send()
             for copy in (*cross[item], *flat[item]):
                 copy.wait_send()
-            if item in core:
+            if item in core and not (item[1] in made and item[0] in order[:-2]):
                 core[item].wait_send()
-        for copy in (*handed.values(), swapped, *hops):
+        for copy in (*handed.values(), *sent.values(), swapped, *hops):
             copy.wait_send()
 
     return enter, step, turns, leave
@@ -750,6 +807,8 @@
             pltpu.VMEM((4, *small.shape), jnp.float32),
             pltpu.VMEM((2 + layers, *small.shape), jnp.float32),
             dma((2, 2 + layers)),
+            pltpu.VMEM((layers, rows, width), jnp.bfloat16),
+            dma((2, layers)),
         ]
     return scratch
 
@@ -767,10 +826,16 @@
     return blocks, shapes
 
 
-def reduce_kernel(layers, shared, count, *refs):
-    parts, small, outs, total = refs[:count], refs[count], refs[count + 1 : 2 * count + 1], refs[2 * count + 1]
+def reduce_kernel(layers, part, left_a, right_a, left_b, right_b, small, sum_a, sum_b, handed, total, ring_a, ring_b, *scratch):
     enter, step, turns, leave = reduce_plan(
-        layers, shared, parts, outs, (small, total), refs[2 * count + 2 :]
+        layers,
+        None,
+        (ring_a, ring_b),
+        (sum_a, sum_b),
+        (small, total),
+        scratch,
+        {0: (left_a, right_a), 1: (left_b, right_b)},
+        (part, handed),
     )
     enter()
     for turn_at in range(turns):
@@ -778,23 +843,155 @@
     leave()
 
 
-def reduce_all(layers, shared, parts, small, collective_id):
-    count = len(parts)
-    blocks, shapes = reduce_shapes(layers, shared, parts)
-    rows, width = shapes[shared].shape[2:]
+def reduce_all(layers, part, products, small, collective_id):
+    rows, width = part.shape[1:]
     near = pl.BlockSpec(memory_space=pltpu.VMEM)
+    ring = pltpu.VMEM((2, 2, 2, rows, width), jnp.bfloat16)
     return pl.pallas_call(
-        partial(reduce_kernel, layers, shared, count),
-        in_specs=[pl.BlockSpec(memory_space=pl.ANY)] * count + [near],
-        out_specs=[near] * (count + 1),
-        out_shape=shapes + [jax.ShapeDtypeStruct(small.shape, jnp.float32)],
-        scratch_shapes=reduce_scratch(count, layers, rows, width, small),
+        partial(reduce_kernel, layers),
+        in_specs=[near] * 6,
+        out_specs=[near] * 4,
+        out_shape=[
+            jax.ShapeDtypeStruct((rows, width), jnp.float32),
+            jax.ShapeDtypeStruct((rows, width), jnp.float32),
+            jax.ShapeDtypeStruct((2, layers, rows, width), jnp.bfloat16),
+            jax.ShapeDtypeStruct(small.shape, jnp.float32),
+        ],
+        scratch_shapes=[ring, ring] + reduce_scratch(2, layers, rows, width, small),
         compiler_params=pltpu.CompilerParams(
             collective_id=collective_id, has_side_effects=True, vmem_limit_bytes=VMEM
         ),
-        cost_estimate=pl.CostEstimate(flops=0, bytes_accessed=300 * 2**20, transcendentals=0),
+        cost_estimate=pl.CostEstimate(
+            flops=8 * 10**9, bytes_accessed=300 * 2**20, transcendentals=0
+        ),
         name="reduce_all",
-    )(*blocks, small)
+    )(part, *(matrix for product in products for matrix in product), small)
+
+
+def run_between(enter, step, turns, leave, at, blocks, body):
+    pl.when(at == 0)(enter)
+    for turn_at in range(min(turns, blocks)):
+        pl.when(at == turn_at)(partial(step, turn_at))
+    body()
+
+    @pl.when(at == blocks - 1)
+    def _():
+        for turn_at in range(blocks, turns):
+            step(turn_at)
+        leave()
+
+
+def norm_stats(values):
+    centred = values - jnp.mean(values, axis=-1, keepdims=True)
+    inverse = lax.rsqrt(jnp.mean(centred * centred, axis=-1, keepdims=True) + EPSILON)
+    return centred * inverse, inverse
+
+
+def norm_back(normal, inverse, gain_vec, upstream):
+    grad = upstream * gain_vec
+    grad_mean = jnp.mean(grad, axis=-1, keepdims=True)
+    grad_along = jnp.mean(grad * normal, axis=-1, keepdims=True)
+    return (
+        (grad - grad_mean - normal * grad_along) * inverse,
+        jnp.sum(upstream * normal, axis=0, keepdims=True),
+    )
+
+
+def ffn_fwd_kernel(x_ref, gain_ref, up_ref, down_ref, y_ref, h_ref, act_ref, slope_ref):
+    @pl.when(pl.program_id(0) == 0)
+    def _():
+        values = x_ref[...].astype(jnp.float32)
+        normal, _ = norm_stats(values)
+        h_ref[...] = (normal * gain_ref[...].astype(jnp.float32)).astype(jnp.bfloat16)
+        y_ref[...] = values
+
+    before = mult_trans(h_ref[...], up_ref[...])
+    squash = 1.0 / (1.0 + jnp.exp(-before))
+    active = before * squash
+    slope_ref[...] = (squash + active * (1.0 - squash)).astype(jnp.bfloat16)
+    active_low = active.astype(jnp.bfloat16)
+    act_ref[...] = active_low
+    y_ref[...] += 0.5 * mult_plain(active_low, down_ref[...])
+
+
+def ffn_blocks(rows, width, block):
+    still = pl.BlockSpec((rows, width), lambda j: (0, 0))
+    vec = pl.BlockSpec((1, width), lambda j: (0, 0))
+    weight = pl.BlockSpec((block, width), lambda j: (j, 0))
+    hidden = pl.BlockSpec((rows, block), lambda j: (0, j))
+    return still, vec, weight, hidden
+
+
+def ffn_fwd(x, gain_vec, up, down):
+    rows, width = x.shape
+    total = up.shape[0]
+    still, vec, weight, hidden = ffn_blocks(rows, width, FF_BLOCK)
+    return pl.pallas_call(
+        ffn_fwd_kernel,
+        grid=(total // FF_BLOCK,),
+        in_specs=[still, vec, weight, weight],
+        out_specs=[still, still, hidden, hidden],
+        out_shape=[
+            jax.ShapeDtypeStruct((rows, width), jnp.float32),
+            jax.ShapeDtypeStruct((rows, width), jnp.bfloat16),
+            jax.ShapeDtypeStruct((rows, total), jnp.bfloat16),
+            jax.ShapeDtypeStruct((rows, total), jnp.bfloat16),
+        ],
+        compiler_params=pltpu.CompilerParams(vmem_limit_bytes=VMEM),
+        cost_estimate=pl.CostEstimate(
+            flops=4 * rows * width * total,
+            bytes_accessed=4 * width * total + 4 * rows * total,
+            transcendentals=rows * total,
+        ),
+        name="ffn_fwd",
+    )(x, gain_vec, up, down)
+
+
+def ffn_bwd_kernel(x_ref, gain_ref, g_ref, slope_ref, up_ref, down_ref, gx_ref, gf_ref, gp_ref, gain_out, sum_s):
+    step = pl.program_id(0)
+
+    @pl.when(step == 0)
+    def _():
+        gf_ref[...] = (0.5 * g_ref[...]).astype(jnp.bfloat16)
+        sum_s[...] = jnp.zeros_like(sum_s)
+
+    grad_act = mult_trans(gf_ref[...], down_ref[...])
+    grad_before = (grad_act * slope_ref[...].astype(jnp.float32)).astype(jnp.bfloat16)
+    gp_ref[...] = grad_before
+    sum_s[...] += mult_plain(grad_before, up_ref[...])
+
+    @pl.when(step == pl.num_programs(0) - 1)
+    def _():
+        normal, inverse = norm_stats(x_ref[...].astype(jnp.float32))
+        grad, gain_grad = norm_back(normal, inverse, gain_ref[...].astype(jnp.float32), sum_s[...])
+        gx_ref[...] = (g_ref[...] + grad).astype(gx_ref.dtype)
+        gain_out[...] = gain_grad
+
+
+def ffn_bwd(x, gain_vec, grad, slope, up, down, out_type):
+    rows, width = x.shape
+    total = up.shape[0]
+    still, vec, weight, hidden = ffn_blocks(rows, width, FF_BLOCK)
+    return pl.pallas_call(
+        ffn_bwd_kernel,
+        grid=(total // FF_BLOCK,),
+        in_specs=[still, vec, still, hidden, weight, weight],
+        out_specs=[still, still, hidden, vec],
+        out_shape=[
+            jax.ShapeDtypeStruct((rows, width), out_type),
+            jax.ShapeDtypeStruct((rows, width), jnp.bfloat16),
+            jax.ShapeDtypeStruct((rows, total), jnp.bfloat16),
+            jax.ShapeDtypeStruct((1, width), jnp.float32),
+        ],
+        scratch_shapes=[pltpu.VMEM((rows, width), jnp.float32)],
+        compiler_params=pltpu.CompilerParams(vmem_limit_bytes=VMEM),
+        cost_estimate=pl.CostEstimate(
+            flops=4 * rows * width * total,
+            bytes_accessed=4 * width * total + 4 * rows * total,
+            transcendentals=0,
+        ),
+        name="ffn_bwd",
+    )(x, gain_vec, grad, slope, up, down)
 
 
 class Hops:
@@ -900,7 +1097,6 @@
         return jnp.stack(pick(x == 0, *got))
 
     frames_own = turn_in(frames)
-    up_first, down_first = gather_all(layers, [first_up, first_down], 1)
     positions = wide_at * quarter + jnp.arange(quarter, dtype=jnp.int32)
     seed_weight = f32(masked) * f32(positions[None, :] < lengths[:, None])
     seed_own_low = low(f32(cotangent) * seed_weight[:, :, None])
@@ -914,37 +1110,39 @@
         return lax.dynamic_slice_in_dim(weight, core * count, count)
 
     band = query_weight.shape[0] // 2
+    odd = lax.rem(lax.axis_index("z"), 2)
+    piece = band // 2
+
+    def own_quarter(weight):
+        return lax.dynamic_slice_in_dim(weight, core * band + odd * piece, piece)
+
     own_bias = own_half(jnp.stack([content_bias, place_bias], axis=1)).T
     attn_chunk = jnp.concatenate(
-        [
-            own_half(query_weight),
-            own_half(key_weight),
-            own_half(value_weight),
-            own_half(place_weight),
-            jnp.pad(own_bias, ((0, 14), (0, channels - band))),
-        ]
-    )
+        [own_quarter(weight) for weight in (query_weight, key_weight, value_weight, place_weight)]
+        + [jnp.pad(own_bias, ((0, 14), (0, channels - band)))]
+    )
+    (up_first, down_first), attn_all = gather_all(layers, [first_up, first_down], attn_chunk, 1)
     conv_chunk = jnp.concatenate([own_half(out_weight), own_half(point_weight), own_half(glu_weight)])
-    attn_all = lax.all_gather(attn_chunk, ("y", "x"), axis=0)
+    conv_chunk, attn_all = lax.optimization_barrier((conv_chunk, attn_all))
     conv_all = lax.all_gather(conv_chunk, ("y", "x"), axis=0)
-    up_second, down_second = (
-        lax.all_gather(shard, ("z", "core", "y", "x"), axis=0, tiled=True)
-        for shard in (second_up, second_down)
-    )
+    attn_all = attn_all.reshape(2, 4, -1, channels)
 
     def heads_of(at):
-        return attn_all[:, at * band : (at + 1) * band].reshape(4 * band, channels)
+        rows_of = attn_all[:, :, at * piece : (at + 1) * piece]
+        return rows_of.transpose(1, 0, 2, 3).reshape(4 * band, channels)
 
     query_own, key_own, value_own, place_own = (heads_of(at) for at in range(4))
-    own_biases = attn_all[:, 4 * band : 4 * band + 2, :band].transpose(1, 0, 2).reshape(2, 4 * band)
+    own_biases = attn_all[0, :, 4 * piece : 4 * piece + 2, :band].transpose(1, 0, 2).reshape(2, 4 * band)
     conv_other = hops.send(conv_all, dc=1)
     conv_both = jnp.stack(pick(core == 0, conv_all, conv_other), axis=1)
     full_out = conv_both[:, :, :band].reshape(8 * band, channels)
     full_point = conv_both[:, :, band : 2 * band].reshape(8 * band, channels)
     full_glu = conv_both[:, :, 2 * band :].reshape(16 * band, channels)
 
-    stream0 = f32(frames_own)
-    stream1, saved_first = ffn_forward(stream0, f32(first_gain), up_first, down_first)
+    stream1, first_low, first_act, first_slope = ffn_fwd(
+        frames_own, first_gain[None], up_first, down_first
+    )
+    stream1, seed_own_low = lax.optimization_barrier((stream1, seed_own_low))
     normed_attn, attn_pull = jax.vjp(norm_rows, stream1, f32(attn_gain))
     attn_half = low(normed_attn)
     attn_other = hops.send(attn_half, dc=1)
@@ -954,8 +1152,18 @@
     key = low(mult_trans(attn_low, key_own))
     value = low(mult_trans(attn_low, value_own))
     place = low(mult_trans(rel_table, place_own))
-    attended, prob = attend_fwd(
-        own_length, query, key, value, place, own_biases[:1], own_biases[1:], ROWS_FWD
+    attended, prob, (up_second, down_second) = attend_fwd(
+        own_length,
+        query,
+        key,
+        value,
+        place,
+        own_biases[:1],
+        own_biases[1:],
+        ROWS_FWD,
+        layers,
+        [second_up, second_down],
+        4,
     )
 
     def halves(matrix):
@@ -980,25 +1188,20 @@
     middle, middle_pull = jax.vjp(norm_rows, conv_out, f32(middle_gain))
     swished = low(jax.nn.silu(middle))
     stream3 = stream2 + mult_trans(swished, full_point)
-    stream4, saved_second = ffn_forward(stream3, f32(second_gain), up_second, down_second)
+    stream4, second_low, second_act, second_slope = ffn_fwd(
+        stream3, second_gain[None], up_second, down_second
+    )
     final_rows, final_pull = jax.vjp(norm_rows, stream4, f32(final_gain))
     output = turn_out(low(final_rows))
 
     seed_own = turn_in(seed_own_low)
     grad4, grad_final_gain = final_pull(f32(seed_own))
 
-    def ffn_back(grad_stream, saved_ffn, up_full, down_full):
-        norm_pull, normed_low, before, active_low = saved_ffn
-        grad_out = low(0.5 * grad_stream)
-        grad_down = low(mult_rows(active_low, grad_out))
-        grad_before = low(mult_trans(grad_out, down_full) * silu_slope(before))
-        grad_up = low(mult_rows(grad_before, normed_low))
-        grad_input, grad_gain = norm_pull(mult_plain(grad_before, up_full))
-        return grad_stream + grad_input, grad_gain, grad_up, grad_down
-
-    grad3, grad_second_gain, grad_up_second, grad_down_second = ffn_back(
-        grad4, saved_second, up_second, down_second
-    )
+    grad3, grad_out2, grad_before2, grad_second_gain = ffn_bwd(
+        stream3, second_gain[None], grad4, second_slope, up_second, down_second, jnp.float32
+    )
+    grad_down_second = low(mult_rows(second_act, grad_out2))
+    grad_up_second = low(mult_rows(grad_before2, second_low))
     grad_branch = low(grad3)
     grad_point = mult_rows(grad_branch, swished)
     grad_middle = mult_plain(grad_branch, full_point) * silu_slope(middle)
@@ -1056,6 +1259,15 @@
     grad_key_w = mult_rows(grad_key, attn_low)
     grad_value_w = mult_rows(grad_value, attn_low)
     grad_place_w = mult_rows(grad_place, rel_table)
+    attn_part = jnp.concatenate(
+        [
+            low(part).reshape(4, layers, -1, channels)
+            for part in (grad_query_w, grad_key_w, grad_value_w, grad_place_w)
+        ],
+        axis=2,
+    )
+    attn_part, grad_query = lax.optimization_barrier((attn_part, grad_query))
+    attn_part = lax.psum_scatter(attn_part, ("y", "x"), scatter_dimension=0, tiled=False)
     grad_normed = (
         mult_plain(grad_query, query_own)
         + mult_plain(grad_key, key_own)
@@ -1064,15 +1276,11 @@
     normed_own, normed_other = halves(grad_normed)
     grad_attn_in, grad_attn_gain = attn_pull(normed_own + f32(hops.send(low(normed_other), dc=1)))
     grad1 = grad2 + grad_attn_in
-    grad0, grad_first_gain, grad_up_first, grad_down_first = ffn_back(
-        grad1, saved_first, up_first, down_first
-    )
-    grad_input = turn_out(low(grad0))
-
-    attn_part = jnp.concatenate(
-        [by_place(part, 1) for part in (grad_query_w, grad_key_w, grad_value_w, grad_place_w)],
-        axis=3,
-    )
+    grad0, grad_out1, grad_before1, grad_first_gain = ffn_bwd(
+        frames_own, first_gain[None], grad1, first_slope, up_first, down_first, jnp.bfloat16
+    )
+    grad_input = turn_out(grad0)
+
     spread = jnp.zeros((2, 4, 2, band), jnp.float32)
     spread = lax.dynamic_update_slice(
         spread, grad_biases[:2].reshape(2, 4, 1, band), (0, 0, core, 0)
@@ -1080,15 +1288,19 @@
     gains = (
         grad_conv_gain,
         grad_middle_gain,
-        grad_second_gain,
+        grad_second_gain[0],
         grad_final_gain,
-        grad_first_gain,
+        grad_first_gain[0],
         grad_attn_gain,
     )
     small = jnp.concatenate([jnp.stack(gains), spread, grad_kernel])
     small = jnp.pad(small, ((0, -small.shape[0] % 8), (0, 0)))
     sum_up_first, sum_down_first, attn_sums, small = reduce_all(
-        layers, 2, [(grad_up_first, 2), (grad_down_first, 2), (attn_part, 1)], small, 2
+        layers,
+        attn_part,
+        [(grad_before1, first_low), (first_act, grad_out1)],
+        small,
+        2,
     )
 
     def owned(sums, start, count):

time: 862 us -> 806 us (0.935)
  matrix products: 163 us -> 59.7 us
  Pallas kernels: 442 us -> 519 us
  waiting for transfers between devices: 49.2 us -> 18.6 us
    pallas_call x3 -> x7, Pallas kernels: 302 us -> 424 us  [the longest x1 137 us: attend_bwd(): pl.pallas_call(partial(attend_bwd_sum_kernel, layers, shared, count, pair...]
    dot_general x11 -> x7, matrix products: 64.1 us -> 17.2 us  [mult_trans(): lax.dot_general(first_mat, second_mat, (((1,), (1,)), ((), ())), preferre...]
    pallas_call x1, Pallas kernels: 140 us -> 95.6 us  [gather_all(): pl.pallas_call(partial(gather_kernel, layers, count), in_specs=[pl.BlockS...]
    all_gather x3 -> x0, waiting for transfers between devices: 40 us -> none  [the longest x2 40 us: per_chip(): lax.all_gather(shard, ('z', 'core', 'y', 'x'), axis=0, tiled=True)]
    dot_general x10 -> x6, matrix products: 46.5 us -> 12.7 us  [mult_plain(): return jnp.dot(first_mat, second_mat, preferred_element_type=jnp.float32)]
    dot_general x11 -> x9, matrix products: 52.7 us -> 29.8 us  [mult_rows(): lax.dot_general(first_mat, second_mat, (((0,), (0,)), ((), ())), preferre...]
    unnamed x284 -> x228, local copies, waits for them, and re-layouts: 28.1 us -> 31.1 us
  transfers between devices with their start and end apart: 20 -> 18, of which waited for: 3 -> 3; matrix products, arithmetic and copies ran while one was open for 19% -> 14% of each run, Pallas kernels for 21% -> 28%
where the time goes in v4:
time: 806 us; the launch traced here: 793 us
  Pallas kernels  519 us (64%)
  other arithmetic  100 us (12%)
  local copies, waits for them, and re-layouts  61.5 us (8%)
  matrix products  59.7 us (7%)
  waiting for transfers between devices  18.6 us (2%)
  starting transfers between devices  17.5 us (2%)
  between operations  15.9 us (2%)
    pallas_call x1, Pallas kernels, attend_bwd(): pl.pallas_call(partial(attend_bwd_sum_kernel, layers, shared, count, pair...  137 us
    pallas_call x1, Pallas kernels, reduce_all(): pl.pallas_call(partial(reduce_kernel, layers), in_specs=[near] * 6, out_s...  122 us
    pallas_call x1, Pallas kernels, gather_all(): pl.pallas_call(partial(gather_kernel, layers, count), in_specs=[pl.BlockS...  95.6 us
    pallas_call x1, Pallas kernels, attend_fwd(): pl.pallas_call(partial(attend_fwd_gather_kernel, layers, count, blocks, s...  90.6 us
    pallas_call x2, Pallas kernels, ffn_bwd(): pl.pallas_call(ffn_bwd_kernel, grid=(total // FF_BLOCK,), in_specs=[still...  38.9 us
    pallas_call x2, Pallas kernels, ffn_fwd(): pl.pallas_call(ffn_fwd_kernel, grid=(total // FF_BLOCK,), in_specs=[still...  35 us
    unnamed x228, local copies, waits for them, and re-layouts  31.1 us
    dot_general x9, matrix products, mult_rows(): lax.dot_general(first_mat, second_mat, (((0,), (0,)), ((), ())), preferre...  29.8 us
  transfers between devices with their start and end apart: 18, of which 3 were waited for; matrix products, arithmetic and copies ran while one was open for 14% of the time, Pallas kernels for 28%

profile of v4, /device:TPU:8, one launch (start us, length us, event | category | flops | bytes accessed | tf_op | source)
XLA Modules:
  0.0 792.5 jit_solution(17299395534766231368)
XLA Ops:
  7.3 2.4 dynamic-slice_bitcast_fusion.3
  9.7 5.3 collective-permute-start
  15.0 1.5 collective-permute-start.1
  21.2 95.6 %gather_all.1 = (bf16[4,2,2,2,128,1024]{5,4,3,2,1,0:T(8,128)(2,1)}, bf16[4,2,2,2,128,1024]{5,4,3,2,1,0:T(8,128)(2,1)}, bf16[2,2,2,272,1024]{4,3,2,1,0:T(8,128)(2,1)}) custom-call(bf16[128,1024]{1,0:T(8,128)(2,1)} %refs_0_.1, bf16[128,1024]{1,0:T(8,128)(2,1)} %refs_1_.1, bf16[272,1024]{1,0:T(8,128)(2,1)} %copy-done.53), custom_call_target="tpu_custom_call" | custom-call | bytes 314572800 | tf_op jit(solution)/shard_map/gather_all/pallas_call | solution.py:572
  119.1 3.8 fusion.168
  124.0 2.3 copy.99
  134.4 17.6 %ffn_fwd.2 = (f32[512,1024]{1,0:T(8,128)}, bf16[512,1024]{1,0:T(8,128)(2,1)}, bf16[512,4096]{1,0:T(8,128)(2,1)}, bf16[512,4096]{1,0:T(8,128)(2,1)}) custom-call(bf16[512,1024]{1,0:T(8,128)(2,1)} %pad_maximum_fusion.17.x_ref, bf16[1,1024]{1,0:T(2,128)(2,1)} %broadcast_in_dim.22.gain_ref, bf16[4096,1024]{1,0:T(8,128)(2,1)} %bitcast.369, ...), custom_call_target="tpu_custom_call" | custom-call | flops 8589934592 | bytes 25165824 | tf_op jit(solution)/shard_map/ffn_fwd/pallas_call | solution.py:929
  151.9 1.9 reduce_sum.507
  155.6 1.5 subtract_convert_fusion
  157.1 3.8 convolution_convert_fusion.3.refs_4_.refs_3_
  162.8 2.3 convolution_convert_fusion.12.refs_1_.refs_0_
  165.1 2.3 convolution_convert_fusion.11.refs_2_.refs_1_
  167.3 2.3 convolution_convert_fusion.10.refs_3_.refs_2_
  169.6 2.5 all-gather.3.cloned.1.call-done
  172.2 90.6 %attend_fwd.1 = (bf16[1024,512]{1,0:T(8,128)(2,1)}, bf16[8,1024,1024]{2,1,0:T(8,128)(2,1)}, bf16[4,2,2,2,128,1024]{5,4,3,2,1,0:T(8,128)(2,1)}, bf16[4,2,2,2,128,1024]{5,4,3,2,1,0:T(8,128)(2,1)}) custom-call(s32[1]{0:T(128)} %dynamic_slice.62.refs_0_, bf16[1024,512]{1,0:T(8,128)(2,1)} %convolution_convert_fusion.12.refs_1_.refs_0_, ...), custom_call_target="tpu_custom_call" | custom-call | flops 40000000000 | bytes 20971520 | tf_op jit(solution)/shard_map/attend_fwd/pallas_call | solution.py:279
  262.8 1.9 constant_dynamic-slice_fusion.2
  267.3 5.3 collective-permute-start.9
  278.0 4.1 select_bitcast_fusion.1
  282.1 1.8 pad_maximum_fusion.5
  285.3 1.4 fusion.176
  287.0 2.4 fusion.160
  290.1 1.4 copy-done.7
  291.6 2.7 broadcast_select_fusion.9
  294.3 1.3 copy.87
  295.7 10.2 %fusion.166 = (f32[512]{0:T(512)S(1)}, f32[512,1024]{1,0:T(8,128)S(1)}) fusion(f32[1024]{0:T(1024)S(1)} %bitcast.280, bf16[15,1024]{1,0:T(8,128)(2,1)S(1)} %get-tuple-element.239, bf16[512,1024]{1,0:T(8,128)(2,1)S(1)} %multiply_convert_fusion.4, f32[1024]{0:T(1024)S(1)} %bitcast.278, f32[1024]{0:T(1024)S(1)} %bitcast.276, f32[1024]{0:T(1024)S(1)} %bitcast.274, ...), kind=kLoop, calls=%fused_computation.459 | loop fusion | flops 95944192 | bytes 3336192 | tf_op jit(solution)/shard_map/jvp()/reduce_sum | solution.py:40
  306.3 2.9 convolution_add_fusion.x_ref
  309.2 17.4 %ffn_fwd.3 = (f32[512,1024]{1,0:T(8,128)}, bf16[512,1024]{1,0:T(8,128)(2,1)}, bf16[512,4096]{1,0:T(8,128)(2,1)}, bf16[512,4096]{1,0:T(8,128)(2,1)}) custom-call(f32[512,1024]{1,0:T(8,128)} %convolution_add_fusion.x_ref, bf16[1,1024]{1,0:T(2,128)(2,1)} %broadcast_in_dim.23.gain_ref, bf16[4096,1024]{1,0:T(8,128)(2,1)} %bitcast.374, bf16[4096,1024]{1,0:T(8,128)(2,1)} %bitcast.376), custom_call_target="tpu_custom_call" | custom-call | flops 8589934592 | bytes 25165824 | tf_op jit(solution)/shard_map/ffn_fwd/pallas_call | solution.py:929
  326.6 1.9 reduce_sum.513
  329.8 1.4 fusion.35
  331.2 1.8 fusion.165
  333.1 1.5 broadcast_add_fusion.g_ref
  334.6 19.6 %ffn_bwd.2 = (f32[512,1024]{1,0:T(8,128)}, bf16[512,1024]{1,0:T(8,128)(2,1)}, bf16[512,4096]{1,0:T(8,128)(2,1)}, f32[1,1024]{1,0:T(1,128)}) custom-call(f32[512,1024]{1,0:T(8,128)} %convolution_add_fusion.x_ref, bf16[1,1024]{1,0:T(2,128)(2,1)} %broadcast_in_dim.23.gain_ref, f32[512,1024]{1,0:T(8,128)} %broadcast_add_fusion.g_ref, ...), custom_call_target="tpu_custom_call" | custom-call | flops 8589934592 | bytes 25165824 | tf_op jit(solution)/shard_map/ffn_bwd/pallas_call | solution.py:975
  354.2 4.3 multiply_reduce_fusion.1
  359.2 8.1 %fusion.82 = (f32[1024]{0:T(1024)}, f32[1024]{0:T(1024)}, f32[1024]{0:T(1024)}, f32[1024]{0:T(1024)}, f32[1024]{0:T(1024)}, /*index=5*/f32[1024]{0:T(1024)}, f32...) fusion(bf16[15,1024]{1,0:T(8,128)(2,1)S(1)} %get-tuple-element.239, ...), kind=kLoop, calls=%fused_computation.222 | loop fusion | flops 29875200 | bytes 4263936 | tf_op jit(solution)/shard_map/reduce_sum | solution.py:1214
  367.4 7.0 convolution_convert_fusion.1
  374.4 6.8 convolution_convert_fusion
  381.2 1.6 convolution_convert_fusion.4
  382.9 1.5 copy.126
  384.4 1.4 copy-done.8
  385.8 16.0 %multiply_convert_fusion.1 = (bf16[512,1024]{1,0:T(8,128)(2,1)S(1)}, f32[512,1024]{1,0:T(8,128)S(1)}) fusion(f32[512,2048]{1,0:T(8,128)S(1)} %copy-done.8, f32[512]{0:T(512)S(1)} %fusion.149, f32[1024]{0:T(1024)S(1)} %bitcast.283, bf16[15,1024]{1,0:T(8,128)(2,1)S(1)} %get-tuple-element.237, bf16[512,1024]{1,0:T(8,128)(2,1)S(1)} %get-tuple-element.143, ...), kind=kLoop, calls=%fused_computation.244 | loop fusion | flops 98566144 | bytes 6481920 | tf_op jit(solution)/shard_map/convert.7
  404.7 3.3 multiply_reduce_fusion.2
  407.9 4.6 convolution_convert_fusion.2
  413.6 1.3 copy-done.13
  415.6 1.3 convolution_convert_fusion.9
  417.7 1.5 fusion.171
  424.8 1.3 copy-done.19
  426.1 4.0 pad_maximum_fusion
  431.2 136.5 %attend_bwd.1 = (bf16[1024,512]{1,0:T(8,128)(2,1)}, bf16[1024,512]{1,0:T(8,128)(2,1)}, bf16[1024,512]{1,0:T(8,128)(2,1)}, bf16[2048,512]{1,0:T(8,128)(2,1)}, f32...) custom-call(bf16[1024,512]{1,0:T(8,128)(2,1)} %convolution_convert_fusion.12.refs_, ...), custom_call_target="tpu_custom_call" | custom-call | flops 99999997952 | bytes 41943040 | tf_op jit(solution)/shard_map/attend_bwd/pallas_call | solution.py:378
  567.8 4.7 fusion.87
  576.4 2.2 pad_maximum_fusion.2
  580.9 2.5 fusion.81
  583.5 2.7 fusion.66
  591.5 2.5 collective-permute-start.13
  594.0 1.9 fusion.65
  596.0 8.3 %collective-permute-done.8 = bf16[256,1024]{1,0:T(8,128)(2,1)S(1)} collective-permute-done((bf16[256,1024]{1,0:T(8,128)(2,1)S(1)}, bf16[256,1024]{1,0:T(8,128)(2,1)S(1)}, u32[]{:S(2)}, u32[]{:S(2)}) %collective-permute-start.8) | collective-permute-done | bytes 524320 | tf_op jit(solution)/shard_map/ppermute | solution.py:1017
  608.4 3.0 multiply_reduce_fusion
  613.0 1.6 add_add_fusion.5.g_ref
  614.6 19.4 %ffn_bwd.3 = (bf16[512,1024]{1,0:T(8,128)(2,1)}, bf16[512,1024]{1,0:T(8,128)(2,1)}, bf16[512,4096]{1,0:T(8,128)(2,1)}, f32[1,1024]{1,0:T(1,128)}) custom-call(bf16[512,1024]{1,0:T(8,128)(2,1)} %pad_maximum_fusion.17.x_ref, bf16[1,1024]{1,0:T(2,128)(2,1)} %broadcast_in_dim.22.gain_ref, f32[512,1024]{1,0:T(8,128)} %add_add_fusion.5.g_ref, ...), custom_call_target="tpu_custom_call" | custom-call | flops 8589934592 | bytes 25165824 | tf_op jit(solution)/shard_map/ffn_bwd/pallas_call | solution.py:975
  637.4 1.6 bitcast_convert_fusion
  640.2 7.7 collective-permute-done.15
  649.0 122.4 %reduce_all.1 = (f32[128,1024]{1,0:T(8,128)}, f32[128,1024]{1,0:T(8,128)}, bf16[2,4,128,1024]{3,2,1,0:T(8,128)(2,1)}, f32[40,1024]{1,0:T(8,128)}) custom-call(bf16[4,128,1024]{2,1,0:T(8,128)(2,1)} %bitcast.373, bf16[512,4096]{1,0:T(8,128)(2,1)} %get-tuple-element.90.left_a, bf16[512,1024]{1,0:T(8,128)(2,1)} %get-tuple-element.91.right_a, ...), custom_call_target="tpu_custom_call" | custom-call | flops 8000000000 | bytes 314572800 | tf_op jit(solution)/shard_map/reduce_all/pallas_call | solution.py:850
  771.5 1.6 fusion.172
  773.8 1.6 slice.697
  775.4 1.7 fusion.170
  (358 shorter events, 75.8 us)
Async XLA Ops:
  7.2 13.2 %copy-start = (bf16[512,1024]{1,0:T(8,128)(2,1)S(1)}, bf16[512,1024]{1,0:T(8,128)(2,1)}, u32[]{:S(2)}) copy-start(bf16[512,1024]{1,0:T(8,128)(2,1)} %param.40) | copy-start | bytes 3145732
  7.2 9.3 %copy-start.94 = (s32[2]{0:T(128)S(1)}, s32[2]{0:T(128)}, u32[]{:S(2)}) copy-start(s32[2]{0:T(128)} %param.25) | copy-start | bytes 28
  7.2 9.3 %copy-start.95 = (bf16[256]{0:T(256)(128)(2,1)S(1)}, bf16[256]{0:T(256)(128)(2,1)}, u32[]{:S(2)}) copy-start(bf16[256]{0:T(256)(128)(2,1)} %param.38) | copy-start | bytes 1540
  7.2 9.3 %copy-start.96 = (bf16[256]{0:T(256)(128)(2,1)S(1)}, bf16[256]{0:T(256)(128)(2,1)}, u32[]{:S(2)}) copy-start(bf16[256]{0:T(256)(128)(2,1)} %param.37) | copy-start | bytes 1540
  7.2 164.9 %all-gather.3.cloned.1.call-start = ((), (), s32[]{:S(2)}) async-start(), calls=%async_computation.1 | async-start | bytes 5242880 | tf_op jit(solution)/shard_map/all_gather | solution.py:1127
  7.3 13.1 %copy-start.63 = (bf16[256,1024]{1,0:T(8,128)(2,1)S(1)}, bf16[256,1024]{1,0:T(8,128)(2,1)}, u32[]{:S(2)}) copy-start(bf16[256,1024]{1,0:T(8,128)(2,1)} %param.43) | copy-start | bytes 1572868
  7.3 13.1 %copy-start.64 = (bf16[256,1024]{1,0:T(8,128)(2,1)S(1)}, bf16[256,1024]{1,0:T(8,128)(2,1)}, u32[]{:S(2)}) copy-start(bf16[256,1024]{1,0:T(8,128)(2,1)} %param.35) | copy-start | bytes 1572868
  9.7 122.4 %collective-permute-start = (bf16[256,1024]{1,0:T(8,128)(2,1)}, bf16[256,1024]{1,0:T(8,128)(2,1)}, u32[]{:S(2)}, u32[]{:S(2)}) collective-permute-start(bf16[256,1024]{1,0:T(8,128)(2,1)} %get-tuple-element.195), channel_id=1, source_target_pairs={{0,0},{1,1},{2,4},{3,5},{4,2},{5,3},{6,6},{7,7},{8,8},{9,9},{10,12... | collective-permute-start | bytes 1572872 | tf_op jit(solution)/shard_map/ppermute | solution.py:1017
  15.0 117.0 %collective-permute-start.1 = (bf16[256,1024]{1,0:T(8,128)(2,1)}, bf16[256,1024]{1,0:T(8,128)(2,1)}, u32[]{:S(2)}, u32[]{:S(2)}) collective-permute-start(bf16[256,1024]{1,0:T(8,128)(2,1)} %get-tuple-element.196), channel_id=1, source_target_pairs={{0,1},{1,0},{2,5},{3,4},{4,3},{5,2},{6,7},{7,6},{8,9},{9,8},{10,13... | collective-permute-start | bytes 1572872 | tf_op jit(solution)/shard_map/ppermute | solution.py:1017
  16.5 144.4 %collective-permute-start.2 = (s32[2]{0:T(128)S(1)}, s32[2]{0:T(128)}, u32[]{:S(2)}, u32[]{:S(2)}) collective-permute-start(s32[2]{0:T(128)S(1)} %copy-done.94), channel_id=1, source_target_pairs={{0,4},{1,5},{2,6},{3,7},{4,0},{5,1},{6,2},{7,3},{8,12},{9,13},{10,... | collective-permute-start | bytes 32 | tf_op jit(solution)/shard_map/ppermute | solution.py:1008
  21.2 97.5 %copy-start.93 = (s32[2,256]{1,0:T(2,128)S(1)}, s32[2,256]{1,0:T(2,128)}, u32[]{:S(2)}) copy-start(s32[2,256]{1,0:T(2,128)} %param.26) | copy-start | bytes 6148
  117.9 531.1 %reduce-scatter.4.cloned.1.call-start = ((), (), s32[]{:S(2)}) async-start(), calls=%async_computation.2 | async-start | bytes 5242880
  119.1 4.3 copy-start.87
  126.3 35.3 %copy-start.65 = (f32[1024]{0:T(1024)}, f32[1024]{0:T(1024)S(1)}, u32[]{:S(2)}) copy-start(f32[1024]{0:T(1024)S(1)} %convert_element_type.398) | copy-start | bytes 12292
  127.4 39.9 %copy-start.22 = (bf16[2,4,64,1024]{3,2,0,1:T(8,128)(2,1)}, bf16[2,4,64,1024]{3,2,0,1:T(8,128)(2,1)S(1)}, u32[]{:S(2)}) copy-start(bf16[2,4,64,1024]{3,2,0,1:T(8,128)(2,1)S(1)} %copy.101) | copy-start | bytes 3145732
  154.2 7.4 copy-start.67
  155.1 6.5 copy-start.69
  155.4 6.1 collective-permute-start.3
  157.1 3.9 copy-start.31
  157.1 3.9 copy-start.33
  162.2 5.1 copy-start.49
  162.2 5.1 copy-start.51
  172.1 105.8 %collective-permute-start.5 = (bf16[4,512,1024]{2,1,0:T(8,128)(2,1)}, bf16[4,512,1024]{2,1,0:T(8,128)(2,1)}, u32[]{:S(2)}, u32[]{:S(2)}) collective-permute-start(bf16[4,512,1024]{2,1,0:T(8,128)(2,1)} %bitcast.229), channel_id=1, source_target_pairs={{0,4},{1,5},{2,6},{3,7},{4,0},{5,1},{6,2},{7,3},{8,12},{9,13},{10,... | collective-permute-start | bytes 12582920 | tf_op jit(solution)/shard_map/ppermute | solution.py:1008
  172.1 92.6 %copy-start.62 = (bf16[31,1024]{1,0:T(8,128)(2,1)S(1)}, bf16[31,1024]{1,0:T(8,128)(2,1)}, u32[]{:S(2)}) copy-start(bf16[31,1024]{1,0:T(8,128)(2,1)} %param.41) | copy-start | bytes 190468
  172.1 92.6 %copy-start.89 = (bf16[1024]{0:T(1024)(128)(2,1)S(1)}, bf16[1024]{0:T(1024)(128)(2,1)}, u32[]{:S(2)}) copy-start(bf16[1024]{0:T(1024)(128)(2,1)} %param.39) | copy-start | bytes 6148
  172.1 92.6 %copy-start.90 = (bf16[1024]{0:T(1024)(128)(2,1)S(1)}, bf16[1024]{0:T(1024)(128)(2,1)}, u32[]{:S(2)}) copy-start(bf16[1024]{0:T(1024)(128)(2,1)} %param.42) | copy-start | bytes 6148
  172.2 92.6 %copy-start.91 = (bf16[1024]{0:T(1024)(128)(2,1)S(1)}, bf16[1024]{0:T(1024)(128)(2,1)}, u32[]{:S(2)}) copy-start(bf16[1024]{0:T(1024)(128)(2,1)} %param.44) | copy-start | bytes 6148
  172.2 93.2 %copy-start.92 = (bf16[1024]{0:T(1024)(128)(2,1)S(1)}, bf16[1024]{0:T(1024)(128)(2,1)}, u32[]{:S(2)}) copy-start(bf16[1024]{0:T(1024)(128)(2,1)} %param.47) | copy-start | bytes 6148
  172.2 94.0 %copy-start.27 = (bf16[2,256,1024]{2,1,0:T(8,128)(2,1)S(1)}, bf16[2,256,1024]{2,1,0:T(8,128)(2,1)}, u32[]{:S(2)}) copy-start(bf16[2,256,1024]{2,1,0:T(8,128)(2,1)} %multiply_convert_fusion.7) | copy-start | bytes 3145732
  264.7 7.9 collective-permute-start.4
  265.4 7.2 copy-start.48
  267.3 24.3 %collective-permute-start.9 = (bf16[256,1024]{1,0:T(8,128)(2,1)}, bf16[256,1024]{1,0:T(8,128)(2,1)}, u32[]{:S(2)}, u32[]{:S(2)}) collective-permute-start(bf16[256,1024]{1,0:T(8,128)(2,1)} %get-tuple-element.187), channel_id=1, source_target_pairs={{0,0},{1,1},{2,4},{3,5},{4,2},{5,3},{6,6},{7,7},{8,8},{9,9},{10,12... | collective-permute-start | bytes 1572872 | tf_op jit(solution)/shard_map/ppermute | solution.py:1017
  272.6 19.0 %collective-permute-start.10 = (bf16[256,1024]{1,0:T(8,128)(2,1)}, bf16[256,1024]{1,0:T(8,128)(2,1)}, u32[]{:S(2)}, u32[]{:S(2)}) collective-permute-start(bf16[256,1024]{1,0:T(8,128)(2,1)} %get-tuple-element.188), channel_id=1, source_target_pairs={{0,1},{1,0},{2,5},{3,4},{4,3},{5,2},{6,7},{7,6},{8,9},{9,8},{10,13... | collective-permute-start | bytes 1572872 | tf_op jit(solution)/shard_map/ppermute | solution.py:1017
  278.0 6.4 copy-start.29
  291.5 67.7 %copy-start.4 = (bf16[512,1024]{1,0:T(8,128)(2,1)}, bf16[512,1024]{1,0:T(8,128)(2,1)S(1)}, u32[]{:S(2)}) copy-start(bf16[512,1024]{1,0:T(8,128)(2,1)S(1)} %multiply_convert_fusion.4) | copy-start | bytes 3145732
  291.5 4.1 collective-permute-start.6
  295.6 10.6 %copy-start.54 = (bf16[15,1024]{1,0:T(8,128)(2,1)}, bf16[15,1024]{1,0:T(8,128)(2,1)S(1)}, u32[]{:S(2)}) copy-start(bf16[15,1024]{1,0:T(8,128)(2,1)S(1)} %get-tuple-element.238) | copy-start | bytes 92164
  295.6 63.5 %copy-start.56 = (bf16[15,1024]{1,0:T(8,128)(2,1)}, bf16[15,1024]{1,0:T(8,128)(2,1)S(1)}, u32[]{:S(2)}) copy-start(bf16[15,1024]{1,0:T(8,128)(2,1)S(1)} %get-tuple-element.239) | copy-start | bytes 92164
  295.6 10.6 %copy-start.17 = (f32[512,1024]{1,0:T(8,128)S(1)}, f32[512,1024]{1,0:T(8,128)}, u32[]{:S(2)}) copy-start(f32[512,1024]{1,0:T(8,128)} %copy-done.16) | copy-start | bytes 6291460
  295.7 10.6 %copy-start.38 = (bf16[4,2,128,1024]{3,2,1,0:T(8,128)(2,1)S(1)}, bf16[4,2,128,1024]{3,2,1,0:T(8,128)(2,1)}, u32[]{:S(2)}) copy-start(bf16[4,2,128,1024]{3,2,1,0:T(8,128)(2,1)} %get-tuple-element.156) | copy-start | bytes 6291460
  334.6 19.6 %copy-start.12 = (f32[512,1024]{1,0:T(8,128)S(1)}, f32[512,1024]{1,0:T(8,128)}, u32[]{:S(2)}) copy-start(f32[512,1024]{1,0:T(8,128)} %copy-done.11) | copy-start | bytes 6291460
  334.6 19.6 %copy-start.39 = (bf16[4,2,128,1024]{3,2,1,0:T(8,128)(2,1)S(1)}, bf16[4,2,128,1024]{3,2,1,0:T(8,128)(2,1)}, u32[]{:S(2)}) copy-start(bf16[4,2,128,1024]{3,2,1,0:T(8,128)(2,1)} %get-tuple-element.156) | copy-start | bytes 6291460
  358.4 8.9 %copy-start.104 = (bf16[512,1024]{1,0:T(8,128)(2,1)S(1)}, bf16[512,1024]{1,0:T(8,128)(2,1)}, u32[]{:S(2)}) copy-start(bf16[512,1024]{1,0:T(8,128)(2,1)} %get-tuple-element.79) | copy-start | bytes 3145732
  359.2 8.2 %copy-start.101 = (bf16[512,4096]{1,0:T(8,128)(2,1)S(1)}, bf16[512,4096]{1,0:T(8,128)(2,1)}, u32[]{:S(2)}) copy-start(bf16[512,4096]{1,0:T(8,128)(2,1)} %get-tuple-element.78) | copy-start | bytes 12582916
  367.3 17.0 %collective-permute-start.11 = (bf16[16,1024]{1,0:T(8,128)(2,1)S(1)}, bf16[16,1024]{1,0:T(8,128)(2,1)S(1)}, u32[]{:S(2)}, u32[]{:S(2)}) collective-permute-start(bf16[16,1024]{1,0:T(8,128)(2,1)S(1)} %slice_select_fusion.2), channel_id=1, source_target_pairs={{0,4},{1,5},{2,6},{3,7},{4,0},{5,1},{6,2},{7,3},{8,12},{9,13},{10,... | collective-permute-start | bytes 98312 | tf_op jit(solution)/shard_map/ppermute | solution.py:1008
  367.4 7.0 copy-start.102
  367.4 7.0 copy-start.103
  374.4 6.8 copy-start.34
  419.9 10.2 %collective-permute-start.12 = (bf16[512,512]{1,0:T(8,128)(2,1)S(1)}, bf16[512,512]{1,0:T(8,128)(2,1)S(1)}, u32[]{:S(2)}, u32[]{:S(2)}) collective-permute-start(bf16[512,512]{1,0:T(8,128)(2,1)S(1)} %bitcast.257), channel_id=1, source_target_pairs={{0,4},{1,5},{2,6},{3,7},{4,0},{5,1},{6,2},{7,3},{8,12},{9,13},{10,... | collective-permute-start | bytes 1572872 | tf_op jit(solution)/shard_map/ppermute | solution.py:1008
  431.2 136.5 %copy-start.32 = (bf16[64,32,512]{2,1,0:T(8,128)(2,1)S(1)}, bf16[64,32,512]{2,1,0:T(8,128)(2,1)}, u32[]{:S(2)}) copy-start(bf16[64,32,512]{2,1,0:T(8,128)(2,1)} %copy-done.31) | copy-start | bytes 6291460
  567.8 4.8 copy-start.40
  567.8 4.8 copy-start.50
  567.8 4.8 copy-start.52
  579.9 16.1 %collective-permute-start.7 = (bf16[256,1024]{1,0:T(8,128)(2,1)S(1)}, bf16[256,1024]{1,0:T(8,128)(2,1)S(1)}, u32[]{:S(2)}, u32[]{:S(2)}) collective-permute-start(bf16[256,1024]{1,0:T(8,128)(2,1)S(1)} %get-tuple-element.191), channel_id=1, source_target_pairs={{0,0},{1,1},{2,4},{3,5},{4,2},{5,3},{6,6},{7,7},{8,8},{9,9},{10,12... | collective-permute-start | bytes 1572872 | tf_op jit(solution)/shard_map/ppermute | solution.py:1017
  580.6 5.6 copy-start.45
  580.6 5.6 copy-start.100
  580.6 23.7 %collective-permute-start.8 = (bf16[256,1024]{1,0:T(8,128)(2,1)S(1)}, bf16[256,1024]{1,0:T(8,128)(2,1)S(1)}, u32[]{:S(2)}, u32[]{:S(2)}) collective-permute-start(bf16[256,1024]{1,0:T(8,128)(2,1)S(1)} %get-tuple-element.192), channel_id=1, source_target_pairs={{0,1},{1,0},{2,5},{3,4},{4,3},{5,2},{6,7},{7,6},{8,9},{9,8},{10,13... | collective-permute-start | bytes 1572872 | tf_op jit(solution)/shard_map/ppermute | solution.py:1017
  590.2 5.7 copy-start.9
  591.5 16.1 %collective-permute-start.13 = (bf16[512,1024]{1,0:T(8,128)(2,1)}, bf16[512,1024]{1,0:T(8,128)(2,1)S(1)}, u32[]{:S(2)}, u32[]{:S(2)}) collective-permute-start(bf16[512,1024]{1,0:T(8,128)(2,1)} %dynamic-slice_convert_fusion), channel_id=1, source_target_pairs={{0,4},{1,5},{2,6},{3,7},{4,0},{5,1},{6,2},{7,3},{8,12},{9,13},{10,... | collective-permute-start | bytes 3145736 | tf_op jit(solution)/shard_map/ppermute | solution.py:1008
  596.0 10.3 %copy-start.35 = (bf16[2,4,128,1024]{3,2,1,0:T(8,128)(2,1)S(1)}, bf16[2,4,128,1024]{3,2,1,0:T(8,128)(2,1)}, u32[]{:S(2)}) copy-start(bf16[2,4,128,1024]{3,2,1,0:T(8,128)(2,1)} %get-tuple-element.101) | copy-start | bytes 6291460
  635.2 5.0 collective-permute-start.14
  636.1 11.8 %collective-permute-start.15 = (bf16[256,1024]{1,0:T(8,128)(2,1)S(1)}, bf16[256,1024]{1,0:T(8,128)(2,1)S(1)}, u32[]{:S(2)}, u32[]{:S(2)}) collective-permute-start(bf16[256,1024]{1,0:T(8,128)(2,1)S(1)} %get-tuple-element.180), channel_id=1, source_target_pairs={{0,1},{1,0},{2,5},{3,4},{4,3},{5,2},{6,7},{7,6},{8,9},{9,8},{10,13... | collective-permute-start | bytes 1572872 | tf_op jit(solution)/shard_map/ppermute | solution.py:1017
  778.3 4.0 copy-start.61
  780.5 4.2 copy-start.58
  (59 other events, 137.1 us)
Sparse Core Ops, SparseCore 0:
  118.0 54.0 all-gather.2
  578.7 59.5 reduce-scatter.3

commit v5 on v4

--- a/solution.py
+++ b/solution.py
@@ -750,12 +750,12 @@
             copy.wait_recv()
         swapped.start()
 
-    lead = 2 if made else 0
-    handed_at = 5 if summed else layers - 1 + 5 + 2 + lead
-    turns = max(len(items) + 5 + lead, handed_at + 4)
+    lead, near, wide = (1, 1, 2) if made else (0, 2, 4)
+    handed_at = 5 if summed else layers - 1 + wide + 2 + lead
+    turns = max(len(items) + wide + lead, handed_at + 4)
 
     def step(turn_at):
-        actions = ((make, 0), (join_core, lead), (join_cross, lead + 3), (join_flat, lead + 5))
+        actions = ((make, 0), (join_core, lead), (join_cross, lead + near), (join_flat, lead + wide))
         for action, lag in actions:
             if 0 <= turn_at - lag < len(items):
                 action(items[turn_at - lag])
@@ -906,7 +906,7 @@
         y_ref[...] = values
 
     before = mult_trans(h_ref[...], up_ref[...])
-    squash = 1.0 / (1.0 + jnp.exp(-before))
+    squash = 0.5 + 0.5 * jnp.tanh(0.5 * before)
     active = before * squash
     slope_ref[...] = (squash + active * (1.0 - squash)).astype(jnp.bfloat16)
     active_low = active.astype(jnp.bfloat16)
@@ -1014,7 +1014,10 @@
                 for w in range(4):
                     to = (z * 2 + w // 2) * 4 + 2 * c + ((w % 2) ^ step)
                     pairs.append(((z * 2 + c) * 4 + w, to))
-        return lax.ppermute(block, ("z", "core", "y", "x"), pairs)
+        got = lax.ppermute(block, ("z", "core", "y", "x"), [pair for pair in pairs if pair[0] != pair[1]])
+        if step:
+            return got
+        return jnp.where(lax.axis_index("core") == lax.axis_index("y"), block, got)
 
 
 def relative_waves(length, channels):
@@ -1202,6 +1205,7 @@
     )
     grad_down_second = low(mult_rows(second_act, grad_out2))
     grad_up_second = low(mult_rows(grad_before2, second_low))
+    grad3, output = lax.optimization_barrier((grad3, output))
     grad_branch = low(grad3)
     grad_point = mult_rows(grad_branch, swished)
     grad_middle = mult_plain(grad_branch, full_point) * silu_slope(middle)

time: 806 us -> 791 us (0.981)
  Pallas kernels: 519 us -> 505 us
    ppermute x8, starting transfers between devices: 3.27 us -> 12.6 us  [send(): return lax.ppermute(block, ('z', 'core', 'y', 'x'), pairs)]
    unnamed x228 -> x218, local copies, waits for them, and re-layouts: 31.1 us -> 29.2 us
  transfers between devices with their start and end apart: 18 -> 18, of which waited for: 3 -> 2; matrix products, arithmetic and copies ran while one was open for 14% -> 15% of each run, Pallas kernels for 28% -> 18%
where the time goes in v5:
time: 791 us; the launch traced here: 785 us
  Pallas kernels  505 us (64%)
  other arithmetic  99.7 us (13%)
  local copies, waits for them, and re-layouts  67.4 us (9%)
  matrix products  58.7 us (7%)
  starting transfers between devices  25.5 us (3%)
  between operations  15.8 us (2%)
  waiting for transfers between devices  12.9 us (2%)
    pallas_call x1, Pallas kernels, attend_bwd(): pl.pallas_call(partial(attend_bwd_sum_kernel, layers, shared, count, pair...  132 us
    pallas_call x1, Pallas kernels, reduce_all(): pl.pallas_call(partial(reduce_kernel, layers), in_specs=[near] * 6, out_s...  118 us
    pallas_call x1, Pallas kernels, gather_all(): pl.pallas_call(partial(gather_kernel, layers, count), in_specs=[pl.BlockS...  94.6 us
    pallas_call x1, Pallas kernels, attend_fwd(): pl.pallas_call(partial(attend_fwd_gather_kernel, layers, count, blocks, s...  88.3 us
    pallas_call x2, Pallas kernels, ffn_bwd(): pl.pallas_call(ffn_bwd_kernel, grid=(total // FF_BLOCK,), in_specs=[still...  38.5 us
    pallas_call x2, Pallas kernels, ffn_fwd(): pl.pallas_call(ffn_fwd_kernel, grid=(total // FF_BLOCK,), in_specs=[still...  33.9 us
    dot_general x9, matrix products, mult_rows(): lax.dot_general(first_mat, second_mat, (((0,), (0,)), ((), ())), preferre...  30.2 us
    unnamed x218, local copies, waits for them, and re-layouts  29.2 us
  transfers between devices with their start and end apart: 18, of which 2 were waited for; matrix products, arithmetic and copies ran while one was open for 15% of the time, Pallas kernels for 18%

profile of v5, /device:TPU:8, one launch (start us, length us, event | category | flops | bytes accessed | tf_op | source)
XLA Modules:
  0.0 784.9 jit_solution(18188026205806543803)
XLA Ops:
  13.8 94.6 %gather_all.1 = (bf16[4,2,2,2,128,1024]{5,4,3,2,1,0:T(8,128)(2,1)}, bf16[4,2,2,2,128,1024]{5,4,3,2,1,0:T(8,128)(2,1)}, bf16[2,2,2,272,1024]{4,3,2,1,0:T(8,128)(2,1)}) custom-call(bf16[128,1024]{1,0:T(8,128)(2,1)} %refs_0_.1, bf16[128,1024]{1,0:T(8,128)(2,1)} %refs_1_.1, bf16[272,1024]{1,0:T(8,128)(2,1)} %copy-done.54), custom_call_target="tpu_custom_call" | custom-call | bytes 314572800 | tf_op jit(solution)/shard_map/gather_all/pallas_call | solution.py:572
  110.5 1.5 collective-permute-start
  112.0 1.5 collective-permute-start.1
  113.5 2.1 collective-permute-start.2
  116.8 4.6 fusion.168
  134.2 17.0 %ffn_fwd.2 = (f32[512,1024]{1,0:T(8,128)}, bf16[512,1024]{1,0:T(8,128)(2,1)}, bf16[512,4096]{1,0:T(8,128)(2,1)}, bf16[512,4096]{1,0:T(8,128)(2,1)}) custom-call(bf16[512,1024]{1,0:T(8,128)(2,1)} %pad_maximum_fusion.17.x_ref, bf16[1,1024]{1,0:T(2,128)(2,1)} %broadcast_in_dim.22.gain_ref, bf16[4096,1024]{1,0:T(8,128)(2,1)} %bitcast.369, ...), custom_call_target="tpu_custom_call" | custom-call | flops 8589934592 | bytes 25165824 | tf_op jit(solution)/shard_map/ffn_fwd/pallas_call | solution.py:929
  151.1 1.9 reduce_sum.507
  154.6 4.9 collective-permute-start.3
  159.5 1.5 subtract_convert_fusion
  161.0 3.9 convolution_convert_fusion.3.refs_4_.refs_3_
  166.2 2.3 convolution_convert_fusion.10.refs_3_.refs_2_
  168.5 2.3 convolution_convert_fusion.11.refs_2_.refs_1_
  170.7 2.3 convolution_convert_fusion.12.refs_1_.refs_0_
  173.6 88.3 %attend_fwd.1 = (bf16[1024,512]{1,0:T(8,128)(2,1)}, bf16[8,1024,1024]{2,1,0:T(8,128)(2,1)}, bf16[4,2,2,2,128,1024]{5,4,3,2,1,0:T(8,128)(2,1)}, bf16[4,2,2,2,128,1024]{5,4,3,2,1,0:T(8,128)(2,1)}) custom-call(s32[1]{0:T(128)} %dynamic_slice.62.refs_0_, bf16[1024,512]{1,0:T(8,128)(2,1)} %convolution_convert_fusion.12.refs_1_.refs_0_, ...), custom_call_target="tpu_custom_call" | custom-call | flops 40000000000 | bytes 20971520 | tf_op jit(solution)/shard_map/attend_fwd/pallas_call | solution.py:279
  261.9 1.9 constant_dynamic-slice_fusion.2
  266.3 1.5 collective-permute-start.7
  267.8 2.6 collective-permute-start.8
  275.7 4.1 select_bitcast_fusion.1
  279.9 1.8 pad_maximum_fusion.5
  283.1 1.4 fusion.176
  284.8 2.4 fusion.160
  287.9 1.4 copy-done.7
  289.3 2.3 collective-permute-start.6
  291.5 2.3 broadcast_select_fusion.15
  295.2 10.2 %fusion.166 = (f32[512]{0:T(512)S(1)}, f32[512,1024]{1,0:T(8,128)S(1)}) fusion(f32[1024]{0:T(1024)S(1)} %bitcast.280, bf16[15,1024]{1,0:T(8,128)(2,1)S(1)} %get-tuple-element.243, bf16[512,1024]{1,0:T(8,128)(2,1)S(1)} %multiply_convert_fusion.4, f32[1024]{0:T(1024)S(1)} %bitcast.278, f32[1024]{0:T(1024)S(1)} %bitcast.276, f32[1024]{0:T(1024)S(1)} %bitcast.274, ...), kind=kLoop, calls=%fused_computation.463 | loop fusion | flops 95944192 | bytes 3336192 | tf_op jit(solution)/shard_map/jvp()/reduce_sum | solution.py:40
  305.8 2.9 convolution_add_fusion.x_ref
  308.7 16.9 %ffn_fwd.3 = (f32[512,1024]{1,0:T(8,128)}, bf16[512,1024]{1,0:T(8,128)(2,1)}, bf16[512,4096]{1,0:T(8,128)(2,1)}, bf16[512,4096]{1,0:T(8,128)(2,1)}) custom-call(f32[512,1024]{1,0:T(8,128)} %convolution_add_fusion.x_ref, bf16[1,1024]{1,0:T(2,128)(2,1)} %broadcast_in_dim.23.gain_ref, bf16[4096,1024]{1,0:T(8,128)(2,1)} %bitcast.374, bf16[4096,1024]{1,0:T(8,128)(2,1)} %bitcast.376), custom_call_target="tpu_custom_call" | custom-call | flops 8589934592 | bytes 25165824 | tf_op jit(solution)/shard_map/ffn_fwd/pallas_call | solution.py:929
  325.6 1.9 reduce_sum.513
  328.8 1.4 fusion.35
  332.0 1.5 broadcast_add_fusion.g_ref
  333.5 19.5 %ffn_bwd.2 = (f32[512,1024]{1,0:T(8,128)}, bf16[512,1024]{1,0:T(8,128)(2,1)}, bf16[512,4096]{1,0:T(8,128)(2,1)}, f32[1,1024]{1,0:T(1,128)}) custom-call(f32[512,1024]{1,0:T(8,128)} %convolution_add_fusion.x_ref, bf16[1,1024]{1,0:T(2,128)(2,1)} %broadcast_in_dim.23.gain_ref, f32[512,1024]{1,0:T(8,128)} %broadcast_add_fusion.g_ref, ...), custom_call_target="tpu_custom_call" | custom-call | flops 8589934592 | bytes 25165824 | tf_op jit(solution)/shard_map/ffn_bwd/pallas_call | solution.py:975
  353.0 10.4 %convolution_convert_fusion = bf16[4096,1024]{1,0:T(8,128)(2,1)} fusion(bf16[512,4096]{1,0:T(8,128)(2,1)} %get-tuple-element.84, bf16[512,1024]{1,0:T(8,128)(2,1)} %get-tuple-element.85), kind=kOutput, calls=%fused_computation.35 | convolution fusion | flops 4299161600 | bytes 13631488 | tf_op jit(solution)/shard_map/dot_general | solution.py:62
  363.5 6.9 convolution_convert_fusion.1
  373.0 2.7 multiply_reduce_fusion.1
  376.4 8.1 %fusion.82 = (f32[1024]{0:T(1024)}, f32[1024]{0:T(1024)}, f32[1024]{0:T(1024)}, f32[1024]{0:T(1024)}, f32[1024]{0:T(1024)}, /*index=5*/f32[1024]{0:T(1024)}, f32...) fusion(bf16[15,1024]{1,0:T(8,128)(2,1)S(1)} %get-tuple-element.243, ...), kind=kLoop, calls=%fused_computation.222 | loop fusion | flops 29875200 | bytes 4263936 | tf_op jit(solution)/shard_map/reduce_sum | solution.py:1218
  384.6 2.7 collective-permute-start.11
  387.3 1.6 convolution_convert_fusion.4
  388.9 1.6 copy.126
  391.9 16.0 %multiply_convert_fusion.1 = (bf16[512,1024]{1,0:T(8,128)(2,1)S(1)}, f32[512,1024]{1,0:T(8,128)S(1)}) fusion(f32[512,2048]{1,0:T(8,128)S(1)} %copy-done.8, f32[512]{0:T(512)S(1)} %fusion.149, f32[1024]{0:T(1024)S(1)} %bitcast.283, bf16[15,1024]{1,0:T(8,128)(2,1)S(1)} %get-tuple-element.241, bf16[512,1024]{1,0:T(8,128)(2,1)S(1)} %get-tuple-element.147, ...), kind=kLoop, calls=%fused_computation.244 | loop fusion | flops 98566144 | bytes 6481920 | tf_op jit(solution)/shard_map/convert.7
  410.8 3.3 multiply_reduce_fusion.2
  414.0 2.5 convolution_convert_fusion.2
  419.8 1.5 copy.127
  421.3 2.5 copy.125
  425.9 1.5 fusion.171
  428.2 1.6 copy-done.13
  429.8 3.8 pad_maximum_fusion
  434.7 131.6 %attend_bwd.1 = (bf16[1024,512]{1,0:T(8,128)(2,1)}, bf16[1024,512]{1,0:T(8,128)(2,1)}, bf16[1024,512]{1,0:T(8,128)(2,1)}, bf16[2048,512]{1,0:T(8,128)(2,1)}, f32...) custom-call(bf16[1024,512]{1,0:T(8,128)(2,1)} %convolution_convert_fusion.12.refs_, ...), custom_call_target="tpu_custom_call" | custom-call | flops 99999997952 | bytes 41943040 | tf_op jit(solution)/shard_map/attend_bwd/pallas_call | solution.py:378
  566.3 2.6 convolution_convert_fusion.8
  572.6 2.3 fusion.87
  575.0 2.3 pad_maximum_fusion.2
  578.5 2.5 fusion.81
  581.0 2.7 fusion.66
  589.1 1.9 fusion.65
  593.2 1.5 fusion.169
  595.9 2.7 multiply_reduce_fusion
  600.6 1.6 add_add_fusion.5.g_ref
  602.2 19.0 %ffn_bwd.3 = (bf16[512,1024]{1,0:T(8,128)(2,1)}, bf16[512,1024]{1,0:T(8,128)(2,1)}, bf16[512,4096]{1,0:T(8,128)(2,1)}, f32[1,1024]{1,0:T(1,128)}) custom-call(bf16[512,1024]{1,0:T(8,128)(2,1)} %pad_maximum_fusion.17.x_ref, bf16[1,1024]{1,0:T(2,128)(2,1)} %broadcast_in_dim.22.gain_ref, f32[512,1024]{1,0:T(8,128)} %add_add_fusion.5.g_ref, ...), custom_call_target="tpu_custom_call" | custom-call | flops 8589934592 | bytes 25165824 | tf_op jit(solution)/shard_map/ffn_bwd/pallas_call | solution.py:975
  623.4 4.1 collective-permute-start.15
  628.7 1.6 bitcast_convert_fusion
  631.5 11.8 %collective-permute-done.15 = bf16[256,1024]{1,0:T(8,128)(2,1)} collective-permute-done((bf16[256,1024]{1,0:T(8,128)(2,1)S(1)}, bf16[256,1024]{1,0:T(8,128)(2,1)}, u32[]{:S(2)}, u32[]{:S(2)}) %collective-permute-start.15) | collective-permute-done | bytes 524320 | tf_op jit(solution)/shard_map/ppermute | solution.py:1017
  645.4 118.3 %reduce_all.1 = (f32[128,1024]{1,0:T(8,128)}, f32[128,1024]{1,0:T(8,128)}, bf16[2,4,128,1024]{3,2,1,0:T(8,128)(2,1)}, f32[40,1024]{1,0:T(8,128)}) custom-call(bf16[4,128,1024]{2,1,0:T(8,128)(2,1)} %bitcast.373, bf16[512,4096]{1,0:T(8,128)(2,1)} %get-tuple-element.94.left_a, bf16[512,1024]{1,0:T(8,128)(2,1)} %get-tuple-element.95.right_a, ...), custom_call_target="tpu_custom_call" | custom-call | flops 8000000000 | bytes 314572800 | tf_op jit(solution)/shard_map/reduce_all/pallas_call | solution.py:850
  763.7 1.6 slice.697
  766.1 1.7 fusion.172
  767.8 1.7 fusion.170
  (348 shorter events, 86.5 us)
Async XLA Ops:
  7.2 6.5 copy-start
  7.2 165.8 %all-gather.3.cloned.1.call-start = ((), (), s32[]{:S(2)}) async-start(), calls=%async_computation.1 | async-start | bytes 5242880 | tf_op jit(solution)/shard_map/all_gather | solution.py:1130
  13.8 95.7 %copy-start.48 = (bf16[2,256,1024]{2,1,0:T(8,128)(2,1)S(1)}, bf16[2,256,1024]{2,1,0:T(8,128)(2,1)}, u32[]{:S(2)}) copy-start(bf16[2,256,1024]{2,1,0:T(8,128)(2,1)} %param.24) | copy-start | bytes 3145732
  109.4 4.1 copy-start.93
  109.4 7.0 copy-start.92
  109.4 536.0 %reduce-scatter.4.cloned.1.call-start = ((), (), s32[]{:S(2)}) async-start(), calls=%async_computation.2 | async-start | bytes 5242880
  110.5 20.3 %collective-permute-start = (bf16[256,1024]{1,0:T(8,128)(2,1)}, bf16[256,1024]{1,0:T(8,128)(2,1)}, u32[]{:S(2)}, u32[]{:S(2)}) collective-permute-start(bf16[256,1024]{1,0:T(8,128)(2,1)} %get-tuple-element.199), channel_id=1, source_target_pairs={{2,4},{3,5},{4,2},{5,3},{10,12},{11,13},{12,10},{13,11},{18,20},{1... | collective-permute-start | bytes 1572872 | tf_op jit(solution)/shard_map/ppermute | solution.py:1017
  112.0 19.8 %collective-permute-start.1 = (bf16[256,1024]{1,0:T(8,128)(2,1)}, bf16[256,1024]{1,0:T(8,128)(2,1)}, u32[]{:S(2)}, u32[]{:S(2)}) collective-permute-start(bf16[256,1024]{1,0:T(8,128)(2,1)} %get-tuple-element.200), channel_id=1, source_target_pairs={{0,1},{1,0},{2,5},{3,4},{4,3},{5,2},{6,7},{7,6},{8,9},{9,8},{10,13... | collective-permute-start | bytes 1572872 | tf_op jit(solution)/shard_map/ppermute | solution.py:1017
  113.5 51.4 %collective-permute-start.2 = (s32[2]{0:T(128)S(1)}, s32[2]{0:T(128)}, u32[]{:S(2)}, u32[]{:S(2)}) collective-permute-start(s32[2]{0:T(128)S(1)} %copy-done.93), channel_id=1, source_target_pairs={{0,4},{1,5},{2,6},{3,7},{4,0},{5,1},{6,2},{7,3},{8,12},{9,13},{10,... | collective-permute-start | bytes 32 | tf_op jit(solution)/shard_map/ppermute | solution.py:1008
  116.8 5.1 copy-start.86
  116.8 5.7 copy-start.87
  122.5 43.0 %copy-start.64 = (f32[1024]{0:T(1024)}, f32[1024]{0:T(1024)S(1)}, u32[]{:S(2)}) copy-start(f32[1024]{0:T(1024)S(1)} %convert_element_type.398) | copy-start | bytes 12292
  123.8 42.4 %copy-start.23 = (bf16[2,4,64,1024]{3,2,0,1:T(8,128)(2,1)}, bf16[2,4,64,1024]{3,2,0,1:T(8,128)(2,1)S(1)}, u32[]{:S(2)}) copy-start(bf16[2,4,64,1024]{3,2,0,1:T(8,128)(2,1)S(1)} %copy.101) | copy-start | bytes 3145732
  126.1 3.5 copy-start.41
  153.4 12.2 %copy-start.66 = (f32[512]{0:T(512)}, f32[512]{0:T(512)S(1)}, u32[]{:S(2)}) copy-start(f32[512]{0:T(512)S(1)} %broadcast_multiply_fusion.3) | copy-start | bytes 6148
  154.2 11.3 %copy-start.68 = (f32[512]{0:T(512)}, f32[512]{0:T(512)S(1)}, u32[]{:S(2)}) copy-start(f32[512]{0:T(512)S(1)} %fusion.150) | copy-start | bytes 6148
  154.6 10.9 %collective-permute-start.3 = (bf16[512,1024]{1,0:T(8,128)(2,1)S(1)}, bf16[512,1024]{1,0:T(8,128)(2,1)S(1)}, u32[]{:S(2)}, u32[]{:S(2)}) collective-permute-start(bf16[512,1024]{1,0:T(8,128)(2,1)S(1)} %multiply_convert_fusion.6), channel_id=1, source_target_pairs={{0,4},{1,5},{2,6},{3,7},{4,0},{5,1},{6,2},{7,3},{8,12},{9,13},{10,... | collective-permute-start | bytes 3145736 | tf_op jit(solution)/shard_map/ppermute | solution.py:1008
  161.0 3.9 copy-start.31
  161.0 3.9 copy-start.33
  166.1 4.6 copy-start.50
  166.2 4.6 copy-start.52
  173.0 102.7 %collective-permute-start.5 = (bf16[4,512,1024]{2,1,0:T(8,128)(2,1)}, bf16[4,512,1024]{2,1,0:T(8,128)(2,1)}, u32[]{:S(2)}, u32[]{:S(2)}) collective-permute-start(bf16[4,512,1024]{2,1,0:T(8,128)(2,1)} %bitcast.229), channel_id=1, source_target_pairs={{0,4},{1,5},{2,6},{3,7},{4,0},{5,1},{6,2},{7,3},{8,12},{9,13},{10,... | collective-permute-start | bytes 12582920 | tf_op jit(solution)/shard_map/ppermute | solution.py:1008
  173.6 90.2 %copy-start.63 = (bf16[31,1024]{1,0:T(8,128)(2,1)S(1)}, bf16[31,1024]{1,0:T(8,128)(2,1)}, u32[]{:S(2)}) copy-start(bf16[31,1024]{1,0:T(8,128)(2,1)} %param.41) | copy-start | bytes 190468
  173.6 90.2 %copy-start.88 = (bf16[1024]{0:T(1024)(128)(2,1)S(1)}, bf16[1024]{0:T(1024)(128)(2,1)}, u32[]{:S(2)}) copy-start(bf16[1024]{0:T(1024)(128)(2,1)} %param.39) | copy-start | bytes 6148
  173.6 90.2 %copy-start.89 = (bf16[1024]{0:T(1024)(128)(2,1)S(1)}, bf16[1024]{0:T(1024)(128)(2,1)}, u32[]{:S(2)}) copy-start(bf16[1024]{0:T(1024)(128)(2,1)} %param.42) | copy-start | bytes 6148
  173.6 90.3 %copy-start.90 = (bf16[1024]{0:T(1024)(128)(2,1)S(1)}, bf16[1024]{0:T(1024)(128)(2,1)}, u32[]{:S(2)}) copy-start(bf16[1024]{0:T(1024)(128)(2,1)} %param.44) | copy-start | bytes 6148
  173.6 90.9 %copy-start.91 = (bf16[1024]{0:T(1024)(128)(2,1)S(1)}, bf16[1024]{0:T(1024)(128)(2,1)}, u32[]{:S(2)}) copy-start(bf16[1024]{0:T(1024)(128)(2,1)} %param.47) | copy-start | bytes 6148
  173.6 91.6 %copy-start.27 = (bf16[2,256,1024]{2,1,0:T(8,128)(2,1)S(1)}, bf16[2,256,1024]{2,1,0:T(8,128)(2,1)}, u32[]{:S(2)}) copy-start(bf16[2,256,1024]{2,1,0:T(8,128)(2,1)} %multiply_convert_fusion.7) | copy-start | bytes 3145732
  263.8 6.6 collective-permute-start.4
  264.5 5.9 copy-start.49
  266.3 25.2 %collective-permute-start.7 = (bf16[256,1024]{1,0:T(8,128)(2,1)}, bf16[256,1024]{1,0:T(8,128)(2,1)}, u32[]{:S(2)}, u32[]{:S(2)}) collective-permute-start(bf16[256,1024]{1,0:T(8,128)(2,1)} %get-tuple-element.197), channel_id=1, source_target_pairs={{2,4},{3,5},{4,2},{5,3},{10,12},{11,13},{12,10},{13,11},{18,20},{1... | collective-permute-start | bytes 1572872 | tf_op jit(solution)/shard_map/ppermute | solution.py:1017
  267.8 23.8 %collective-permute-start.8 = (bf16[256,1024]{1,0:T(8,128)(2,1)}, bf16[256,1024]{1,0:T(8,128)(2,1)}, u32[]{:S(2)}, u32[]{:S(2)}) collective-permute-start(bf16[256,1024]{1,0:T(8,128)(2,1)} %get-tuple-element.198), channel_id=1, source_target_pairs={{0,1},{1,0},{2,5},{3,4},{4,3},{5,2},{6,7},{7,6},{8,9},{9,8},{10,13... | collective-permute-start | bytes 1572872 | tf_op jit(solution)/shard_map/ppermute | solution.py:1017
  275.7 6.4 copy-start.29
  289.2 87.2 %copy-start.4 = (bf16[512,1024]{1,0:T(8,128)(2,1)}, bf16[512,1024]{1,0:T(8,128)(2,1)S(1)}, u32[]{:S(2)}) copy-start(bf16[512,1024]{1,0:T(8,128)(2,1)S(1)} %multiply_convert_fusion.4) | copy-start | bytes 3145732
  289.3 4.5 copy-start.30
  289.3 5.9 collective-permute-start.6
  295.2 10.6 %copy-start.55 = (bf16[15,1024]{1,0:T(8,128)(2,1)}, bf16[15,1024]{1,0:T(8,128)(2,1)S(1)}, u32[]{:S(2)}) copy-start(bf16[15,1024]{1,0:T(8,128)(2,1)S(1)} %get-tuple-element.242) | copy-start | bytes 92164
  295.2 81.3 %copy-start.57 = (bf16[15,1024]{1,0:T(8,128)(2,1)}, bf16[15,1024]{1,0:T(8,128)(2,1)S(1)}, u32[]{:S(2)}) copy-start(bf16[15,1024]{1,0:T(8,128)(2,1)S(1)} %get-tuple-element.243) | copy-start | bytes 92164
  295.2 10.6 %copy-start.15 = (f32[512,1024]{1,0:T(8,128)S(1)}, f32[512,1024]{1,0:T(8,128)}, u32[]{:S(2)}) copy-start(f32[512,1024]{1,0:T(8,128)} %copy-done.14) | copy-start | bytes 6291460
  295.2 10.6 %copy-start.38 = (bf16[4,2,128,1024]{3,2,1,0:T(8,128)(2,1)S(1)}, bf16[4,2,128,1024]{3,2,1,0:T(8,128)(2,1)}, u32[]{:S(2)}) copy-start(bf16[4,2,128,1024]{3,2,1,0:T(8,128)(2,1)} %get-tuple-element.160) | copy-start | bytes 6291460
  305.4 3.3 copy-start.11
  331.2 39.2 %collective-permute-start.10 = (bf16[256,1024]{1,0:T(8,128)(2,1)S(1)}, bf16[256,1024]{1,0:T(8,128)(2,1)S(1)}, u32[]{:S(2)}, u32[]{:S(2)}) collective-permute-start(bf16[256,1024]{1,0:T(8,128)(2,1)S(1)} %get-tuple-element.196), channel_id=1, source_target_pairs={{0,1},{1,0},{2,5},{3,4},{4,3},{5,2},{6,7},{7,6},{8,9},{9,8},{10,13... | collective-permute-start | bytes 1572872 | tf_op jit(solution)/shard_map/ppermute | solution.py:1017
  331.3 39.2 %collective-permute-start.9 = (bf16[256,1024]{1,0:T(8,128)(2,1)S(1)}, bf16[256,1024]{1,0:T(8,128)(2,1)S(1)}, u32[]{:S(2)}, u32[]{:S(2)}) collective-permute-start(bf16[256,1024]{1,0:T(8,128)(2,1)S(1)} %get-tuple-element.195), channel_id=1, source_target_pairs={{2,4},{3,5},{4,2},{5,3},{10,12},{11,13},{12,10},{13,11},{18,20},{1... | collective-permute-start | bytes 1572872 | tf_op jit(solution)/shard_map/ppermute | solution.py:1017
  353.0 10.4 %copy-start.97 = (bf16[512,4096]{1,0:T(8,128)(2,1)S(1)}, bf16[512,4096]{1,0:T(8,128)(2,1)}, u32[]{:S(2)}) copy-start(bf16[512,4096]{1,0:T(8,128)(2,1)} %get-tuple-element.82) | copy-start | bytes 12582916
  353.0 10.4 %copy-start.99 = (bf16[512,1024]{1,0:T(8,128)(2,1)S(1)}, bf16[512,1024]{1,0:T(8,128)(2,1)}, u32[]{:S(2)}) copy-start(bf16[512,1024]{1,0:T(8,128)(2,1)} %get-tuple-element.83) | copy-start | bytes 3145732
  363.4 8.2 %copy-start.39 = (bf16[4,2,128,1024]{3,2,1,0:T(8,128)(2,1)S(1)}, bf16[4,2,128,1024]{3,2,1,0:T(8,128)(2,1)}, u32[]{:S(2)}) copy-start(bf16[4,2,128,1024]{3,2,1,0:T(8,128)(2,1)} %get-tuple-element.160) | copy-start | bytes 6291460
  384.6 5.9 collective-permute-start.11
  417.6 6.2 copy-start.17
  428.1 5.5 collective-permute-start.12
  434.7 131.6 %copy-start.51 = (bf16[512,1024]{1,0:T(8,128)(2,1)S(1)}, bf16[512,1024]{1,0:T(8,128)(2,1)}, u32[]{:S(2)}) copy-start(bf16[512,1024]{1,0:T(8,128)(2,1)} %copy-done.50) | copy-start | bytes 3145732
  434.7 131.6 %copy-start.53 = (bf16[512,1024]{1,0:T(8,128)(2,1)S(1)}, bf16[512,1024]{1,0:T(8,128)(2,1)}, u32[]{:S(2)}) copy-start(bf16[512,1024]{1,0:T(8,128)(2,1)} %copy-done.52) | copy-start | bytes 3145732
  577.3 3.7 copy-start.56
  578.5 5.2 copy-start.45
  578.5 5.2 copy-start.96
  587.8 3.2 copy-start.9
  589.1 6.7 collective-permute-start.13
  595.8 3.1 copy-start.10
  622.5 8.9 %collective-permute-start.14 = (bf16[256,1024]{1,0:T(8,128)(2,1)S(1)}, bf16[256,1024]{1,0:T(8,128)(2,1)S(1)}, u32[]{:S(2)}, u32[]{:S(2)}) collective-permute-start(bf16[256,1024]{1,0:T(8,128)(2,1)S(1)} %get-tuple-element.189), channel_id=1, source_target_pairs={{2,4},{3,5},{4,2},{5,3},{10,12},{11,13},{12,10},{13,11},{18,20},{1... | collective-permute-start | bytes 1572872 | tf_op jit(solution)/shard_map/ppermute | solution.py:1017
  623.4 19.8 %collective-permute-start.15 = (bf16[256,1024]{1,0:T(8,128)(2,1)S(1)}, bf16[256,1024]{1,0:T(8,128)(2,1)}, u32[]{:S(2)}, u32[]{:S(2)}) collective-permute-start(bf16[256,1024]{1,0:T(8,128)(2,1)S(1)} %get-tuple-element.190), channel_id=1, source_target_pairs={{0,1},{1,0},{2,5},{3,4},{4,3},{5,2},{6,7},{7,6},{8,9},{9,8},{10,13... | collective-permute-start | bytes 1572872 | tf_op jit(solution)/shard_map/ppermute | solution.py:1017
  770.6 4.0 copy-start.62
  771.7 3.7 copy-start.61
  772.9 3.4 copy-start.60
  772.9 4.2 copy-start.59
  774.6 3.2 copy-start.1
  (54 other events, 120.5 us)
Sparse Core Ops, SparseCore 0:
  109.5 58.2 all-gather.2
  577.4 59.6 reduce-scatter.3

commit v6 on v5

--- a/solution.py
+++ b/solution.py
@@ -15,7 +15,7 @@
 PAIR = 128
 ROWS_FWD = 256
 ROWS_BWD = 256
-FF_BLOCK = 512
+FF_BLOCK = 1024
 VMEM = 58 * 2**20
 
 

time: 791 us -> 785 us (level)
  no operation moved by 1% of the time
where the time goes in v6:
time: 785 us; the launch traced here: 780 us
  Pallas kernels  500 us (64%)
  other arithmetic  99.8 us (13%)
  local copies, waits for them, and re-layouts  67.4 us (9%)
  matrix products  58.6 us (7%)
  starting transfers between devices  22.4 us (3%)
  waiting for transfers between devices  15.8 us (2%)
  between operations  15.8 us (2%)
    pallas_call x1, Pallas kernels, attend_bwd(): pl.pallas_call(partial(attend_bwd_sum_kernel, layers, shared, count, pair...  132 us
    pallas_call x1, Pallas kernels, reduce_all(): pl.pallas_call(partial(reduce_kernel, layers), in_specs=[near] * 6, out_s...  118 us
    pallas_call x1, Pallas kernels, gather_all(): pl.pallas_call(partial(gather_kernel, layers, count), in_specs=[pl.BlockS...  94.6 us
    pallas_call x1, Pallas kernels, attend_fwd(): pl.pallas_call(partial(attend_fwd_gather_kernel, layers, count, blocks, s...  88.7 us
    pallas_call x2, Pallas kernels, ffn_bwd(): pl.pallas_call(ffn_bwd_kernel, grid=(total // FF_BLOCK,), in_specs=[still...  36.3 us
    pallas_call x2, Pallas kernels, ffn_fwd(): pl.pallas_call(ffn_fwd_kernel, grid=(total // FF_BLOCK,), in_specs=[still...  31.1 us
    dot_general x9, matrix products, mult_rows(): lax.dot_general(first_mat, second_mat, (((0,), (0,)), ((), ())), preferre...  30.2 us
    unnamed x218, local copies, waits for them, and re-layouts  29.1 us
  transfers between devices with their start and end apart: 18, of which 2 were waited for; matrix products, arithmetic and copies ran while one was open for 15% of the time, Pallas kernels for 18%

profile of v6, /device:TPU:8, one launch (start us, length us, event | category | flops | bytes accessed | tf_op | source)
XLA Modules:
  0.0 780.4 jit_solution(6519894555943130526)
XLA Ops:
  13.8 94.6 %gather_all.1 = (bf16[4,2,2,2,128,1024]{5,4,3,2,1,0:T(8,128)(2,1)}, bf16[4,2,2,2,128,1024]{5,4,3,2,1,0:T(8,128)(2,1)}, bf16[2,2,2,272,1024]{4,3,2,1,0:T(8,128)(2,1)}) custom-call(bf16[128,1024]{1,0:T(8,128)(2,1)} %refs_0_.1, bf16[128,1024]{1,0:T(8,128)(2,1)} %refs_1_.1, bf16[272,1024]{1,0:T(8,128)(2,1)} %copy-done.54), custom_call_target="tpu_custom_call" | custom-call | bytes 314572800 | tf_op jit(solution)/shard_map/gather_all/pallas_call | solution.py:572
  110.5 1.5 collective-permute-start
  112.0 1.5 collective-permute-start.1
  113.5 2.1 collective-permute-start.2
  116.8 4.6 fusion.168
  134.2 15.9 %ffn_fwd.2 = (f32[512,1024]{1,0:T(8,128)}, bf16[512,1024]{1,0:T(8,128)(2,1)}, bf16[512,4096]{1,0:T(8,128)(2,1)}, bf16[512,4096]{1,0:T(8,128)(2,1)}) custom-call(bf16[512,1024]{1,0:T(8,128)(2,1)} %pad_maximum_fusion.17.x_ref, bf16[1,1024]{1,0:T(2,128)(2,1)} %broadcast_in_dim.22.gain_ref, bf16[4096,1024]{1,0:T(8,128)(2,1)} %bitcast.369, ...), custom_call_target="tpu_custom_call" | custom-call | flops 8589934592 | bytes 25165824 | tf_op jit(solution)/shard_map/ffn_fwd/pallas_call | solution.py:929
  150.1 1.9 reduce_sum.507
  153.5 3.6 collective-permute-start.3
  157.1 1.5 subtract_convert_fusion
  158.7 3.9 convolution_convert_fusion.3.refs_4_.refs_3_
  163.9 2.3 convolution_convert_fusion.10.refs_3_.refs_2_
  166.1 2.3 convolution_convert_fusion.11.refs_2_.refs_1_
  168.4 2.3 convolution_convert_fusion.12.refs_1_.refs_0_
  171.3 88.7 %attend_fwd.1 = (bf16[1024,512]{1,0:T(8,128)(2,1)}, bf16[8,1024,1024]{2,1,0:T(8,128)(2,1)}, bf16[4,2,2,2,128,1024]{5,4,3,2,1,0:T(8,128)(2,1)}, bf16[4,2,2,2,128,1024]{5,4,3,2,1,0:T(8,128)(2,1)}) custom-call(s32[1]{0:T(128)} %dynamic_slice.62.refs_0_, bf16[1024,512]{1,0:T(8,128)(2,1)} %convolution_convert_fusion.12.refs_1_.refs_0_, ...), custom_call_target="tpu_custom_call" | custom-call | flops 40000000000 | bytes 20971520 | tf_op jit(solution)/shard_map/attend_fwd/pallas_call | solution.py:279
  260.1 1.9 constant_dynamic-slice_fusion.2
  264.5 1.5 collective-permute-start.7
  265.9 3.2 collective-permute-start.8
  274.5 4.1 select_bitcast_fusion.1
  278.7 1.8 pad_maximum_fusion.5
  281.9 1.4 fusion.176
  283.6 2.4 fusion.160
  286.7 1.4 copy-done.7
  288.1 2.3 collective-permute-start.6
  290.3 2.3 broadcast_select_fusion.15
  294.0 10.2 %fusion.166 = (f32[512]{0:T(512)S(1)}, f32[512,1024]{1,0:T(8,128)S(1)}) fusion(f32[1024]{0:T(1024)S(1)} %bitcast.280, bf16[15,1024]{1,0:T(8,128)(2,1)S(1)} %get-tuple-element.243, bf16[512,1024]{1,0:T(8,128)(2,1)S(1)} %multiply_convert_fusion.4, f32[1024]{0:T(1024)S(1)} %bitcast.278, f32[1024]{0:T(1024)S(1)} %bitcast.276, f32[1024]{0:T(1024)S(1)} %bitcast.274, ...), kind=kLoop, calls=%fused_computation.463 | loop fusion | flops 95944192 | bytes 3336192 | tf_op jit(solution)/shard_map/jvp()/reduce_sum | solution.py:40
  304.6 2.9 convolution_add_fusion.x_ref
  307.5 15.2 %ffn_fwd.3 = (f32[512,1024]{1,0:T(8,128)}, bf16[512,1024]{1,0:T(8,128)(2,1)}, bf16[512,4096]{1,0:T(8,128)(2,1)}, bf16[512,4096]{1,0:T(8,128)(2,1)}) custom-call(f32[512,1024]{1,0:T(8,128)} %convolution_add_fusion.x_ref, bf16[1,1024]{1,0:T(2,128)(2,1)} %broadcast_in_dim.23.gain_ref, bf16[4096,1024]{1,0:T(8,128)(2,1)} %bitcast.374, bf16[4096,1024]{1,0:T(8,128)(2,1)} %bitcast.376), custom_call_target="tpu_custom_call" | custom-call | flops 8589934592 | bytes 25165824 | tf_op jit(solution)/shard_map/ffn_fwd/pallas_call | solution.py:929
  322.8 1.9 reduce_sum.513
  326.0 1.4 fusion.35
  329.1 1.5 broadcast_add_fusion.g_ref
  330.7 18.3 %ffn_bwd.2 = (f32[512,1024]{1,0:T(8,128)}, bf16[512,1024]{1,0:T(8,128)(2,1)}, bf16[512,4096]{1,0:T(8,128)(2,1)}, f32[1,1024]{1,0:T(1,128)}) custom-call(f32[512,1024]{1,0:T(8,128)} %convolution_add_fusion.x_ref, bf16[1,1024]{1,0:T(2,128)(2,1)} %broadcast_in_dim.23.gain_ref, f32[512,1024]{1,0:T(8,128)} %broadcast_add_fusion.g_ref, ...), custom_call_target="tpu_custom_call" | custom-call | flops 8589934592 | bytes 25165824 | tf_op jit(solution)/shard_map/ffn_bwd/pallas_call | solution.py:975
  349.0 10.4 %convolution_convert_fusion = bf16[4096,1024]{1,0:T(8,128)(2,1)} fusion(bf16[512,4096]{1,0:T(8,128)(2,1)} %get-tuple-element.84, bf16[512,1024]{1,0:T(8,128)(2,1)} %get-tuple-element.85), kind=kOutput, calls=%fused_computation.35 | convolution fusion | flops 4299161600 | bytes 13631488 | tf_op jit(solution)/shard_map/dot_general | solution.py:62
  359.4 6.9 convolution_convert_fusion.1
  369.0 2.7 multiply_reduce_fusion.1
  372.4 8.1 %fusion.82 = (f32[1024]{0:T(1024)}, f32[1024]{0:T(1024)}, f32[1024]{0:T(1024)}, f32[1024]{0:T(1024)}, f32[1024]{0:T(1024)}, /*index=5*/f32[1024]{0:T(1024)}, f32...) fusion(bf16[15,1024]{1,0:T(8,128)(2,1)S(1)} %get-tuple-element.243, ...), kind=kLoop, calls=%fused_computation.222 | loop fusion | flops 29875200 | bytes 4263936 | tf_op jit(solution)/shard_map/reduce_sum | solution.py:1218
  380.6 2.7 collective-permute-start.11
  383.3 1.6 convolution_convert_fusion.4
  384.9 1.6 copy.126
  387.8 16.0 %multiply_convert_fusion.1 = (bf16[512,1024]{1,0:T(8,128)(2,1)S(1)}, f32[512,1024]{1,0:T(8,128)S(1)}) fusion(f32[512,2048]{1,0:T(8,128)S(1)} %copy-done.8, f32[512]{0:T(512)S(1)} %fusion.149, f32[1024]{0:T(1024)S(1)} %bitcast.283, bf16[15,1024]{1,0:T(8,128)(2,1)S(1)} %get-tuple-element.241, bf16[512,1024]{1,0:T(8,128)(2,1)S(1)} %get-tuple-element.147, ...), kind=kLoop, calls=%fused_computation.244 | loop fusion | flops 98566144 | bytes 6481920 | tf_op jit(solution)/shard_map/convert.7
  406.7 3.3 multiply_reduce_fusion.2
  410.0 2.5 convolution_convert_fusion.2
  415.8 1.5 copy.127
  417.3 2.5 copy.125
  421.9 1.5 fusion.171
  424.1 1.6 copy-done.13
  425.8 3.8 pad_maximum_fusion
  430.7 131.6 %attend_bwd.1 = (bf16[1024,512]{1,0:T(8,128)(2,1)}, bf16[1024,512]{1,0:T(8,128)(2,1)}, bf16[1024,512]{1,0:T(8,128)(2,1)}, bf16[2048,512]{1,0:T(8,128)(2,1)}, f32...) custom-call(bf16[1024,512]{1,0:T(8,128)(2,1)} %convolution_convert_fusion.12.refs_, ...), custom_call_target="tpu_custom_call" | custom-call | flops 99999997952 | bytes 41943040 | tf_op jit(solution)/shard_map/attend_bwd/pallas_call | solution.py:378
  562.3 2.6 convolution_convert_fusion.8
  568.6 2.3 fusion.87
  570.9 2.3 pad_maximum_fusion.2
  574.4 2.5 fusion.81
  576.9 2.7 fusion.66
  585.1 1.9 fusion.65
  589.2 1.6 fusion.169
  591.9 2.8 multiply_reduce_fusion
  596.8 1.6 add_add_fusion.5.g_ref
  598.4 18.0 %ffn_bwd.3 = (bf16[512,1024]{1,0:T(8,128)(2,1)}, bf16[512,1024]{1,0:T(8,128)(2,1)}, bf16[512,4096]{1,0:T(8,128)(2,1)}, f32[1,1024]{1,0:T(1,128)}) custom-call(bf16[512,1024]{1,0:T(8,128)(2,1)} %pad_maximum_fusion.17.x_ref, bf16[1,1024]{1,0:T(2,128)(2,1)} %broadcast_in_dim.22.gain_ref, f32[512,1024]{1,0:T(8,128)} %add_add_fusion.5.g_ref, ...), custom_call_target="tpu_custom_call" | custom-call | flops 8589934592 | bytes 25165824 | tf_op jit(solution)/shard_map/ffn_bwd/pallas_call | solution.py:975
  618.5 1.7 collective-permute-start.15
  621.4 1.6 bitcast_convert_fusion
  624.1 14.7 %collective-permute-done.15 = bf16[256,1024]{1,0:T(8,128)(2,1)} collective-permute-done((bf16[256,1024]{1,0:T(8,128)(2,1)S(1)}, bf16[256,1024]{1,0:T(8,128)(2,1)}, u32[]{:S(2)}, u32[]{:S(2)}) %collective-permute-start.15) | collective-permute-done | bytes 524320 | tf_op jit(solution)/shard_map/ppermute | solution.py:1017
  641.0 118.2 %reduce_all.1 = (f32[128,1024]{1,0:T(8,128)}, f32[128,1024]{1,0:T(8,128)}, bf16[2,4,128,1024]{3,2,1,0:T(8,128)(2,1)}, f32[40,1024]{1,0:T(8,128)}) custom-call(bf16[4,128,1024]{2,1,0:T(8,128)(2,1)} %bitcast.373, bf16[512,4096]{1,0:T(8,128)(2,1)} %get-tuple-element.94.left_a, bf16[512,1024]{1,0:T(8,128)(2,1)} %get-tuple-element.95.right_a, ...), custom_call_target="tpu_custom_call" | custom-call | flops 8000000000 | bytes 314572800 | tf_op jit(solution)/shard_map/reduce_all/pallas_call | solution.py:850
  759.2 1.6 slice.697
  761.5 1.7 fusion.172
  763.2 1.7 fusion.170
  (348 shorter events, 86.4 us)
Async XLA Ops:
  7.2 6.5 copy-start
  7.2 163.5 %all-gather.3.cloned.1.call-start = ((), (), s32[]{:S(2)}) async-start(), calls=%async_computation.1 | async-start | bytes 5242880 | tf_op jit(solution)/shard_map/all_gather | solution.py:1130
  13.8 95.7 %copy-start.48 = (bf16[2,256,1024]{2,1,0:T(8,128)(2,1)S(1)}, bf16[2,256,1024]{2,1,0:T(8,128)(2,1)}, u32[]{:S(2)}) copy-start(bf16[2,256,1024]{2,1,0:T(8,128)(2,1)} %param.24) | copy-start | bytes 3145732
  109.4 4.1 copy-start.93
  109.4 7.0 copy-start.92
  109.4 531.6 %reduce-scatter.4.cloned.1.call-start = ((), (), s32[]{:S(2)}) async-start(), calls=%async_computation.2 | async-start | bytes 5242880
  110.5 20.2 %collective-permute-start = (bf16[256,1024]{1,0:T(8,128)(2,1)}, bf16[256,1024]{1,0:T(8,128)(2,1)}, u32[]{:S(2)}, u32[]{:S(2)}) collective-permute-start(bf16[256,1024]{1,0:T(8,128)(2,1)} %get-tuple-element.199), channel_id=1, source_target_pairs={{2,4},{3,5},{4,2},{5,3},{10,12},{11,13},{12,10},{13,11},{18,20},{1... | collective-permute-start | bytes 1572872 | tf_op jit(solution)/shard_map/ppermute | solution.py:1017
  112.0 19.8 %collective-permute-start.1 = (bf16[256,1024]{1,0:T(8,128)(2,1)}, bf16[256,1024]{1,0:T(8,128)(2,1)}, u32[]{:S(2)}, u32[]{:S(2)}) collective-permute-start(bf16[256,1024]{1,0:T(8,128)(2,1)} %get-tuple-element.200), channel_id=1, source_target_pairs={{0,1},{1,0},{2,5},{3,4},{4,3},{5,2},{6,7},{7,6},{8,9},{9,8},{10,13... | collective-permute-start | bytes 1572872 | tf_op jit(solution)/shard_map/ppermute | solution.py:1017
  113.5 49.0 %collective-permute-start.2 = (s32[2]{0:T(128)S(1)}, s32[2]{0:T(128)}, u32[]{:S(2)}, u32[]{:S(2)}) collective-permute-start(s32[2]{0:T(128)S(1)} %copy-done.93), channel_id=1, source_target_pairs={{0,4},{1,5},{2,6},{3,7},{4,0},{5,1},{6,2},{7,3},{8,12},{9,13},{10,... | collective-permute-start | bytes 32 | tf_op jit(solution)/shard_map/ppermute | solution.py:1008
  116.8 5.1 copy-start.86
  116.8 5.7 copy-start.87
  122.5 40.7 %copy-start.64 = (f32[1024]{0:T(1024)}, f32[1024]{0:T(1024)S(1)}, u32[]{:S(2)}) copy-start(f32[1024]{0:T(1024)S(1)} %convert_element_type.398) | copy-start | bytes 12292
  123.8 40.0 %copy-start.23 = (bf16[2,4,64,1024]{3,2,0,1:T(8,128)(2,1)}, bf16[2,4,64,1024]{3,2,0,1:T(8,128)(2,1)S(1)}, u32[]{:S(2)}) copy-start(bf16[2,4,64,1024]{3,2,0,1:T(8,128)(2,1)S(1)} %copy.101) | copy-start | bytes 3145732
  126.1 3.5 copy-start.41
  152.3 10.9 %copy-start.66 = (f32[512]{0:T(512)}, f32[512]{0:T(512)S(1)}, u32[]{:S(2)}) copy-start(f32[512]{0:T(512)S(1)} %broadcast_multiply_fusion.3) | copy-start | bytes 6148
  153.2 10.0 %copy-start.68 = (f32[512]{0:T(512)}, f32[512]{0:T(512)S(1)}, u32[]{:S(2)}) copy-start(f32[512]{0:T(512)S(1)} %fusion.150) | copy-start | bytes 6148
  153.5 9.7 %collective-permute-start.3 = (bf16[512,1024]{1,0:T(8,128)(2,1)S(1)}, bf16[512,1024]{1,0:T(8,128)(2,1)S(1)}, u32[]{:S(2)}, u32[]{:S(2)}) collective-permute-start(bf16[512,1024]{1,0:T(8,128)(2,1)S(1)} %multiply_convert_fusion.6), channel_id=1, source_target_pairs={{0,4},{1,5},{2,6},{3,7},{4,0},{5,1},{6,2},{7,3},{8,12},{9,13},{10,... | collective-permute-start | bytes 3145736 | tf_op jit(solution)/shard_map/ppermute | solution.py:1008
  158.7 3.9 copy-start.31
  158.7 3.9 copy-start.33
  163.8 4.6 copy-start.50
  163.8 4.6 copy-start.52
  170.7 103.9 %collective-permute-start.5 = (bf16[4,512,1024]{2,1,0:T(8,128)(2,1)}, bf16[4,512,1024]{2,1,0:T(8,128)(2,1)}, u32[]{:S(2)}, u32[]{:S(2)}) collective-permute-start(bf16[4,512,1024]{2,1,0:T(8,128)(2,1)} %bitcast.229), channel_id=1, source_target_pairs={{0,4},{1,5},{2,6},{3,7},{4,0},{5,1},{6,2},{7,3},{8,12},{9,13},{10,... | collective-permute-start | bytes 12582920 | tf_op jit(solution)/shard_map/ppermute | solution.py:1008
  171.3 90.7 %copy-start.63 = (bf16[31,1024]{1,0:T(8,128)(2,1)S(1)}, bf16[31,1024]{1,0:T(8,128)(2,1)}, u32[]{:S(2)}) copy-start(bf16[31,1024]{1,0:T(8,128)(2,1)} %param.41) | copy-start | bytes 190468
  171.3 90.7 %copy-start.88 = (bf16[1024]{0:T(1024)(128)(2,1)S(1)}, bf16[1024]{0:T(1024)(128)(2,1)}, u32[]{:S(2)}) copy-start(bf16[1024]{0:T(1024)(128)(2,1)} %param.39) | copy-start | bytes 6148
  171.3 90.7 %copy-start.89 = (bf16[1024]{0:T(1024)(128)(2,1)S(1)}, bf16[1024]{0:T(1024)(128)(2,1)}, u32[]{:S(2)}) copy-start(bf16[1024]{0:T(1024)(128)(2,1)} %param.42) | copy-start | bytes 6148
  171.3 90.8 %copy-start.90 = (bf16[1024]{0:T(1024)(128)(2,1)S(1)}, bf16[1024]{0:T(1024)(128)(2,1)}, u32[]{:S(2)}) copy-start(bf16[1024]{0:T(1024)(128)(2,1)} %param.44) | copy-start | bytes 6148
  171.3 91.4 %copy-start.91 = (bf16[1024]{0:T(1024)(128)(2,1)S(1)}, bf16[1024]{0:T(1024)(128)(2,1)}, u32[]{:S(2)}) copy-start(bf16[1024]{0:T(1024)(128)(2,1)} %param.47) | copy-start | bytes 6148
  171.3 92.1 %copy-start.27 = (bf16[2,256,1024]{2,1,0:T(8,128)(2,1)S(1)}, bf16[2,256,1024]{2,1,0:T(8,128)(2,1)}, u32[]{:S(2)}) copy-start(bf16[2,256,1024]{2,1,0:T(8,128)(2,1)} %multiply_convert_fusion.7) | copy-start | bytes 3145732
  261.9 7.2 collective-permute-start.4
  262.6 6.5 copy-start.49
  264.5 25.9 %collective-permute-start.7 = (bf16[256,1024]{1,0:T(8,128)(2,1)}, bf16[256,1024]{1,0:T(8,128)(2,1)}, u32[]{:S(2)}, u32[]{:S(2)}) collective-permute-start(bf16[256,1024]{1,0:T(8,128)(2,1)} %get-tuple-element.197), channel_id=1, source_target_pairs={{2,4},{3,5},{4,2},{5,3},{10,12},{11,13},{12,10},{13,11},{18,20},{1... | collective-permute-start | bytes 1572872 | tf_op jit(solution)/shard_map/ppermute | solution.py:1017
  265.9 24.4 %collective-permute-start.8 = (bf16[256,1024]{1,0:T(8,128)(2,1)}, bf16[256,1024]{1,0:T(8,128)(2,1)}, u32[]{:S(2)}, u32[]{:S(2)}) collective-permute-start(bf16[256,1024]{1,0:T(8,128)(2,1)} %get-tuple-element.198), channel_id=1, source_target_pairs={{0,1},{1,0},{2,5},{3,4},{4,3},{5,2},{6,7},{7,6},{8,9},{9,8},{10,13... | collective-permute-start | bytes 1572872 | tf_op jit(solution)/shard_map/ppermute | solution.py:1017
  274.5 6.4 copy-start.29
  288.1 84.3 %copy-start.4 = (bf16[512,1024]{1,0:T(8,128)(2,1)}, bf16[512,1024]{1,0:T(8,128)(2,1)S(1)}, u32[]{:S(2)}) copy-start(bf16[512,1024]{1,0:T(8,128)(2,1)S(1)} %multiply_convert_fusion.4) | copy-start | bytes 3145732
  288.1 4.5 copy-start.30
  288.1 5.9 collective-permute-start.6
  294.0 10.6 %copy-start.55 = (bf16[15,1024]{1,0:T(8,128)(2,1)}, bf16[15,1024]{1,0:T(8,128)(2,1)S(1)}, u32[]{:S(2)}) copy-start(bf16[15,1024]{1,0:T(8,128)(2,1)S(1)} %get-tuple-element.242) | copy-start | bytes 92164
  294.0 78.4 %copy-start.57 = (bf16[15,1024]{1,0:T(8,128)(2,1)}, bf16[15,1024]{1,0:T(8,128)(2,1)S(1)}, u32[]{:S(2)}) copy-start(bf16[15,1024]{1,0:T(8,128)(2,1)S(1)} %get-tuple-element.243) | copy-start | bytes 92164
  294.0 10.6 %copy-start.15 = (f32[512,1024]{1,0:T(8,128)S(1)}, f32[512,1024]{1,0:T(8,128)}, u32[]{:S(2)}) copy-start(f32[512,1024]{1,0:T(8,128)} %copy-done.14) | copy-start | bytes 6291460
  294.0 10.6 %copy-start.38 = (bf16[4,2,128,1024]{3,2,1,0:T(8,128)(2,1)S(1)}, bf16[4,2,128,1024]{3,2,1,0:T(8,128)(2,1)}, u32[]{:S(2)}) copy-start(bf16[4,2,128,1024]{3,2,1,0:T(8,128)(2,1)} %get-tuple-element.160) | copy-start | bytes 6291460
  304.2 3.3 copy-start.11
  328.3 38.1 %collective-permute-start.10 = (bf16[256,1024]{1,0:T(8,128)(2,1)S(1)}, bf16[256,1024]{1,0:T(8,128)(2,1)S(1)}, u32[]{:S(2)}, u32[]{:S(2)}) collective-permute-start(bf16[256,1024]{1,0:T(8,128)(2,1)S(1)} %get-tuple-element.196), channel_id=1, source_target_pairs={{0,1},{1,0},{2,5},{3,4},{4,3},{5,2},{6,7},{7,6},{8,9},{9,8},{10,13... | collective-permute-start | bytes 1572872 | tf_op jit(solution)/shard_map/ppermute | solution.py:1017
  328.4 38.0 %collective-permute-start.9 = (bf16[256,1024]{1,0:T(8,128)(2,1)S(1)}, bf16[256,1024]{1,0:T(8,128)(2,1)S(1)}, u32[]{:S(2)}, u32[]{:S(2)}) collective-permute-start(bf16[256,1024]{1,0:T(8,128)(2,1)S(1)} %get-tuple-element.195), channel_id=1, source_target_pairs={{2,4},{3,5},{4,2},{5,3},{10,12},{11,13},{12,10},{13,11},{18,20},{1... | collective-permute-start | bytes 1572872 | tf_op jit(solution)/shard_map/ppermute | solution.py:1017
  349.0 10.4 %copy-start.97 = (bf16[512,4096]{1,0:T(8,128)(2,1)S(1)}, bf16[512,4096]{1,0:T(8,128)(2,1)}, u32[]{:S(2)}) copy-start(bf16[512,4096]{1,0:T(8,128)(2,1)} %get-tuple-element.82) | copy-start | bytes 12582916
  349.0 10.4 %copy-start.99 = (bf16[512,1024]{1,0:T(8,128)(2,1)S(1)}, bf16[512,1024]{1,0:T(8,128)(2,1)}, u32[]{:S(2)}) copy-start(bf16[512,1024]{1,0:T(8,128)(2,1)} %get-tuple-element.83) | copy-start | bytes 3145732
  359.4 8.2 %copy-start.39 = (bf16[4,2,128,1024]{3,2,1,0:T(8,128)(2,1)S(1)}, bf16[4,2,128,1024]{3,2,1,0:T(8,128)(2,1)}, u32[]{:S(2)}) copy-start(bf16[4,2,128,1024]{3,2,1,0:T(8,128)(2,1)} %get-tuple-element.160) | copy-start | bytes 6291460
  380.6 5.9 collective-permute-start.11
  413.6 6.2 copy-start.17
  424.0 5.5 collective-permute-start.12
  430.7 131.6 %copy-start.51 = (bf16[512,1024]{1,0:T(8,128)(2,1)S(1)}, bf16[512,1024]{1,0:T(8,128)(2,1)}, u32[]{:S(2)}) copy-start(bf16[512,1024]{1,0:T(8,128)(2,1)} %copy-done.50) | copy-start | bytes 3145732
  430.7 131.6 %copy-start.53 = (bf16[512,1024]{1,0:T(8,128)(2,1)S(1)}, bf16[512,1024]{1,0:T(8,128)(2,1)}, u32[]{:S(2)}) copy-start(bf16[512,1024]{1,0:T(8,128)(2,1)} %copy-done.52) | copy-start | bytes 3145732
  573.2 3.7 copy-start.56
  574.4 5.2 copy-start.45
  574.4 5.2 copy-start.96
  583.8 3.2 copy-start.9
  585.1 6.8 collective-permute-start.13
  591.9 3.1 copy-start.10
  617.6 6.5 collective-permute-start.14
  618.5 20.4 %collective-permute-start.15 = (bf16[256,1024]{1,0:T(8,128)(2,1)S(1)}, bf16[256,1024]{1,0:T(8,128)(2,1)}, u32[]{:S(2)}, u32[]{:S(2)}) collective-permute-start(bf16[256,1024]{1,0:T(8,128)(2,1)S(1)} %get-tuple-element.190), channel_id=1, source_target_pairs={{0,1},{1,0},{2,5},{3,4},{4,3},{5,2},{6,7},{7,6},{8,9},{9,8},{10,13... | collective-permute-start | bytes 1572872 | tf_op jit(solution)/shard_map/ppermute | solution.py:1017
  766.1 4.0 copy-start.62
  767.2 3.7 copy-start.61
  768.3 3.4 copy-start.60
  768.4 4.2 copy-start.59
  770.1 3.2 copy-start.1
  (54 other events, 121.3 us)
Sparse Core Ops, SparseCore 0:
  109.5 58.2 all-gather.2
  573.3 61.7 reduce-scatter.3
